TPU v7x, 32 devices: a whole 2x2x4 slice. The times are simulated.
32 devices in a mesh: groups: 2 (over x), space: 8 (over z, y), member: 2 (over core).
Axes of the slice: x: 2, y: 2, z: 4, core: 2. Of those that a mesh axis runs over, the one named last changes fastest.
Arguments:
- latents: bfloat16 [8, 256, 1024], P(('groups', 'member'), 'space'), parts along dimension 0, may hold values from -6 to 6
- grid_embed: bfloat16 [4096, 1024], P(('groups', 'space')), parts along dimension 0, may hold values from -40 to 40
- norm_gain: float32 [1024], replicated, may hold values from 0.5 to 1.5
- w_msg: bfloat16 [1024, 1024], replicated, may hold values from -0.1875 to 0.1875
- w_hidden: bfloat16 [1024, 1024], replicated, may hold values from -0.1875 to 0.1875
- variable_projection: bfloat16 [1024, 100], replicated, may hold values from -0.1875 to 0.1875
- present_condition: float32 [8, 100, 2048], P(('groups', 'member'), None, 'space'), parts along dimension 0, may hold values from -6 to 6
- verifying_field: float32 [100, 4096], P(None, ('groups', 'space')), parts along dimension 1, may hold values from -6 to 6
- cell_surface: float32 [4096], P(('groups', 'space')), parts along dimension 0, may hold values from 0.6 to 12.6
- send_rows: int32 [8, 8, 8], P('space'), may hold values from 0 to 31, as said below
- edge_slot: int32 [12288], P('space'), may hold values from 0 to 63, as said below
- edge_dst: int32 [12288], P('space'), may hold values from 0 to 256, as said below
- edge_weight: float32 [12288], P('space'), may hold values from 0.25 to 4
Outputs:
- latent_grad: bfloat16 [8, 256, 1024], P(('groups', 'member'), 'space'), parts along dimension 0
- loss: float32 [2], P('groups'), parts along dimension 0
- msg_weight_grad: float32 [2048, 1024], P(('groups', 'space', 'member')), parts along dimension 0
- hidden_weight_grad: float32 [2048, 1024], P(('groups', 'space', 'member')), parts along dimension 0
- out_weight_grad: float32 [2048, 100], P(('groups', 'space', 'member')), parts along dimension 0
There are 2 independent parts, one for each index of `groups`. A program takes and returns all parts, laid end to end along the dimension named above; an argument that names none is the same for every part. Nothing has to cross between parts.
Inputs may be any that keep to these rules, and one draw needn't show every extreme that they name: Each list send_rows[s, r] holds 8 different local rows of shard s. `edge_slot`: every value 0 to 63 is named by some live edge of every shard; padded entries hold 0. `edge_dst`: within each shard's block the values never fall; every grid point receives 2 to 6 live edges; padded entries, all at the end of a shard's block, hold 256; in every draw one shard has no padded entry.
All inputs are finite; a program needn't handle non-finite values.
Results may differ from a plain program's by a relative error of at most 0.017.
Values may be sent and summed in bfloat16 or wider, within the bound.
No kernel may reach another device: no remote copies, remote signals or barrier semaphores. Data moves between devices by JAX's collectives and lax.ppermute only.
A program may use at most 128 MiB of HBM per device.

v0:
```python
import functools

import jax
import jax.numpy as jnp
from jax import lax
from jax.experimental import pallas as pl
from jax.experimental.pallas import tpu as pltpu
from jax.sharding import PartitionSpec as P

smoothing = 0.1
epsilon = 1e-06
tile = 256
lanes = 128
f32 = jnp.float32
bf16 = jnp.bfloat16


def mm(left, right, left_dim, right_dim):
    return lax.dot_general(
        left, right, (((left_dim,), (right_dim,)), ((), ())), preferred_element_type=f32
    )


def call(body, outs, args, scratch=(), limit=16, scalars=(), scalar_outs=(), places=(), after=()):
    whole = pl.BlockSpec(memory_space=pltpu.VMEM)
    small = pl.BlockSpec(memory_space=pltpu.SMEM)
    far_place = pl.BlockSpec(memory_space=pltpu.HBM)
    any_place = pl.BlockSpec(memory_space=pl.ANY)
    count = len(after)
    args = [pltpu.with_memory_space_constraint(x, pltpu.HBM) if i in places else x for i, x in enumerate(args)]

    def inner(*refs):
        body(*refs[count:])

    specs = [small if i in scalars else far_place if i in places else whole for i in range(len(args))]
    return pl.pallas_call(
        inner if count else body,
        out_shape=[jax.ShapeDtypeStruct(dims, kind) for dims, kind in outs],
        in_specs=[any_place] * count + specs,
        out_specs=[small if i in scalar_outs else whole for i in range(len(outs))],
        scratch_shapes=scratch,
        compiler_params=pltpu.CompilerParams(vmem_limit_bytes=limit * 2**20),
        cost_estimate=pl.CostEstimate(flops=0, bytes_accessed=0, transcendentals=0),
    )(*after, *args)


def place():
    space = lax.axis_index("space")
    return lax.div(space, 2), lax.rem(space, 2), lax.axis_index("member")


def swap(value, axis, size, step):
    return lax.ppermute(value, axis, [(i, i ^ step) for i in range(size)])


def select_kernel(lists_ref, latents_ref, send_ref, pick_ref, small_ref, table_ref, sems):
    _, peers, cap = lists_ref.shape
    members, nodes, width = latents_ref.shape
    lists = pltpu.make_async_copy(lists_ref, small_ref, sems.at[0])
    table = pltpu.make_async_copy(latents_ref, table_ref, sems.at[1])
    lists.start()
    table.start()
    lists.wait()
    at = lax.broadcasted_iota(jnp.int32, (cap, members * nodes), 0)
    column = lax.broadcasted_iota(jnp.int32, (cap, members * nodes), 1)
    rows = []
    for peer in range(peers):
        wanted = jnp.zeros((cap, members * nodes), jnp.int32)
        for j in range(cap):
            wanted = jnp.where(at == j, small_ref[0, peer, j], wanted)
        for member in range(members):
            rows.append((column == wanted + member * nodes).astype(f32))
    pick = jnp.concatenate(rows, axis=0).astype(bf16)
    pick_ref[...] = pick
    table.wait()
    sent = mm(pick, table_ref[...].reshape(members * nodes, width), 1, 0)
    send_ref[...] = sent.astype(bf16).reshape(send_ref.shape)


def stage_kernel(
    cap, members, slot_ref, dst_ref, weight_ref, w_msg_ref, w_hidden_ref, embed_ref, gain_ref,
    project_ref, present_ref, share_ref, *rest,
):
    staged_refs, sems = rest[:-1], rest[-1]
    sources = (w_msg_ref, w_hidden_ref, embed_ref, gain_ref, project_ref, present_ref)
    copies = [
        pltpu.make_async_copy(source, target, sems.at[i])
        for i, (source, target) in enumerate(zip(sources, staged_refs, strict=True))
    ]
    for copy in copies:
        copy.start()
    edge_part(cap, members, slot_ref, dst_ref, weight_ref, share_ref)
    for copy in copies:
        copy.wait()


def edge_part(cap, members, slot_ref, dst_ref, weight_ref, share_ref):
    edges = slot_ref.shape[0]
    slot = slot_ref[...].reshape(1, edges)
    dst = dst_ref[...].reshape(1, edges)
    weight = weight_ref[...].reshape(1, edges)
    rows = share_ref.shape[0] // 2
    points = share_ref.shape[1] // members
    sender = lax.div(slot, cap)
    spot = sender * (members * cap) + (slot - sender * cap)
    hit = lax.broadcasted_iota(jnp.int32, (rows, edges), 0) == spot
    into = (lax.broadcasted_iota(jnp.int32, (points, edges), 0) == dst).astype(f32).astype(bf16)
    high = weight.astype(bf16).astype(f32)
    table = mm(jnp.where(hit, high, 0.0).astype(bf16), into, 1, 1) + mm(
        jnp.where(hit, weight - high, 0.0).astype(bf16), into, 1, 1
    )
    table = table / jnp.sum(table, axis=0, keepdims=True)
    for member in range(members):
        high = table.astype(bf16)
        columns = slice(member * points, (member + 1) * points)
        share_ref[0:rows, columns] = high
        share_ref[rows : 2 * rows, columns] = (table - high.astype(f32)).astype(bf16)
        table = jnp.concatenate([table[rows - cap :], table[: rows - cap]], axis=0)


def forward_kernel(
    received_ref, w_msg_ref, share_ref, embed_ref, gain_ref, w_hidden_ref, project_ref, present_ref,
    field_ref, sent_ref, normed_ref, active_ref, slope_ref, unit_ref, inverse_ref,
):
    points, width = embed_ref.shape
    variables, members, _ = present_ref.shape
    messages = mm(received_ref[...], w_msg_ref[...], 1, 0).astype(bf16)
    messages = jnp.concatenate([messages, messages], axis=0)
    gain = gain_ref[...].reshape(1, width)
    for begin in range(0, members * points, lanes):
        rows = slice(begin, begin + lanes)
        source = slice(begin % points, begin % points + lanes)
        hidden = embed_ref[source, :].astype(f32) + mm(share_ref[:, rows], messages, 0, 0)
        inverse = lax.rsqrt(jnp.mean(hidden * hidden, axis=-1, keepdims=True) + epsilon)
        unit = hidden * inverse
        unit_ref[rows, :] = unit
        inverse_ref[rows, :] = inverse
        normed_ref[rows, :] = (unit * gain).astype(bf16)
    root = 0.7978845608028654
    cubic = 0.044715
    for member in range(members):
        rows = slice(member * points, (member + 1) * points)
        for begin in range(0, width, tile):
            columns = slice(begin, begin + tile)
            inner = mm(normed_ref[rows, :], w_hidden_ref[:, columns], 1, 0)
            square = inner * inner
            bend = jnp.tanh(inner * (root + root * cubic * square))
            half = 0.5 + 0.5 * bend
            active_ref[rows, columns] = (inner * half).astype(bf16)
            slope_ref[rows, columns] = half + (0.5 * inner) * (1.0 - bend * bend) * (
                root + 3.0 * root * cubic * square
            )
        field = present_ref[:, member, :] + mm(project_ref[...], active_ref[rows, :], 1, 1)
        field_ref[member] = field
        sent_ref[member] = field.astype(bf16)


def turn_kernel(normed_ref, active_ref, received_ref, normed_t_ref, active_t_ref, keep_ref, give_ref):
    _, _, levels, block, _ = normed_t_ref.shape
    width = normed_ref.shape[1]
    level, line, core = place()
    for source, targets in (
        (received_ref, (keep_ref, give_ref)), (normed_ref, normed_t_ref), (active_ref, active_t_ref)
    ):
        for begin in range(0, width, tile):
            turned = source[:, begin : begin + tile].T
            for piece in range(0, tile, block):
                index = (begin + piece) // block
                far = (index // 2 % 2) ^ line
                step = (index // 4) ^ level
                side = (index % 2) ^ core
                value = turned[piece : piece + block]
                if source is received_ref:
                    for which in range(2):
                        @pl.when(side == which)
                        def _(target=targets[which]):
                            target[1 - far, levels - 1 - step] = value
                else:
                    targets[side, 1 - far, levels - 1 - step] = value


def split_loss(part, variables):
    column = lax.broadcasted_iota(jnp.int32, part.shape, 1)
    spots = (column == variables) | (column == variables + 1)
    total = jnp.sum(jnp.where(spots, part, 0.0), axis=1, keepdims=True)
    high = total.astype(bf16).astype(f32)
    return jnp.where(column == variables, high, jnp.where(column == variables + 1, total - high, part))


def score_kernel(
    own_ref, other_ref, truth_ref, cell_ref, project_ref, slope_ref, normed_t_ref, active_t_ref,
    inner_ref, pred_ref, loss_ref, far_ref, near_ref, hold_ref,
):
    members, variables, points = own_ref.shape
    width = slope_ref.shape[1]
    total = 2 * members
    pairs = total * (total - 1)

    def eased(delta):
        square = delta * delta + smoothing * smoothing
        inverse = lax.rsqrt(square)
        return square * inverse, delta * inverse

    truth, cell = truth_ref[...], cell_ref[...].reshape(1, points)
    own = [own_ref[m] for m in range(members)]
    other = [other_ref[m].astype(f32) for m in range(members)]
    score = jnp.zeros_like(truth)
    pulls = [jnp.zeros_like(truth) for _ in own]
    grads = []
    for m in range(members):
        size, sign = eased(own[m] - truth)
        score = score + size * (1.0 / total)
        grads.append(sign * (1.0 / total))
    for m in range(members):
        for n in range(m + 1, members):
            size, sign = eased(own[m] - own[n])
            score = score - size * (1.0 / pairs)
            pulls[m] = pulls[m] + sign
            pulls[n] = pulls[n] - sign
        for n in range(members):
            size, sign = eased(own[m] - other[n])
            score = score - size * (0.5 / pairs)
            pulls[m] = pulls[m] + sign
    loss = jnp.sum(score * cell)
    loss_ref[0] = loss
    hold_ref[...] = jnp.zeros_like(hold_ref)
    for m in range(members):
        grad = (grads[m] - pulls[m] * (1.0 / pairs)) * cell
        hold_ref[0:variables, m * points : (m + 1) * points] = grad
    pred = hold_ref[...].astype(bf16)
    pred_ref[...] = pred
    for m in range(members):
        rows = slice(m * points, (m + 1) * points)
        part = pred[:variables, rows]
        for begin in range(0, width, tile):
            columns = slice(begin, begin + tile)
            grad = mm(part, project_ref[:, columns], 0, 0)
            inner_ref[rows, columns] = (grad * slope_ref[rows, columns]).astype(bf16)
    weight_parts(normed_t_ref, active_t_ref, inner_ref, pred, loss, variables, 1, 0, far_ref)
    weight_parts(normed_t_ref, active_t_ref, inner_ref, pred, loss, variables, 1, 1, near_ref)


def weight_parts(normed_t_ref, active_t_ref, inner_ref, pred, loss, variables, side, half, out_ref):
    width = inner_ref.shape[1]
    depth = normed_t_ref.shape[-1]
    normed = normed_t_ref[side, half].reshape(-1, depth)
    for begin in range(0, width, tile):
        columns = slice(begin, begin + tile)
        out_ref[:, columns] = mm(normed, inner_ref[:, columns], 1, 0).astype(out_ref.dtype)
    part = mm(active_t_ref[side, half].reshape(-1, depth), pred, 1, 1)
    part = jnp.where(lax.broadcasted_iota(jnp.int32, part.shape, 1) == variables, loss, part)
    out_ref[:, width:] = split_loss(part, variables).astype(out_ref.dtype)


def pair_kernel(
    variables, half, loss_ref, normed_t_ref, active_t_ref, inner_ref, pred_ref, arrived_ref, *out_refs
):
    hold_ref = out_refs[-1]
    width = inner_ref.shape[1]
    weight_parts(
        normed_t_ref, active_t_ref, inner_ref, pred_ref[...], loss_ref[0], variables, 0, half, hold_ref
    )
    count = hold_ref.shape[0] // (len(out_refs) - 1)
    for i, out_ref in enumerate(out_refs[:-1]):
        rows = slice(i * count, (i + 1) * count)
        total = hold_ref[rows, :] + arrived_ref[rows, :].astype(f32)
        out_ref[:, :width] = total[:, :width].astype(out_ref.dtype)
        out_ref[:, width:] = split_loss(total[:, width:], variables).astype(out_ref.dtype)


def line_kernel(variables, width, kept_ref, arrived_ref, *out_refs):
    block = out_refs[0].shape[0]
    for i, out_ref in enumerate(out_refs):
        rows = slice(i * block, (i + 1) * block)
        total = kept_ref[rows, :] + arrived_ref[rows, :].astype(f32)
        out_ref[:, :width] = total[:, :width].astype(out_ref.dtype)
        if out_ref.shape[1] > width:
            out_ref[:, width:] = split_loss(total[:, width:], variables).astype(out_ref.dtype)


def back_kernel(inner_ref, w_hidden_ref, gain_ref, unit_ref, inverse_ref, grad_ref, scaled_ref):
    rows_all, width = inner_ref.shape
    gain = gain_ref[...].reshape(1, width)
    for begin_row in range(0, rows_all, tile):
        rows = slice(begin_row, begin_row + tile)
        dots = jnp.zeros((tile, 1), f32)
        for begin in range(0, width, tile):
            columns = slice(begin, begin + tile)
            scaled = mm(inner_ref[rows, :], w_hidden_ref[columns, :], 1, 1) * gain[:, columns]
            dots = dots + jnp.sum(scaled * unit_ref[rows, columns], axis=-1, keepdims=True)
            scaled_ref[rows, columns] = scaled
        dots = dots * (1.0 / width)
        inverse = inverse_ref[rows, :]
        for begin in range(0, width, tile):
            columns = slice(begin, begin + tile)
            grad_ref[rows, columns] = (
                (scaled_ref[rows, columns] - unit_ref[rows, columns] * dots) * inverse
            ).astype(bf16)


def slot_kernel(share_ref, grad_ref, slots_ref):
    rows = share_ref.shape[0] // 2
    for begin in range(0, grad_ref.shape[1], tile):
        columns = slice(begin, begin + tile)
        both = mm(share_ref[...], grad_ref[:, columns], 1, 0)
        slots_ref[:, columns] = (both[:rows] + both[rows:]).astype(bf16)


def owner_kernel(pick_ref, arrived_ref, w_msg_ref, grad_ref):
    rows = mm(pick_ref[...], arrived_ref[...], 0, 0).astype(bf16)
    grad_ref[...] = mm(rows, w_msg_ref[...], 1, 1).astype(bf16).reshape(grad_ref.shape)


def message_kernel(keep_ref, give_ref, slots_ref, other_ref, far_ref, near_ref, copy_ref):
    copy_ref[...] = slots_ref[...].reshape(copy_ref.shape)
    depth = keep_ref.shape[-1]
    for half, out_ref in ((0, far_ref), (1, near_ref)):
        own = keep_ref[half].reshape(-1, depth)
        other = give_ref[half].reshape(-1, depth)
        for begin in range(0, out_ref.shape[1], tile):
            columns = slice(begin, begin + tile)
            total = mm(own, slots_ref[:, columns], 1, 0) + mm(other, other_ref[:, columns], 1, 0)
            out_ref[:, columns] = total.astype(out_ref.dtype)


def hidden_sum_kernel(variables, scale, own_ref, *rest):
    hidden_ref, out_ref, loss_ref = rest[-3:]
    total = own_ref[...]
    for r in rest[:-3]:
        total = total + r[...].astype(f32)
    width = hidden_ref.shape[1]
    hidden_ref[...] = total[:, :width]
    part = total[:, width:]
    out_ref[...] = part[:, :variables]
    column = lax.broadcasted_iota(jnp.int32, (8, part.shape[1]), 1)
    spots = (column == variables) | (column == variables + 1)
    first = lax.broadcasted_iota(jnp.int32, (8, part.shape[1]), 0) == 0
    loss_ref[0] = jnp.sum(jnp.where(spots & first, part[:8], 0.0)) * scale


def sum_kernel(own_ref, *rest):
    total = own_ref[...]
    for r in rest[:-1]:
        total = total + r[...].astype(f32)
    rest[-1][...] = total


def on_device(
    latents, grid_embed, norm_gain, w_msg, w_hidden, variable_projection, present_condition, verifying_field,
    cell_surface, send_rows, edge_slot, edge_dst, edge_weight,
):
    members, nodes, width = latents.shape
    points = grid_embed.shape[0]
    variables = variable_projection.shape[1]
    peers = lax.axis_size("space")
    cores = lax.axis_size("member")
    cap = send_rows.shape[2]
    rows_peer = members * cap
    rows_slot = peers * rows_peer
    rows_all = members * points
    levels = peers // 2
    block = width // (peers * cores)
    half = levels * block
    wide = width + -(-(variables + 2) // lanes) * lanes
    project = variable_projection.T

    exchange = functools.partial(
        lax.all_to_all, axis_name="space", split_axis=0, concat_axis=0, tiled=True
    )
    send, pick = call(
        select_kernel,
        [((peers, rows_peer, width), bf16), ((rows_slot, members * nodes), bf16)],
        [send_rows, latents],
        scratch=[
            pltpu.SMEM(send_rows.shape, jnp.int32),
            pltpu.VMEM(latents.shape, bf16),
            pltpu.SemaphoreType.DMA((2,)),
        ],
        limit=4,
        places=(0, 1),
    )
    received = exchange(send).reshape(rows_slot, width)
    present = present_condition.transpose(1, 0, 2)
    fixed = [w_msg, w_hidden, grid_embed, norm_gain, project, present]
    share, *staged = call(
        functools.partial(stage_kernel, cap, members),
        [((2 * rows_slot, rows_all), bf16)] + [(x.shape, x.dtype) for x in fixed],
        [edge_slot, edge_dst, edge_weight] + fixed,
        scratch=[pltpu.SemaphoreType.DMA((len(fixed),))],
        limit=16,
        places=tuple(range(3, 3 + len(fixed))),
        after=[pick],
    )
    w_msg_near, w_hidden_near, embed, gain, project_near, present = staged
    field, sent, normed, active, slope, unit, inverse = call(
        forward_kernel,
        [
            ((members, variables, points), f32),
            ((members, variables, points), bf16),
            ((rows_all, width), bf16),
            ((rows_all, width), bf16),
            ((rows_all, width), f32),
            ((rows_all, width), f32),
            ((rows_all, 1), f32),
        ],
        [received, w_msg_near, share, embed, gain, w_hidden_near, project_near, present],
        limit=20,
    )
    other = swap(sent, "member", cores, 1)
    normed_t, active_t, received_keep, received_give = call(
        turn_kernel,
        [((cores, 2, levels, block, rows_all), bf16)] * 2 + [((2, levels, block, rows_slot), bf16)] * 2,
        [normed, active, received],
        limit=8,
    )
    received_other = swap(received_give, "member", cores, 1)
    grad_inner, pred, loss_part, far, near = call(
        score_kernel,
        [
            ((rows_all, width), bf16),
            ((lanes, rows_all), bf16),
            ((1,), f32),
            ((half, wide), bf16),
            ((half, wide), bf16),
        ],
        [field, other, verifying_field, cell_surface, project_near, slope, normed_t, active_t],
        scratch=[pltpu.VMEM((lanes, rows_all), f32)],
        limit=16,
        scalar_outs=(2,),
    )
    far_other = swap(far, "member", cores, 1)
    near_other = swap(near, "member", cores, 1)
    (grad_hidden,) = call(
        back_kernel,
        [((rows_all, width), bf16)],
        [grad_inner, w_hidden_near, gain, unit, inverse],
        scratch=[pltpu.VMEM((rows_all, width), f32)],
        limit=14,
    )
    parts = [loss_part, normed_t, active_t, grad_inner, pred]
    (hidden_far,) = call(
        functools.partial(pair_kernel, variables, 0),
        [((half, wide), bf16)],
        parts + [far_other],
        scratch=[pltpu.VMEM((half, wide), f32)],
        limit=12,
        scalars=(0,),
        after=[grad_hidden],
    )
    hidden_arrived = swap(hidden_far, "space", peers, 1)
    (slots,) = call(
        slot_kernel, [((rows_slot, width), bf16)], [share, grad_hidden], limit=6, after=[hidden_far]
    )
    slots_other = swap(slots, "member", cores, 1)
    message_far, message_near, slots_out = call(
        message_kernel,
        [((half, width), bf16), ((half, width), f32), ((peers, rows_peer, width), bf16)],
        [received_keep, received_other, slots, slots_other],
        limit=8,
    )
    message_arrived = swap(message_far, "space", peers, 1)
    back = exchange(slots_out).reshape(rows_slot, width)
    (hidden_near,) = call(
        functools.partial(pair_kernel, variables, 1),
        [((half, wide), f32)],
        parts + [near_other],
        scratch=[pltpu.VMEM((half, wide), f32)],
        limit=12,
        scalars=(0,),
        after=[message_far],
    )

    def spread(near, arrived):
        *sent, own = call(
            functools.partial(line_kernel, variables, width),
            [((block, near.shape[1]), bf16)] * (levels - 1) + [((block, near.shape[1]), f32)],
            [near, arrived],
            limit=6,
        )
        return own, [swap(x, "space", peers, 2 * (levels - 1 - i)) for i, x in enumerate(sent)]

    hidden_own, hidden_parts = spread(hidden_near, hidden_arrived)
    message_own, message_parts = spread(message_near, message_arrived)
    (latent_grad,) = call(
        owner_kernel, [(latents.shape, bf16)], [pick, back, w_msg], limit=8, after=[hidden_own]
    )
    hidden_weight_grad, out_weight_grad, loss = call(
        functools.partial(hidden_sum_kernel, variables, 1.0 / (points * peers * variables)),
        [((block, width), f32), ((block, variables), f32), ((1,), f32)],
        [hidden_own] + hidden_parts,
        limit=6,
        scalar_outs=(2,),
        after=[message_own],
    )
    (msg_weight_grad,) = call(
        sum_kernel,
        [((block, width), f32)],
        [message_own] + message_parts,
        limit=6,
        after=[hidden_weight_grad],
    )
    return (latent_grad, loss, msg_weight_grad, hidden_weight_grad, out_weight_grad)


def solution(mesh):
    placed = (
        P(("groups", "member"), "space", None),
        P(("groups", "space"), None),
        P(),
        P(),
        P(),
        P(),
        P(("groups", "member"), None, "space"),
        P(None, ("groups", "space")),
        P(("groups", "space")),
        P("space", None, None),
        P("space"),
        P("space"),
        P("space"),
    )
    return jax.shard_map(
        on_device,
        mesh=mesh,
        in_specs=placed,
        out_specs=(
            P(("groups", "member"), "space", None),
            P("groups"),
            P(("groups", "space", "member"), None),
            P(("groups", "space", "member"), None),
            P(("groups", "space", "member"), None),
        ),
        check_vma=False,
    )
```

profile of v0, /device:TPU:0, one launch (start us, length us, event | category | flops | bytes accessed | tf_op | source)
XLA Modules:
  0.0 81.5 jit_solution(8158721234460829701)
XLA Ops:
  0.6 1.8 %shard_map.164 = (bf16[8,16,1024]{2,1,0:T(8,128)(2,1)}, bf16[128,64]{1,0:T(8,128)(2,1)S(1)}) custom-call(s32[1,8,8]{2,1,0:T(8,128)} %lists_ref.1, bf16[2,32,1024]{2,1,0:T(8,128)(2,1)} %latents_ref.1), custom_call_target="tpu_custom_call" | custom-call | tf_op jit(solution)/shard_map/pallas_call | solution.py:36
  2.5 7.3 %all-to-all-start = ((bf16[8,16,1024]{2,1,0:T(8,128)(2,1)}), bf16[8,16,1024]{2,1,0:T(8,128)(2,1)S(1)}, u32[]{:S(2)}, u32[]{:S(2)}) async-start(bf16[8,16,1024]{2,1,0:T(8,128)(2,1)} %get-tuple-element.44), calls=%async_computation | async-start | bytes 524288 | tf_op jit(solution)/shard_map/all_to_all | solution.py:382
  11.9 2.5 %shard_map.165 = (bf16[256,512]{1,0:T(8,128)(2,1)S(1)}, bf16[1024,1024]{1,0:T(8,128)(2,1)S(1)}, bf16[1024,1024]{1,0:T(8,128)(2,1)S(1)}, bf16[256,1024]{1,0:T(8,1...) custom-call(bf16[128,64]{1,0:T(8,128)(2,1)S(1)} %get-tuple-element.45.refs_0_.refs_1_, ...), custom_call_target="tpu_custom_call" | custom-call | tf_op jit(solution)/shard_map/pallas_call | solution.py:36
  14.4 1.3 %copy-done.3 = bf16[1024,1024]{1,0:T(8,128)(2,1)} copy-done((bf16[1024,1024]{1,0:T(8,128)(2,1)}, bf16[1024,1024]{1,0:T(8,128)(2,1)S(1)}, u32[]{:S(2)}) %copy-start.3) | copy-done | bytes 2097176
  16.5 2.2 %all-to-all-done = bf16[8,16,1024]{2,1,0:T(8,128)(2,1)S(1)} async-done(((bf16[8,16,1024]{2,1,0:T(8,128)(2,1)}), bf16[8,16,1024]{2,1,0:T(8,128)(2,1)S(1)}, u32[]{:S(2)}, u32[]{:S(2)}) %all-to-all-start) | async-done | bytes 262176 | tf_op jit(solution)/shard_map/all_to_all | solution.py:382
  18.7 1.6 %copy-done.4 = bf16[1024,1024]{1,0:T(8,128)(2,1)S(1)} copy-done((bf16[1024,1024]{1,0:T(8,128)(2,1)S(1)}, bf16[1024,1024]{1,0:T(8,128)(2,1)}, u32[]{:S(2)}) %copy-start.4) | copy-done | bytes 2097176
  20.3 0.9 %copy-done.12 = f32[100,2,256]{2,1,0:T(2,128)S(1)} copy-done((f32[100,2,256]{2,1,0:T(2,128)S(1)}, f32[100,2,256]{2,1,0:T(2,128)}, u32[]{:S(2)}) %copy-start.12) | copy-done | bytes 204824
  21.2 3.5 %shard_map.166 = (f32[2,100,256]{2,1,0:T(8,128)S(1)}, bf16[2,100,256]{2,1,0:T(8,128)(2,1)S(1)}, bf16[512,1024]{1,0:T(8,128)(2,1)S(1)}, bf16[512,1024]{1,0:T(8,12...) custom-call(bf16[128,1024]{1,0:T(8,128)(2,1)S(1)} %bitcast.4, ...), custom_call_target="tpu_custom_call" | custom-call | tf_op jit(solution)/shard_map/pallas_call | solution.py:36
  24.8 0.9 %shard_map.167 = (bf16[2,2,4,64,512]{4,3,2,1,0:T(8,128)(2,1)S(1)}, bf16[2,2,4,64,512]{4,3,2,1,0:T(8,128)(2,1)S(1)}, bf16[2,4,64,128]{3,2,1,0:T(8,128)(2,1)S(1)}, bf16[2,4,64,128]{3,2,1,0:T(8,128)(2,1)S(1)}) custom-call(bf16[512,1024]{1,0:T(8,128)(2,1)S(1)} %get-tuple-element.53.normed_ref, bf16[512,1024]{1,0:T(8,128)(2,1)S(1)} %get-tuple-element.54.active_ref, ...), custom_call_target="tpu_custom_call" | custom-call | tf_op jit(solution)/shard_map/pallas_call | solution.py:36
  26.1 2.2 %shard_map.168 = (bf16[512,1024]{1,0:T(8,128)(2,1)S(1)}, bf16[128,512]{1,0:T(8,128)(2,1)S(1)}, f32[1]{0:T(128)}, bf16[256,1152]{1,0:T(8,128)(2,1)S(1)}, bf16[256,1152]{1,0:T(8,128)(2,1)}) custom-call(f32[2,100,256]{2,1,0:T(8,128)S(1)} %get-tuple-element.57.own_ref, bf16[2,100,256]{2,1,0:T(8,128)(2,1)S(1)} %collective-permute-done.1.other_ref, ...), custom_call_target="tpu_custom_call" | custom-call | tf_op jit(solution)/shard_map/pallas_call | solution.py:36
  28.6 1.7 %shard_map.169.refs_0_.refs_2_ = bf16[512,1024]{1,0:T(8,128)(2,1)S(1)} custom-call(bf16[512,1024]{1,0:T(8,128)(2,1)S(1)} %get-tuple-element.62.inner_ref.refs_4_, bf16[1024,1024]{1,0:T(8,128)(2,1)S(1)} %copy-done.2, f32[1024]{0:T(1024)S(1)} %get-tuple-element.49.gain_ref, f32[512,1024]{1,0:T(8,128)S(1)} %get-tuple-element.63.unit_ref, ...), custom_call_target="tpu_custom_call" | custom-call | tf_op jit(solution)/shard_map/pallas_call | solution.py:36
  30.5 2.1 %shard_map.170.refs_0_ = bf16[256,1152]{1,0:T(8,128)(2,1)} custom-call(bf16[512,1024]{1,0:T(8,128)(2,1)S(1)} %shard_map.169.refs_0_.refs_2_, f32[1]{0:T(128)} %get-tuple-element.65.refs_1_, bf16[2,2,4,64,512]{4,3,2,1,0:T(8,128)(2,1)S(1)} %get-tuple-element.60.normed_t_ref.refs_2_, bf16[2,2,4,64,512]{4,3,2,1,0:T(8,128)(2,1)S(1)} %get-tuple-element.61.active_t_ref.refs_3_, ...), custom_call_target="tpu_custom_call" | custom-call | tf_op jit(solution)/shard_map/pallas_call | solution.py:36
  33.6 1.4 %collective-permute-start.5 = (bf16[256,1152]{1,0:T(8,128)(2,1)}, bf16[256,1152]{1,0:T(8,128)(2,1)}, u32[]{:S(2)}, u32[]{:S(2)}) collective-permute-start(bf16[256,1152]{1,0:T(8,128)(2,1)} %shard_map.170.refs_0_), channel_id=1, source_target_pairs={{0,2},{2,0},{4,6},{6,4},{8,10},{10,8},{12,14},{14,12},{1,3},{3,1},... | collective-permute-start | bytes 1769480 | tf_op jit(solution)/shard_map/ppermute | solution.py:53
  35.0 1.3 %collective-permute-done.give_ref = bf16[2,4,64,128]{3,2,1,0:T(8,128)(2,1)S(1)} collective-permute-done((bf16[2,4,64,128]{3,2,1,0:T(8,128)(2,1)S(1)}, bf16[2,4,64,128]{3,2,1,0:T(8,128)(2,1)S(1)}, u32[]{:S(2)}, u32[]{:S(2)}) %collective-permute-start) | collective-permute-done | bytes 131104 | tf_op jit(solution)/shard_map/ppermute | solution.py:53
  36.4 1.2 %shard_map.172 = (bf16[256,1024]{1,0:T(8,128)(2,1)}, f32[256,1024]{1,0:T(8,128)S(1)}, bf16[8,16,1024]{2,1,0:T(8,128)(2,1)S(1)}) custom-call(bf16[2,4,64,128]{3,2,1,0:T(8,128)(2,1)S(1)} %get-tuple-element.55.keep_ref, bf16[2,4,64,128]{3,2,1,0:T(8,128)(2,1)S(1)} %collective-permute-done.give_ref, bf16[128,1024]{1,0:T(8,128)(2,1)S(1)} %shard_map.171.slots_ref, ...), custom_call_target="tpu_custom_call" | custom-call | tf_op jit(solution)/shard_map/pallas_call | solution.py:36
  37.6 1.0 %copy-done.5 = f32[256,1024]{1,0:T(8,128)} copy-done((f32[256,1024]{1,0:T(8,128)}, f32[256,1024]{1,0:T(8,128)S(1)}, u32[]{:S(2)}) %copy-start.5) | copy-done | bytes 1048600
  39.3 4.5 %all-to-all-start.1 = ((bf16[8,16,1024]{2,1,0:T(8,128)(2,1)}), bf16[8,16,1024]{2,1,0:T(8,128)(2,1)S(1)}, u32[]{:S(2)}, u32[]{:S(2)}) async-start(bf16[8,16,1024]{2,1,0:T(8,128)(2,1)} %copy-done.9), calls=%async_computation.1 | async-start | bytes 524288 | tf_op jit(solution)/shard_map/all_to_all | solution.py:462
  43.8 2.5 %shard_map.173.kept_ref = f32[256,1152]{1,0:T(8,128)S(1)} custom-call(bf16[256,1024]{1,0:T(8,128)(2,1)} %get-tuple-element.68.refs_0_, f32[1]{0:T(128)} %get-tuple-element.65.refs_1_, bf16[2,2,4,64,512]{4,3,2,1,0:T(8,128)(2,1)S(1)} %get-tuple-element.60.normed_t_ref.refs_2_, bf16[2,2,4,64,512]{4,3,2,1,0:T(8,128)(2,1)S(1)} %get-tuple-element.61.active_t_ref.refs_3_, ...), custom_call_target="tpu_custom_call" | custom-call | tf_op jit(solution)/shard_map/pallas_call | solution.py:36
  46.3 5.5 %collective-permute-done.5.arrived_ref = bf16[256,1152]{1,0:T(8,128)(2,1)} collective-permute-done((bf16[256,1152]{1,0:T(8,128)(2,1)}, bf16[256,1152]{1,0:T(8,128)(2,1)}, u32[]{:S(2)}, u32[]{:S(2)}) %collective-permute-start.5) | collective-permute-done | bytes 589856 | tf_op jit(solution)/shard_map/ppermute | solution.py:53
  51.9 1.9 %shard_map.174 = (bf16[64,1152]{1,0:T(8,128)(2,1)S(1)}, bf16[64,1152]{1,0:T(8,128)(2,1)}, bf16[64,1152]{1,0:T(8,128)(2,1)}, f32[64,1152]{1,0:T(8,128)S(1)}) custom-call(f32[256,1152]{1,0:T(8,128)S(1)} %shard_map.173.kept_ref, bf16[256,1152]{1,0:T(8,128)(2,1)} %collective-permute-done.5.arrived_ref), custom_call_target="tpu_custom_call" | custom-call | tf_op jit(solution)/shard_map/pallas_call | solution.py:36
  53.8 2.8 %collective-permute-start.7 = (bf16[64,1152]{1,0:T(8,128)(2,1)S(1)}, bf16[64,1152]{1,0:T(8,128)(2,1)S(1)}, u32[]{:S(2)}, u32[]{:S(2)}) collective-permute-start(bf16[64,1152]{1,0:T(8,128)(2,1)S(1)} %get-tuple-element.74), channel_id=1, source_target_pairs={{0,12},{2,14},{4,8},{6,10},{8,4},{10,6},{12,0},{14,2},{1,13},{3,15... | collective-permute-start | bytes 442376 | tf_op jit(solution)/shard_map/ppermute | solution.py:53
  56.6 1.6 %collective-permute-start.9 = (bf16[64,1152]{1,0:T(8,128)(2,1)}, bf16[64,1152]{1,0:T(8,128)(2,1)S(1)}, u32[]{:S(2)}, u32[]{:S(2)}) collective-permute-start(bf16[64,1152]{1,0:T(8,128)(2,1)} %get-tuple-element.76), channel_id=1, source_target_pairs={{0,4},{2,6},{4,0},{6,2},{8,12},{10,14},{12,8},{14,10},{1,5},{3,7},... | collective-permute-start | bytes 442376 | tf_op jit(solution)/shard_map/ppermute | solution.py:53
  58.2 4.9 %collective-permute-done.6.arrived_ref = bf16[256,1024]{1,0:T(8,128)(2,1)} collective-permute-done((bf16[256,1024]{1,0:T(8,128)(2,1)}, bf16[256,1024]{1,0:T(8,128)(2,1)}, u32[]{:S(2)}, u32[]{:S(2)}) %collective-permute-start.6) | collective-permute-done | bytes 524320 | tf_op jit(solution)/shard_map/ppermute | solution.py:53
  63.1 1.9 %shard_map.176 = (bf16[64,1024]{1,0:T(8,128)(2,1)}, bf16[64,1024]{1,0:T(8,128)(2,1)}, bf16[64,1024]{1,0:T(8,128)(2,1)}, f32[64,1024]{1,0:T(8,128)S(1)}) custom-call(f32[256,1024]{1,0:T(8,128)S(1)} %copy-done.6, bf16[256,1024]{1,0:T(8,128)(2,1)} %collective-permute-done.6.arrived_ref), custom_call_target="tpu_custom_call" | custom-call | tf_op jit(solution)/shard_map/pallas_call | solution.py:36
  64.9 2.4 %collective-permute-start.10 = (bf16[64,1024]{1,0:T(8,128)(2,1)}, bf16[64,1024]{1,0:T(8,128)(2,1)S(1)}, u32[]{:S(2)}, u32[]{:S(2)}) collective-permute-start(bf16[64,1024]{1,0:T(8,128)(2,1)} %get-tuple-element.79), channel_id=1, source_target_pairs={{0,12},{2,14},{4,8},{6,10},{8,4},{10,6},{12,0},{14,2},{1,13},{3,15... | collective-permute-start | bytes 393224 | tf_op jit(solution)/shard_map/ppermute | solution.py:53
  67.4 1.9 %collective-permute-start.12 = (bf16[64,1024]{1,0:T(8,128)(2,1)}, bf16[64,1024]{1,0:T(8,128)(2,1)}, u32[]{:S(2)}, u32[]{:S(2)}) collective-permute-start(bf16[64,1024]{1,0:T(8,128)(2,1)} %get-tuple-element.81), channel_id=1, source_target_pairs={{0,4},{2,6},{4,0},{6,2},{8,12},{10,14},{12,8},{14,10},{1,5},{3,7},... | collective-permute-start | bytes 393224 | tf_op jit(solution)/shard_map/ppermute | solution.py:53
  69.3 1.5 %shard_map.175 = bf16[2,32,1024]{2,1,0:T(8,128)(2,1)} custom-call(f32[64,1152]{1,0:T(8,128)S(1)} %get-tuple-element.70.refs_0_.refs_1_, bf16[128,64]{1,0:T(8,128)(2,1)S(1)} %copy-done.14, bf16[128,1024]{1,0:T(8,128)(2,1)S(1)} %bitcast.6, bf16[1024,1024]{1,0:T(8,128)(2,1)S(1)} %copy-done), custom_call_target="tpu_custom_call" | custom-call | tf_op jit(solution)/shard_map/pallas_call | solution.py:36
  70.8 0.8 shard_map.177
  71.7 1.7 %collective-permute-done.10.refs_2_ = bf16[64,1024]{1,0:T(8,128)(2,1)S(1)} collective-permute-done((bf16[64,1024]{1,0:T(8,128)(2,1)}, bf16[64,1024]{1,0:T(8,128)(2,1)S(1)}, u32[]{:S(2)}, u32[]{:S(2)}) %collective-permute-start.10) | collective-permute-done | bytes 131104 | tf_op jit(solution)/shard_map/ppermute | solution.py:53
  73.4 5.4 %collective-permute-done.11.refs_3_ = bf16[64,1024]{1,0:T(8,128)(2,1)} collective-permute-done((bf16[64,1024]{1,0:T(8,128)(2,1)}, bf16[64,1024]{1,0:T(8,128)(2,1)}, u32[]{:S(2)}, u32[]{:S(2)}) %collective-permute-start.11) | collective-permute-done | bytes 131104 | tf_op jit(solution)/shard_map/ppermute | solution.py:53
  78.8 0.9 %copy-done.10 = f32[64,1024]{1,0:T(8,128)S(1)} copy-done((f32[64,1024]{1,0:T(8,128)S(1)}, f32[64,1024]{1,0:T(8,128)}, u32[]{:S(2)}) %copy-start.10) | copy-done | bytes 262168
  79.7 1.7 %shard_map.178 = f32[64,1024]{1,0:T(8,128)} custom-call(f32[64,1024]{1,0:T(8,128)S(1)} %copy-done.10, f32[64,1024]{1,0:T(8,128)S(1)} %get-tuple-element.73.refs_0_.refs_1_, bf16[64,1024]{1,0:T(8,128)(2,1)S(1)} %collective-permute-done.10.refs_2_, bf16[64,1024]{1,0:T(8,128)(2,1)} %collective-permute-done.11.refs_3_, ...), custom_call_target="tpu_custom_call" | custom-call | tf_op jit(solution)/shard_map/pallas_call | solution.py:36
  (53 shorter events, 5.5 us)
Async XLA Ops:
  2.5 12.0 %copy-start.13 = (bf16[128,64]{1,0:T(8,128)(2,1)}, bf16[128,64]{1,0:T(8,128)(2,1)S(1)}, u32[]{:S(2)}) copy-start(bf16[128,64]{1,0:T(8,128)(2,1)S(1)} %get-tuple-element.45.refs_0_.refs_1_) | copy-start | bytes 49156
  2.5 16.2 %all-to-all-start = ((bf16[8,16,1024]{2,1,0:T(8,128)(2,1)}), bf16[8,16,1024]{2,1,0:T(8,128)(2,1)S(1)}, u32[]{:S(2)}, u32[]{:S(2)}) async-start(bf16[8,16,1024]{2,1,0:T(8,128)(2,1)} %get-tuple-element.44), calls=%async_computation | async-start | bytes 524288 | tf_op jit(solution)/shard_map/all_to_all | solution.py:382
  11.2 0.7 copy-start.18
  14.4 1.4 %copy-start.3 = (bf16[1024,1024]{1,0:T(8,128)(2,1)}, bf16[1024,1024]{1,0:T(8,128)(2,1)S(1)}, u32[]{:S(2)}) copy-start(bf16[1024,1024]{1,0:T(8,128)(2,1)S(1)} %get-tuple-element.46.w_msg_ref) | copy-start | bytes 6291460
  16.5 8.2 %copy-start.1 = (bf16[1024,1024]{1,0:T(8,128)(2,1)}, bf16[1024,1024]{1,0:T(8,128)(2,1)S(1)}, u32[]{:S(2)}) copy-start(bf16[1024,1024]{1,0:T(8,128)(2,1)S(1)} %get-tuple-element.50.w_hidden_ref) | copy-start | bytes 6291460
  16.5 8.2 %copy-start.7 = (bf16[100,1024]{1,0:T(8,128)(2,1)}, bf16[100,1024]{1,0:T(8,128)(2,1)S(1)}, u32[]{:S(2)}) copy-start(bf16[100,1024]{1,0:T(8,128)(2,1)S(1)} %get-tuple-element.51.project_ref) | copy-start | bytes 614404
  18.7 1.6 %copy-start.4 = (bf16[1024,1024]{1,0:T(8,128)(2,1)S(1)}, bf16[1024,1024]{1,0:T(8,128)(2,1)}, u32[]{:S(2)}) copy-start(bf16[1024,1024]{1,0:T(8,128)(2,1)} %copy-done.3) | copy-start | bytes 6291460
  20.3 0.9 %copy-start.12 = (f32[100,2,256]{2,1,0:T(2,128)S(1)}, f32[100,2,256]{2,1,0:T(2,128)}, u32[]{:S(2)}) copy-start(f32[100,2,256]{2,1,0:T(2,128)} %copy-done.11) | copy-start | bytes 614404
  24.7 1.4 %copy-start.15 = (f32[100,256]{1,0:T(8,128)S(1)}, f32[100,256]{1,0:T(8,128)}, u32[]{:S(2)}) copy-start(f32[100,256]{1,0:T(8,128)} %truth_ref.1) | copy-start | bytes 307204
  24.7 1.4 %copy-start.19 = (f32[256]{0:T(256)S(1)}, f32[256]{0:T(256)}, u32[]{:S(2)}) copy-start(f32[256]{0:T(256)} %cell_ref.1) | copy-start | bytes 3076
  24.7 1.4 %copy-start.8 = (bf16[100,1024]{1,0:T(8,128)(2,1)S(1)}, bf16[100,1024]{1,0:T(8,128)(2,1)}, u32[]{:S(2)}) copy-start(bf16[100,1024]{1,0:T(8,128)(2,1)} %copy-done.7) | copy-start | bytes 614404
  24.7 1.4 %collective-permute-start.1 = (bf16[2,100,256]{2,1,0:T(8,128)(2,1)S(1)}, bf16[2,100,256]{2,1,0:T(8,128)(2,1)S(1)}, u32[]{:S(2)}, u32[]{:S(2)}) collective-permute-start(bf16[2,100,256]{2,1,0:T(8,128)(2,1)S(1)} %get-tuple-element.58), channel_id=1, source_target_pairs={{0,1},{1,0},{2,3},{3,2},{4,5},{5,4},{6,7},{7,6},{8,9},{9,8},{10,11... | collective-permute-start | bytes 307208 | tf_op jit(solution)/shard_map/ppermute | solution.py:53
  26.1 2.5 %copy-start.2 = (bf16[1024,1024]{1,0:T(8,128)(2,1)S(1)}, bf16[1024,1024]{1,0:T(8,128)(2,1)}, u32[]{:S(2)}) copy-start(bf16[1024,1024]{1,0:T(8,128)(2,1)} %copy-done.1) | copy-start | bytes 6291460
  28.4 2.1 %collective-permute-start.2 = (bf16[256,1152]{1,0:T(8,128)(2,1)S(1)}, bf16[256,1152]{1,0:T(8,128)(2,1)S(1)}, u32[]{:S(2)}, u32[]{:S(2)}) collective-permute-start(bf16[256,1152]{1,0:T(8,128)(2,1)S(1)} %get-tuple-element.67), channel_id=1, source_target_pairs={{0,1},{1,0},{2,3},{3,2},{4,5},{5,4},{6,7},{7,6},{8,9},{9,8},{10,11... | collective-permute-start | bytes 1769480 | tf_op jit(solution)/shard_map/ppermute | solution.py:53
  33.0 3.3 %collective-permute-start.3 = (bf16[128,1024]{1,0:T(8,128)(2,1)S(1)}, bf16[128,1024]{1,0:T(8,128)(2,1)S(1)}, u32[]{:S(2)}, u32[]{:S(2)}) collective-permute-start(bf16[128,1024]{1,0:T(8,128)(2,1)S(1)} %shard_map.171.slots_ref), channel_id=1, source_target_pairs={{0,1},{1,0},{2,3},{3,2},{4,5},{5,4},{6,7},{7,6},{8,9},{9,8},{10,11... | collective-permute-start | bytes 786440 | tf_op jit(solution)/shard_map/ppermute | solution.py:53
  33.3 10.5 %collective-permute-start.4 = (bf16[256,1152]{1,0:T(8,128)(2,1)}, bf16[256,1152]{1,0:T(8,128)(2,1)}, u32[]{:S(2)}, u32[]{:S(2)}) collective-permute-start(bf16[256,1152]{1,0:T(8,128)(2,1)} %get-tuple-element.69), channel_id=1, source_target_pairs={{0,1},{1,0},{2,3},{3,2},{4,5},{5,4},{6,7},{7,6},{8,9},{9,8},{10,11... | collective-permute-start | bytes 1769480 | tf_op jit(solution)/shard_map/ppermute | solution.py:53
  33.6 18.2 %collective-permute-start.5 = (bf16[256,1152]{1,0:T(8,128)(2,1)}, bf16[256,1152]{1,0:T(8,128)(2,1)}, u32[]{:S(2)}, u32[]{:S(2)}) collective-permute-start(bf16[256,1152]{1,0:T(8,128)(2,1)} %shard_map.170.refs_0_), channel_id=1, source_target_pairs={{0,2},{2,0},{4,6},{6,4},{8,10},{10,8},{12,14},{14,12},{1,3},{3,1},... | collective-permute-start | bytes 1769480 | tf_op jit(solution)/shard_map/ppermute | solution.py:53
  35.0 1.3 %collective-permute-start = (bf16[2,4,64,128]{3,2,1,0:T(8,128)(2,1)S(1)}, bf16[2,4,64,128]{3,2,1,0:T(8,128)(2,1)S(1)}, u32[]{:S(2)}, u32[]{:S(2)}) collective-permute-start(bf16[2,4,64,128]{3,2,1,0:T(8,128)(2,1)S(1)} %get-tuple-element.56), channel_id=1, source_target_pairs={{0,1},{1,0},{2,3},{3,2},{4,5},{5,4},{6,7},{7,6},{8,9},{9,8},{10,11... | collective-permute-start | bytes 393224 | tf_op jit(solution)/shard_map/ppermute | solution.py:53
  37.6 1.0 %copy-start.5 = (f32[256,1024]{1,0:T(8,128)}, f32[256,1024]{1,0:T(8,128)S(1)}, u32[]{:S(2)}) copy-start(f32[256,1024]{1,0:T(8,128)S(1)} %get-tuple-element.72.kept_ref) | copy-start | bytes 3145732
  38.6 0.7 copy-start.9
  38.6 24.5 %collective-permute-start.6 = (bf16[256,1024]{1,0:T(8,128)(2,1)}, bf16[256,1024]{1,0:T(8,128)(2,1)}, u32[]{:S(2)}, u32[]{:S(2)}) collective-permute-start(bf16[256,1024]{1,0:T(8,128)(2,1)} %get-tuple-element.68.refs_0_), channel_id=1, source_target_pairs={{0,2},{2,0},{4,6},{6,4},{8,10},{10,8},{12,14},{14,12},{1,3},{3,1},... | collective-permute-start | bytes 1572872 | tf_op jit(solution)/shard_map/ppermute | solution.py:53
  39.3 30.0 %all-to-all-start.1 = ((bf16[8,16,1024]{2,1,0:T(8,128)(2,1)}), bf16[8,16,1024]{2,1,0:T(8,128)(2,1)S(1)}, u32[]{:S(2)}, u32[]{:S(2)}) async-start(bf16[8,16,1024]{2,1,0:T(8,128)(2,1)} %copy-done.9), calls=%async_computation.1 | async-start | bytes 524288 | tf_op jit(solution)/shard_map/all_to_all | solution.py:462
  43.8 19.2 %copy-start.6 = (f32[256,1024]{1,0:T(8,128)S(1)}, f32[256,1024]{1,0:T(8,128)}, u32[]{:S(2)}) copy-start(f32[256,1024]{1,0:T(8,128)} %copy-done.5) | copy-start | bytes 3145732
  46.3 23.0 %copy-start = (bf16[1024,1024]{1,0:T(8,128)(2,1)S(1)}, bf16[1024,1024]{1,0:T(8,128)(2,1)}, u32[]{:S(2)}) copy-start(bf16[1024,1024]{1,0:T(8,128)(2,1)} %refs_3_.3) | copy-start | bytes 6291460
  46.3 23.0 %copy-start.14 = (bf16[128,64]{1,0:T(8,128)(2,1)S(1)}, bf16[128,64]{1,0:T(8,128)(2,1)}, u32[]{:S(2)}) copy-start(bf16[128,64]{1,0:T(8,128)(2,1)} %copy-done.13) | copy-start | bytes 49156
  53.8 13.7 %collective-permute-start.7 = (bf16[64,1152]{1,0:T(8,128)(2,1)S(1)}, bf16[64,1152]{1,0:T(8,128)(2,1)S(1)}, u32[]{:S(2)}, u32[]{:S(2)}) collective-permute-start(bf16[64,1152]{1,0:T(8,128)(2,1)S(1)} %get-tuple-element.74), channel_id=1, source_target_pairs={{0,12},{2,14},{4,8},{6,10},{8,4},{10,6},{12,0},{14,2},{1,13},{3,15... | collective-permute-start | bytes 442376 | tf_op jit(solution)/shard_map/ppermute | solution.py:53
  56.6 14.3 %collective-permute-start.8 = (bf16[64,1152]{1,0:T(8,128)(2,1)}, bf16[64,1152]{1,0:T(8,128)(2,1)S(1)}, u32[]{:S(2)}, u32[]{:S(2)}) collective-permute-start(bf16[64,1152]{1,0:T(8,128)(2,1)} %get-tuple-element.75), channel_id=1, source_target_pairs={{0,8},{2,10},{4,12},{6,14},{8,0},{10,2},{12,4},{14,6},{1,9},{3,11}... | collective-permute-start | bytes 442376 | tf_op jit(solution)/shard_map/ppermute | solution.py:53
  56.6 14.3 %collective-permute-start.9 = (bf16[64,1152]{1,0:T(8,128)(2,1)}, bf16[64,1152]{1,0:T(8,128)(2,1)S(1)}, u32[]{:S(2)}, u32[]{:S(2)}) collective-permute-start(bf16[64,1152]{1,0:T(8,128)(2,1)} %get-tuple-element.76), channel_id=1, source_target_pairs={{0,4},{2,6},{4,0},{6,2},{8,12},{10,14},{12,8},{14,10},{1,5},{3,7},... | collective-permute-start | bytes 442376 | tf_op jit(solution)/shard_map/ppermute | solution.py:53
  64.9 8.4 %collective-permute-start.10 = (bf16[64,1024]{1,0:T(8,128)(2,1)}, bf16[64,1024]{1,0:T(8,128)(2,1)S(1)}, u32[]{:S(2)}, u32[]{:S(2)}) collective-permute-start(bf16[64,1024]{1,0:T(8,128)(2,1)} %get-tuple-element.79), channel_id=1, source_target_pairs={{0,12},{2,14},{4,8},{6,10},{8,4},{10,6},{12,0},{14,2},{1,13},{3,15... | collective-permute-start | bytes 393224 | tf_op jit(solution)/shard_map/ppermute | solution.py:53
  67.3 11.4 %collective-permute-start.11 = (bf16[64,1024]{1,0:T(8,128)(2,1)}, bf16[64,1024]{1,0:T(8,128)(2,1)}, u32[]{:S(2)}, u32[]{:S(2)}) collective-permute-start(bf16[64,1024]{1,0:T(8,128)(2,1)} %get-tuple-element.80), channel_id=1, source_target_pairs={{0,8},{2,10},{4,12},{6,14},{8,0},{10,2},{12,4},{14,6},{1,9},{3,11}... | collective-permute-start | bytes 393224 | tf_op jit(solution)/shard_map/ppermute | solution.py:53
  67.4 11.3 %collective-permute-start.12 = (bf16[64,1024]{1,0:T(8,128)(2,1)}, bf16[64,1024]{1,0:T(8,128)(2,1)}, u32[]{:S(2)}, u32[]{:S(2)}) collective-permute-start(bf16[64,1024]{1,0:T(8,128)(2,1)} %get-tuple-element.81), channel_id=1, source_target_pairs={{0,4},{2,6},{4,0},{6,2},{8,12},{10,14},{12,8},{14,10},{1,5},{3,7},... | collective-permute-start | bytes 393224 | tf_op jit(solution)/shard_map/ppermute | solution.py:53
  78.8 1.0 %copy-start.10 = (f32[64,1024]{1,0:T(8,128)S(1)}, f32[64,1024]{1,0:T(8,128)}, u32[]{:S(2)}) copy-start(f32[64,1024]{1,0:T(8,128)} %get-tuple-element.42.refs_0_) | copy-start | bytes 786436
  (3 other events, 2.1 us)
where the time goes:
time: 82.2 us; the launch traced here: 81.5 us
  Pallas kernels  26.8 us (33%)
  starting transfers between devices  23.6 us (29%)
  waiting for transfers between devices  21.7 us (26%)
  local copies, waits for them, and re-layouts  8.6 us (10%)
  between operations  0.84 us (1%)
    pallas_call x15, Pallas kernels, call(): pl.pallas_call(inner if count else body, out_shape=[jax.ShapeDtypeStruct(...  26.8 us
    ppermute x13, waiting for transfers between devices, swap(): return lax.ppermute(value, axis, [(i, i ^ step) for i in range(size)])  19.4 us
    ppermute x13, starting transfers between devices, swap(): return lax.ppermute(value, axis, [(i, i ^ step) for i in range(size)])  11.8 us
    unnamed x40, local copies, waits for them, and re-layouts  8.6 us
    all_to_all x1, starting transfers between devices, on_device(): received = exchange(send).reshape(rows_slot, width)  7.29 us
    all_to_all x1, starting transfers between devices, on_device(): back = exchange(slots_out).reshape(rows_slot, width)  4.52 us
    all_to_all x1, waiting for transfers between devices, on_device(): received = exchange(send).reshape(rows_slot, width)  2.22 us
  transfers between devices with their start and end apart: 15, of which 8 were waited for; matrix products, arithmetic and copies ran while one was open for 0% of the time, Pallas kernels for 18%

commit v1 on v0

--- a/solution.py
+++ b/solution.py
@@ -11,6 +11,7 @@
 epsilon = 1e-06
 tile = 256
 lanes = 128
+packed = 16
 f32 = jnp.float32
 bf16 = jnp.bfloat16
 
@@ -21,7 +22,7 @@
     )
 
 
-def call(body, outs, args, scratch=(), limit=16, scalars=(), scalar_outs=(), places=(), after=()):
+def call(body, outs, args, scratch=(), limit=16, scalars=(), scalar_outs=(), places=(), after=(), cost=0):
     whole = pl.BlockSpec(memory_space=pltpu.VMEM)
     small = pl.BlockSpec(memory_space=pltpu.SMEM)
     far_place = pl.BlockSpec(memory_space=pltpu.HBM)
@@ -40,7 +41,7 @@
         out_specs=[small if i in scalar_outs else whole for i in range(len(outs))],
         scratch_shapes=scratch,
         compiler_params=pltpu.CompilerParams(vmem_limit_bytes=limit * 2**20),
-        cost_estimate=pl.CostEstimate(flops=0, bytes_accessed=0, transcendentals=0),
+        cost_estimate=pl.CostEstimate(flops=cost, bytes_accessed=0, transcendentals=0),
     )(*after, *args)
 
 
@@ -77,20 +78,21 @@
     send_ref[...] = sent.astype(bf16).reshape(send_ref.shape)
 
 
-def stage_kernel(
-    cap, members, slot_ref, dst_ref, weight_ref, w_msg_ref, w_hidden_ref, embed_ref, gain_ref,
-    project_ref, present_ref, share_ref, *rest,
-):
-    staged_refs, sems = rest[:-1], rest[-1]
-    sources = (w_msg_ref, w_hidden_ref, embed_ref, gain_ref, project_ref, present_ref)
+def stage_kernel(cap, members, count, *refs):
+    edge_refs, source_refs, share_ref = refs[:3], refs[3 : 3 + count], refs[3 + count]
+    staged_refs, held_refs, sems = refs[4 + count : 4 + 2 * count], refs[4 + 2 * count : -1], refs[-1]
     copies = [
         pltpu.make_async_copy(source, target, sems.at[i])
-        for i, (source, target) in enumerate(zip(sources, staged_refs, strict=True))
+        for i, (source, target) in enumerate(
+            zip(edge_refs + source_refs, held_refs + staged_refs, strict=True)
+        )
     ]
     for copy in copies:
         copy.start()
-    edge_part(cap, members, slot_ref, dst_ref, weight_ref, share_ref)
-    for copy in copies:
+    for copy in copies[:3]:
+        copy.wait()
+    edge_part(cap, members, *held_refs, share_ref)
+    for copy in copies[3:]:
         copy.wait()
 
 
@@ -120,9 +122,11 @@
 
 def forward_kernel(
     received_ref, w_msg_ref, share_ref, embed_ref, gain_ref, w_hidden_ref, project_ref, present_ref,
-    field_ref, sent_ref, normed_ref, active_ref, slope_ref, unit_ref, inverse_ref,
+    field_ref, sent_ref, normed_ref, active_ref, slope_ref, unit_ref, inverse_ref, weights_ref, sem,
 ):
     points, width = embed_ref.shape
+    weights = pltpu.make_async_copy(w_hidden_ref, weights_ref, sem)
+    weights.start()
     variables, members, _ = present_ref.shape
     messages = mm(received_ref[...], w_msg_ref[...], 1, 0).astype(bf16)
     messages = jnp.concatenate([messages, messages], axis=0)
@@ -136,13 +140,14 @@
         unit_ref[rows, :] = unit
         inverse_ref[rows, :] = inverse
         normed_ref[rows, :] = (unit * gain).astype(bf16)
+    weights.wait()
     root = 0.7978845608028654
     cubic = 0.044715
     for member in range(members):
         rows = slice(member * points, (member + 1) * points)
         for begin in range(0, width, tile):
             columns = slice(begin, begin + tile)
-            inner = mm(normed_ref[rows, :], w_hidden_ref[:, columns], 1, 0)
+            inner = mm(normed_ref[rows, :], weights_ref[:, columns], 1, 0)
             square = inner * inner
             bend = jnp.tanh(inner * (root + root * cubic * square))
             half = 0.5 + 0.5 * bend
@@ -252,30 +257,101 @@
     out_ref[:, width:] = split_loss(part, variables).astype(out_ref.dtype)
 
 
-def pair_kernel(
-    variables, half, loss_ref, normed_t_ref, active_t_ref, inner_ref, pred_ref, arrived_ref, *out_refs
+def pack(out_ref, begin, part):
+    pad = part.shape[1]
+    for i in range(part.shape[0] // packed):
+        out_ref[begin : begin + packed, i * pad : (i + 1) * pad] = part[i * packed : (i + 1) * packed]
+
+
+def unpack(in_ref, begin, count, pad):
+    parts = [in_ref[begin : begin + packed, i * pad : (i + 1) * pad] for i in range(count // packed)]
+    return jnp.concatenate(parts, axis=0).astype(f32)
+
+
+def far_kernel(
+    variables, loss_ref, normed_t_ref, active_t_ref, inner_ref, pred_ref, arrived_ref, slots_ref,
+    first_ref, second_ref, hold_ref,
 ):
-    hold_ref = out_refs[-1]
     width = inner_ref.shape[1]
-    weight_parts(
-        normed_t_ref, active_t_ref, inner_ref, pred_ref[...], loss_ref[0], variables, 0, half, hold_ref
-    )
-    count = hold_ref.shape[0] // (len(out_refs) - 1)
-    for i, out_ref in enumerate(out_refs[:-1]):
-        rows = slice(i * count, (i + 1) * count)
-        total = hold_ref[rows, :] + arrived_ref[rows, :].astype(f32)
-        out_ref[:, :width] = total[:, :width].astype(out_ref.dtype)
-        out_ref[:, width:] = split_loss(total[:, width:], variables).astype(out_ref.dtype)
-
-
-def line_kernel(variables, width, kept_ref, arrived_ref, *out_refs):
-    block = out_refs[0].shape[0]
+    weight_parts(normed_t_ref, active_t_ref, inner_ref, pred_ref[...], loss_ref[0], variables, 0, 0, hold_ref)
+    count = second_ref.shape[0] - packed
+    for begin in (0, count):
+        rows = slice(begin, begin + count)
+        total = hold_ref[rows, :width] + arrived_ref[rows, :width].astype(f32)
+        part = hold_ref[rows, width:] + arrived_ref[rows, width:].astype(f32)
+        part = split_loss(part, variables).astype(bf16)
+        if begin == 0:
+            first_ref[rows, :width] = total.astype(bf16)
+            first_ref[rows, width:] = part
+        else:
+            second_ref[0:count, :] = total.astype(bf16)
+            pack(second_ref, count, part)
+    peers, rows, _ = slots_ref.shape
+    level, line, _ = place()
+    levels = peers // 2
+    first_ref[count:, width:] = jnp.zeros((levels * rows, first_ref.shape[1] - width), bf16)
+    for i in range(levels):
+        at = count + i * rows
+        first_ref[at : at + rows, :width] = slots_ref[(level ^ (levels - 1 - i)) * 2 + 1 - line]
+
+
+def near_kernel(
+    variables, loss_ref, normed_t_ref, active_t_ref, inner_ref, pred_ref, arrived_ref, out_ref, hold_ref
+):
+    weight_parts(normed_t_ref, active_t_ref, inner_ref, pred_ref[...], loss_ref[0], variables, 0, 1, hold_ref)
+    out_ref[...] = hold_ref[...] + arrived_ref[...].astype(f32)
+
+
+def early_kernel(variables, kept_ref, ride_ref, slots_ref, *out_refs):
+    peers, rows, width = slots_ref.shape
+    level, line, _ = place()
+    levels = peers // 2
+    block = kept_ref.shape[0] // levels
     for i, out_ref in enumerate(out_refs):
-        rows = slice(i * block, (i + 1) * block)
-        total = kept_ref[rows, :] + arrived_ref[rows, :].astype(f32)
-        out_ref[:, :width] = total[:, :width].astype(out_ref.dtype)
-        if out_ref.shape[1] > width:
-            out_ref[:, width:] = split_loss(total[:, width:], variables).astype(out_ref.dtype)
+        here = slice(i * block, (i + 1) * block)
+        total = kept_ref[here, :] + ride_ref[here, :].astype(f32)
+        out_ref[0:block, :width] = total[:, :width].astype(bf16)
+        out_ref[0:block, width:] = split_loss(total[:, width:], variables).astype(bf16)
+        out_ref[block:, width:] = jnp.zeros((2 * rows, out_ref.shape[1] - width), bf16)
+        out_ref[block : block + rows, :width] = slots_ref[(level ^ (levels - 1 - i)) * 2 + line]
+        at = levels // 2 * block + i * rows
+        out_ref[block + rows :, :width] = ride_ref[at : at + rows, :width]
+
+
+def late_kernel(variables, early, kept_ref, message_ref, arrived_ref, ride_ref, slots_ref, *out_refs):
+    hidden_ref, own_ref = out_refs[-2:]
+    peers, rows, width = slots_ref.shape
+    level, line, _ = place()
+    levels = peers // 2
+    block = kept_ref.shape[0] // levels
+    count = (levels - early) * block
+    part = unpack(arrived_ref, count, count, kept_ref.shape[1] - width)
+    for i in range(early, levels):
+        here, there = slice(i * block, (i + 1) * block), slice((i - early) * block, (i - early + 1) * block)
+        total = kept_ref[here, :width] + arrived_ref[there, :].astype(f32)
+        out = split_loss(kept_ref[here, width:] + part[there], variables)
+        if i == levels - 1:
+            hidden_ref[:, :width] = total
+            hidden_ref[:, width:] = out
+            continue
+        out_ref = out_refs[i - early]
+        out_ref[0:block, :] = total.astype(bf16)
+        at = 2 * block
+        out_ref[at : at + rows, :] = slots_ref[(level ^ (levels - 1 - i)) * 2 + line]
+        ride = early * block + i * rows
+        out_ref[at + rows : at + 2 * rows, :] = ride_ref[ride : ride + rows, :width]
+        out_ref[at + 2 * rows :, :] = jnp.zeros((packed, width), bf16)
+        pack(out_ref, at + 2 * rows, out.astype(bf16))
+    for i in range(levels):
+        here = slice(i * block, (i + 1) * block)
+        at = count + packed + i * block
+        total = message_ref[here, :] + arrived_ref[at : at + block, :].astype(f32)
+        if i == levels - 1:
+            own_ref[...] = total
+        elif i >= early:
+            out_refs[i - early][block : 2 * block, :] = total.astype(bf16)
+        else:
+            out_refs[levels - 1 - early + i][...] = total.astype(bf16)
 
 
 def back_kernel(inner_ref, w_hidden_ref, gain_ref, unit_ref, inverse_ref, grad_ref, scaled_ref):
@@ -299,38 +375,63 @@
 
 
 def slot_kernel(share_ref, grad_ref, slots_ref):
-    rows = share_ref.shape[0] // 2
-    for begin in range(0, grad_ref.shape[1], tile):
+    peers, each, width = slots_ref.shape
+    rows = peers * each
+    for begin in range(0, width, tile):
         columns = slice(begin, begin + tile)
         both = mm(share_ref[...], grad_ref[:, columns], 1, 0)
-        slots_ref[:, columns] = (both[:rows] + both[rows:]).astype(bf16)
-
-
-def owner_kernel(pick_ref, arrived_ref, w_msg_ref, grad_ref):
-    rows = mm(pick_ref[...], arrived_ref[...], 0, 0).astype(bf16)
-    grad_ref[...] = mm(rows, w_msg_ref[...], 1, 1).astype(bf16).reshape(grad_ref.shape)
-
-
-def message_kernel(keep_ref, give_ref, slots_ref, other_ref, far_ref, near_ref, copy_ref):
-    copy_ref[...] = slots_ref[...].reshape(copy_ref.shape)
-    depth = keep_ref.shape[-1]
-    for half, out_ref in ((0, far_ref), (1, near_ref)):
+        slots_ref[:, :, columns] = (both[:rows] + both[rows:]).astype(bf16).reshape(peers, each, tile)
+
+
+def owner_kernel(early, block, pick_ref, w_msg_ref, slots_ref, ride_ref, *rest):
+    arrived_refs, (grad_ref, token_ref, held_ref) = rest[:-3], rest[-3:]
+    token_ref[...] = jnp.zeros_like(token_ref)
+    peers, rows, width = slots_ref.shape
+    level, line, _ = place()
+    levels = peers // 2
+    mine = level * 2 + line
+    held_ref[mine] = slots_ref[mine]
+    held_ref[mine ^ 1] = ride_ref[ride_ref.shape[0] - rows :, :width]
+    for i, arrived_ref in enumerate(arrived_refs):
+        spot = (level ^ (levels - 1 - i)) * 2 + line
+        at = block if i < early else 2 * block
+        held_ref[spot] = arrived_ref[at : at + rows, :width]
+        held_ref[spot ^ 1] = arrived_ref[at + rows : at + 2 * rows, :width]
+    nodes = mm(pick_ref[...], held_ref[...].reshape(peers * rows, width), 0, 0).astype(bf16)
+    grad_ref[...] = mm(nodes, w_msg_ref[...], 1, 1).astype(bf16).reshape(grad_ref.shape)
+
+
+def message_kernel(keep_ref, give_ref, slots_ref, other_ref, second_ref, far_ref, near_ref):
+    depth, width = keep_ref.shape[-1], near_ref.shape[1]
+    begin_far = second_ref.shape[0]
+    far_ref[0:begin_far, :] = second_ref[...]
+    for half in range(2):
         own = keep_ref[half].reshape(-1, depth)
         other = give_ref[half].reshape(-1, depth)
-        for begin in range(0, out_ref.shape[1], tile):
+        for begin in range(0, width, tile):
             columns = slice(begin, begin + tile)
-            total = mm(own, slots_ref[:, columns], 1, 0) + mm(other, other_ref[:, columns], 1, 0)
-            out_ref[:, columns] = total.astype(out_ref.dtype)
-
-
-def hidden_sum_kernel(variables, scale, own_ref, *rest):
-    hidden_ref, out_ref, loss_ref = rest[-3:]
-    total = own_ref[...]
-    for r in rest[:-3]:
-        total = total + r[...].astype(f32)
-    width = hidden_ref.shape[1]
-    hidden_ref[...] = total[:, :width]
-    part = total[:, width:]
+            here = slots_ref[:, :, columns].reshape(depth, tile)
+            there = other_ref[:, :, columns].reshape(depth, tile)
+            total = mm(own, here, 1, 0) + mm(other, there, 1, 0)
+            if half == 0:
+                far_ref[begin_far:, columns] = total.astype(bf16)
+            else:
+                near_ref[:, columns] = total
+
+
+def hidden_sum_kernel(variables, scale, early, own_ref, *rest):
+    hidden_ref, out_ref, loss_ref, token_ref = rest[-4:]
+    token_ref[...] = jnp.zeros_like(token_ref)
+    block, width = hidden_ref.shape
+    total = own_ref[:, :width]
+    part = own_ref[:, width:]
+    for i, r in enumerate(rest[:-4]):
+        total = total + r[0:block, :width].astype(f32)
+        if i < early:
+            part = part + r[0:block, width:].astype(f32)
+        else:
+            part = part + unpack(r, r.shape[0] - packed, block, part.shape[1])
+    hidden_ref[...] = total
     out_ref[...] = part[:, :variables]
     column = lax.broadcasted_iota(jnp.int32, (8, part.shape[1]), 1)
     spots = (column == variables) | (column == variables + 1)
@@ -338,10 +439,12 @@
     loss_ref[0] = jnp.sum(jnp.where(spots & first, part[:8], 0.0)) * scale
 
 
-def sum_kernel(own_ref, *rest):
+def sum_kernel(early, own_ref, *rest):
+    block = own_ref.shape[0]
     total = own_ref[...]
-    for r in rest[:-1]:
-        total = total + r[...].astype(f32)
+    for i, r in enumerate(rest[:-1]):
+        begin = 0 if i < early else block
+        total = total + r[begin : begin + block, :].astype(f32)
     rest[-1][...] = total
 
 
@@ -381,17 +484,19 @@
     )
     received = exchange(send).reshape(rows_slot, width)
     present = present_condition.transpose(1, 0, 2)
-    fixed = [w_msg, w_hidden, grid_embed, norm_gain, project, present]
+    fixed = [w_msg, grid_embed, norm_gain, project, present]
+    edges = [edge_slot, edge_dst, edge_weight]
     share, *staged = call(
-        functools.partial(stage_kernel, cap, members),
+        functools.partial(stage_kernel, cap, members, len(fixed)),
         [((2 * rows_slot, rows_all), bf16)] + [(x.shape, x.dtype) for x in fixed],
-        [edge_slot, edge_dst, edge_weight] + fixed,
-        scratch=[pltpu.SemaphoreType.DMA((len(fixed),))],
+        edges + fixed,
+        scratch=[pltpu.VMEM(x.shape, x.dtype) for x in edges]
+        + [pltpu.SemaphoreType.DMA((3 + len(fixed),))],
         limit=16,
-        places=tuple(range(3, 3 + len(fixed))),
+        places=tuple(range(3 + len(fixed))),
         after=[pick],
     )
-    w_msg_near, w_hidden_near, embed, gain, project_near, present = staged
+    w_msg_near, embed, gain, project_near, present = staged
     field, sent, normed, active, slope, unit, inverse = call(
         forward_kernel,
         [
@@ -403,8 +508,10 @@
             ((rows_all, width), f32),
             ((rows_all, 1), f32),
         ],
-        [received, w_msg_near, share, embed, gain, w_hidden_near, project_near, present],
-        limit=20,
+        [received, w_msg_near, share, embed, gain, w_hidden, project_near, present],
+        scratch=[pltpu.VMEM(w_hidden.shape, bf16), pltpu.SemaphoreType.DMA],
+        limit=22,
+        places=(5,),
     )
     other = swap(sent, "member", cores, 1)
     normed_t, active_t, received_keep, received_give = call(
@@ -433,71 +540,94 @@
     (grad_hidden,) = call(
         back_kernel,
         [((rows_all, width), bf16)],
-        [grad_inner, w_hidden_near, gain, unit, inverse],
+        [grad_inner, w_hidden, gain, unit, inverse],
         scratch=[pltpu.VMEM((rows_all, width), f32)],
         limit=14,
     )
     parts = [loss_part, normed_t, active_t, grad_inner, pred]
-    (hidden_far,) = call(
-        functools.partial(pair_kernel, variables, 0),
-        [((half, wide), bf16)],
-        parts + [far_other],
+    (slots,) = call(
+        slot_kernel, [((peers, rows_peer, width), bf16)], [share, grad_hidden], limit=6
+    )
+    early_count = levels // 2
+    count = half // 2
+    first, second = call(
+        functools.partial(far_kernel, variables),
+        [((count + levels * rows_peer, wide), bf16), ((count + packed, width), bf16)],
+        parts + [far_other, slots],
         scratch=[pltpu.VMEM((half, wide), f32)],
         limit=12,
         scalars=(0,),
-        after=[grad_hidden],
-    )
-    hidden_arrived = swap(hidden_far, "space", peers, 1)
-    (slots,) = call(
-        slot_kernel, [((rows_slot, width), bf16)], [share, grad_hidden], limit=6, after=[hidden_far]
-    )
+    )
+    ride = swap(first, "space", peers, 1)
     slots_other = swap(slots, "member", cores, 1)
-    message_far, message_near, slots_out = call(
-        message_kernel,
-        [((half, width), bf16), ((half, width), f32), ((peers, rows_peer, width), bf16)],
-        [received_keep, received_other, slots, slots_other],
-        limit=8,
-    )
-    message_arrived = swap(message_far, "space", peers, 1)
-    back = exchange(slots_out).reshape(rows_slot, width)
     (hidden_near,) = call(
-        functools.partial(pair_kernel, variables, 1),
+        functools.partial(near_kernel, variables),
         [((half, wide), f32)],
         parts + [near_other],
         scratch=[pltpu.VMEM((half, wide), f32)],
         limit=12,
         scalars=(0,),
-        after=[message_far],
-    )
-
-    def spread(near, arrived):
-        *sent, own = call(
-            functools.partial(line_kernel, variables, width),
-            [((block, near.shape[1]), bf16)] * (levels - 1) + [((block, near.shape[1]), f32)],
-            [near, arrived],
-            limit=6,
-        )
-        return own, [swap(x, "space", peers, 2 * (levels - 1 - i)) for i, x in enumerate(sent)]
-
-    hidden_own, hidden_parts = spread(hidden_near, hidden_arrived)
-    message_own, message_parts = spread(message_near, message_arrived)
-    (latent_grad,) = call(
-        owner_kernel, [(latents.shape, bf16)], [pick, back, w_msg], limit=8, after=[hidden_own]
-    )
-    hidden_weight_grad, out_weight_grad, loss = call(
-        functools.partial(hidden_sum_kernel, variables, 1.0 / (points * peers * variables)),
-        [((block, width), f32), ((block, variables), f32), ((1,), f32)],
-        [hidden_own] + hidden_parts,
+        after=[first],
+    )
+    message_far, message_near = call(
+        message_kernel,
+        [((count + packed + half, width), bf16), ((half, width), f32)],
+        [received_keep, received_other, slots, slots_other, second],
+        limit=8,
+        after=[hidden_near],
+    )
+    arrived = swap(message_far, "space", peers, 1)
+    steps = [2 * (levels - 1 - i) for i in range(levels - 1)]
+    early = call(
+        functools.partial(early_kernel, variables),
+        [((block + 2 * rows_peer, wide), bf16)] * early_count,
+        [hidden_near, ride, slots],
+        limit=6,
+        cost=2 * 10**10,
+    )
+    early_parts = [swap(x, "space", peers, k) for x, k in zip(early, steps[:early_count], strict=True)]
+    *rest, hidden_own, message_own = call(
+        functools.partial(late_kernel, variables, early_count),
+        [((2 * block + 2 * rows_peer + packed, width), bf16)] * (levels - 1 - early_count)
+        + [((block, width), bf16)] * early_count
+        + [((block, wide), f32), ((block, width), f32)],
+        [hidden_near, message_near, arrived, ride, slots],
+        limit=8,
+        after=early_parts,
+    )
+    late_parts = [
+        swap(x, "space", peers, k)
+        for x, k in zip(rest[: levels - 1 - early_count], steps[early_count:], strict=True)
+    ]
+    message_parts = [
+        swap(x, "space", peers, k)
+        for x, k in zip(rest[levels - 1 - early_count :], steps[:early_count], strict=True)
+    ]
+    token = ((8, lanes), f32)
+    latent_grad, latent_done = call(
+        functools.partial(owner_kernel, early_count, block),
+        [(latents.shape, bf16), token],
+        [pick, w_msg, slots, ride] + early_parts + late_parts,
+        scratch=[pltpu.VMEM((peers, rows_peer, width), bf16)],
+        limit=8,
+        after=[message_own],
+    )
+    hidden_weight_grad, out_weight_grad, loss, hidden_done = call(
+        functools.partial(
+            hidden_sum_kernel, variables, 1.0 / (points * peers * variables), early_count
+        ),
+        [((block, width), f32), ((block, variables), f32), ((1,), f32), token],
+        [hidden_own] + early_parts + late_parts,
         limit=6,
         scalar_outs=(2,),
-        after=[message_own],
+        after=[latent_done],
     )
     (msg_weight_grad,) = call(
-        sum_kernel,
+        functools.partial(sum_kernel, early_count),
         [((block, width), f32)],
-        [message_own] + message_parts,
+        [message_own] + message_parts + late_parts,
         limit=6,
-        after=[hidden_weight_grad],
+        after=[hidden_done],
     )
     return (latent_grad, loss, msg_weight_grad, hidden_weight_grad, out_weight_grad)
 

time: 82.2 us -> 83 us (level)
  waiting for transfers between devices: 21.7 us -> 44.3 us
  Pallas kernels: 26.8 us -> 19.1 us
  local copies, waits for them, and re-layouts: 8.6 us -> 1.62 us
  starting transfers between devices: 23.6 us -> 16.7 us
    ppermute x13 -> x12, waiting for transfers between devices: 19.4 us -> 38 us  [swap(): return lax.ppermute(value, axis, [(i, i ^ step) for i in range(size)])]
    pallas_call x15, Pallas kernels: 26.8 us -> 19.1 us  [call(): pl.pallas_call(inner if count else body, out_shape=[jax.ShapeDtypeStruct(...]
    unnamed x40 -> x12, local copies, waits for them, and re-layouts: 8.6 us -> 1.62 us
    all_to_all x1 -> x0, starting transfers between devices: 4.52 us -> none  [on_device(): back = exchange(slots_out).reshape(rows_slot, width)]
    all_to_all x1, waiting for transfers between devices: 2.22 us -> 6.31 us  [on_device(): received = exchange(send).reshape(rows_slot, width)]
    ppermute x13 -> x12, starting transfers between devices: 11.8 us -> 9.45 us  [swap(): return lax.ppermute(value, axis, [(i, i ^ step) for i in range(size)])]
  transfers between devices with their start and end apart: 15 -> 13, of which waited for: 8 -> 6; matrix products, arithmetic and copies ran while one was open for 0% -> 0% of each run, Pallas kernels for 18% -> 13%
where the time goes in v1:
time: 83 us; the launch traced here: 82.7 us
  waiting for transfers between devices  44.3 us (53%)
  Pallas kernels  19.1 us (23%)
  starting transfers between devices  16.7 us (20%)
  local copies, waits for them, and re-layouts  1.62 us (2%)
    ppermute x12, waiting for transfers between devices, swap(): return lax.ppermute(value, axis, [(i, i ^ step) for i in range(size)])  38 us
    pallas_call x15, Pallas kernels, call(): pl.pallas_call(inner if count else body, out_shape=[jax.ShapeDtypeStruct(...  19.1 us
    ppermute x12, starting transfers between devices, swap(): return lax.ppermute(value, axis, [(i, i ^ step) for i in range(size)])  9.45 us
    all_to_all x1, starting transfers between devices, on_device(): received = exchange(send).reshape(rows_slot, width)  7.29 us
    all_to_all x1, waiting for transfers between devices, on_device(): received = exchange(send).reshape(rows_slot, width)  6.31 us
  transfers between devices with their start and end apart: 13, of which 6 were waited for; matrix products, arithmetic and copies ran while one was open for 0% of the time, Pallas kernels for 13%

profile of v1, /device:TPU:0, one launch (start us, length us, event | category | flops | bytes accessed | tf_op | source)
XLA Modules:
  0.0 82.7 jit_solution(3369070343284522947)
XLA Ops:
  0.6 1.8 %shard_map.164 = (bf16[8,16,1024]{2,1,0:T(8,128)(2,1)}, bf16[128,64]{1,0:T(8,128)(2,1)S(1)}) custom-call(s32[1,8,8]{2,1,0:T(8,128)} %lists_ref.1, bf16[2,32,1024]{2,1,0:T(8,128)(2,1)} %latents_ref.1), custom_call_target="tpu_custom_call" | custom-call | tf_op jit(solution)/shard_map/pallas_call | solution.py:37
  2.5 7.3 %all-to-all-start = ((bf16[8,16,1024]{2,1,0:T(8,128)(2,1)}), bf16[8,16,1024]{2,1,0:T(8,128)(2,1)S(1)}, u32[]{:S(2)}, u32[]{:S(2)}) async-start(bf16[8,16,1024]{2,1,0:T(8,128)(2,1)} %get-tuple-element.46), calls=%async_computation | async-start | bytes 524288 | tf_op jit(solution)/shard_map/all_to_all | solution.py:485
  9.8 1.9 %shard_map.165 = (bf16[256,512]{1,0:T(8,128)(2,1)S(1)}, bf16[1024,1024]{1,0:T(8,128)(2,1)S(1)}, bf16[256,1024]{1,0:T(8,128)(2,1)S(1)}, f32[1024]{0:T(1024)S(1)},...) custom-call(bf16[128,64]{1,0:T(8,128)(2,1)S(1)} %get-tuple-element.47.refs_0_.refs_1_, s32[1536]{0:T(1024)} %refs_1_.1, ...), custom_call_target="tpu_custom_call" | custom-call | tf_op jit(solution)/shard_map/pallas_call | solution.py:37
  11.7 0.7 copy-done.2
  12.4 6.3 %all-to-all-done = bf16[8,16,1024]{2,1,0:T(8,128)(2,1)S(1)} async-done(((bf16[8,16,1024]{2,1,0:T(8,128)(2,1)}), bf16[8,16,1024]{2,1,0:T(8,128)(2,1)S(1)}, u32[]{:S(2)}, u32[]{:S(2)}) %all-to-all-start) | async-done | bytes 262176 | tf_op jit(solution)/shard_map/all_to_all | solution.py:485
  18.7 0.9 %copy-done.3 = f32[100,2,256]{2,1,0:T(2,128)S(1)} copy-done((f32[100,2,256]{2,1,0:T(2,128)S(1)}, f32[100,2,256]{2,1,0:T(2,128)}, u32[]{:S(2)}) %copy-start.3) | copy-done | bytes 204824
  19.6 4.1 %shard_map.166 = (f32[2,100,256]{2,1,0:T(8,128)S(1)}, bf16[2,100,256]{2,1,0:T(8,128)(2,1)S(1)}, bf16[512,1024]{1,0:T(8,128)(2,1)S(1)}, bf16[512,1024]{1,0:T(8,12...) custom-call(bf16[128,1024]{1,0:T(8,128)(2,1)S(1)} %bitcast.3, ...), custom_call_target="tpu_custom_call" | custom-call | tf_op jit(solution)/shard_map/pallas_call | solution.py:37
  23.9 0.9 %shard_map.167 = (bf16[2,2,4,64,512]{4,3,2,1,0:T(8,128)(2,1)S(1)}, bf16[2,2,4,64,512]{4,3,2,1,0:T(8,128)(2,1)S(1)}, bf16[2,4,64,128]{3,2,1,0:T(8,128)(2,1)S(1)}, bf16[2,4,64,128]{3,2,1,0:T(8,128)(2,1)S(1)}) custom-call(bf16[512,1024]{1,0:T(8,128)(2,1)S(1)} %get-tuple-element.57.normed_ref, bf16[512,1024]{1,0:T(8,128)(2,1)S(1)} %get-tuple-element.58.active_ref, ...), custom_call_target="tpu_custom_call" | custom-call | tf_op jit(solution)/shard_map/pallas_call | solution.py:37
  24.8 0.4 collective-permute-done.other_ref
  25.2 1.5 %shard_map.168 = (bf16[512,1024]{1,0:T(8,128)(2,1)S(1)}, bf16[128,512]{1,0:T(8,128)(2,1)S(1)}, f32[1]{0:T(128)}, bf16[256,1152]{1,0:T(8,128)(2,1)S(1)}, bf16[256,1152]{1,0:T(8,128)(2,1)S(1)}) custom-call(f32[2,100,256]{2,1,0:T(8,128)S(1)} %get-tuple-element.54.own_ref, bf16[2,100,256]{2,1,0:T(8,128)(2,1)S(1)} %collective-permute-done.other_ref, ...), custom_call_target="tpu_custom_call" | custom-call | tf_op jit(solution)/shard_map/pallas_call | solution.py:37
  26.7 0.2 collective-permute-start.1
  27.0 0.3 collective-permute-start.2
  27.3 1.6 %shard_map.169.grad_ref = bf16[512,1024]{1,0:T(8,128)(2,1)S(1)} custom-call(bf16[512,1024]{1,0:T(8,128)(2,1)S(1)} %get-tuple-element.62.inner_ref.refs_4_, bf16[1024,1024]{1,0:T(8,128)(2,1)S(1)} %copy-done, f32[1024]{0:T(1024)S(1)} %get-tuple-element.51.gain_ref, f32[512,1024]{1,0:T(8,128)S(1)} %get-tuple-element.65.unit_ref, ...), custom_call_target="tpu_custom_call" | custom-call | tf_op jit(solution)/shard_map/pallas_call | solution.py:37
  28.9 0.4 shard_map.170.slots_ref.refs_3_.refs_6_
  29.4 1.4 %shard_map.171 = (bf16[192,1152]{1,0:T(8,128)(2,1)S(1)}, bf16[144,1024]{1,0:T(8,128)(2,1)S(1)}) custom-call(f32[1]{0:T(128)} %get-tuple-element.61.loss_ref.refs_1_, bf16[2,2,4,64,512]{4,3,2,1,0:T(8,128)(2,1)S(1)} %get-tuple-element.59.normed_t_ref.refs_2_, bf16[2,2,4,64,512]{4,3,2,1,0:T(8,128)(2,1)S(1)} %get-tuple-element.60.active_t_ref.refs_3_, ...), custom_call_target="tpu_custom_call" | custom-call | tf_op jit(solution)/shard_map/pallas_call | solution.py:37
  30.8 1.5 %collective-permute-start.3 = (bf16[192,1152]{1,0:T(8,128)(2,1)S(1)}, bf16[192,1152]{1,0:T(8,128)(2,1)S(1)}, u32[]{:S(2)}, u32[]{:S(2)}) collective-permute-start(bf16[192,1152]{1,0:T(8,128)(2,1)S(1)} %get-tuple-element.67.refs_0_), channel_id=1, source_target_pairs={{0,2},{2,0},{4,6},{6,4},{8,10},{10,8},{12,14},{14,12},{1,3},{3,1},... | collective-permute-start | bytes 1327112 | tf_op jit(solution)/shard_map/ppermute | solution.py:54
  32.2 0.5 collective-permute-start.6
  32.8 1.3 %shard_map.172.kept_ref.refs_0_.refs_2_ = f32[256,1152]{1,0:T(8,128)S(1)} custom-call(bf16[192,1152]{1,0:T(8,128)(2,1)S(1)} %get-tuple-element.67.refs_0_, f32[1]{0:T(128)} %get-tuple-element.61.loss_ref.refs_1_, bf16[2,2,4,64,512]{4,3,2,1,0:T(8,128)(2,1)S(1)} %get-tuple-element.59.normed_t_ref.refs_2_, ...), custom_call_target="tpu_custom_call" | custom-call | tf_op jit(solution)/shard_map/pallas_call | solution.py:37
  34.0 0.7 shard_map.174
  34.8 0.7 collective-permute-start.8
  35.4 8.4 %collective-permute-done.3.ride_ref.refs_5_.refs_4_ = bf16[192,1152]{1,0:T(8,128)(2,1)S(1)} collective-permute-done((bf16[192,1152]{1,0:T(8,128)(2,1)S(1)}, bf16[192,1152]{1,0:T(8,128)(2,1)S(1)}, u32[]{:S(2)}, u32[]{:S(2)}) %collective-permute-start.3) | collective-permute-done | bytes 442400 | tf_op jit(solution)/shard_map/ppermute | solution.py:54
  43.9 1.2 %collective-permute-start.4 = (bf16[96,1152]{1,0:T(8,128)(2,1)S(1)}, bf16[96,1152]{1,0:T(8,128)(2,1)S(1)}, u32[]{:S(2)}, u32[]{:S(2)}) collective-permute-start(bf16[96,1152]{1,0:T(8,128)(2,1)S(1)} %get-tuple-element.69), channel_id=1, source_target_pairs={{0,12},{2,14},{4,8},{6,10},{8,4},{10,6},{12,0},{14,2},{1,13},{3,15... | collective-permute-start | bytes 663560 | tf_op jit(solution)/shard_map/ppermute | solution.py:54
  45.1 1.4 %collective-permute-start.5 = (bf16[96,1152]{1,0:T(8,128)(2,1)S(1)}, bf16[96,1152]{1,0:T(8,128)(2,1)S(1)}, u32[]{:S(2)}, u32[]{:S(2)}) collective-permute-start(bf16[96,1152]{1,0:T(8,128)(2,1)S(1)} %get-tuple-element.70), channel_id=1, source_target_pairs={{0,8},{2,10},{4,12},{6,14},{8,0},{10,2},{12,4},{14,6},{1,9},{3,11}... | collective-permute-start | bytes 663560 | tf_op jit(solution)/shard_map/ppermute | solution.py:54
  46.5 7.7 %collective-permute-done.4.refs_0_.refs_5_.refs_2_ = bf16[96,1152]{1,0:T(8,128)(2,1)S(1)} collective-permute-done((bf16[96,1152]{1,0:T(8,128)(2,1)S(1)}, bf16[96,1152]{1,0:T(8,128)(2,1)S(1)}, u32[]{:S(2)}, u32[]{:S(2)}) %collective-permute-start.4) | collective-permute-done | bytes 221216 | tf_op jit(solution)/shard_map/ppermute | solution.py:54
  54.2 10.5 %collective-permute-done.5.refs_1_.refs_6_.refs_3_ = bf16[96,1152]{1,0:T(8,128)(2,1)S(1)} collective-permute-done((bf16[96,1152]{1,0:T(8,128)(2,1)S(1)}, bf16[96,1152]{1,0:T(8,128)(2,1)S(1)}, u32[]{:S(2)}, u32[]{:S(2)}) %collective-permute-start.5) | collective-permute-done | bytes 221216 | tf_op jit(solution)/shard_map/ppermute | solution.py:54
  64.7 0.2 shard_map.175
  64.9 1.5 %collective-permute-start.10 = (bf16[64,1024]{1,0:T(8,128)(2,1)S(1)}, bf16[64,1024]{1,0:T(8,128)(2,1)S(1)}, u32[]{:S(2)}, u32[]{:S(2)}) collective-permute-start(bf16[64,1024]{1,0:T(8,128)(2,1)S(1)} %get-tuple-element.83), channel_id=1, source_target_pairs={{0,12},{2,14},{4,8},{6,10},{8,4},{10,6},{12,0},{14,2},{1,13},{3,15... | collective-permute-start | bytes 393224 | tf_op jit(solution)/shard_map/ppermute | solution.py:54
  66.5 1.9 %collective-permute-start.11 = (bf16[64,1024]{1,0:T(8,128)(2,1)S(1)}, bf16[64,1024]{1,0:T(8,128)(2,1)S(1)}, u32[]{:S(2)}, u32[]{:S(2)}) collective-permute-start(bf16[64,1024]{1,0:T(8,128)(2,1)S(1)} %get-tuple-element.84), channel_id=1, source_target_pairs={{0,8},{2,10},{4,12},{6,14},{8,0},{10,2},{12,4},{14,6},{1,9},{3,11}... | collective-permute-start | bytes 393224 | tf_op jit(solution)/shard_map/ppermute | solution.py:54
  68.4 11.1 %collective-permute-done.9.refs_7_.refs_4_ = bf16[176,1024]{1,0:T(8,128)(2,1)S(1)} collective-permute-done((bf16[176,1024]{1,0:T(8,128)(2,1)S(1)}, bf16[176,1024]{1,0:T(8,128)(2,1)S(1)}, u32[]{:S(2)}, u32[]{:S(2)}) %collective-permute-start.9) | collective-permute-done | bytes 360480 | tf_op jit(solution)/shard_map/ppermute | solution.py:54
  79.5 1.5 %shard_map.176 = (bf16[2,32,1024]{2,1,0:T(8,128)(2,1)}, f32[8,128]{1,0:T(8,128)S(1)}) custom-call(f32[64,1024]{1,0:T(8,128)S(1)} %get-tuple-element.76.refs_0_.refs_1_, bf16[128,64]{1,0:T(8,128)(2,1)S(1)} %get-tuple-element.47.refs_0_.refs_1_, bf16[1024,1024]{1,0:T(8,128)(2,1)S(1)} %copy-done.1, ...), custom_call_target="tpu_custom_call" | custom-call | tf_op jit(solution)/shard_map/pallas_call | solution.py:37
  81.1 0.8 shard_map.177
  81.9 0.8 shard_map.178
  (21 shorter events, 0.3 us)
Async XLA Ops:
  2.5 16.2 %all-to-all-start = ((bf16[8,16,1024]{2,1,0:T(8,128)(2,1)}), bf16[8,16,1024]{2,1,0:T(8,128)(2,1)S(1)}, u32[]{:S(2)}, u32[]{:S(2)}) async-start(bf16[8,16,1024]{2,1,0:T(8,128)(2,1)} %get-tuple-element.46), calls=%async_computation | async-start | bytes 524288 | tf_op jit(solution)/shard_map/all_to_all | solution.py:485
  11.7 0.7 copy-start.2
  18.7 0.9 %copy-start.3 = (f32[100,2,256]{2,1,0:T(2,128)S(1)}, f32[100,2,256]{2,1,0:T(2,128)}, u32[]{:S(2)}) copy-start(f32[100,2,256]{2,1,0:T(2,128)} %copy-done.2) | copy-start | bytes 614404
  23.8 1.4 %copy-start.4 = (f32[100,256]{1,0:T(8,128)S(1)}, f32[100,256]{1,0:T(8,128)}, u32[]{:S(2)}) copy-start(f32[100,256]{1,0:T(8,128)} %truth_ref.1) | copy-start | bytes 307204
  23.8 1.4 %copy-start.5 = (f32[256]{0:T(256)S(1)}, f32[256]{0:T(256)}, u32[]{:S(2)}) copy-start(f32[256]{0:T(256)} %cell_ref.1) | copy-start | bytes 3076
  23.8 1.4 %collective-permute-start = (bf16[2,100,256]{2,1,0:T(8,128)(2,1)S(1)}, bf16[2,100,256]{2,1,0:T(8,128)(2,1)S(1)}, u32[]{:S(2)}, u32[]{:S(2)}) collective-permute-start(bf16[2,100,256]{2,1,0:T(8,128)(2,1)S(1)} %get-tuple-element.55), channel_id=1, source_target_pairs={{0,1},{1,0},{2,3},{3,2},{4,5},{5,4},{6,7},{7,6},{8,9},{9,8},{10,11... | collective-permute-start | bytes 307208 | tf_op jit(solution)/shard_map/ppermute | solution.py:54
  25.2 2.1 %copy-start = (bf16[1024,1024]{1,0:T(8,128)(2,1)S(1)}, bf16[1024,1024]{1,0:T(8,128)(2,1)}, u32[]{:S(2)}) copy-start(bf16[1024,1024]{1,0:T(8,128)(2,1)} %w_hidden_ref.3) | copy-start | bytes 6291460
  26.7 2.7 %collective-permute-start.1 = (bf16[256,1152]{1,0:T(8,128)(2,1)S(1)}, bf16[256,1152]{1,0:T(8,128)(2,1)S(1)}, u32[]{:S(2)}, u32[]{:S(2)}) collective-permute-start(bf16[256,1152]{1,0:T(8,128)(2,1)S(1)} %get-tuple-element.64), channel_id=1, source_target_pairs={{0,1},{1,0},{2,3},{3,2},{4,5},{5,4},{6,7},{7,6},{8,9},{9,8},{10,11... | collective-permute-start | bytes 1769480 | tf_op jit(solution)/shard_map/ppermute | solution.py:54
  27.0 5.8 %collective-permute-start.2 = (bf16[256,1152]{1,0:T(8,128)(2,1)S(1)}, bf16[256,1152]{1,0:T(8,128)(2,1)S(1)}, u32[]{:S(2)}, u32[]{:S(2)}) collective-permute-start(bf16[256,1152]{1,0:T(8,128)(2,1)S(1)} %get-tuple-element.68), channel_id=1, source_target_pairs={{0,1},{1,0},{2,3},{3,2},{4,5},{5,4},{6,7},{7,6},{8,9},{9,8},{10,11... | collective-permute-start | bytes 1769480 | tf_op jit(solution)/shard_map/ppermute | solution.py:54
  30.8 13.1 %collective-permute-start.3 = (bf16[192,1152]{1,0:T(8,128)(2,1)S(1)}, bf16[192,1152]{1,0:T(8,128)(2,1)S(1)}, u32[]{:S(2)}, u32[]{:S(2)}) collective-permute-start(bf16[192,1152]{1,0:T(8,128)(2,1)S(1)} %get-tuple-element.67.refs_0_), channel_id=1, source_target_pairs={{0,2},{2,0},{4,6},{6,4},{8,10},{10,8},{12,14},{14,12},{1,3},{3,1},... | collective-permute-start | bytes 1327112 | tf_op jit(solution)/shard_map/ppermute | solution.py:54
  32.2 1.8 %collective-permute-start.7 = (bf16[8,16,1024]{2,1,0:T(8,128)(2,1)S(1)}, bf16[8,16,1024]{2,1,0:T(8,128)(2,1)S(1)}, u32[]{:S(2)}, u32[]{:S(2)}) collective-permute-start(bf16[8,16,1024]{2,1,0:T(8,128)(2,1)S(1)} %shard_map.170.slots_ref.refs_3_.refs_6_), channel_id=1, source_target_pairs={{0,1},{1,0},{2,3},{3,2},{4,5},{5,4},{6,7},{7,6},{8,9},{9,8},{10,11... | collective-permute-start | bytes 786440 | tf_op jit(solution)/shard_map/ppermute | solution.py:54
  32.2 1.8 %collective-permute-start.6 = (bf16[2,4,64,128]{3,2,1,0:T(8,128)(2,1)S(1)}, bf16[2,4,64,128]{3,2,1,0:T(8,128)(2,1)S(1)}, u32[]{:S(2)}, u32[]{:S(2)}) collective-permute-start(bf16[2,4,64,128]{3,2,1,0:T(8,128)(2,1)S(1)} %get-tuple-element.72), channel_id=1, source_target_pairs={{0,1},{1,0},{2,3},{3,2},{4,5},{5,4},{6,7},{7,6},{8,9},{9,8},{10,11... | collective-permute-start | bytes 393224 | tf_op jit(solution)/shard_map/ppermute | solution.py:54
  34.8 29.9 %collective-permute-start.8 = (bf16[400,1024]{1,0:T(8,128)(2,1)S(1)}, bf16[400,1024]{1,0:T(8,128)(2,1)S(1)}, u32[]{:S(2)}, u32[]{:S(2)}) collective-permute-start(bf16[400,1024]{1,0:T(8,128)(2,1)S(1)} %get-tuple-element.75), channel_id=1, source_target_pairs={{0,2},{2,0},{4,6},{6,4},{8,10},{10,8},{12,14},{14,12},{1,3},{3,1},... | collective-permute-start | bytes 2457608 | tf_op jit(solution)/shard_map/ppermute | solution.py:54
  43.9 10.3 %collective-permute-start.4 = (bf16[96,1152]{1,0:T(8,128)(2,1)S(1)}, bf16[96,1152]{1,0:T(8,128)(2,1)S(1)}, u32[]{:S(2)}, u32[]{:S(2)}) collective-permute-start(bf16[96,1152]{1,0:T(8,128)(2,1)S(1)} %get-tuple-element.69), channel_id=1, source_target_pairs={{0,12},{2,14},{4,8},{6,10},{8,4},{10,6},{12,0},{14,2},{1,13},{3,15... | collective-permute-start | bytes 663560 | tf_op jit(solution)/shard_map/ppermute | solution.py:54
  45.1 19.5 %collective-permute-start.5 = (bf16[96,1152]{1,0:T(8,128)(2,1)S(1)}, bf16[96,1152]{1,0:T(8,128)(2,1)S(1)}, u32[]{:S(2)}, u32[]{:S(2)}) collective-permute-start(bf16[96,1152]{1,0:T(8,128)(2,1)S(1)} %get-tuple-element.70), channel_id=1, source_target_pairs={{0,8},{2,10},{4,12},{6,14},{8,0},{10,2},{12,4},{14,6},{1,9},{3,11}... | collective-permute-start | bytes 663560 | tf_op jit(solution)/shard_map/ppermute | solution.py:54
  64.7 14.9 %copy-start.1 = (bf16[1024,1024]{1,0:T(8,128)(2,1)S(1)}, bf16[1024,1024]{1,0:T(8,128)(2,1)}, u32[]{:S(2)}) copy-start(bf16[1024,1024]{1,0:T(8,128)(2,1)} %refs_2_.3) | copy-start | bytes 6291460
  64.9 14.7 %collective-permute-start.9 = (bf16[176,1024]{1,0:T(8,128)(2,1)S(1)}, bf16[176,1024]{1,0:T(8,128)(2,1)S(1)}, u32[]{:S(2)}, u32[]{:S(2)}) collective-permute-start(bf16[176,1024]{1,0:T(8,128)(2,1)S(1)} %get-tuple-element.77), channel_id=1, source_target_pairs={{0,4},{2,6},{4,0},{6,2},{8,12},{10,14},{12,8},{14,10},{1,5},{3,7},... | collective-permute-start | bytes 1081352 | tf_op jit(solution)/shard_map/ppermute | solution.py:54
  64.9 16.9 %collective-permute-start.10 = (bf16[64,1024]{1,0:T(8,128)(2,1)S(1)}, bf16[64,1024]{1,0:T(8,128)(2,1)S(1)}, u32[]{:S(2)}, u32[]{:S(2)}) collective-permute-start(bf16[64,1024]{1,0:T(8,128)(2,1)S(1)} %get-tuple-element.83), channel_id=1, source_target_pairs={{0,12},{2,14},{4,8},{6,10},{8,4},{10,6},{12,0},{14,2},{1,13},{3,15... | collective-permute-start | bytes 393224 | tf_op jit(solution)/shard_map/ppermute | solution.py:54
  66.5 15.4 %collective-permute-start.11 = (bf16[64,1024]{1,0:T(8,128)(2,1)S(1)}, bf16[64,1024]{1,0:T(8,128)(2,1)S(1)}, u32[]{:S(2)}, u32[]{:S(2)}) collective-permute-start(bf16[64,1024]{1,0:T(8,128)(2,1)S(1)} %get-tuple-element.84), channel_id=1, source_target_pairs={{0,8},{2,10},{4,12},{6,14},{8,0},{10,2},{12,4},{14,6},{1,9},{3,11}... | collective-permute-start | bytes 393224 | tf_op jit(solution)/shard_map/ppermute | solution.py:54

commit v2 on v0

--- a/solution.py
+++ b/solution.py
@@ -11,6 +11,15 @@
 epsilon = 1e-06
 tile = 256
 lanes = 128
+packed = 16
+cost_hints = {
+    "back_kernel": 8,
+    "slot_kernel": 4,
+    "hidden_early_kernel": 4,
+    "message_early_kernel": 4,
+    "late_kernel": 4,
+    "message_sum_kernel": 8,
+}
 f32 = jnp.float32
 bf16 = jnp.bfloat16
 
@@ -27,6 +36,7 @@
     far_place = pl.BlockSpec(memory_space=pltpu.HBM)
     any_place = pl.BlockSpec(memory_space=pl.ANY)
     count = len(after)
+    cost = cost_hints.get(getattr(body, "func", body).__name__, 0) * 10**9
     args = [pltpu.with_memory_space_constraint(x, pltpu.HBM) if i in places else x for i, x in enumerate(args)]
 
     def inner(*refs):
@@ -40,7 +50,7 @@
         out_specs=[small if i in scalar_outs else whole for i in range(len(outs))],
         scratch_shapes=scratch,
         compiler_params=pltpu.CompilerParams(vmem_limit_bytes=limit * 2**20),
-        cost_estimate=pl.CostEstimate(flops=0, bytes_accessed=0, transcendentals=0),
+        cost_estimate=pl.CostEstimate(flops=cost, bytes_accessed=0, transcendentals=0),
     )(*after, *args)
 
 
@@ -77,20 +87,21 @@
     send_ref[...] = sent.astype(bf16).reshape(send_ref.shape)
 
 
-def stage_kernel(
-    cap, members, slot_ref, dst_ref, weight_ref, w_msg_ref, w_hidden_ref, embed_ref, gain_ref,
-    project_ref, present_ref, share_ref, *rest,
-):
-    staged_refs, sems = rest[:-1], rest[-1]
-    sources = (w_msg_ref, w_hidden_ref, embed_ref, gain_ref, project_ref, present_ref)
+def stage_kernel(cap, members, count, *refs):
+    edge_refs, source_refs, share_ref = refs[:3], refs[3 : 3 + count], refs[3 + count]
+    staged_refs, held_refs, sems = refs[4 + count : 4 + 2 * count], refs[4 + 2 * count : -1], refs[-1]
     copies = [
         pltpu.make_async_copy(source, target, sems.at[i])
-        for i, (source, target) in enumerate(zip(sources, staged_refs, strict=True))
+        for i, (source, target) in enumerate(
+            zip(edge_refs + source_refs, held_refs + staged_refs, strict=True)
+        )
     ]
     for copy in copies:
         copy.start()
-    edge_part(cap, members, slot_ref, dst_ref, weight_ref, share_ref)
-    for copy in copies:
+    for copy in copies[:3]:
+        copy.wait()
+    edge_part(cap, members, *held_refs, share_ref)
+    for copy in copies[3:]:
         copy.wait()
 
 
@@ -119,14 +130,21 @@
 
 
 def forward_kernel(
-    received_ref, w_msg_ref, share_ref, embed_ref, gain_ref, w_hidden_ref, project_ref, present_ref,
+    received_ref, w_msg_ref, share_ref, gain_ref, embed_hbm, w_hidden_hbm, project_hbm, present_hbm,
     field_ref, sent_ref, normed_ref, active_ref, slope_ref, unit_ref, inverse_ref,
+    embed_ref, weights_ref, project_ref, present_ref, sems,
 ):
     points, width = embed_ref.shape
+    far = (embed_hbm, w_hidden_hbm, project_hbm, present_hbm)
+    close = (embed_ref, weights_ref, project_ref, present_ref)
+    copies = [pltpu.make_async_copy(x, y, sems.at[i]) for i, (x, y) in enumerate(zip(far, close, strict=True))]
+    for copy in copies:
+        copy.start()
     variables, members, _ = present_ref.shape
     messages = mm(received_ref[...], w_msg_ref[...], 1, 0).astype(bf16)
     messages = jnp.concatenate([messages, messages], axis=0)
     gain = gain_ref[...].reshape(1, width)
+    copies[0].wait()
     for begin in range(0, members * points, lanes):
         rows = slice(begin, begin + lanes)
         source = slice(begin % points, begin % points + lanes)
@@ -136,13 +154,15 @@
         unit_ref[rows, :] = unit
         inverse_ref[rows, :] = inverse
         normed_ref[rows, :] = (unit * gain).astype(bf16)
+    for copy in copies[1:]:
+        copy.wait()
     root = 0.7978845608028654
     cubic = 0.044715
     for member in range(members):
         rows = slice(member * points, (member + 1) * points)
         for begin in range(0, width, tile):
             columns = slice(begin, begin + tile)
-            inner = mm(normed_ref[rows, :], w_hidden_ref[:, columns], 1, 0)
+            inner = mm(normed_ref[rows, :], weights_ref[:, columns], 1, 0)
             square = inner * inner
             bend = jnp.tanh(inner * (root + root * cubic * square))
             half = 0.5 + 0.5 * bend
@@ -252,30 +272,109 @@
     out_ref[:, width:] = split_loss(part, variables).astype(out_ref.dtype)
 
 
-def pair_kernel(
-    variables, half, loss_ref, normed_t_ref, active_t_ref, inner_ref, pred_ref, arrived_ref, *out_refs
+def pack(out_ref, begin, part):
+    pad = part.shape[1]
+    for i in range(part.shape[0] // packed):
+        out_ref[begin : begin + packed, i * pad : (i + 1) * pad] = part[i * packed : (i + 1) * packed]
+
+
+def unpack(in_ref, begin, count, pad):
+    parts = [in_ref[begin : begin + packed, i * pad : (i + 1) * pad] for i in range(count // packed)]
+    return jnp.concatenate(parts, axis=0).astype(f32)
+
+
+def local_kernel(variables, loss_ref, normed_t_ref, active_t_ref, inner_ref, pred_ref, far_ref, near_ref):
+    for half, out_ref in ((0, far_ref), (1, near_ref)):
+        weight_parts(
+            normed_t_ref, active_t_ref, inner_ref, pred_ref[...], loss_ref[0], variables, 0, half, out_ref
+        )
+
+
+def pair_sum(variables, width, held_ref, other_ref, begin, count):
+    rows = slice(begin, begin + count)
+    total = held_ref[rows, :width] + other_ref[rows, :width].astype(f32)
+    part = held_ref[rows, width:] + other_ref[rows, width:].astype(f32)
+    return total, split_loss(part, variables)
+
+
+def first_kernel(variables, width, held_ref, other_ref, out_ref):
+    total, part = pair_sum(variables, width, held_ref, other_ref, 0, out_ref.shape[0])
+    out_ref[:, :width] = total.astype(bf16)
+    out_ref[:, width:] = part.astype(bf16)
+
+
+def message_kernel(
+    variables, early, levels, keep_ref, give_ref, slots_ref, other_ref, held_ref, far_other_ref,
+    first_ref, middle_ref, last_ref, near_ref,
 ):
-    hold_ref = out_refs[-1]
-    width = inner_ref.shape[1]
-    weight_parts(
-        normed_t_ref, active_t_ref, inner_ref, pred_ref[...], loss_ref[0], variables, 0, half, hold_ref
-    )
-    count = hold_ref.shape[0] // (len(out_refs) - 1)
-    for i, out_ref in enumerate(out_refs[:-1]):
-        rows = slice(i * count, (i + 1) * count)
-        total = hold_ref[rows, :] + arrived_ref[rows, :].astype(f32)
-        out_ref[:, :width] = total[:, :width].astype(out_ref.dtype)
-        out_ref[:, width:] = split_loss(total[:, width:], variables).astype(out_ref.dtype)
-
-
-def line_kernel(variables, width, kept_ref, arrived_ref, *out_refs):
+    depth, width = keep_ref.shape[-1], near_ref.shape[1]
+    block = near_ref.shape[0] // levels
+    count, rest = early * block, (levels - 1 - early) * block
+    for begin, size, out_ref in ((count, rest, middle_ref), (count + rest, block, last_ref)):
+        total, part = pair_sum(variables, width, held_ref, far_other_ref, begin, size)
+        out_ref[0:size, :] = total.astype(bf16)
+        out_ref[size : size + packed, :] = jnp.zeros((packed, width), bf16)
+        pack(out_ref, size, part.astype(bf16))
+    for half in range(2):
+        own = keep_ref[half].reshape(-1, depth)
+        other = give_ref[half].reshape(-1, depth)
+        for begin in range(0, width, tile):
+            columns = slice(begin, begin + tile)
+            here = slots_ref[:, :, columns].reshape(depth, tile)
+            there = other_ref[:, :, columns].reshape(depth, tile)
+            total = mm(own, here, 1, 0) + mm(other, there, 1, 0)
+            if half == 0:
+                total = total.astype(bf16)
+                first_ref[:, columns] = total[:count]
+                middle_ref[rest + packed :, columns] = total[count : count + rest]
+                last_ref[block + packed :, columns] = total[count + rest :]
+            else:
+                near_ref[:, columns] = total
+
+
+def ride_kernel(last_ref, slots_ref, *rest):
+    arrived_refs, out_ref = rest[:-1], rest[-1]
+    rows = slots_ref.shape[1]
+    level, line, _ = place()
+    begin = last_ref.shape[0]
+    out_ref[0:begin, :] = last_ref[...]
+    for i, arrived_ref in enumerate(arrived_refs):
+        out_ref[begin + i * rows : begin + (i + 1) * rows, :] = arrived_ref[rows:, :]
+    out_ref[begin + len(arrived_refs) * rows :, :] = slots_ref[level * 2 + 1 - line]
+
+
+def hidden_early_kernel(variables, width, held_ref, other_ref, arrived_ref, *out_refs):
     block = out_refs[0].shape[0]
     for i, out_ref in enumerate(out_refs):
-        rows = slice(i * block, (i + 1) * block)
-        total = kept_ref[rows, :] + arrived_ref[rows, :].astype(f32)
-        out_ref[:, :width] = total[:, :width].astype(out_ref.dtype)
-        if out_ref.shape[1] > width:
-            out_ref[:, width:] = split_loss(total[:, width:], variables).astype(out_ref.dtype)
+        total, part = pair_sum(variables, width, held_ref, other_ref, i * block, block)
+        here = slice(i * block, (i + 1) * block)
+        out_ref[:, :width] = (total + arrived_ref[here, :width].astype(f32)).astype(bf16)
+        part = split_loss(part + arrived_ref[here, width:].astype(f32), variables)
+        out_ref[:, width:] = part.astype(bf16)
+
+
+def message_early_kernel(near_ref, arrived_ref, *out_refs):
+    block = out_refs[0].shape[0]
+    for i, out_ref in enumerate(out_refs):
+        here = slice(i * block, (i + 1) * block)
+        out_ref[...] = (near_ref[here, :] + arrived_ref[here, :].astype(f32)).astype(bf16)
+
+
+def late_kernel(variables, early, held_ref, other_ref, near_ref, arrived_ref, *out_refs):
+    width = near_ref.shape[1]
+    block = (out_refs[0].shape[0] - packed) // 2
+    count = block * len(out_refs)
+    parts = unpack(arrived_ref, count, count, held_ref.shape[1] - width)
+    for i, out_ref in enumerate(out_refs):
+        begin = (early + i) * block
+        total, part = pair_sum(variables, width, held_ref, other_ref, begin, block)
+        here = slice(i * block, (i + 1) * block)
+        out_ref[0:block, :] = (total + arrived_ref[here, :].astype(f32)).astype(bf16)
+        there = slice(count + packed + i * block, count + packed + (i + 1) * block)
+        total = near_ref[begin : begin + block, :] + arrived_ref[there, :].astype(f32)
+        out_ref[block : 2 * block, :] = total.astype(bf16)
+        out_ref[2 * block :, :] = jnp.zeros((packed, width), bf16)
+        pack(out_ref, 2 * block, split_loss(part + parts[here], variables).astype(bf16))
 
 
 def back_kernel(inner_ref, w_hidden_ref, gain_ref, unit_ref, inverse_ref, grad_ref, scaled_ref):
@@ -298,51 +397,67 @@
             ).astype(bf16)
 
 
-def slot_kernel(share_ref, grad_ref, slots_ref):
-    rows = share_ref.shape[0] // 2
-    for begin in range(0, grad_ref.shape[1], tile):
+def slot_kernel(share_ref, grad_ref, slots_ref, *send_refs):
+    peers, each, width = slots_ref.shape
+    rows = peers * each
+    for begin in range(0, width, tile):
         columns = slice(begin, begin + tile)
         both = mm(share_ref[...], grad_ref[:, columns], 1, 0)
-        slots_ref[:, columns] = (both[:rows] + both[rows:]).astype(bf16)
-
-
-def owner_kernel(pick_ref, arrived_ref, w_msg_ref, grad_ref):
-    rows = mm(pick_ref[...], arrived_ref[...], 0, 0).astype(bf16)
-    grad_ref[...] = mm(rows, w_msg_ref[...], 1, 1).astype(bf16).reshape(grad_ref.shape)
-
-
-def message_kernel(keep_ref, give_ref, slots_ref, other_ref, far_ref, near_ref, copy_ref):
-    copy_ref[...] = slots_ref[...].reshape(copy_ref.shape)
-    depth = keep_ref.shape[-1]
-    for half, out_ref in ((0, far_ref), (1, near_ref)):
-        own = keep_ref[half].reshape(-1, depth)
-        other = give_ref[half].reshape(-1, depth)
-        for begin in range(0, out_ref.shape[1], tile):
-            columns = slice(begin, begin + tile)
-            total = mm(own, slots_ref[:, columns], 1, 0) + mm(other, other_ref[:, columns], 1, 0)
-            out_ref[:, columns] = total.astype(out_ref.dtype)
-
-
-def hidden_sum_kernel(variables, scale, own_ref, *rest):
-    hidden_ref, out_ref, loss_ref = rest[-3:]
-    total = own_ref[...]
-    for r in rest[:-3]:
-        total = total + r[...].astype(f32)
-    width = hidden_ref.shape[1]
-    hidden_ref[...] = total[:, :width]
-    part = total[:, width:]
+        slots_ref[:, :, columns] = (both[:rows] + both[rows:]).astype(bf16).reshape(peers, each, tile)
+    level, line, _ = place()
+    levels = peers // 2
+    for i, send_ref in enumerate(send_refs):
+        spot = (level ^ (levels - 1 - i)) * 2 + line
+        send_ref[0:each, :] = slots_ref[spot]
+        send_ref[each:, :] = slots_ref[spot ^ 1]
+
+
+def owner_kernel(pick_ref, w_msg_ref, slots_ref, last_ref, *rest):
+    arrived_refs, (grad_ref, token_ref, held_ref) = rest[:-3], rest[-3:]
+    token_ref[...] = jnp.zeros_like(token_ref)
+    peers, rows, width = slots_ref.shape
+    level, line, _ = place()
+    levels = peers // 2
+    begin = last_ref.shape[0] - levels * rows
+    for i in range(levels):
+        spot = (level ^ (levels - 1 - i)) * 2 + line
+        held_ref[spot] = slots_ref[spot] if i == levels - 1 else arrived_refs[i][0:rows, :]
+        held_ref[spot ^ 1] = last_ref[begin + i * rows : begin + (i + 1) * rows, :]
+    nodes = mm(pick_ref[...], held_ref[...].reshape(peers * rows, width), 0, 0).astype(bf16)
+    grad_ref[...] = mm(nodes, w_msg_ref[...], 1, 1).astype(bf16).reshape(grad_ref.shape)
+
+
+def hidden_sum_kernel(variables, scale, early, held_ref, other_ref, last_ref, *rest):
+    hidden_ref, out_ref, loss_ref, token_ref = rest[-4:]
+    token_ref[...] = jnp.zeros_like(token_ref)
+    block, width = hidden_ref.shape
+    pad = held_ref.shape[1] - width
+    total, part = pair_sum(variables, width, held_ref, other_ref, held_ref.shape[0] - block, block)
+    total = total + last_ref[0:block, :].astype(f32)
+    part = part + unpack(last_ref, block, block, pad)
+    for i, r in enumerate(rest[:-4]):
+        total = total + r[0:block, :width].astype(f32)
+        if i < early:
+            part = part + r[:, width:].astype(f32)
+        else:
+            part = part + unpack(r, 2 * block, block, pad)
+    hidden_ref[...] = total
     out_ref[...] = part[:, :variables]
-    column = lax.broadcasted_iota(jnp.int32, (8, part.shape[1]), 1)
+    column = lax.broadcasted_iota(jnp.int32, (8, pad), 1)
     spots = (column == variables) | (column == variables + 1)
-    first = lax.broadcasted_iota(jnp.int32, (8, part.shape[1]), 0) == 0
+    first = lax.broadcasted_iota(jnp.int32, (8, pad), 0) == 0
     loss_ref[0] = jnp.sum(jnp.where(spots & first, part[:8], 0.0)) * scale
 
 
-def sum_kernel(own_ref, *rest):
-    total = own_ref[...]
-    for r in rest[:-1]:
-        total = total + r[...].astype(f32)
-    rest[-1][...] = total
+def message_sum_kernel(early, near_ref, last_ref, *rest):
+    out_ref = rest[-1]
+    block = out_ref.shape[0]
+    total = near_ref[near_ref.shape[0] - block :, :]
+    total = total + last_ref[block + packed : 2 * block + packed, :].astype(f32)
+    for i, r in enumerate(rest[:-1]):
+        begin = 0 if i < early else block
+        total = total + r[begin : begin + block, :].astype(f32)
+    out_ref[...] = total
 
 
 def on_device(
@@ -381,17 +496,20 @@
     )
     received = exchange(send).reshape(rows_slot, width)
     present = present_condition.transpose(1, 0, 2)
-    fixed = [w_msg, w_hidden, grid_embed, norm_gain, project, present]
+    fixed = [w_msg]
+    direct = [grid_embed, w_hidden, project, present]
+    edges = [edge_slot, edge_dst, edge_weight]
     share, *staged = call(
-        functools.partial(stage_kernel, cap, members),
+        functools.partial(stage_kernel, cap, members, len(fixed)),
         [((2 * rows_slot, rows_all), bf16)] + [(x.shape, x.dtype) for x in fixed],
-        [edge_slot, edge_dst, edge_weight] + fixed,
-        scratch=[pltpu.SemaphoreType.DMA((len(fixed),))],
+        edges + fixed,
+        scratch=[pltpu.VMEM(x.shape, x.dtype) for x in edges]
+        + [pltpu.SemaphoreType.DMA((3 + len(fixed),))],
         limit=16,
-        places=tuple(range(3, 3 + len(fixed))),
+        places=tuple(range(3 + len(fixed))),
         after=[pick],
     )
-    w_msg_near, w_hidden_near, embed, gain, project_near, present = staged
+    (w_msg_near,) = staged
     field, sent, normed, active, slope, unit, inverse = call(
         forward_kernel,
         [
@@ -403,8 +521,10 @@
             ((rows_all, width), f32),
             ((rows_all, 1), f32),
         ],
-        [received, w_msg_near, share, embed, gain, w_hidden_near, project_near, present],
-        limit=20,
+        [received, w_msg_near, share, norm_gain] + direct,
+        scratch=[pltpu.VMEM(x.shape, x.dtype) for x in direct] + [pltpu.SemaphoreType.DMA((len(direct),))],
+        limit=22,
+        places=(4, 5, 6, 7),
     )
     other = swap(sent, "member", cores, 1)
     normed_t, active_t, received_keep, received_give = call(
@@ -423,81 +543,113 @@
             ((half, wide), bf16),
             ((half, wide), bf16),
         ],
-        [field, other, verifying_field, cell_surface, project_near, slope, normed_t, active_t],
+        [field, other, verifying_field, cell_surface, project, slope, normed_t, active_t],
         scratch=[pltpu.VMEM((lanes, rows_all), f32)],
         limit=16,
         scalar_outs=(2,),
     )
     far_other = swap(far, "member", cores, 1)
     near_other = swap(near, "member", cores, 1)
+    held_far, held_near = call(
+        functools.partial(local_kernel, variables),
+        [((half, wide), f32)] * 2,
+        [loss_part, normed_t, active_t, grad_inner, pred],
+        limit=12,
+        scalars=(0,),
+    )
+    early = levels // 2
+    count, rest = early * block, (levels - 1 - early) * block
+    steps = [2 * (levels - 1 - i) for i in range(levels - 1)]
+
+    def spread(values, part):
+        return [swap(x, "space", peers, k) for x, k in zip(values, part, strict=True)]
+
+    (first,) = call(
+        functools.partial(first_kernel, variables, width),
+        [((count, wide), bf16)],
+        [held_far, far_other],
+        limit=6,
+    )
+    first_other = swap(first, "space", peers, 1)
     (grad_hidden,) = call(
         back_kernel,
         [((rows_all, width), bf16)],
-        [grad_inner, w_hidden_near, gain, unit, inverse],
+        [grad_inner, w_hidden, norm_gain, unit, inverse],
         scratch=[pltpu.VMEM((rows_all, width), f32)],
         limit=14,
-    )
-    parts = [loss_part, normed_t, active_t, grad_inner, pred]
-    (hidden_far,) = call(
-        functools.partial(pair_kernel, variables, 0),
-        [((half, wide), bf16)],
-        parts + [far_other],
-        scratch=[pltpu.VMEM((half, wide), f32)],
-        limit=12,
-        scalars=(0,),
-        after=[grad_hidden],
-    )
-    hidden_arrived = swap(hidden_far, "space", peers, 1)
-    (slots,) = call(
-        slot_kernel, [((rows_slot, width), bf16)], [share, grad_hidden], limit=6, after=[hidden_far]
+        after=[first],
+    )
+    slots, *slots_sent = call(
+        slot_kernel,
+        [((peers, rows_peer, width), bf16)] + [((2 * rows_peer, width), bf16)] * (levels - 1),
+        [share, grad_hidden],
+        limit=6,
     )
     slots_other = swap(slots, "member", cores, 1)
-    message_far, message_near, slots_out = call(
-        message_kernel,
-        [((half, width), bf16), ((half, width), f32), ((peers, rows_peer, width), bf16)],
-        [received_keep, received_other, slots, slots_other],
+    slots_arrived = spread(slots_sent, steps)
+    message_first, middle, last, message_near = call(
+        functools.partial(message_kernel, variables, early, levels),
+        [
+            ((count, width), bf16),
+            ((2 * rest + packed, width), bf16),
+            ((2 * block + packed, width), bf16),
+            ((half, width), f32),
+        ],
+        [received_keep, received_other, slots, slots_other, held_far, far_other],
+        limit=10,
+    )
+    message_first_other = swap(message_first, "space", peers, 1)
+    middle_other = swap(middle, "space", peers, 1)
+    (last,) = call(
+        ride_kernel,
+        [((2 * block + packed + levels * rows_peer, width), bf16)],
+        [last, slots] + slots_arrived,
+        limit=4,
+    )
+    last_other = swap(last, "space", peers, 1)
+    hidden_early = call(
+        functools.partial(hidden_early_kernel, variables, width),
+        [((block, wide), bf16)] * early,
+        [held_near, near_other, first_other],
+        limit=6,
+    )
+    hidden_parts = spread(hidden_early, steps[:early])
+    message_early = call(
+        message_early_kernel,
+        [((block, width), bf16)] * early,
+        [message_near, message_first_other],
+        limit=6,
+    )
+    message_parts = spread(message_early, steps[:early])
+    late = call(
+        functools.partial(late_kernel, variables, early),
+        [((2 * block + packed, width), bf16)] * (levels - 1 - early),
+        [held_near, near_other, message_near, middle_other],
+        limit=6,
+    )
+    late_parts = spread(late, steps[early:])
+    token = ((8, lanes), f32)
+    latent_grad, latent_done = call(
+        owner_kernel,
+        [(latents.shape, bf16), token],
+        [pick, w_msg, slots, last_other] + slots_arrived,
+        scratch=[pltpu.VMEM((peers, rows_peer, width), bf16)],
         limit=8,
     )
-    message_arrived = swap(message_far, "space", peers, 1)
-    back = exchange(slots_out).reshape(rows_slot, width)
-    (hidden_near,) = call(
-        functools.partial(pair_kernel, variables, 1),
-        [((half, wide), f32)],
-        parts + [near_other],
-        scratch=[pltpu.VMEM((half, wide), f32)],
-        limit=12,
-        scalars=(0,),
-        after=[message_far],
-    )
-
-    def spread(near, arrived):
-        *sent, own = call(
-            functools.partial(line_kernel, variables, width),
-            [((block, near.shape[1]), bf16)] * (levels - 1) + [((block, near.shape[1]), f32)],
-            [near, arrived],
-            limit=6,
-        )
-        return own, [swap(x, "space", peers, 2 * (levels - 1 - i)) for i, x in enumerate(sent)]
-
-    hidden_own, hidden_parts = spread(hidden_near, hidden_arrived)
-    message_own, message_parts = spread(message_near, message_arrived)
-    (latent_grad,) = call(
-        owner_kernel, [(latents.shape, bf16)], [pick, back, w_msg], limit=8, after=[hidden_own]
-    )
-    hidden_weight_grad, out_weight_grad, loss = call(
-        functools.partial(hidden_sum_kernel, variables, 1.0 / (points * peers * variables)),
-        [((block, width), f32), ((block, variables), f32), ((1,), f32)],
-        [hidden_own] + hidden_parts,
+    hidden_weight_grad, out_weight_grad, loss, hidden_done = call(
+        functools.partial(hidden_sum_kernel, variables, 1.0 / (points * peers * variables), early),
+        [((block, width), f32), ((block, variables), f32), ((1,), f32), token],
+        [held_near, near_other, last_other] + hidden_parts + late_parts,
+        limit=8,
+        scalar_outs=(2,),
+        after=[latent_done],
+    )
+    (msg_weight_grad,) = call(
+        functools.partial(message_sum_kernel, early),
+        [((block, width), f32)],
+        [message_near, last_other] + message_parts + late_parts,
         limit=6,
-        scalar_outs=(2,),
-        after=[message_own],
-    )
-    (msg_weight_grad,) = call(
-        sum_kernel,
-        [((block, width), f32)],
-        [message_own] + message_parts,
-        limit=6,
-        after=[hidden_weight_grad],
+        after=[hidden_done],
     )
     return (latent_grad, loss, msg_weight_grad, hidden_weight_grad, out_weight_grad)
 

time: 82.2 us -> 70.8 us (0.86)
  local copies, waits for them, and re-layouts: 8.6 us -> 0.03 us
  waiting for transfers between devices: 21.7 us -> 29.8 us
  Pallas kernels: 26.8 us -> 19.3 us
  starting transfers between devices: 23.6 us -> 20.6 us
    unnamed x40 -> x12, local copies, waits for them, and re-layouts: 8.6 us -> 0.03 us
    pallas_call x15 -> x17, Pallas kernels: 26.8 us -> 19.3 us  [call(): pl.pallas_call(inner if count else body, out_shape=[jax.ShapeDtypeStruct(...]
    all_to_all x1, waiting for transfers between devices: 2.22 us -> 7.24 us  [on_device(): received = exchange(send).reshape(rows_slot, width)]
    all_to_all x1 -> x0, starting transfers between devices: 4.52 us -> none  [on_device(): back = exchange(slots_out).reshape(rows_slot, width)]
    ppermute x13 -> x17, waiting for transfers between devices: 19.4 us -> 22.5 us  [swap(): return lax.ppermute(value, axis, [(i, i ^ step) for i in range(size)])]
    ppermute x13 -> x17, starting transfers between devices: 11.8 us -> 13.3 us  [swap(): return lax.ppermute(value, axis, [(i, i ^ step) for i in range(size)])]
  transfers between devices with their start and end apart: 15 -> 18, of which waited for: 8 -> 8; matrix products, arithmetic and copies ran while one was open for 0% -> 0% of each run, Pallas kernels for 18% -> 15%
where the time goes in v2:
time: 70.8 us; the launch traced here: 70.5 us
  waiting for transfers between devices  29.8 us (42%)
  starting transfers between devices  20.6 us (29%)
  Pallas kernels  19.3 us (27%)
  between operations  0.84 us (1%)
    ppermute x17, waiting for transfers between devices, swap(): return lax.ppermute(value, axis, [(i, i ^ step) for i in range(size)])  22.5 us
    pallas_call x17, Pallas kernels, call(): pl.pallas_call(inner if count else body, out_shape=[jax.ShapeDtypeStruct(...  19.3 us
    ppermute x17, starting transfers between devices, swap(): return lax.ppermute(value, axis, [(i, i ^ step) for i in range(size)])  13.3 us
    all_to_all x1, starting transfers between devices, on_device(): received = exchange(send).reshape(rows_slot, width)  7.29 us
    all_to_all x1, waiting for transfers between devices, on_device(): received = exchange(send).reshape(rows_slot, width)  7.24 us
  transfers between devices with their start and end apart: 18, of which 8 were waited for; matrix products, arithmetic and copies ran while one was open for 0% of the time, Pallas kernels for 15%

profile of v2, /device:TPU:0, one launch (start us, length us, event | category | flops | bytes accessed | tf_op | source)
XLA Modules:
  0.0 70.5 jit_solution(2785192958536049017)
XLA Ops:
  0.6 1.8 %shard_map.164 = (bf16[8,16,1024]{2,1,0:T(8,128)(2,1)}, bf16[128,64]{1,0:T(8,128)(2,1)S(1)}) custom-call(s32[1,8,8]{2,1,0:T(8,128)} %lists_ref.1, bf16[2,32,1024]{2,1,0:T(8,128)(2,1)} %latents_ref.1), custom_call_target="tpu_custom_call" | custom-call | tf_op jit(solution)/shard_map/pallas_call | solution.py:46
  2.5 7.3 %all-to-all-start = ((bf16[8,16,1024]{2,1,0:T(8,128)(2,1)}), bf16[8,16,1024]{2,1,0:T(8,128)(2,1)S(1)}, u32[]{:S(2)}, u32[]{:S(2)}) async-start(bf16[8,16,1024]{2,1,0:T(8,128)(2,1)} %get-tuple-element.47), calls=%async_computation | async-start | bytes 524288 | tf_op jit(solution)/shard_map/all_to_all | solution.py:497
  9.8 1.7 %shard_map.165 = (bf16[256,512]{1,0:T(8,128)(2,1)S(1)}, bf16[1024,1024]{1,0:T(8,128)(2,1)S(1)}) custom-call(bf16[128,64]{1,0:T(8,128)(2,1)S(1)} %get-tuple-element.45.refs_0_.pick_ref, s32[1536]{0:T(1024)} %refs_1_.1, s32[1536]{0:T(1024)} %refs_2_.2, f32[1536]{0:T(1024)} %refs_3_.2, bf16[1024,1024]{1,0:T(8,128)(2,1)} %w_msg_ref.1), custom_call_target="tpu_custom_call" | custom-call | tf_op jit(solution)/shard_map/pallas_call | solution.py:46
  11.5 7.2 %all-to-all-done = bf16[8,16,1024]{2,1,0:T(8,128)(2,1)S(1)} async-done(((bf16[8,16,1024]{2,1,0:T(8,128)(2,1)}), bf16[8,16,1024]{2,1,0:T(8,128)(2,1)S(1)}, u32[]{:S(2)}, u32[]{:S(2)}) %all-to-all-start) | async-done | bytes 262176 | tf_op jit(solution)/shard_map/all_to_all | solution.py:497
  18.7 4.7 %shard_map.166 = (f32[2,100,256]{2,1,0:T(8,128)S(1)}, bf16[2,100,256]{2,1,0:T(8,128)(2,1)S(1)}, bf16[512,1024]{1,0:T(8,128)(2,1)S(1)}, bf16[512,1024]{1,0:T(8,12...) custom-call(bf16[128,1024]{1,0:T(8,128)(2,1)S(1)} %bitcast.3, ...), custom_call_target="tpu_custom_call" | custom-call | tf_op jit(solution)/shard_map/pallas_call | solution.py:46
  23.5 0.9 %shard_map.167 = (bf16[2,2,4,64,512]{4,3,2,1,0:T(8,128)(2,1)S(1)}, bf16[2,2,4,64,512]{4,3,2,1,0:T(8,128)(2,1)S(1)}, bf16[2,4,64,128]{3,2,1,0:T(8,128)(2,1)S(1)}, bf16[2,4,64,128]{3,2,1,0:T(8,128)(2,1)S(1)}) custom-call(bf16[512,1024]{1,0:T(8,128)(2,1)S(1)} %get-tuple-element.52.normed_ref, bf16[512,1024]{1,0:T(8,128)(2,1)S(1)} %get-tuple-element.53.active_ref, ...), custom_call_target="tpu_custom_call" | custom-call | tf_op jit(solution)/shard_map/pallas_call | solution.py:46
  24.4 0.4 collective-permute-done.other_ref
  24.8 1.6 %shard_map.168 = (bf16[512,1024]{1,0:T(8,128)(2,1)S(1)}, bf16[128,512]{1,0:T(8,128)(2,1)S(1)}, f32[1]{0:T(128)}, bf16[256,1152]{1,0:T(8,128)(2,1)S(1)}, bf16[256,1152]{1,0:T(8,128)(2,1)S(1)}) custom-call(f32[2,100,256]{2,1,0:T(8,128)S(1)} %get-tuple-element.49.own_ref, bf16[2,100,256]{2,1,0:T(8,128)(2,1)S(1)} %collective-permute-done.other_ref, ...), custom_call_target="tpu_custom_call" | custom-call | tf_op jit(solution)/shard_map/pallas_call | solution.py:46
  26.4 0.2 collective-permute-start.1
  26.6 0.3 collective-permute-start.8
  27.0 1.7 %shard_map.169 = (f32[256,1152]{1,0:T(8,128)S(1)}, f32[256,1152]{1,0:T(8,128)S(1)}) custom-call(f32[1]{0:T(128)} %get-tuple-element.56.loss_ref, bf16[2,2,4,64,512]{4,3,2,1,0:T(8,128)(2,1)S(1)} %get-tuple-element.54.normed_t_ref, bf16[2,2,4,64,512]{4,3,2,1,0:T(8,128)(2,1)S(1)} %get-tuple-element.55.active_t_ref, ...), custom_call_target="tpu_custom_call" | custom-call | tf_op jit(solution)/shard_map/pallas_call | solution.py:46
  28.9 1.7 %shard_map.171.grad_ref = bf16[512,1024]{1,0:T(8,128)(2,1)S(1)} custom-call(bf16[128,1152]{1,0:T(8,128)(2,1)S(1)} %shard_map.170.refs_0_, bf16[512,1024]{1,0:T(8,128)(2,1)S(1)} %get-tuple-element.57.inner_ref.refs_1_, bf16[1024,1024]{1,0:T(8,128)(2,1)S(1)} %copy-done.1, f32[1024]{0:T(1024)S(1)} %copy-done.4, f32[512,1024]{1,0:T(8,128)S(1)} %get-tuple-element.61.refs_4_, ...), custom_call_target="tpu_custom_call" | custom-call | flops 8000000000 | tf_op jit(solution)/shard_map/pallas_call | solution.py:46
  30.6 0.5 shard_map.172
  31.3 1.4 %collective-permute-start.9 = (bf16[128,1152]{1,0:T(8,128)(2,1)S(1)}, bf16[128,1152]{1,0:T(8,128)(2,1)S(1)}, u32[]{:S(2)}, u32[]{:S(2)}) collective-permute-start(bf16[128,1152]{1,0:T(8,128)(2,1)S(1)} %shard_map.170.refs_0_), channel_id=1, source_target_pairs={{0,2},{2,0},{4,6},{6,4},{8,10},{10,8},{12,14},{14,12},{1,3},{3,1},... | collective-permute-start | bytes 884744 | tf_op jit(solution)/shard_map/ppermute | solution.py:63
  32.8 1.5 %collective-permute-start.4 = (bf16[32,1024]{1,0:T(8,128)(2,1)S(1)}, bf16[32,1024]{1,0:T(8,128)(2,1)S(1)}, u32[]{:S(2)}, u32[]{:S(2)}) collective-permute-start(bf16[32,1024]{1,0:T(8,128)(2,1)S(1)} %get-tuple-element.67), channel_id=1, source_target_pairs={{0,12},{2,14},{4,8},{6,10},{8,4},{10,6},{12,0},{14,2},{1,13},{3,15... | collective-permute-start | bytes 196616 | tf_op jit(solution)/shard_map/ppermute | solution.py:63
  34.3 2.9 %collective-permute-start.6 = (bf16[32,1024]{1,0:T(8,128)(2,1)S(1)}, bf16[32,1024]{1,0:T(8,128)(2,1)S(1)}, u32[]{:S(2)}, u32[]{:S(2)}) collective-permute-start(bf16[32,1024]{1,0:T(8,128)(2,1)S(1)} %get-tuple-element.69), channel_id=1, source_target_pairs={{0,4},{2,6},{4,0},{6,2},{8,12},{10,14},{12,8},{14,10},{1,5},{3,7},... | collective-permute-start | bytes 196616 | tf_op jit(solution)/shard_map/ppermute | solution.py:63
  37.2 0.7 %shard_map.173 = (bf16[128,1024]{1,0:T(8,128)(2,1)S(1)}, bf16[144,1024]{1,0:T(8,128)(2,1)S(1)}, bf16[144,1024]{1,0:T(8,128)(2,1)S(1)}, f32[256,1024]{1,0:T(8,128)S(1)}) custom-call(bf16[2,4,64,128]{3,2,1,0:T(8,128)(2,1)S(1)} %get-tuple-element.64.keep_ref, bf16[2,4,64,128]{3,2,1,0:T(8,128)(2,1)S(1)} %collective-permute-done.2.give_ref, ...), custom_call_target="tpu_custom_call" | custom-call | tf_op jit(solution)/shard_map/pallas_call | solution.py:46
  37.9 1.7 %collective-permute-done.4.rest_0_ = bf16[32,1024]{1,0:T(8,128)(2,1)S(1)} collective-permute-done((bf16[32,1024]{1,0:T(8,128)(2,1)S(1)}, bf16[32,1024]{1,0:T(8,128)(2,1)S(1)}, u32[]{:S(2)}, u32[]{:S(2)}) %collective-permute-start.4) | collective-permute-done | bytes 65568 | tf_op jit(solution)/shard_map/ppermute | solution.py:63
  39.6 0.6 collective-permute-start.14
  40.2 1.7 %collective-permute-done.5.rest_1_ = bf16[32,1024]{1,0:T(8,128)(2,1)S(1)} collective-permute-done((bf16[32,1024]{1,0:T(8,128)(2,1)S(1)}, bf16[32,1024]{1,0:T(8,128)(2,1)S(1)}, u32[]{:S(2)}, u32[]{:S(2)}) %collective-permute-start.5) | collective-permute-done | bytes 65568 | tf_op jit(solution)/shard_map/ppermute | solution.py:63
  41.8 0.7 %collective-permute-start.12 = (bf16[144,1024]{1,0:T(8,128)(2,1)S(1)}, bf16[144,1024]{1,0:T(8,128)(2,1)S(1)}, u32[]{:S(2)}, u32[]{:S(2)}) collective-permute-start(bf16[144,1024]{1,0:T(8,128)(2,1)S(1)} %get-tuple-element.77), channel_id=1, source_target_pairs={{0,2},{2,0},{4,6},{6,4},{8,10},{10,8},{12,14},{14,12},{1,3},{3,1},... | collective-permute-start | bytes 884744 | tf_op jit(solution)/shard_map/ppermute | solution.py:63
  42.6 1.4 %collective-permute-start.7 = (bf16[208,1024]{1,0:T(8,128)(2,1)S(1)}, bf16[208,1024]{1,0:T(8,128)(2,1)S(1)}, u32[]{:S(2)}, u32[]{:S(2)}) collective-permute-start(bf16[208,1024]{1,0:T(8,128)(2,1)S(1)} %shard_map.174), channel_id=1, source_target_pairs={{0,2},{2,0},{4,6},{6,4},{8,10},{10,8},{12,14},{14,12},{1,3},{3,1},... | collective-permute-start | bytes 1277960 | tf_op jit(solution)/shard_map/ppermute | solution.py:63
  44.2 1.5 %collective-permute-start.10 = (bf16[64,1152]{1,0:T(8,128)(2,1)S(1)}, bf16[64,1152]{1,0:T(8,128)(2,1)S(1)}, u32[]{:S(2)}, u32[]{:S(2)}) collective-permute-start(bf16[64,1152]{1,0:T(8,128)(2,1)S(1)} %get-tuple-element.74), channel_id=1, source_target_pairs={{0,12},{2,14},{4,8},{6,10},{8,4},{10,6},{12,0},{14,2},{1,13},{3,15... | collective-permute-start | bytes 442376 | tf_op jit(solution)/shard_map/ppermute | solution.py:63
  45.7 9.4 %collective-permute-done.12.arrived_ref = bf16[144,1024]{1,0:T(8,128)(2,1)S(1)} collective-permute-done((bf16[144,1024]{1,0:T(8,128)(2,1)S(1)}, bf16[144,1024]{1,0:T(8,128)(2,1)S(1)}, u32[]{:S(2)}, u32[]{:S(2)}) %collective-permute-start.12) | collective-permute-done | bytes 294944 | tf_op jit(solution)/shard_map/ppermute | solution.py:63
  55.5 1.9 %collective-permute-start.15 = (bf16[64,1024]{1,0:T(8,128)(2,1)S(1)}, bf16[64,1024]{1,0:T(8,128)(2,1)S(1)}, u32[]{:S(2)}, u32[]{:S(2)}) collective-permute-start(bf16[64,1024]{1,0:T(8,128)(2,1)S(1)} %get-tuple-element.81), channel_id=1, source_target_pairs={{0,12},{2,14},{4,8},{6,10},{8,4},{10,6},{12,0},{14,2},{1,13},{3,15... | collective-permute-start | bytes 393224 | tf_op jit(solution)/shard_map/ppermute | solution.py:63
  57.4 5.0 %collective-permute-done.7.last_ref.refs_3_.refs_2_ = bf16[208,1024]{1,0:T(8,128)(2,1)S(1)} collective-permute-done((bf16[208,1024]{1,0:T(8,128)(2,1)S(1)}, bf16[208,1024]{1,0:T(8,128)(2,1)S(1)}, u32[]{:S(2)}, u32[]{:S(2)}) %collective-permute-start.7) | collective-permute-done | bytes 426016 | tf_op jit(solution)/shard_map/ppermute | solution.py:63
  62.4 0.3 collective-permute-start.16
  62.7 1.5 %shard_map.175 = (bf16[2,32,1024]{2,1,0:T(8,128)(2,1)}, f32[8,128]{1,0:T(8,128)S(1)}) custom-call(bf16[128,64]{1,0:T(8,128)(2,1)S(1)} %get-tuple-element.45.refs_0_.pick_ref, bf16[1024,1024]{1,0:T(8,128)(2,1)S(1)} %copy-done, bf16[8,16,1024]{2,1,0:T(8,128)(2,1)S(1)} %get-tuple-element.63.slots_ref, ...), custom_call_target="tpu_custom_call" | custom-call | tf_op jit(solution)/shard_map/pallas_call | solution.py:46
  64.2 3.6 %collective-permute-done.13.refs_6_.refs_5_ = bf16[144,1024]{1,0:T(8,128)(2,1)S(1)} collective-permute-done((bf16[144,1024]{1,0:T(8,128)(2,1)S(1)}, bf16[144,1024]{1,0:T(8,128)(2,1)S(1)}, u32[]{:S(2)}, u32[]{:S(2)}) %collective-permute-start.13) | collective-permute-done | bytes 294944 | tf_op jit(solution)/shard_map/ppermute | solution.py:63
  67.8 1.0 %shard_map.178 = (f32[64,1024]{1,0:T(8,128)}, f32[64,100]{1,0:T(8,128)}, f32[1]{0:T(128)}, f32[8,128]{1,0:T(8,128)S(1)}) custom-call(f32[8,128]{1,0:T(8,128)S(1)} %get-tuple-element.71.refs_0_, f32[256,1152]{1,0:T(8,128)S(1)} %get-tuple-element.72.held_ref.refs_1_, bf16[256,1152]{1,0:T(8,128)(2,1)S(1)} %collective-permute-done.8.other_ref.refs_2_, ...), custom_call_target="tpu_custom_call" | custom-call | tf_op jit(solution)/shard_map/pallas_call | solution.py:46
  68.8 0.9 %collective-permute-done.16.refs_4_ = bf16[64,1024]{1,0:T(8,128)(2,1)S(1)} collective-permute-done((bf16[64,1024]{1,0:T(8,128)(2,1)S(1)}, bf16[64,1024]{1,0:T(8,128)(2,1)S(1)}, u32[]{:S(2)}, u32[]{:S(2)}) %collective-permute-start.16) | collective-permute-done | bytes 131104 | tf_op jit(solution)/shard_map/ppermute | solution.py:63
  69.7 0.8 %shard_map.180 = f32[64,1024]{1,0:T(8,128)} custom-call(f32[8,128]{1,0:T(8,128)S(1)} %get-tuple-element.79.refs_0_, f32[256,1024]{1,0:T(8,128)S(1)} %get-tuple-element.76.near_ref.refs_1_, bf16[208,1024]{1,0:T(8,128)(2,1)S(1)} %collective-permute-done.7.last_ref.refs_3_.refs_2_, bf16[64,1024]{1,0:T(8,128)(2,1)S(1)} %collective-permute-done.15.refs_3_, ...), custom_call_target="tpu_custom_call" | custom-call | flops 8000000000 | tf_op jit(solution)/shard_map/pallas_call | solution.py:46
  (33 shorter events, 1.3 us)
Async XLA Ops:
  0.6 18.1 %copy-start.4 = (f32[1024]{0:T(1024)S(1)}, f32[1024]{0:T(1024)}, u32[]{:S(2)}) copy-start(f32[1024]{0:T(1024)} %refs_3_.3) | copy-start | bytes 12292
  2.5 16.2 %all-to-all-start = ((bf16[8,16,1024]{2,1,0:T(8,128)(2,1)}), bf16[8,16,1024]{2,1,0:T(8,128)(2,1)S(1)}, u32[]{:S(2)}, u32[]{:S(2)}) async-start(bf16[8,16,1024]{2,1,0:T(8,128)(2,1)} %get-tuple-element.47), calls=%async_computation | async-start | bytes 524288 | tf_op jit(solution)/shard_map/all_to_all | solution.py:497
  23.4 1.4 %copy-start.2 = (bf16[1024,100]{0,1:T(8,128)(2,1)S(1)}, bf16[1024,100]{0,1:T(8,128)(2,1)}, u32[]{:S(2)}) copy-start(bf16[1024,100]{0,1:T(8,128)(2,1)} %param.18) | copy-start | bytes 614404
  23.4 1.4 %copy-start.3 = (f32[100,256]{1,0:T(8,128)S(1)}, f32[100,256]{1,0:T(8,128)}, u32[]{:S(2)}) copy-start(f32[100,256]{1,0:T(8,128)} %truth_ref.1) | copy-start | bytes 307204
  23.4 1.4 %copy-start.5 = (f32[256]{0:T(256)S(1)}, f32[256]{0:T(256)}, u32[]{:S(2)}) copy-start(f32[256]{0:T(256)} %cell_ref.1) | copy-start | bytes 3076
  23.4 1.4 %collective-permute-start = (bf16[2,100,256]{2,1,0:T(8,128)(2,1)S(1)}, bf16[2,100,256]{2,1,0:T(8,128)(2,1)S(1)}, u32[]{:S(2)}, u32[]{:S(2)}) collective-permute-start(bf16[2,100,256]{2,1,0:T(8,128)(2,1)S(1)} %get-tuple-element.50), channel_id=1, source_target_pairs={{0,1},{1,0},{2,3},{3,2},{4,5},{5,4},{6,7},{7,6},{8,9},{9,8},{10,11... | collective-permute-start | bytes 307208 | tf_op jit(solution)/shard_map/ppermute | solution.py:63
  26.4 2.3 %collective-permute-start.1 = (bf16[256,1152]{1,0:T(8,128)(2,1)S(1)}, bf16[256,1152]{1,0:T(8,128)(2,1)S(1)}, u32[]{:S(2)}, u32[]{:S(2)}) collective-permute-start(bf16[256,1152]{1,0:T(8,128)(2,1)S(1)} %get-tuple-element.60), channel_id=1, source_target_pairs={{0,1},{1,0},{2,3},{3,2},{4,5},{5,4},{6,7},{7,6},{8,9},{9,8},{10,11... | collective-permute-start | bytes 1769480 | tf_op jit(solution)/shard_map/ppermute | solution.py:63
  26.6 17.3 %collective-permute-start.8 = (bf16[256,1152]{1,0:T(8,128)(2,1)S(1)}, bf16[256,1152]{1,0:T(8,128)(2,1)S(1)}, u32[]{:S(2)}, u32[]{:S(2)}) collective-permute-start(bf16[256,1152]{1,0:T(8,128)(2,1)S(1)} %get-tuple-element.73), channel_id=1, source_target_pairs={{0,1},{1,0},{2,3},{3,2},{4,5},{5,4},{6,7},{7,6},{8,9},{9,8},{10,11... | collective-permute-start | bytes 1769480 | tf_op jit(solution)/shard_map/ppermute | solution.py:63
  27.0 2.0 %copy-start.1 = (bf16[1024,1024]{1,0:T(8,128)(2,1)S(1)}, bf16[1024,1024]{1,0:T(8,128)(2,1)}, u32[]{:S(2)}) copy-start(bf16[1024,1024]{1,0:T(8,128)(2,1)} %refs_2_.3) | copy-start | bytes 6291460
  31.1 3.2 %collective-permute-start.3 = (bf16[8,16,1024]{2,1,0:T(8,128)(2,1)S(1)}, bf16[8,16,1024]{2,1,0:T(8,128)(2,1)S(1)}, u32[]{:S(2)}, u32[]{:S(2)}) collective-permute-start(bf16[8,16,1024]{2,1,0:T(8,128)(2,1)S(1)} %get-tuple-element.63.slots_ref), channel_id=1, source_target_pairs={{0,1},{1,0},{2,3},{3,2},{4,5},{5,4},{6,7},{7,6},{8,9},{9,8},{10,11... | collective-permute-start | bytes 786440 | tf_op jit(solution)/shard_map/ppermute | solution.py:63
  31.3 12.7 %collective-permute-start.9 = (bf16[128,1152]{1,0:T(8,128)(2,1)S(1)}, bf16[128,1152]{1,0:T(8,128)(2,1)S(1)}, u32[]{:S(2)}, u32[]{:S(2)}) collective-permute-start(bf16[128,1152]{1,0:T(8,128)(2,1)S(1)} %shard_map.170.refs_0_), channel_id=1, source_target_pairs={{0,2},{2,0},{4,6},{6,4},{8,10},{10,8},{12,14},{14,12},{1,3},{3,1},... | collective-permute-start | bytes 884744 | tf_op jit(solution)/shard_map/ppermute | solution.py:63
  32.7 1.5 %collective-permute-start.2 = (bf16[2,4,64,128]{3,2,1,0:T(8,128)(2,1)S(1)}, bf16[2,4,64,128]{3,2,1,0:T(8,128)(2,1)S(1)}, u32[]{:S(2)}, u32[]{:S(2)}) collective-permute-start(bf16[2,4,64,128]{3,2,1,0:T(8,128)(2,1)S(1)} %get-tuple-element.65), channel_id=1, source_target_pairs={{0,1},{1,0},{2,3},{3,2},{4,5},{5,4},{6,7},{7,6},{8,9},{9,8},{10,11... | collective-permute-start | bytes 393224 | tf_op jit(solution)/shard_map/ppermute | solution.py:63
  32.8 6.8 %collective-permute-start.4 = (bf16[32,1024]{1,0:T(8,128)(2,1)S(1)}, bf16[32,1024]{1,0:T(8,128)(2,1)S(1)}, u32[]{:S(2)}, u32[]{:S(2)}) collective-permute-start(bf16[32,1024]{1,0:T(8,128)(2,1)S(1)} %get-tuple-element.67), channel_id=1, source_target_pairs={{0,12},{2,14},{4,8},{6,10},{8,4},{10,6},{12,0},{14,2},{1,13},{3,15... | collective-permute-start | bytes 196616 | tf_op jit(solution)/shard_map/ppermute | solution.py:63
  34.2 7.6 %collective-permute-start.5 = (bf16[32,1024]{1,0:T(8,128)(2,1)S(1)}, bf16[32,1024]{1,0:T(8,128)(2,1)S(1)}, u32[]{:S(2)}, u32[]{:S(2)}) collective-permute-start(bf16[32,1024]{1,0:T(8,128)(2,1)S(1)} %get-tuple-element.68), channel_id=1, source_target_pairs={{0,8},{2,10},{4,12},{6,14},{8,0},{10,2},{12,4},{14,6},{1,9},{3,11}... | collective-permute-start | bytes 196616 | tf_op jit(solution)/shard_map/ppermute | solution.py:63
  34.3 8.3 %collective-permute-start.6 = (bf16[32,1024]{1,0:T(8,128)(2,1)S(1)}, bf16[32,1024]{1,0:T(8,128)(2,1)S(1)}, u32[]{:S(2)}, u32[]{:S(2)}) collective-permute-start(bf16[32,1024]{1,0:T(8,128)(2,1)S(1)} %get-tuple-element.69), channel_id=1, source_target_pairs={{0,4},{2,6},{4,0},{6,2},{8,12},{10,14},{12,8},{14,10},{1,5},{3,7},... | collective-permute-start | bytes 196616 | tf_op jit(solution)/shard_map/ppermute | solution.py:63
  39.6 15.9 %collective-permute-start.14 = (bf16[128,1024]{1,0:T(8,128)(2,1)S(1)}, bf16[128,1024]{1,0:T(8,128)(2,1)S(1)}, u32[]{:S(2)}, u32[]{:S(2)}) collective-permute-start(bf16[128,1024]{1,0:T(8,128)(2,1)S(1)} %get-tuple-element.80), channel_id=1, source_target_pairs={{0,2},{2,0},{4,6},{6,4},{8,10},{10,8},{12,14},{14,12},{1,3},{3,1},... | collective-permute-start | bytes 786440 | tf_op jit(solution)/shard_map/ppermute | solution.py:63
  41.8 13.3 %collective-permute-start.12 = (bf16[144,1024]{1,0:T(8,128)(2,1)S(1)}, bf16[144,1024]{1,0:T(8,128)(2,1)S(1)}, u32[]{:S(2)}, u32[]{:S(2)}) collective-permute-start(bf16[144,1024]{1,0:T(8,128)(2,1)S(1)} %get-tuple-element.77), channel_id=1, source_target_pairs={{0,2},{2,0},{4,6},{6,4},{8,10},{10,8},{12,14},{14,12},{1,3},{3,1},... | collective-permute-start | bytes 884744 | tf_op jit(solution)/shard_map/ppermute | solution.py:63
  42.6 19.8 %collective-permute-start.7 = (bf16[208,1024]{1,0:T(8,128)(2,1)S(1)}, bf16[208,1024]{1,0:T(8,128)(2,1)S(1)}, u32[]{:S(2)}, u32[]{:S(2)}) collective-permute-start(bf16[208,1024]{1,0:T(8,128)(2,1)S(1)} %shard_map.174), channel_id=1, source_target_pairs={{0,2},{2,0},{4,6},{6,4},{8,10},{10,8},{12,14},{14,12},{1,3},{3,1},... | collective-permute-start | bytes 1277960 | tf_op jit(solution)/shard_map/ppermute | solution.py:63
  44.2 20.0 %collective-permute-start.10 = (bf16[64,1152]{1,0:T(8,128)(2,1)S(1)}, bf16[64,1152]{1,0:T(8,128)(2,1)S(1)}, u32[]{:S(2)}, u32[]{:S(2)}) collective-permute-start(bf16[64,1152]{1,0:T(8,128)(2,1)S(1)} %get-tuple-element.74), channel_id=1, source_target_pairs={{0,12},{2,14},{4,8},{6,10},{8,4},{10,6},{12,0},{14,2},{1,13},{3,15... | collective-permute-start | bytes 442376 | tf_op jit(solution)/shard_map/ppermute | solution.py:63
  45.7 18.5 %collective-permute-start.11 = (bf16[64,1152]{1,0:T(8,128)(2,1)S(1)}, bf16[64,1152]{1,0:T(8,128)(2,1)S(1)}, u32[]{:S(2)}, u32[]{:S(2)}) collective-permute-start(bf16[64,1152]{1,0:T(8,128)(2,1)S(1)} %get-tuple-element.75), channel_id=1, source_target_pairs={{0,8},{2,10},{4,12},{6,14},{8,0},{10,2},{12,4},{14,6},{1,9},{3,11}... | collective-permute-start | bytes 442376 | tf_op jit(solution)/shard_map/ppermute | solution.py:63
  55.3 7.3 %copy-start = (bf16[1024,1024]{1,0:T(8,128)(2,1)S(1)}, bf16[1024,1024]{1,0:T(8,128)(2,1)}, u32[]{:S(2)}) copy-start(bf16[1024,1024]{1,0:T(8,128)(2,1)} %w_msg_ref.1) | copy-start | bytes 6291460
  55.4 12.5 %collective-permute-start.13 = (bf16[144,1024]{1,0:T(8,128)(2,1)S(1)}, bf16[144,1024]{1,0:T(8,128)(2,1)S(1)}, u32[]{:S(2)}, u32[]{:S(2)}) collective-permute-start(bf16[144,1024]{1,0:T(8,128)(2,1)S(1)} %shard_map.177), channel_id=1, source_target_pairs={{0,4},{2,6},{4,0},{6,2},{8,12},{10,14},{12,8},{14,10},{1,5},{3,7},... | collective-permute-start | bytes 884744 | tf_op jit(solution)/shard_map/ppermute | solution.py:63
  55.5 13.3 %collective-permute-start.15 = (bf16[64,1024]{1,0:T(8,128)(2,1)S(1)}, bf16[64,1024]{1,0:T(8,128)(2,1)S(1)}, u32[]{:S(2)}, u32[]{:S(2)}) collective-permute-start(bf16[64,1024]{1,0:T(8,128)(2,1)S(1)} %get-tuple-element.81), channel_id=1, source_target_pairs={{0,12},{2,14},{4,8},{6,10},{8,4},{10,6},{12,0},{14,2},{1,13},{3,15... | collective-permute-start | bytes 393224 | tf_op jit(solution)/shard_map/ppermute | solution.py:63
  62.4 7.3 %collective-permute-start.16 = (bf16[64,1024]{1,0:T(8,128)(2,1)S(1)}, bf16[64,1024]{1,0:T(8,128)(2,1)S(1)}, u32[]{:S(2)}, u32[]{:S(2)}) collective-permute-start(bf16[64,1024]{1,0:T(8,128)(2,1)S(1)} %get-tuple-element.82), channel_id=1, source_target_pairs={{0,8},{2,10},{4,12},{6,14},{8,0},{10,2},{12,4},{14,6},{1,9},{3,11}... | collective-permute-start | bytes 393224 | tf_op jit(solution)/shard_map/ppermute | solution.py:63

commit v3 on v2

--- a/solution.py
+++ b/solution.py
@@ -63,7 +63,7 @@
     return lax.ppermute(value, axis, [(i, i ^ step) for i in range(size)])
 
 
-def select_kernel(lists_ref, latents_ref, send_ref, pick_ref, small_ref, table_ref, sems):
+def select_kernel(lists_ref, latents_ref, pick_ref, own_ref, send_ref, small_ref, table_ref, sems):
     _, peers, cap = lists_ref.shape
     members, nodes, width = latents_ref.shape
     lists = pltpu.make_async_copy(lists_ref, small_ref, sems.at[0])
@@ -71,20 +71,31 @@
     lists.start()
     table.start()
     lists.wait()
+    me = lax.axis_index("space")
     at = lax.broadcasted_iota(jnp.int32, (cap, members * nodes), 0)
     column = lax.broadcasted_iota(jnp.int32, (cap, members * nodes), 1)
     rows = []
-    for peer in range(peers):
+    for step in range(peers):
         wanted = jnp.zeros((cap, members * nodes), jnp.int32)
         for j in range(cap):
-            wanted = jnp.where(at == j, small_ref[0, peer, j], wanted)
+            wanted = jnp.where(at == j, small_ref[0, me ^ step, j], wanted)
         for member in range(members):
             rows.append((column == wanted + member * nodes).astype(f32))
     pick = jnp.concatenate(rows, axis=0).astype(bf16)
     pick_ref[...] = pick
     table.wait()
     sent = mm(pick, table_ref[...].reshape(members * nodes, width), 1, 0)
-    send_ref[...] = sent.astype(bf16).reshape(send_ref.shape)
+    sent = sent.astype(bf16).reshape(peers // 2, 2, members * cap, width)
+    own_ref[...] = sent[:, 0]
+    send_ref[...] = sent[:, 1]
+
+
+def merge_kernel(own_ref, arrived_ref, *out_refs):
+    rows = own_ref.shape[1]
+    for i, out_ref in enumerate(out_refs):
+        step = len(out_refs) - i
+        out_ref[0:rows, :] = own_ref[step]
+        out_ref[rows:, :] = arrived_ref[step]
 
 
 def stage_kernel(cap, members, count, *refs):
@@ -113,7 +124,7 @@
     rows = share_ref.shape[0] // 2
     points = share_ref.shape[1] // members
     sender = lax.div(slot, cap)
-    spot = sender * (members * cap) + (slot - sender * cap)
+    spot = (sender ^ lax.axis_index("space")) * (members * cap) + (slot - sender * cap)
     hit = lax.broadcasted_iota(jnp.int32, (rows, edges), 0) == spot
     into = (lax.broadcasted_iota(jnp.int32, (points, edges), 0) == dst).astype(f32).astype(bf16)
     high = weight.astype(bf16).astype(f32)
@@ -129,22 +140,21 @@
         table = jnp.concatenate([table[rows - cap :], table[: rows - cap]], axis=0)
 
 
+def gathered(own_ref, near_ref, far_refs):
+    return jnp.concatenate([own_ref[0], near_ref[0]] + [r[...] for r in far_refs[::-1]], axis=0)
+
+
 def forward_kernel(
-    received_ref, w_msg_ref, share_ref, gain_ref, embed_hbm, w_hidden_hbm, project_hbm, present_hbm,
-    field_ref, sent_ref, normed_ref, active_ref, slope_ref, unit_ref, inverse_ref,
-    embed_ref, weights_ref, project_ref, present_ref, sems,
+    far, w_msg_ref, share_ref, gain_ref, embed_ref, weights_ref, project_ref, present_ref,
+    own_ref, near_ref, *rest,
 ):
+    far_refs = rest[:far]
+    field_ref, sent_ref, normed_ref, active_ref, slope_ref, unit_ref, inverse_ref = rest[far:]
     points, width = embed_ref.shape
-    far = (embed_hbm, w_hidden_hbm, project_hbm, present_hbm)
-    close = (embed_ref, weights_ref, project_ref, present_ref)
-    copies = [pltpu.make_async_copy(x, y, sems.at[i]) for i, (x, y) in enumerate(zip(far, close, strict=True))]
-    for copy in copies:
-        copy.start()
     variables, members, _ = present_ref.shape
-    messages = mm(received_ref[...], w_msg_ref[...], 1, 0).astype(bf16)
+    messages = mm(gathered(own_ref, near_ref, far_refs), w_msg_ref[...], 1, 0).astype(bf16)
     messages = jnp.concatenate([messages, messages], axis=0)
     gain = gain_ref[...].reshape(1, width)
-    copies[0].wait()
     for begin in range(0, members * points, lanes):
         rows = slice(begin, begin + lanes)
         source = slice(begin % points, begin % points + lanes)
@@ -154,8 +164,6 @@
         unit_ref[rows, :] = unit
         inverse_ref[rows, :] = inverse
         normed_ref[rows, :] = (unit * gain).astype(bf16)
-    for copy in copies[1:]:
-        copy.wait()
     root = 0.7978845608028654
     cubic = 0.044715
     for member in range(members):
@@ -175,13 +183,13 @@
         sent_ref[member] = field.astype(bf16)
 
 
-def turn_kernel(normed_ref, active_ref, received_ref, normed_t_ref, active_t_ref, keep_ref, give_ref):
+def turn_kernel(normed_ref, active_ref, own_ref, near_ref, *rest):
+    far_refs, (normed_t_ref, active_t_ref, keep_ref, give_ref) = rest[:-4], rest[-4:]
     _, _, levels, block, _ = normed_t_ref.shape
     width = normed_ref.shape[1]
     level, line, core = place()
-    for source, targets in (
-        (received_ref, (keep_ref, give_ref)), (normed_ref, normed_t_ref), (active_ref, active_t_ref)
-    ):
+    received = gathered(own_ref, near_ref, far_refs)
+    for source, target in ((received, None), (normed_ref, normed_t_ref), (active_ref, active_t_ref)):
         for begin in range(0, width, tile):
             turned = source[:, begin : begin + tile].T
             for piece in range(0, tile, block):
@@ -190,13 +198,13 @@
                 step = (index // 4) ^ level
                 side = (index % 2) ^ core
                 value = turned[piece : piece + block]
-                if source is received_ref:
-                    for which in range(2):
-                        @pl.when(side == which)
-                        def _(target=targets[which]):
-                            target[1 - far, levels - 1 - step] = value
-                else:
-                    targets[side, 1 - far, levels - 1 - step] = value
+                if target is not None:
+                    target[side, 1 - far, levels - 1 - step] = value
+                    continue
+                for which, part_ref in enumerate((keep_ref, give_ref)):
+                    @pl.when(side == which)
+                    def _(part_ref=part_ref):
+                        part_ref[1 - far, levels - 1 - step] = value
 
 
 def split_loss(part, variables):
@@ -335,12 +343,11 @@
 def ride_kernel(last_ref, slots_ref, *rest):
     arrived_refs, out_ref = rest[:-1], rest[-1]
     rows = slots_ref.shape[1]
-    level, line, _ = place()
     begin = last_ref.shape[0]
     out_ref[0:begin, :] = last_ref[...]
     for i, arrived_ref in enumerate(arrived_refs):
         out_ref[begin + i * rows : begin + (i + 1) * rows, :] = arrived_ref[rows:, :]
-    out_ref[begin + len(arrived_refs) * rows :, :] = slots_ref[level * 2 + 1 - line]
+    out_ref[begin + len(arrived_refs) * rows :, :] = slots_ref[1]
 
 
 def hidden_early_kernel(variables, width, held_ref, other_ref, arrived_ref, *out_refs):
@@ -404,25 +411,22 @@
         columns = slice(begin, begin + tile)
         both = mm(share_ref[...], grad_ref[:, columns], 1, 0)
         slots_ref[:, :, columns] = (both[:rows] + both[rows:]).astype(bf16).reshape(peers, each, tile)
-    level, line, _ = place()
-    levels = peers // 2
     for i, send_ref in enumerate(send_refs):
-        spot = (level ^ (levels - 1 - i)) * 2 + line
-        send_ref[0:each, :] = slots_ref[spot]
-        send_ref[each:, :] = slots_ref[spot ^ 1]
+        step = len(send_refs) - i
+        send_ref[0:each, :] = slots_ref[2 * step]
+        send_ref[each:, :] = slots_ref[2 * step + 1]
 
 
 def owner_kernel(pick_ref, w_msg_ref, slots_ref, last_ref, *rest):
     arrived_refs, (grad_ref, token_ref, held_ref) = rest[:-3], rest[-3:]
     token_ref[...] = jnp.zeros_like(token_ref)
     peers, rows, width = slots_ref.shape
-    level, line, _ = place()
     levels = peers // 2
     begin = last_ref.shape[0] - levels * rows
     for i in range(levels):
-        spot = (level ^ (levels - 1 - i)) * 2 + line
-        held_ref[spot] = slots_ref[spot] if i == levels - 1 else arrived_refs[i][0:rows, :]
-        held_ref[spot ^ 1] = last_ref[begin + i * rows : begin + (i + 1) * rows, :]
+        spot = 2 * (levels - 1 - i)
+        held_ref[spot] = slots_ref[0] if i == levels - 1 else arrived_refs[i][0:rows, :]
+        held_ref[spot + 1] = last_ref[begin + i * rows : begin + (i + 1) * rows, :]
     nodes = mm(pick_ref[...], held_ref[...].reshape(peers * rows, width), 0, 0).astype(bf16)
     grad_ref[...] = mm(nodes, w_msg_ref[...], 1, 1).astype(bf16).reshape(grad_ref.shape)
 
@@ -479,12 +483,16 @@
     wide = width + -(-(variables + 2) // lanes) * lanes
     project = variable_projection.T
 
-    exchange = functools.partial(
-        lax.all_to_all, axis_name="space", split_axis=0, concat_axis=0, tiled=True
-    )
-    send, pick = call(
+    early = levels // 2
+    count, rest = early * block, (levels - 1 - early) * block
+    steps = [2 * (levels - 1 - i) for i in range(levels - 1)]
+
+    def spread(values, part):
+        return [swap(x, "space", peers, k) for x, k in zip(values, part, strict=True)]
+
+    pick, own_rows, send = call(
         select_kernel,
-        [((peers, rows_peer, width), bf16), ((rows_slot, members * nodes), bf16)],
+        [((rows_slot, members * nodes), bf16)] + [((levels, rows_peer, width), bf16)] * 2,
         [send_rows, latents],
         scratch=[
             pltpu.SMEM(send_rows.shape, jnp.int32),
@@ -494,10 +502,8 @@
         limit=4,
         places=(0, 1),
     )
-    received = exchange(send).reshape(rows_slot, width)
-    present = present_condition.transpose(1, 0, 2)
-    fixed = [w_msg]
-    direct = [grid_embed, w_hidden, project, present]
+    near_rows = swap(send, "space", peers, 1)
+    fixed = [w_msg, norm_gain, grid_embed, w_hidden, project, present_condition.transpose(1, 0, 2)]
     edges = [edge_slot, edge_dst, edge_weight]
     share, *staged = call(
         functools.partial(stage_kernel, cap, members, len(fixed)),
@@ -509,9 +515,17 @@
         places=tuple(range(3 + len(fixed))),
         after=[pick],
     )
-    (w_msg_near,) = staged
+    merged = call(
+        merge_kernel,
+        [((2 * rows_peer, width), bf16)] * (levels - 1),
+        [own_rows, near_rows],
+        limit=4,
+        after=[share],
+    )
+    received = [own_rows, near_rows] + spread(merged, steps)
+    w_msg_near, gain, embed, w_hidden_near, project_near, present = staged
     field, sent, normed, active, slope, unit, inverse = call(
-        forward_kernel,
+        functools.partial(forward_kernel, levels - 1),
         [
             ((members, variables, points), f32),
             ((members, variables, points), bf16),
@@ -521,16 +535,14 @@
             ((rows_all, width), f32),
             ((rows_all, 1), f32),
         ],
-        [received, w_msg_near, share, norm_gain] + direct,
-        scratch=[pltpu.VMEM(x.shape, x.dtype) for x in direct] + [pltpu.SemaphoreType.DMA((len(direct),))],
-        limit=22,
-        places=(4, 5, 6, 7),
+        [w_msg_near, share, gain, embed, w_hidden_near, project_near, present] + received,
+        limit=20,
     )
     other = swap(sent, "member", cores, 1)
     normed_t, active_t, received_keep, received_give = call(
         turn_kernel,
         [((cores, 2, levels, block, rows_all), bf16)] * 2 + [((2, levels, block, rows_slot), bf16)] * 2,
-        [normed, active, received],
+        [normed, active] + received,
         limit=8,
     )
     received_other = swap(received_give, "member", cores, 1)
@@ -543,7 +555,7 @@
             ((half, wide), bf16),
             ((half, wide), bf16),
         ],
-        [field, other, verifying_field, cell_surface, project, slope, normed_t, active_t],
+        [field, other, verifying_field, cell_surface, project_near, slope, normed_t, active_t],
         scratch=[pltpu.VMEM((lanes, rows_all), f32)],
         limit=16,
         scalar_outs=(2,),
@@ -557,13 +569,6 @@
         limit=12,
         scalars=(0,),
     )
-    early = levels // 2
-    count, rest = early * block, (levels - 1 - early) * block
-    steps = [2 * (levels - 1 - i) for i in range(levels - 1)]
-
-    def spread(values, part):
-        return [swap(x, "space", peers, k) for x, k in zip(values, part, strict=True)]
-
     (first,) = call(
         functools.partial(first_kernel, variables, width),
         [((count, wide), bf16)],
@@ -574,7 +579,7 @@
     (grad_hidden,) = call(
         back_kernel,
         [((rows_all, width), bf16)],
-        [grad_inner, w_hidden, norm_gain, unit, inverse],
+        [grad_inner, w_hidden_near, gain, unit, inverse],
         scratch=[pltpu.VMEM((rows_all, width), f32)],
         limit=14,
         after=[first],
@@ -584,6 +589,7 @@
         [((peers, rows_peer, width), bf16)] + [((2 * rows_peer, width), bf16)] * (levels - 1),
         [share, grad_hidden],
         limit=6,
+        after=[near_other, received_other],
     )
     slots_other = swap(slots, "member", cores, 1)
     slots_arrived = spread(slots_sent, steps)

time: 70.8 us -> 67.8 us (0.958)
  waiting for transfers between devices: 29.8 us -> 26.6 us
  starting transfers between devices: 20.6 us -> 22 us
  Pallas kernels: 19.3 us -> 18.1 us
    ppermute x17 -> x21, starting transfers between devices: 13.3 us -> 22 us  [swap(): return lax.ppermute(value, axis, [(i, i ^ step) for i in range(size)])]
    all_to_all x1 -> x0, starting transfers between devices: 7.29 us -> none  [on_device(): received = exchange(send).reshape(rows_slot, width)]
    all_to_all x1 -> x0, waiting for transfers between devices: 7.24 us -> none  [on_device(): received = exchange(send).reshape(rows_slot, width)]
    ppermute x17 -> x21, waiting for transfers between devices: 22.5 us -> 26.6 us  [swap(): return lax.ppermute(value, axis, [(i, i ^ step) for i in range(size)])]
    pallas_call x17 -> x18, Pallas kernels: 19.3 us -> 18.1 us  [call(): pl.pallas_call(inner if count else body, out_shape=[jax.ShapeDtypeStruct(...]
  transfers between devices with their start and end apart: 18 -> 21, of which waited for: 8 -> 10; matrix products, arithmetic and copies ran while one was open for 0% -> 0% of each run, Pallas kernels for 15% -> 16%
where the time goes in v3:
time: 67.8 us; the launch traced here: 67.5 us
  waiting for transfers between devices  26.6 us (39%)
  starting transfers between devices  22 us (32%)
  Pallas kernels  18.1 us (27%)
  between operations  0.83 us (1%)
    ppermute x21, waiting for transfers between devices, swap(): return lax.ppermute(value, axis, [(i, i ^ step) for i in range(size)])  26.6 us
    ppermute x21, starting transfers between devices, swap(): return lax.ppermute(value, axis, [(i, i ^ step) for i in range(size)])  22 us
    pallas_call x18, Pallas kernels, call(): pl.pallas_call(inner if count else body, out_shape=[jax.ShapeDtypeStruct(...  18.1 us
  transfers between devices with their start and end apart: 21, of which 10 were waited for; matrix products, arithmetic and copies ran while one was open for 0% of the time, Pallas kernels for 16%

profile of v3, /device:TPU:0, one launch (start us, length us, event | category | flops | bytes accessed | tf_op | source)
XLA Modules:
  0.0 67.5 jit_solution(11454718366629969615)
XLA Ops:
  0.6 1.1 %shard_map.164 = (bf16[128,64]{1,0:T(8,128)(2,1)S(1)}, bf16[4,16,1024]{2,1,0:T(8,128)(2,1)S(1)}, bf16[4,16,1024]{2,1,0:T(8,128)(2,1)S(1)}) custom-call(s32[1,8,8]{2,1,0:T(8,128)} %lists_ref.1, bf16[2,32,1024]{2,1,0:T(8,128)(2,1)} %latents_ref.1), custom_call_target="tpu_custom_call" | custom-call | tf_op jit(solution)/shard_map/pallas_call | solution.py:46
  1.8 3.0 %collective-permute-start = (bf16[4,16,1024]{2,1,0:T(8,128)(2,1)S(1)}, bf16[4,16,1024]{2,1,0:T(8,128)(2,1)S(1)}, u32[]{:S(2)}, u32[]{:S(2)}) collective-permute-start(bf16[4,16,1024]{2,1,0:T(8,128)(2,1)S(1)} %get-tuple-element.63), channel_id=1, source_target_pairs={{0,2},{2,0},{4,6},{6,4},{8,10},{10,8},{12,14},{14,12},{1,3},{3,1},... | collective-permute-start | bytes 393224 | tf_op jit(solution)/shard_map/ppermute | solution.py:63
  4.8 2.6 %shard_map.165 = (bf16[256,512]{1,0:T(8,128)(2,1)S(1)}, bf16[1024,1024]{1,0:T(8,128)(2,1)S(1)}, f32[1024]{0:T(1024)S(1)}, bf16[256,1024]{1,0:T(8,128)(2,1)S(1)},...) custom-call(bf16[128,64]{1,0:T(8,128)(2,1)S(1)} %get-tuple-element.54.refs_0_.pick_ref, ...), custom_call_target="tpu_custom_call" | custom-call | tf_op jit(solution)/shard_map/pallas_call | solution.py:46
  7.4 0.9 %collective-permute-done.refs_2_.near_ref = bf16[4,16,1024]{2,1,0:T(8,128)(2,1)S(1)} collective-permute-done((bf16[4,16,1024]{2,1,0:T(8,128)(2,1)S(1)}, bf16[4,16,1024]{2,1,0:T(8,128)(2,1)S(1)}, u32[]{:S(2)}, u32[]{:S(2)}) %collective-permute-start) | collective-permute-done | bytes 131104 | tf_op jit(solution)/shard_map/ppermute | solution.py:63
  8.3 3.9 %collective-permute-start.1 = (bf16[32,1024]{1,0:T(8,128)(2,1)S(1)}, bf16[32,1024]{1,0:T(8,128)(2,1)S(1)}, u32[]{:S(2)}, u32[]{:S(2)}) collective-permute-start(bf16[32,1024]{1,0:T(8,128)(2,1)S(1)} %get-tuple-element.64), channel_id=1, source_target_pairs={{0,12},{2,14},{4,8},{6,10},{8,4},{10,6},{12,0},{14,2},{1,13},{3,15... | collective-permute-start | bytes 196616 | tf_op jit(solution)/shard_map/ppermute | solution.py:63
  12.2 0.6 collective-permute-start.3
  12.8 2.0 %collective-permute-done.1.rest_0_ = bf16[32,1024]{1,0:T(8,128)(2,1)S(1)} collective-permute-done((bf16[32,1024]{1,0:T(8,128)(2,1)S(1)}, bf16[32,1024]{1,0:T(8,128)(2,1)S(1)}, u32[]{:S(2)}, u32[]{:S(2)}) %collective-permute-start.1) | collective-permute-done | bytes 65568 | tf_op jit(solution)/shard_map/ppermute | solution.py:63
  14.9 2.7 %collective-permute-done.2.rest_1_ = bf16[32,1024]{1,0:T(8,128)(2,1)S(1)} collective-permute-done((bf16[32,1024]{1,0:T(8,128)(2,1)S(1)}, bf16[32,1024]{1,0:T(8,128)(2,1)S(1)}, u32[]{:S(2)}, u32[]{:S(2)}) %collective-permute-start.2) | collective-permute-done | bytes 65568 | tf_op jit(solution)/shard_map/ppermute | solution.py:63
  17.6 3.5 %shard_map.167 = (f32[2,100,256]{2,1,0:T(8,128)S(1)}, bf16[2,100,256]{2,1,0:T(8,128)(2,1)S(1)}, bf16[512,1024]{1,0:T(8,128)(2,1)S(1)}, bf16[512,1024]{1,0:T(8,12...) custom-call(bf16[1024,1024]{1,0:T(8,128)(2,1)S(1)} %get-tuple-element.55.w_msg_ref, ...), custom_call_target="tpu_custom_call" | custom-call | tf_op jit(solution)/shard_map/pallas_call | solution.py:46
  21.1 0.9 %shard_map.168 = (bf16[2,2,4,64,512]{4,3,2,1,0:T(8,128)(2,1)S(1)}, bf16[2,2,4,64,512]{4,3,2,1,0:T(8,128)(2,1)S(1)}, bf16[2,4,64,128]{3,2,1,0:T(8,128)(2,1)S(1)}, bf16[2,4,64,128]{3,2,1,0:T(8,128)(2,1)S(1)}) custom-call(bf16[512,1024]{1,0:T(8,128)(2,1)S(1)} %get-tuple-element.70.normed_ref, bf16[512,1024]{1,0:T(8,128)(2,1)S(1)} %get-tuple-element.71.active_ref, ...), custom_call_target="tpu_custom_call" | custom-call | tf_op jit(solution)/shard_map/pallas_call | solution.py:46
  22.4 1.6 %shard_map.169 = (bf16[512,1024]{1,0:T(8,128)(2,1)S(1)}, bf16[128,512]{1,0:T(8,128)(2,1)S(1)}, f32[1]{0:T(128)}, bf16[256,1152]{1,0:T(8,128)(2,1)S(1)}, bf16[256,1152]{1,0:T(8,128)(2,1)S(1)}) custom-call(f32[2,100,256]{2,1,0:T(8,128)S(1)} %get-tuple-element.67.own_ref, bf16[2,100,256]{2,1,0:T(8,128)(2,1)S(1)} %collective-permute-done.4.other_ref, ...), custom_call_target="tpu_custom_call" | custom-call | tf_op jit(solution)/shard_map/pallas_call | solution.py:46
  24.7 1.6 %shard_map.170 = (f32[256,1152]{1,0:T(8,128)S(1)}, f32[256,1152]{1,0:T(8,128)S(1)}) custom-call(f32[1]{0:T(128)} %get-tuple-element.76.loss_ref, bf16[2,2,4,64,512]{4,3,2,1,0:T(8,128)(2,1)S(1)} %get-tuple-element.72.normed_t_ref, bf16[2,2,4,64,512]{4,3,2,1,0:T(8,128)(2,1)S(1)} %get-tuple-element.73.active_t_ref, ...), custom_call_target="tpu_custom_call" | custom-call | tf_op jit(solution)/shard_map/pallas_call | solution.py:46
  26.6 1.6 %collective-permute-start.13 = (bf16[128,1152]{1,0:T(8,128)(2,1)S(1)}, bf16[128,1152]{1,0:T(8,128)(2,1)S(1)}, u32[]{:S(2)}, u32[]{:S(2)}) collective-permute-start(bf16[128,1152]{1,0:T(8,128)(2,1)S(1)} %shard_map.171.refs_0_), channel_id=1, source_target_pairs={{0,2},{2,0},{4,6},{6,4},{8,10},{10,8},{12,14},{14,12},{1,3},{3,1},... | collective-permute-start | bytes 884744 | tf_op jit(solution)/shard_map/ppermute | solution.py:63
  28.2 1.7 %shard_map.172.refs_3_ = bf16[512,1024]{1,0:T(8,128)(2,1)S(1)} custom-call(bf16[128,1152]{1,0:T(8,128)(2,1)S(1)} %shard_map.171.refs_0_, bf16[512,1024]{1,0:T(8,128)(2,1)S(1)} %get-tuple-element.77.inner_ref.refs_1_, bf16[1024,1024]{1,0:T(8,128)(2,1)S(1)} %get-tuple-element.59.weights_ref.refs_2_, f32[1024]{0:T(1024)S(1)} %get-tuple-element.57.gain_ref.refs_3_, ...), custom_call_target="tpu_custom_call" | custom-call | flops 8000000000 | tf_op jit(solution)/shard_map/pallas_call | solution.py:46
  30.4 2.2 %collective-permute-start.9 = (bf16[32,1024]{1,0:T(8,128)(2,1)S(1)}, bf16[32,1024]{1,0:T(8,128)(2,1)S(1)}, u32[]{:S(2)}, u32[]{:S(2)}) collective-permute-start(bf16[32,1024]{1,0:T(8,128)(2,1)S(1)} %get-tuple-element.86), channel_id=1, source_target_pairs={{0,12},{2,14},{4,8},{6,10},{8,4},{10,6},{12,0},{14,2},{1,13},{3,15... | collective-permute-start | bytes 196616 | tf_op jit(solution)/shard_map/ppermute | solution.py:63
  32.7 2.2 %collective-permute-start.11 = (bf16[32,1024]{1,0:T(8,128)(2,1)S(1)}, bf16[32,1024]{1,0:T(8,128)(2,1)S(1)}, u32[]{:S(2)}, u32[]{:S(2)}) collective-permute-start(bf16[32,1024]{1,0:T(8,128)(2,1)S(1)} %get-tuple-element.88), channel_id=1, source_target_pairs={{0,4},{2,6},{4,0},{6,2},{8,12},{10,14},{12,8},{14,10},{1,5},{3,7},... | collective-permute-start | bytes 196616 | tf_op jit(solution)/shard_map/ppermute | solution.py:63
  34.9 0.7 %shard_map.174 = (bf16[128,1024]{1,0:T(8,128)(2,1)S(1)}, bf16[144,1024]{1,0:T(8,128)(2,1)S(1)}, bf16[144,1024]{1,0:T(8,128)(2,1)S(1)}, f32[256,1024]{1,0:T(8,128)S(1)}) custom-call(bf16[2,4,64,128]{3,2,1,0:T(8,128)(2,1)S(1)} %get-tuple-element.84.keep_ref, bf16[2,4,64,128]{3,2,1,0:T(8,128)(2,1)S(1)} %collective-permute-done.6.refs_1_.give_ref, ...), custom_call_target="tpu_custom_call" | custom-call | tf_op jit(solution)/shard_map/pallas_call | solution.py:46
  35.6 0.5 collective-permute-start.18
  36.1 1.1 %collective-permute-done.9.rest_0_ = bf16[32,1024]{1,0:T(8,128)(2,1)S(1)} collective-permute-done((bf16[32,1024]{1,0:T(8,128)(2,1)S(1)}, bf16[32,1024]{1,0:T(8,128)(2,1)S(1)}, u32[]{:S(2)}, u32[]{:S(2)}) %collective-permute-start.9) | collective-permute-done | bytes 65568 | tf_op jit(solution)/shard_map/ppermute | solution.py:63
  37.3 0.5 collective-permute-start.16
  37.7 1.8 %collective-permute-done.10.rest_1_ = bf16[32,1024]{1,0:T(8,128)(2,1)S(1)} collective-permute-done((bf16[32,1024]{1,0:T(8,128)(2,1)S(1)}, bf16[32,1024]{1,0:T(8,128)(2,1)S(1)}, u32[]{:S(2)}, u32[]{:S(2)}) %collective-permute-start.10) | collective-permute-done | bytes 65568 | tf_op jit(solution)/shard_map/ppermute | solution.py:63
  39.6 0.5 collective-permute-start.12
  40.3 2.4 %collective-permute-start.14 = (bf16[64,1152]{1,0:T(8,128)(2,1)S(1)}, bf16[64,1152]{1,0:T(8,128)(2,1)S(1)}, u32[]{:S(2)}, u32[]{:S(2)}) collective-permute-start(bf16[64,1152]{1,0:T(8,128)(2,1)S(1)} %get-tuple-element.92), channel_id=1, source_target_pairs={{0,12},{2,14},{4,8},{6,10},{8,4},{10,6},{12,0},{14,2},{1,13},{3,15... | collective-permute-start | bytes 442376 | tf_op jit(solution)/shard_map/ppermute | solution.py:63
  42.7 8.5 %collective-permute-done.16.arrived_ref = bf16[144,1024]{1,0:T(8,128)(2,1)S(1)} collective-permute-done((bf16[144,1024]{1,0:T(8,128)(2,1)S(1)}, bf16[144,1024]{1,0:T(8,128)(2,1)S(1)}, u32[]{:S(2)}, u32[]{:S(2)}) %collective-permute-start.16) | collective-permute-done | bytes 294944 | tf_op jit(solution)/shard_map/ppermute | solution.py:63
  51.6 2.4 %collective-permute-start.19 = (bf16[64,1024]{1,0:T(8,128)(2,1)S(1)}, bf16[64,1024]{1,0:T(8,128)(2,1)S(1)}, u32[]{:S(2)}, u32[]{:S(2)}) collective-permute-start(bf16[64,1024]{1,0:T(8,128)(2,1)S(1)} %get-tuple-element.99), channel_id=1, source_target_pairs={{0,12},{2,14},{4,8},{6,10},{8,4},{10,6},{12,0},{14,2},{1,13},{3,15... | collective-permute-start | bytes 393224 | tf_op jit(solution)/shard_map/ppermute | solution.py:63
  54.0 4.9 %collective-permute-done.12.last_ref.refs_3_.refs_2_ = bf16[208,1024]{1,0:T(8,128)(2,1)S(1)} collective-permute-done((bf16[208,1024]{1,0:T(8,128)(2,1)S(1)}, bf16[208,1024]{1,0:T(8,128)(2,1)S(1)}, u32[]{:S(2)}, u32[]{:S(2)}) %collective-permute-start.12) | collective-permute-done | bytes 426016 | tf_op jit(solution)/shard_map/ppermute | solution.py:63
  58.9 1.0 %collective-permute-start.20 = (bf16[64,1024]{1,0:T(8,128)(2,1)S(1)}, bf16[64,1024]{1,0:T(8,128)(2,1)S(1)}, u32[]{:S(2)}, u32[]{:S(2)}) collective-permute-start(bf16[64,1024]{1,0:T(8,128)(2,1)S(1)} %get-tuple-element.100), channel_id=1, source_target_pairs={{0,8},{2,10},{4,12},{6,14},{8,0},{10,2},{12,4},{14,6},{1,9},{3,11}... | collective-permute-start | bytes 393224 | tf_op jit(solution)/shard_map/ppermute | solution.py:63
  59.9 1.5 %shard_map.176 = (bf16[2,32,1024]{2,1,0:T(8,128)(2,1)}, f32[8,128]{1,0:T(8,128)S(1)}) custom-call(bf16[128,64]{1,0:T(8,128)(2,1)S(1)} %get-tuple-element.54.refs_0_.pick_ref, bf16[1024,1024]{1,0:T(8,128)(2,1)S(1)} %copy-done, bf16[8,16,1024]{2,1,0:T(8,128)(2,1)S(1)} %get-tuple-element.83.slots_ref, ...), custom_call_target="tpu_custom_call" | custom-call | tf_op jit(solution)/shard_map/pallas_call | solution.py:46
  61.5 2.7 %collective-permute-done.17.refs_6_.refs_5_ = bf16[144,1024]{1,0:T(8,128)(2,1)S(1)} collective-permute-done((bf16[144,1024]{1,0:T(8,128)(2,1)S(1)}, bf16[144,1024]{1,0:T(8,128)(2,1)S(1)}, u32[]{:S(2)}, u32[]{:S(2)}) %collective-permute-start.17) | collective-permute-done | bytes 294944 | tf_op jit(solution)/shard_map/ppermute | solution.py:63
  64.2 1.0 %shard_map.179 = (f32[64,1024]{1,0:T(8,128)}, f32[64,100]{1,0:T(8,128)}, f32[1]{0:T(128)}, f32[8,128]{1,0:T(8,128)S(1)}) custom-call(f32[8,128]{1,0:T(8,128)S(1)} %get-tuple-element.90.refs_0_, f32[256,1152]{1,0:T(8,128)S(1)} %get-tuple-element.91.held_ref.refs_1_, bf16[256,1152]{1,0:T(8,128)(2,1)S(1)} %collective-permute-done.5.refs_0_.other_ref.refs_2_, ...), custom_call_target="tpu_custom_call" | custom-call | tf_op jit(solution)/shard_map/pallas_call | solution.py:46
  65.2 1.6 %collective-permute-done.20.refs_4_ = bf16[64,1024]{1,0:T(8,128)(2,1)S(1)} collective-permute-done((bf16[64,1024]{1,0:T(8,128)(2,1)S(1)}, bf16[64,1024]{1,0:T(8,128)(2,1)S(1)}, u32[]{:S(2)}, u32[]{:S(2)}) %collective-permute-start.20) | collective-permute-done | bytes 131104 | tf_op jit(solution)/shard_map/ppermute | solution.py:63
  66.7 0.8 %shard_map.181 = f32[64,1024]{1,0:T(8,128)} custom-call(f32[8,128]{1,0:T(8,128)S(1)} %get-tuple-element.97.refs_0_, f32[256,1024]{1,0:T(8,128)S(1)} %get-tuple-element.94.near_ref.refs_1_, bf16[208,1024]{1,0:T(8,128)(2,1)S(1)} %collective-permute-done.12.last_ref.refs_3_.refs_2_, bf16[64,1024]{1,0:T(8,128)(2,1)S(1)} %collective-permute-done.19.refs_3_, ...), custom_call_target="tpu_custom_call" | custom-call | flops 8000000000 | tf_op jit(solution)/shard_map/pallas_call | solution.py:46
  (34 shorter events, 2.6 us)
Async XLA Ops:
  1.8 6.5 %collective-permute-start = (bf16[4,16,1024]{2,1,0:T(8,128)(2,1)S(1)}, bf16[4,16,1024]{2,1,0:T(8,128)(2,1)S(1)}, u32[]{:S(2)}, u32[]{:S(2)}) collective-permute-start(bf16[4,16,1024]{2,1,0:T(8,128)(2,1)S(1)} %get-tuple-element.63), channel_id=1, source_target_pairs={{0,2},{2,0},{4,6},{6,4},{8,10},{10,8},{12,14},{14,12},{1,3},{3,1},... | collective-permute-start | bytes 393224 | tf_op jit(solution)/shard_map/ppermute | solution.py:63
  8.3 6.6 %collective-permute-start.1 = (bf16[32,1024]{1,0:T(8,128)(2,1)S(1)}, bf16[32,1024]{1,0:T(8,128)(2,1)S(1)}, u32[]{:S(2)}, u32[]{:S(2)}) collective-permute-start(bf16[32,1024]{1,0:T(8,128)(2,1)S(1)} %get-tuple-element.64), channel_id=1, source_target_pairs={{0,12},{2,14},{4,8},{6,10},{8,4},{10,6},{12,0},{14,2},{1,13},{3,15... | collective-permute-start | bytes 196616 | tf_op jit(solution)/shard_map/ppermute | solution.py:63
  12.2 5.4 %collective-permute-start.2 = (bf16[32,1024]{1,0:T(8,128)(2,1)S(1)}, bf16[32,1024]{1,0:T(8,128)(2,1)S(1)}, u32[]{:S(2)}, u32[]{:S(2)}) collective-permute-start(bf16[32,1024]{1,0:T(8,128)(2,1)S(1)} %get-tuple-element.65), channel_id=1, source_target_pairs={{0,8},{2,10},{4,12},{6,14},{8,0},{10,2},{12,4},{14,6},{1,9},{3,11}... | collective-permute-start | bytes 196616 | tf_op jit(solution)/shard_map/ppermute | solution.py:63
  12.2 5.4 %collective-permute-start.3 = (bf16[32,1024]{1,0:T(8,128)(2,1)S(1)}, bf16[32,1024]{1,0:T(8,128)(2,1)S(1)}, u32[]{:S(2)}, u32[]{:S(2)}) collective-permute-start(bf16[32,1024]{1,0:T(8,128)(2,1)S(1)} %get-tuple-element.66), channel_id=1, source_target_pairs={{0,4},{2,6},{4,0},{6,2},{8,12},{10,14},{12,8},{14,10},{1,5},{3,7},... | collective-permute-start | bytes 196616 | tf_op jit(solution)/shard_map/ppermute | solution.py:63
  21.0 1.4 %copy-start.1 = (f32[100,256]{1,0:T(8,128)S(1)}, f32[100,256]{1,0:T(8,128)}, u32[]{:S(2)}) copy-start(f32[100,256]{1,0:T(8,128)} %truth_ref.1) | copy-start | bytes 307204
  21.1 1.4 %copy-start.2 = (f32[256]{0:T(256)S(1)}, f32[256]{0:T(256)}, u32[]{:S(2)}) copy-start(f32[256]{0:T(256)} %cell_ref.1) | copy-start | bytes 3076
  21.1 1.4 %collective-permute-start.4 = (bf16[2,100,256]{2,1,0:T(8,128)(2,1)S(1)}, bf16[2,100,256]{2,1,0:T(8,128)(2,1)S(1)}, u32[]{:S(2)}, u32[]{:S(2)}) collective-permute-start(bf16[2,100,256]{2,1,0:T(8,128)(2,1)S(1)} %get-tuple-element.68), channel_id=1, source_target_pairs={{0,1},{1,0},{2,3},{3,2},{4,5},{5,4},{6,7},{7,6},{8,9},{9,8},{10,11... | collective-permute-start | bytes 307208 | tf_op jit(solution)/shard_map/ppermute | solution.py:63
  24.0 2.3 %collective-permute-start.7 = (bf16[256,1152]{1,0:T(8,128)(2,1)S(1)}, bf16[256,1152]{1,0:T(8,128)(2,1)S(1)}, u32[]{:S(2)}, u32[]{:S(2)}) collective-permute-start(bf16[256,1152]{1,0:T(8,128)(2,1)S(1)} %get-tuple-element.80), channel_id=1, source_target_pairs={{0,1},{1,0},{2,3},{3,2},{4,5},{5,4},{6,7},{7,6},{8,9},{9,8},{10,11... | collective-permute-start | bytes 1769480 | tf_op jit(solution)/shard_map/ppermute | solution.py:63
  24.2 5.6 %collective-permute-start.6 = (bf16[2,4,64,128]{3,2,1,0:T(8,128)(2,1)S(1)}, bf16[2,4,64,128]{3,2,1,0:T(8,128)(2,1)S(1)}, u32[]{:S(2)}, u32[]{:S(2)}) collective-permute-start(bf16[2,4,64,128]{3,2,1,0:T(8,128)(2,1)S(1)} %get-tuple-element.75), channel_id=1, source_target_pairs={{0,1},{1,0},{2,3},{3,2},{4,5},{5,4},{6,7},{7,6},{8,9},{9,8},{10,11... | collective-permute-start | bytes 393224 | tf_op jit(solution)/shard_map/ppermute | solution.py:63
  24.6 5.3 %collective-permute-start.5 = (bf16[256,1152]{1,0:T(8,128)(2,1)S(1)}, bf16[256,1152]{1,0:T(8,128)(2,1)S(1)}, u32[]{:S(2)}, u32[]{:S(2)}) collective-permute-start(bf16[256,1152]{1,0:T(8,128)(2,1)S(1)} %get-tuple-element.74), channel_id=1, source_target_pairs={{0,1},{1,0},{2,3},{3,2},{4,5},{5,4},{6,7},{7,6},{8,9},{9,8},{10,11... | collective-permute-start | bytes 1769480 | tf_op jit(solution)/shard_map/ppermute | solution.py:63
  26.6 13.6 %collective-permute-start.13 = (bf16[128,1152]{1,0:T(8,128)(2,1)S(1)}, bf16[128,1152]{1,0:T(8,128)(2,1)S(1)}, u32[]{:S(2)}, u32[]{:S(2)}) collective-permute-start(bf16[128,1152]{1,0:T(8,128)(2,1)S(1)} %shard_map.171.refs_0_), channel_id=1, source_target_pairs={{0,2},{2,0},{4,6},{6,4},{8,10},{10,8},{12,14},{14,12},{1,3},{3,1},... | collective-permute-start | bytes 884744 | tf_op jit(solution)/shard_map/ppermute | solution.py:63
  30.3 4.5 %collective-permute-start.8 = (bf16[8,16,1024]{2,1,0:T(8,128)(2,1)S(1)}, bf16[8,16,1024]{2,1,0:T(8,128)(2,1)S(1)}, u32[]{:S(2)}, u32[]{:S(2)}) collective-permute-start(bf16[8,16,1024]{2,1,0:T(8,128)(2,1)S(1)} %get-tuple-element.83.slots_ref), channel_id=1, source_target_pairs={{0,1},{1,0},{2,3},{3,2},{4,5},{5,4},{6,7},{7,6},{8,9},{9,8},{10,11... | collective-permute-start | bytes 786440 | tf_op jit(solution)/shard_map/ppermute | solution.py:63
  30.4 6.8 %collective-permute-start.9 = (bf16[32,1024]{1,0:T(8,128)(2,1)S(1)}, bf16[32,1024]{1,0:T(8,128)(2,1)S(1)}, u32[]{:S(2)}, u32[]{:S(2)}) collective-permute-start(bf16[32,1024]{1,0:T(8,128)(2,1)S(1)} %get-tuple-element.86), channel_id=1, source_target_pairs={{0,12},{2,14},{4,8},{6,10},{8,4},{10,6},{12,0},{14,2},{1,13},{3,15... | collective-permute-start | bytes 196616 | tf_op jit(solution)/shard_map/ppermute | solution.py:63
  32.7 6.9 %collective-permute-start.10 = (bf16[32,1024]{1,0:T(8,128)(2,1)S(1)}, bf16[32,1024]{1,0:T(8,128)(2,1)S(1)}, u32[]{:S(2)}, u32[]{:S(2)}) collective-permute-start(bf16[32,1024]{1,0:T(8,128)(2,1)S(1)} %get-tuple-element.87), channel_id=1, source_target_pairs={{0,8},{2,10},{4,12},{6,14},{8,0},{10,2},{12,4},{14,6},{1,9},{3,11}... | collective-permute-start | bytes 196616 | tf_op jit(solution)/shard_map/ppermute | solution.py:63
  32.7 6.9 %collective-permute-start.11 = (bf16[32,1024]{1,0:T(8,128)(2,1)S(1)}, bf16[32,1024]{1,0:T(8,128)(2,1)S(1)}, u32[]{:S(2)}, u32[]{:S(2)}) collective-permute-start(bf16[32,1024]{1,0:T(8,128)(2,1)S(1)} %get-tuple-element.88), channel_id=1, source_target_pairs={{0,4},{2,6},{4,0},{6,2},{8,12},{10,14},{12,8},{14,10},{1,5},{3,7},... | collective-permute-start | bytes 196616 | tf_op jit(solution)/shard_map/ppermute | solution.py:63
  35.6 15.9 %collective-permute-start.18 = (bf16[128,1024]{1,0:T(8,128)(2,1)S(1)}, bf16[128,1024]{1,0:T(8,128)(2,1)S(1)}, u32[]{:S(2)}, u32[]{:S(2)}) collective-permute-start(bf16[128,1024]{1,0:T(8,128)(2,1)S(1)} %get-tuple-element.98), channel_id=1, source_target_pairs={{0,2},{2,0},{4,6},{6,4},{8,10},{10,8},{12,14},{14,12},{1,3},{3,1},... | collective-permute-start | bytes 786440 | tf_op jit(solution)/shard_map/ppermute | solution.py:63
  37.3 14.0 %collective-permute-start.16 = (bf16[144,1024]{1,0:T(8,128)(2,1)S(1)}, bf16[144,1024]{1,0:T(8,128)(2,1)S(1)}, u32[]{:S(2)}, u32[]{:S(2)}) collective-permute-start(bf16[144,1024]{1,0:T(8,128)(2,1)S(1)} %get-tuple-element.95), channel_id=1, source_target_pairs={{0,2},{2,0},{4,6},{6,4},{8,10},{10,8},{12,14},{14,12},{1,3},{3,1},... | collective-permute-start | bytes 884744 | tf_op jit(solution)/shard_map/ppermute | solution.py:63
  39.6 19.4 %collective-permute-start.12 = (bf16[208,1024]{1,0:T(8,128)(2,1)S(1)}, bf16[208,1024]{1,0:T(8,128)(2,1)S(1)}, u32[]{:S(2)}, u32[]{:S(2)}) collective-permute-start(bf16[208,1024]{1,0:T(8,128)(2,1)S(1)} %shard_map.175), channel_id=1, source_target_pairs={{0,2},{2,0},{4,6},{6,4},{8,10},{10,8},{12,14},{14,12},{1,3},{3,1},... | collective-permute-start | bytes 1277960 | tf_op jit(solution)/shard_map/ppermute | solution.py:63
  40.3 21.1 %collective-permute-start.14 = (bf16[64,1152]{1,0:T(8,128)(2,1)S(1)}, bf16[64,1152]{1,0:T(8,128)(2,1)S(1)}, u32[]{:S(2)}, u32[]{:S(2)}) collective-permute-start(bf16[64,1152]{1,0:T(8,128)(2,1)S(1)} %get-tuple-element.92), channel_id=1, source_target_pairs={{0,12},{2,14},{4,8},{6,10},{8,4},{10,6},{12,0},{14,2},{1,13},{3,15... | collective-permute-start | bytes 442376 | tf_op jit(solution)/shard_map/ppermute | solution.py:63
  42.7 18.7 %collective-permute-start.15 = (bf16[64,1152]{1,0:T(8,128)(2,1)S(1)}, bf16[64,1152]{1,0:T(8,128)(2,1)S(1)}, u32[]{:S(2)}, u32[]{:S(2)}) collective-permute-start(bf16[64,1152]{1,0:T(8,128)(2,1)S(1)} %get-tuple-element.93), channel_id=1, source_target_pairs={{0,8},{2,10},{4,12},{6,14},{8,0},{10,2},{12,4},{14,6},{1,9},{3,11}... | collective-permute-start | bytes 442376 | tf_op jit(solution)/shard_map/ppermute | solution.py:63
  51.4 8.5 %copy-start = (bf16[1024,1024]{1,0:T(8,128)(2,1)S(1)}, bf16[1024,1024]{1,0:T(8,128)(2,1)}, u32[]{:S(2)}) copy-start(bf16[1024,1024]{1,0:T(8,128)(2,1)} %w_msg_ref.1) | copy-start | bytes 6291460
  51.5 12.7 %collective-permute-start.17 = (bf16[144,1024]{1,0:T(8,128)(2,1)S(1)}, bf16[144,1024]{1,0:T(8,128)(2,1)S(1)}, u32[]{:S(2)}, u32[]{:S(2)}) collective-permute-start(bf16[144,1024]{1,0:T(8,128)(2,1)S(1)} %shard_map.178), channel_id=1, source_target_pairs={{0,4},{2,6},{4,0},{6,2},{8,12},{10,14},{12,8},{14,10},{1,5},{3,7},... | collective-permute-start | bytes 884744 | tf_op jit(solution)/shard_map/ppermute | solution.py:63
  51.6 13.6 %collective-permute-start.19 = (bf16[64,1024]{1,0:T(8,128)(2,1)S(1)}, bf16[64,1024]{1,0:T(8,128)(2,1)S(1)}, u32[]{:S(2)}, u32[]{:S(2)}) collective-permute-start(bf16[64,1024]{1,0:T(8,128)(2,1)S(1)} %get-tuple-element.99), channel_id=1, source_target_pairs={{0,12},{2,14},{4,8},{6,10},{8,4},{10,6},{12,0},{14,2},{1,13},{3,15... | collective-permute-start | bytes 393224 | tf_op jit(solution)/shard_map/ppermute | solution.py:63
  58.9 7.8 %collective-permute-start.20 = (bf16[64,1024]{1,0:T(8,128)(2,1)S(1)}, bf16[64,1024]{1,0:T(8,128)(2,1)S(1)}, u32[]{:S(2)}, u32[]{:S(2)}) collective-permute-start(bf16[64,1024]{1,0:T(8,128)(2,1)S(1)} %get-tuple-element.100), channel_id=1, source_target_pairs={{0,8},{2,10},{4,12},{6,14},{8,0},{10,2},{12,4},{14,6},{1,9},{3,11}... | collective-permute-start | bytes 393224 | tf_op jit(solution)/shard_map/ppermute | solution.py:63

commit v4 on v3

--- a/solution.py
+++ b/solution.py
@@ -13,12 +13,12 @@
 lanes = 128
 packed = 16
 cost_hints = {
-    "back_kernel": 8,
-    "slot_kernel": 4,
-    "hidden_early_kernel": 4,
-    "message_early_kernel": 4,
-    "late_kernel": 4,
-    "message_sum_kernel": 8,
+    "partial_kernel": 4,
+    "hidden_early_kernel": 3,
+    "local_kernel": 8,
+    "message_sum_kernel": 5,
+    "slot_kernel": 5,
+    "message_early_kernel": 5,
 }
 f32 = jnp.float32
 bf16 = jnp.bfloat16
@@ -311,18 +311,22 @@
     out_ref[:, width:] = part.astype(bf16)
 
 
-def message_kernel(
-    variables, early, levels, keep_ref, give_ref, slots_ref, other_ref, held_ref, far_other_ref,
-    first_ref, middle_ref, last_ref, near_ref,
-):
+def across_kernel(variables, begin, near_ref, near_other_ref, far_ref, far_other_ref, *out_refs):
+    width = out_refs[0].shape[1]
+    block = out_refs[0].shape[0] // 2 - packed
+    for i, out_ref in enumerate(out_refs):
+        for line, (held_ref, other_ref) in enumerate(((near_ref, near_other_ref), (far_ref, far_other_ref))):
+            total, part = pair_sum(variables, width, held_ref, other_ref, begin + i * block, block)
+            at = line * (block + packed)
+            out_ref[at : at + block, :] = total.astype(bf16)
+            out_ref[at + block : at + block + packed, :] = jnp.zeros((packed, width), bf16)
+            pack(out_ref, at + block, part.astype(bf16))
+
+
+def message_kernel(keep_ref, give_ref, slots_ref, other_ref, first_ref, own_ref, near_ref, *out_refs):
     depth, width = keep_ref.shape[-1], near_ref.shape[1]
-    block = near_ref.shape[0] // levels
-    count, rest = early * block, (levels - 1 - early) * block
-    for begin, size, out_ref in ((count, rest, middle_ref), (count + rest, block, last_ref)):
-        total, part = pair_sum(variables, width, held_ref, far_other_ref, begin, size)
-        out_ref[0:size, :] = total.astype(bf16)
-        out_ref[size : size + packed, :] = jnp.zeros((packed, width), bf16)
-        pack(out_ref, size, part.astype(bf16))
+    rows = slots_ref.shape[1]
+    count, block = first_ref.shape[0], own_ref.shape[0]
     for half in range(2):
         own = keep_ref[half].reshape(-1, depth)
         other = give_ref[half].reshape(-1, depth)
@@ -332,22 +336,48 @@
             there = other_ref[:, :, columns].reshape(depth, tile)
             total = mm(own, here, 1, 0) + mm(other, there, 1, 0)
             if half == 0:
-                total = total.astype(bf16)
-                first_ref[:, columns] = total[:count]
-                middle_ref[rest + packed :, columns] = total[count : count + rest]
-                last_ref[block + packed :, columns] = total[count + rest :]
+                first_ref[:, columns] = total[:count].astype(bf16)
+                own_ref[:, columns] = total[total.shape[0] - block :]
             else:
                 near_ref[:, columns] = total
-
-
-def ride_kernel(last_ref, slots_ref, *rest):
+            for i, out_ref in enumerate(out_refs):
+                at = (1 - half) * block
+                out_ref[at : at + block, columns] = total[count + i * block : count + (i + 1) * block].astype(bf16)
+    for i, out_ref in enumerate(out_refs):
+        step = len(out_refs) - i
+        out_ref[2 * block : 2 * block + rows, :] = slots_ref[2 * step]
+        out_ref[2 * block + rows :, :] = slots_ref[2 * step + 1]
+
+
+def own_kernel(variables, width, held_ref, other_ref, *rest):
     arrived_refs, out_ref = rest[:-1], rest[-1]
-    rows = slots_ref.shape[1]
-    begin = last_ref.shape[0]
-    out_ref[0:begin, :] = last_ref[...]
-    for i, arrived_ref in enumerate(arrived_refs):
-        out_ref[begin + i * rows : begin + (i + 1) * rows, :] = arrived_ref[rows:, :]
-    out_ref[begin + len(arrived_refs) * rows :, :] = slots_ref[1]
+    block = out_ref.shape[0]
+    total, part = pair_sum(variables, width, held_ref, other_ref, held_ref.shape[0] - block, block)
+    for r in arrived_refs:
+        at = block + packed
+        total = total + r[at : at + block, :].astype(f32)
+        part = part + unpack(r, at + block, block, part.shape[1])
+    out_ref[:, :width] = total
+    out_ref[:, width:] = split_loss(part, variables)
+
+
+def last_kernel(early, hidden_ref, own_ref, slots_ref, *rest):
+    arrived_refs, out_ref = rest[:-1], rest[-1]
+    rows, width = slots_ref.shape[1:]
+    block = own_ref.shape[0]
+    out_ref[0:block, :] = hidden_ref[:, :width].astype(bf16)
+    out_ref[block : block + packed, :] = jnp.zeros((packed, width), bf16)
+    pack(out_ref, block, hidden_ref[:, width:].astype(bf16))
+    total = own_ref[...]
+    for r in arrived_refs[early:]:
+        total = total + r[block : 2 * block, :].astype(f32)
+    at = 2 * block + packed
+    out_ref[block + packed : at, :] = total.astype(bf16)
+    for i, r in enumerate(arrived_refs):
+        begin = rows if i < early else 2 * block + rows
+        out_ref[at : at + rows, :] = r[begin : begin + rows, :]
+        at += rows
+    out_ref[at:, :] = slots_ref[1]
 
 
 def hidden_early_kernel(variables, width, held_ref, other_ref, arrived_ref, *out_refs):
@@ -365,23 +395,6 @@
     for i, out_ref in enumerate(out_refs):
         here = slice(i * block, (i + 1) * block)
         out_ref[...] = (near_ref[here, :] + arrived_ref[here, :].astype(f32)).astype(bf16)
-
-
-def late_kernel(variables, early, held_ref, other_ref, near_ref, arrived_ref, *out_refs):
-    width = near_ref.shape[1]
-    block = (out_refs[0].shape[0] - packed) // 2
-    count = block * len(out_refs)
-    parts = unpack(arrived_ref, count, count, held_ref.shape[1] - width)
-    for i, out_ref in enumerate(out_refs):
-        begin = (early + i) * block
-        total, part = pair_sum(variables, width, held_ref, other_ref, begin, block)
-        here = slice(i * block, (i + 1) * block)
-        out_ref[0:block, :] = (total + arrived_ref[here, :].astype(f32)).astype(bf16)
-        there = slice(count + packed + i * block, count + packed + (i + 1) * block)
-        total = near_ref[begin : begin + block, :] + arrived_ref[there, :].astype(f32)
-        out_ref[block : 2 * block, :] = total.astype(bf16)
-        out_ref[2 * block :, :] = jnp.zeros((packed, width), bf16)
-        pack(out_ref, 2 * block, split_loss(part + parts[here], variables).astype(bf16))
 
 
 def back_kernel(inner_ref, w_hidden_ref, gain_ref, unit_ref, inverse_ref, grad_ref, scaled_ref):
@@ -412,12 +425,12 @@
         both = mm(share_ref[...], grad_ref[:, columns], 1, 0)
         slots_ref[:, :, columns] = (both[:rows] + both[rows:]).astype(bf16).reshape(peers, each, tile)
     for i, send_ref in enumerate(send_refs):
-        step = len(send_refs) - i
+        step = peers // 2 - 1 - i
         send_ref[0:each, :] = slots_ref[2 * step]
         send_ref[each:, :] = slots_ref[2 * step + 1]
 
 
-def owner_kernel(pick_ref, w_msg_ref, slots_ref, last_ref, *rest):
+def owner_kernel(early, block, pick_ref, w_msg_ref, slots_ref, last_ref, *rest):
     arrived_refs, (grad_ref, token_ref, held_ref) = rest[:-3], rest[-3:]
     token_ref[...] = jnp.zeros_like(token_ref)
     peers, rows, width = slots_ref.shape
@@ -425,27 +438,36 @@
     begin = last_ref.shape[0] - levels * rows
     for i in range(levels):
         spot = 2 * (levels - 1 - i)
-        held_ref[spot] = slots_ref[0] if i == levels - 1 else arrived_refs[i][0:rows, :]
+        if i == levels - 1:
+            held_ref[spot] = slots_ref[0]
+        else:
+            at = 0 if i < early else 2 * block
+            held_ref[spot] = arrived_refs[i][at : at + rows, :]
         held_ref[spot + 1] = last_ref[begin + i * rows : begin + (i + 1) * rows, :]
     nodes = mm(pick_ref[...], held_ref[...].reshape(peers * rows, width), 0, 0).astype(bf16)
     grad_ref[...] = mm(nodes, w_msg_ref[...], 1, 1).astype(bf16).reshape(grad_ref.shape)
 
 
-def hidden_sum_kernel(variables, scale, early, held_ref, other_ref, last_ref, *rest):
-    hidden_ref, out_ref, loss_ref, token_ref = rest[-4:]
-    token_ref[...] = jnp.zeros_like(token_ref)
-    block, width = hidden_ref.shape
-    pad = held_ref.shape[1] - width
+def partial_kernel(variables, width, early, held_ref, other_ref, *rest):
+    arrived_refs, out_ref = rest[:-1], rest[-1]
+    block = out_ref.shape[0]
     total, part = pair_sum(variables, width, held_ref, other_ref, held_ref.shape[0] - block, block)
-    total = total + last_ref[0:block, :].astype(f32)
-    part = part + unpack(last_ref, block, block, pad)
-    for i, r in enumerate(rest[:-4]):
+    for i, r in enumerate(arrived_refs):
         total = total + r[0:block, :width].astype(f32)
         if i < early:
             part = part + r[:, width:].astype(f32)
         else:
-            part = part + unpack(r, 2 * block, block, pad)
-    hidden_ref[...] = total
+            part = part + unpack(r, block, block, part.shape[1])
+    out_ref[:, :width] = total
+    out_ref[:, width:] = part
+
+
+def hidden_sum_kernel(variables, scale, partial_ref, last_ref, hidden_ref, out_ref, loss_ref, token_ref):
+    token_ref[...] = jnp.zeros_like(token_ref)
+    block, width = hidden_ref.shape
+    pad = partial_ref.shape[1] - width
+    part = partial_ref[:, width:] + unpack(last_ref, block, block, pad)
+    hidden_ref[...] = partial_ref[:, :width] + last_ref[0:block, :].astype(f32)
     out_ref[...] = part[:, :variables]
     column = lax.broadcasted_iota(jnp.int32, (8, pad), 1)
     spots = (column == variables) | (column == variables + 1)
@@ -453,14 +475,13 @@
     loss_ref[0] = jnp.sum(jnp.where(spots & first, part[:8], 0.0)) * scale
 
 
-def message_sum_kernel(early, near_ref, last_ref, *rest):
+def message_sum_kernel(near_ref, last_ref, *rest):
     out_ref = rest[-1]
     block = out_ref.shape[0]
     total = near_ref[near_ref.shape[0] - block :, :]
     total = total + last_ref[block + packed : 2 * block + packed, :].astype(f32)
-    for i, r in enumerate(rest[:-1]):
-        begin = 0 if i < early else block
-        total = total + r[begin : begin + block, :].astype(f32)
+    for r in rest[:-1]:
+        total = total + r[0:block, :].astype(f32)
     out_ref[...] = total
 
 
@@ -576,48 +597,53 @@
         limit=6,
     )
     first_other = swap(first, "space", peers, 1)
+    across = call(
+        functools.partial(across_kernel, variables, count),
+        [((2 * block + 2 * packed, width), bf16)] * (levels - 1 - early),
+        [held_near, near_other, held_far, far_other],
+        limit=6,
+        after=[first],
+    )
+    across_parts = spread(across, steps[early:])
     (grad_hidden,) = call(
         back_kernel,
         [((rows_all, width), bf16)],
         [grad_inner, w_hidden_near, gain, unit, inverse],
         scratch=[pltpu.VMEM((rows_all, width), f32)],
         limit=14,
-        after=[first],
+        after=[across[0]],
     )
     slots, *slots_sent = call(
         slot_kernel,
-        [((peers, rows_peer, width), bf16)] + [((2 * rows_peer, width), bf16)] * (levels - 1),
+        [((peers, rows_peer, width), bf16)] + [((2 * rows_peer, width), bf16)] * early,
         [share, grad_hidden],
         limit=6,
-        after=[near_other, received_other],
+        after=[received_other],
     )
     slots_other = swap(slots, "member", cores, 1)
-    slots_arrived = spread(slots_sent, steps)
-    message_first, middle, last, message_near = call(
-        functools.partial(message_kernel, variables, early, levels),
-        [
-            ((count, width), bf16),
-            ((2 * rest + packed, width), bf16),
-            ((2 * block + packed, width), bf16),
-            ((half, width), f32),
-        ],
-        [received_keep, received_other, slots, slots_other, held_far, far_other],
+    slots_arrived = spread(slots_sent, steps[:early])
+    message_first, message_own, message_near, *message_across = call(
+        message_kernel,
+        [((count, width), bf16), ((block, width), f32), ((half, width), f32)]
+        + [((2 * block + 2 * rows_peer, width), bf16)] * (levels - 1 - early),
+        [received_keep, received_other, slots, slots_other],
         limit=10,
     )
     message_first_other = swap(message_first, "space", peers, 1)
-    middle_other = swap(middle, "space", peers, 1)
-    (last,) = call(
-        ride_kernel,
-        [((2 * block + packed + levels * rows_peer, width), bf16)],
-        [last, slots] + slots_arrived,
+    message_across_parts = spread(message_across, steps[early:])
+    slots_arrived += message_across_parts
+    (hidden_own,) = call(
+        functools.partial(own_kernel, variables, width),
+        [((block, wide), f32)],
+        [held_far, far_other] + across_parts,
         limit=4,
     )
-    last_other = swap(last, "space", peers, 1)
     hidden_early = call(
         functools.partial(hidden_early_kernel, variables, width),
         [((block, wide), bf16)] * early,
         [held_near, near_other, first_other],
         limit=6,
+        after=[message_first, hidden_own, slots_arrived[0]],
     )
     hidden_parts = spread(hidden_early, steps[:early])
     message_early = call(
@@ -625,35 +651,43 @@
         [((block, width), bf16)] * early,
         [message_near, message_first_other],
         limit=6,
+        after=hidden_early[:1],
     )
     message_parts = spread(message_early, steps[:early])
-    late = call(
-        functools.partial(late_kernel, variables, early),
-        [((2 * block + packed, width), bf16)] * (levels - 1 - early),
-        [held_near, near_other, message_near, middle_other],
-        limit=6,
-    )
-    late_parts = spread(late, steps[early:])
+    (last,) = call(
+        functools.partial(last_kernel, early),
+        [((2 * block + packed + levels * rows_peer, width), bf16)],
+        [hidden_own, message_own, slots] + slots_arrived,
+        limit=4,
+    )
+    last_other = swap(last, "space", peers, 1)
+    (partial,) = call(
+        functools.partial(partial_kernel, variables, width, early),
+        [((block, wide), f32)],
+        [held_near, near_other] + hidden_parts + across_parts,
+        limit=4,
+    )
     token = ((8, lanes), f32)
     latent_grad, latent_done = call(
-        owner_kernel,
+        functools.partial(owner_kernel, early, block),
         [(latents.shape, bf16), token],
         [pick, w_msg, slots, last_other] + slots_arrived,
         scratch=[pltpu.VMEM((peers, rows_peer, width), bf16)],
         limit=8,
+        after=[partial],
     )
     hidden_weight_grad, out_weight_grad, loss, hidden_done = call(
-        functools.partial(hidden_sum_kernel, variables, 1.0 / (points * peers * variables), early),
+        functools.partial(hidden_sum_kernel, variables, 1.0 / (points * peers * variables)),
         [((block, width), f32), ((block, variables), f32), ((1,), f32), token],
-        [held_near, near_other, last_other] + hidden_parts + late_parts,
+        [partial, last_other],
         limit=8,
         scalar_outs=(2,),
         after=[latent_done],
     )
     (msg_weight_grad,) = call(
-        functools.partial(message_sum_kernel, early),
+        message_sum_kernel,
         [((block, width), f32)],
-        [message_near, last_other] + message_parts + late_parts,
+        [message_near, last_other] + message_parts + message_across_parts,
         limit=6,
         after=[hidden_done],
     )

time: 67.8 us -> 69.4 us (1.024)
  starting transfers between devices: 22 us -> 24.5 us
  waiting for transfers between devices: 26.6 us -> 25.9 us
    ppermute x21 -> x20, starting transfers between devices: 22 us -> 24.5 us  [swap(): return lax.ppermute(value, axis, [(i, i ^ step) for i in range(size)])]
    ppermute x21 -> x20, waiting for transfers between devices: 26.6 us -> 25.9 us  [swap(): return lax.ppermute(value, axis, [(i, i ^ step) for i in range(size)])]
    pallas_call x18 -> x20, Pallas kernels: 18.1 us -> 17.9 us  [call(): pl.pallas_call(inner if count else body, out_shape=[jax.ShapeDtypeStruct(...]
  transfers between devices with their start and end apart: 21 -> 20, of which waited for: 10 -> 10; matrix products, arithmetic and copies ran while one was open for 0% -> 0% of each run, Pallas kernels for 16% -> 18%
where the time goes in v4:
time: 69.4 us; the launch traced here: 69.1 us
  waiting for transfers between devices  25.9 us (37%)
  starting transfers between devices  24.5 us (35%)
  Pallas kernels  17.9 us (26%)
  between operations  0.83 us (1%)
    ppermute x20, waiting for transfers between devices, swap(): return lax.ppermute(value, axis, [(i, i ^ step) for i in range(size)])  25.9 us
    ppermute x20, starting transfers between devices, swap(): return lax.ppermute(value, axis, [(i, i ^ step) for i in range(size)])  24.5 us
    pallas_call x20, Pallas kernels, call(): pl.pallas_call(inner if count else body, out_shape=[jax.ShapeDtypeStruct(...  17.9 us
  transfers between devices with their start and end apart: 20, of which 10 were waited for; matrix products, arithmetic and copies ran while one was open for 0% of the time, Pallas kernels for 18%

profile of v4, /device:TPU:0, one launch (start us, length us, event | category | flops | bytes accessed | tf_op | source)
XLA Modules:
  0.0 69.1 jit_solution(10698708321743979251)
XLA Ops:
  0.6 1.1 %shard_map.164 = (bf16[128,64]{1,0:T(8,128)(2,1)S(1)}, bf16[4,16,1024]{2,1,0:T(8,128)(2,1)S(1)}, bf16[4,16,1024]{2,1,0:T(8,128)(2,1)S(1)}) custom-call(s32[1,8,8]{2,1,0:T(8,128)} %lists_ref.1, bf16[2,32,1024]{2,1,0:T(8,128)(2,1)} %latents_ref.1), custom_call_target="tpu_custom_call" | custom-call | tf_op jit(solution)/shard_map/pallas_call | solution.py:46
  1.8 3.0 %collective-permute-start = (bf16[4,16,1024]{2,1,0:T(8,128)(2,1)S(1)}, bf16[4,16,1024]{2,1,0:T(8,128)(2,1)S(1)}, u32[]{:S(2)}, u32[]{:S(2)}) collective-permute-start(bf16[4,16,1024]{2,1,0:T(8,128)(2,1)S(1)} %get-tuple-element.62), channel_id=1, source_target_pairs={{0,2},{2,0},{4,6},{6,4},{8,10},{10,8},{12,14},{14,12},{1,3},{3,1},... | collective-permute-start | bytes 393224 | tf_op jit(solution)/shard_map/ppermute | solution.py:63
  4.8 2.6 %shard_map.165 = (bf16[256,512]{1,0:T(8,128)(2,1)S(1)}, bf16[1024,1024]{1,0:T(8,128)(2,1)S(1)}, f32[1024]{0:T(1024)S(1)}, bf16[256,1024]{1,0:T(8,128)(2,1)S(1)},...) custom-call(bf16[128,64]{1,0:T(8,128)(2,1)S(1)} %get-tuple-element.53.refs_0_.refs_1_, ...), custom_call_target="tpu_custom_call" | custom-call | tf_op jit(solution)/shard_map/pallas_call | solution.py:46
  7.4 0.9 %collective-permute-done.refs_2_.near_ref = bf16[4,16,1024]{2,1,0:T(8,128)(2,1)S(1)} collective-permute-done((bf16[4,16,1024]{2,1,0:T(8,128)(2,1)S(1)}, bf16[4,16,1024]{2,1,0:T(8,128)(2,1)S(1)}, u32[]{:S(2)}, u32[]{:S(2)}) %collective-permute-start) | collective-permute-done | bytes 131104 | tf_op jit(solution)/shard_map/ppermute | solution.py:63
  8.3 3.9 %collective-permute-start.1 = (bf16[32,1024]{1,0:T(8,128)(2,1)S(1)}, bf16[32,1024]{1,0:T(8,128)(2,1)S(1)}, u32[]{:S(2)}, u32[]{:S(2)}) collective-permute-start(bf16[32,1024]{1,0:T(8,128)(2,1)S(1)} %get-tuple-element.63), channel_id=1, source_target_pairs={{0,12},{2,14},{4,8},{6,10},{8,4},{10,6},{12,0},{14,2},{1,13},{3,15... | collective-permute-start | bytes 196616 | tf_op jit(solution)/shard_map/ppermute | solution.py:63
  12.2 0.6 collective-permute-start.3
  12.8 2.0 %collective-permute-done.1.rest_0_ = bf16[32,1024]{1,0:T(8,128)(2,1)S(1)} collective-permute-done((bf16[32,1024]{1,0:T(8,128)(2,1)S(1)}, bf16[32,1024]{1,0:T(8,128)(2,1)S(1)}, u32[]{:S(2)}, u32[]{:S(2)}) %collective-permute-start.1) | collective-permute-done | bytes 65568 | tf_op jit(solution)/shard_map/ppermute | solution.py:63
  14.9 2.7 %collective-permute-done.2.rest_1_ = bf16[32,1024]{1,0:T(8,128)(2,1)S(1)} collective-permute-done((bf16[32,1024]{1,0:T(8,128)(2,1)S(1)}, bf16[32,1024]{1,0:T(8,128)(2,1)S(1)}, u32[]{:S(2)}, u32[]{:S(2)}) %collective-permute-start.2) | collective-permute-done | bytes 65568 | tf_op jit(solution)/shard_map/ppermute | solution.py:63
  17.6 3.5 %shard_map.167 = (f32[2,100,256]{2,1,0:T(8,128)S(1)}, bf16[2,100,256]{2,1,0:T(8,128)(2,1)S(1)}, bf16[512,1024]{1,0:T(8,128)(2,1)S(1)}, bf16[512,1024]{1,0:T(8,12...) custom-call(bf16[1024,1024]{1,0:T(8,128)(2,1)S(1)} %get-tuple-element.54.w_msg_ref, ...), custom_call_target="tpu_custom_call" | custom-call | tf_op jit(solution)/shard_map/pallas_call | solution.py:46
  21.2 0.9 %shard_map.168 = (bf16[2,2,4,64,512]{4,3,2,1,0:T(8,128)(2,1)S(1)}, bf16[2,2,4,64,512]{4,3,2,1,0:T(8,128)(2,1)S(1)}, bf16[2,4,64,128]{3,2,1,0:T(8,128)(2,1)S(1)}, bf16[2,4,64,128]{3,2,1,0:T(8,128)(2,1)S(1)}) custom-call(bf16[512,1024]{1,0:T(8,128)(2,1)S(1)} %get-tuple-element.69.normed_ref, bf16[512,1024]{1,0:T(8,128)(2,1)S(1)} %get-tuple-element.70.active_ref, ...), custom_call_target="tpu_custom_call" | custom-call | tf_op jit(solution)/shard_map/pallas_call | solution.py:46
  22.1 0.6 collective-permute-start.6
  22.7 1.5 %shard_map.169 = (bf16[512,1024]{1,0:T(8,128)(2,1)S(1)}, bf16[128,512]{1,0:T(8,128)(2,1)S(1)}, f32[1]{0:T(128)}, bf16[256,1152]{1,0:T(8,128)(2,1)S(1)}, bf16[256,1152]{1,0:T(8,128)(2,1)S(1)}) custom-call(f32[2,100,256]{2,1,0:T(8,128)S(1)} %get-tuple-element.66.own_ref, bf16[2,100,256]{2,1,0:T(8,128)(2,1)S(1)} %collective-permute-done.4.other_ref, ...), custom_call_target="tpu_custom_call" | custom-call | tf_op jit(solution)/shard_map/pallas_call | solution.py:46
  24.8 1.6 %shard_map.170 = (f32[256,1152]{1,0:T(8,128)S(1)}, f32[256,1152]{1,0:T(8,128)S(1)}) custom-call(f32[1]{0:T(128)} %get-tuple-element.73.loss_ref, bf16[2,2,4,64,512]{4,3,2,1,0:T(8,128)(2,1)S(1)} %get-tuple-element.71.normed_t_ref, bf16[2,2,4,64,512]{4,3,2,1,0:T(8,128)(2,1)S(1)} %get-tuple-element.72.active_t_ref, ...), custom_call_target="tpu_custom_call" | custom-call | flops 8000000000 | tf_op jit(solution)/shard_map/pallas_call | solution.py:46
  26.4 0.8 %collective-permute-done.7.other_ref.refs_4_ = bf16[256,1152]{1,0:T(8,128)(2,1)S(1)} collective-permute-done((bf16[256,1152]{1,0:T(8,128)(2,1)S(1)}, bf16[256,1152]{1,0:T(8,128)(2,1)S(1)}, u32[]{:S(2)}, u32[]{:S(2)}) %collective-permute-start.7) | collective-permute-done | bytes 589856 | tf_op jit(solution)/shard_map/ppermute | solution.py:63
  27.5 0.5 collective-permute-start.9
  28.0 1.6 %shard_map.173.refs_2_ = bf16[512,1024]{1,0:T(8,128)(2,1)S(1)} custom-call(bf16[160,1024]{1,0:T(8,128)(2,1)S(1)} %shard_map.172.refs_0_, bf16[512,1024]{1,0:T(8,128)(2,1)S(1)} %get-tuple-element.74.inner_ref.refs_1_, bf16[1024,1024]{1,0:T(8,128)(2,1)S(1)} %get-tuple-element.58.weights_ref.refs_2_, f32[1024]{0:T(1024)S(1)} %get-tuple-element.56.gain_ref.refs_3_, ...), custom_call_target="tpu_custom_call" | custom-call | tf_op jit(solution)/shard_map/pallas_call | solution.py:46
  30.2 1.6 %collective-permute-start.11 = (bf16[128,1152]{1,0:T(8,128)(2,1)S(1)}, bf16[128,1152]{1,0:T(8,128)(2,1)S(1)}, u32[]{:S(2)}, u32[]{:S(2)}) collective-permute-start(bf16[128,1152]{1,0:T(8,128)(2,1)S(1)} %shard_map.171.refs_0_), channel_id=1, source_target_pairs={{0,2},{2,0},{4,6},{6,4},{8,10},{10,8},{12,14},{14,12},{1,3},{3,1},... | collective-permute-start | bytes 884744 | tf_op jit(solution)/shard_map/ppermute | solution.py:63
  31.7 2.8 %collective-permute-start.10 = (bf16[32,1024]{1,0:T(8,128)(2,1)S(1)}, bf16[32,1024]{1,0:T(8,128)(2,1)S(1)}, u32[]{:S(2)}, u32[]{:S(2)}) collective-permute-start(bf16[32,1024]{1,0:T(8,128)(2,1)S(1)} %get-tuple-element.86), channel_id=1, source_target_pairs={{0,12},{2,14},{4,8},{6,10},{8,4},{10,6},{12,0},{14,2},{1,13},{3,15... | collective-permute-start | bytes 196616 | tf_op jit(solution)/shard_map/ppermute | solution.py:63
  34.6 0.7 shard_map.175
  35.4 1.5 %collective-permute-start.14 = (bf16[32,1024]{1,0:T(8,128)(2,1)S(1)}, bf16[32,1024]{1,0:T(8,128)(2,1)S(1)}, u32[]{:S(2)}, u32[]{:S(2)}) collective-permute-start(bf16[32,1024]{1,0:T(8,128)(2,1)S(1)} %get-tuple-element.90), channel_id=1, source_target_pairs={{0,8},{2,10},{4,12},{6,14},{8,0},{10,2},{12,4},{14,6},{1,9},{3,11}... | collective-permute-start | bytes 196616 | tf_op jit(solution)/shard_map/ppermute | solution.py:63
  37.3 1.9 %collective-permute-start.17 = (bf16[128,1024]{1,0:T(8,128)(2,1)S(1)}, bf16[128,1024]{1,0:T(8,128)(2,1)S(1)}, u32[]{:S(2)}, u32[]{:S(2)}) collective-permute-start(bf16[128,1024]{1,0:T(8,128)(2,1)S(1)} %get-tuple-element.85.refs_0_), channel_id=1, source_target_pairs={{0,2},{2,0},{4,6},{6,4},{8,10},{10,8},{12,14},{14,12},{1,3},{3,1},... | collective-permute-start | bytes 786440 | tf_op jit(solution)/shard_map/ppermute | solution.py:63
  39.4 1.4 %collective-permute-done.10.refs_2_.rest_0_.refs_5_ = bf16[32,1024]{1,0:T(8,128)(2,1)S(1)} collective-permute-done((bf16[32,1024]{1,0:T(8,128)(2,1)S(1)}, bf16[32,1024]{1,0:T(8,128)(2,1)S(1)}, u32[]{:S(2)}, u32[]{:S(2)}) %collective-permute-start.10) | collective-permute-done | bytes 65568 | tf_op jit(solution)/shard_map/ppermute | solution.py:63
  41.0 2.2 %collective-permute-start.13 = (bf16[64,1152]{1,0:T(8,128)(2,1)S(1)}, bf16[64,1152]{1,0:T(8,128)(2,1)S(1)}, u32[]{:S(2)}, u32[]{:S(2)}) collective-permute-start(bf16[64,1152]{1,0:T(8,128)(2,1)S(1)} %get-tuple-element.88), channel_id=1, source_target_pairs={{0,8},{2,10},{4,12},{6,14},{8,0},{10,2},{12,4},{14,6},{1,9},{3,11}... | collective-permute-start | bytes 442376 | tf_op jit(solution)/shard_map/ppermute | solution.py:63
  43.2 2.0 %collective-permute-start.12 = (bf16[64,1152]{1,0:T(8,128)(2,1)S(1)}, bf16[64,1152]{1,0:T(8,128)(2,1)S(1)}, u32[]{:S(2)}, u32[]{:S(2)}) collective-permute-start(bf16[64,1152]{1,0:T(8,128)(2,1)S(1)} %get-tuple-element.87.refs_0_), channel_id=1, source_target_pairs={{0,12},{2,14},{4,8},{6,10},{8,4},{10,6},{12,0},{14,2},{1,13},{3,15... | collective-permute-start | bytes 442376 | tf_op jit(solution)/shard_map/ppermute | solution.py:63
  45.5 4.5 %collective-permute-done.15.rest_2_.refs_7_.refs_5_ = bf16[160,1024]{1,0:T(8,128)(2,1)S(1)} collective-permute-done((bf16[160,1024]{1,0:T(8,128)(2,1)S(1)}, bf16[160,1024]{1,0:T(8,128)(2,1)S(1)}, u32[]{:S(2)}, u32[]{:S(2)}) %collective-permute-start.15) | collective-permute-done | bytes 327712 | tf_op jit(solution)/shard_map/ppermute | solution.py:63
  50.1 1.1 %collective-permute-start.16 = (bf16[208,1024]{1,0:T(8,128)(2,1)S(1)}, bf16[208,1024]{1,0:T(8,128)(2,1)S(1)}, u32[]{:S(2)}, u32[]{:S(2)}) collective-permute-start(bf16[208,1024]{1,0:T(8,128)(2,1)S(1)} %shard_map.179), channel_id=1, source_target_pairs={{0,2},{2,0},{4,6},{6,4},{8,10},{10,8},{12,14},{14,12},{1,3},{3,1},... | collective-permute-start | bytes 1277960 | tf_op jit(solution)/shard_map/ppermute | solution.py:63
  51.2 1.5 %collective-permute-start.18 = (bf16[64,1024]{1,0:T(8,128)(2,1)S(1)}, bf16[64,1024]{1,0:T(8,128)(2,1)S(1)}, u32[]{:S(2)}, u32[]{:S(2)}) collective-permute-start(bf16[64,1024]{1,0:T(8,128)(2,1)S(1)} %get-tuple-element.97), channel_id=1, source_target_pairs={{0,12},{2,14},{4,8},{6,10},{8,4},{10,6},{12,0},{14,2},{1,13},{3,15... | collective-permute-start | bytes 393224 | tf_op jit(solution)/shard_map/ppermute | solution.py:63
  53.1 8.8 %collective-permute-done.13.rest_1_ = bf16[64,1152]{1,0:T(8,128)(2,1)S(1)} collective-permute-done((bf16[64,1152]{1,0:T(8,128)(2,1)S(1)}, bf16[64,1152]{1,0:T(8,128)(2,1)S(1)}, u32[]{:S(2)}, u32[]{:S(2)}) %collective-permute-start.13) | collective-permute-done | bytes 147488 | tf_op jit(solution)/shard_map/ppermute | solution.py:63
  62.0 1.5 %shard_map.180 = (bf16[2,32,1024]{2,1,0:T(8,128)(2,1)}, f32[8,128]{1,0:T(8,128)S(1)}) custom-call(f32[64,1152]{1,0:T(8,128)S(1)} %shard_map.178.refs_0_.refs_1_, bf16[128,64]{1,0:T(8,128)(2,1)S(1)} %get-tuple-element.53.refs_0_.refs_1_, bf16[1024,1024]{1,0:T(8,128)(2,1)S(1)} %copy-done, bf16[8,16,1024]{2,1,0:T(8,128)(2,1)S(1)} %get-tuple-element.84.slots_ref.refs_3_, ...), custom_call_target="tpu_custom_call" | custom-call | tf_op jit(solution)/shard_map/pallas_call | solution.py:46
  63.5 0.7 %shard_map.181 = (f32[64,1024]{1,0:T(8,128)}, f32[64,100]{1,0:T(8,128)}, f32[1]{0:T(128)}, f32[8,128]{1,0:T(8,128)S(1)}) custom-call(f32[8,128]{1,0:T(8,128)S(1)} %get-tuple-element.93.refs_0_, f32[64,1152]{1,0:T(8,128)S(1)} %shard_map.178.refs_0_.refs_1_, bf16[208,1024]{1,0:T(8,128)(2,1)S(1)} %collective-permute-done.16.refs_4_.refs_2_), custom_call_target="tpu_custom_call" | custom-call | tf_op jit(solution)/shard_map/pallas_call | solution.py:46
  64.3 4.1 %collective-permute-done.19.refs_4_ = bf16[64,1024]{1,0:T(8,128)(2,1)S(1)} collective-permute-done((bf16[64,1024]{1,0:T(8,128)(2,1)S(1)}, bf16[64,1024]{1,0:T(8,128)(2,1)S(1)}, u32[]{:S(2)}, u32[]{:S(2)}) %collective-permute-start.19) | collective-permute-done | bytes 131104 | tf_op jit(solution)/shard_map/ppermute | solution.py:63
  68.4 0.8 %shard_map.183 = f32[64,1024]{1,0:T(8,128)} custom-call(f32[8,128]{1,0:T(8,128)S(1)} %get-tuple-element.95.refs_0_, f32[256,1024]{1,0:T(8,128)S(1)} %get-tuple-element.96.refs_1_, bf16[208,1024]{1,0:T(8,128)(2,1)S(1)} %collective-permute-done.16.refs_4_.refs_2_, bf16[64,1024]{1,0:T(8,128)(2,1)S(1)} %collective-permute-done.18.refs_3_, ...), custom_call_target="tpu_custom_call" | custom-call | flops 5000000000 | tf_op jit(solution)/shard_map/pallas_call | solution.py:46
  (34 shorter events, 3.3 us)
Async XLA Ops:
  1.8 6.5 %collective-permute-start = (bf16[4,16,1024]{2,1,0:T(8,128)(2,1)S(1)}, bf16[4,16,1024]{2,1,0:T(8,128)(2,1)S(1)}, u32[]{:S(2)}, u32[]{:S(2)}) collective-permute-start(bf16[4,16,1024]{2,1,0:T(8,128)(2,1)S(1)} %get-tuple-element.62), channel_id=1, source_target_pairs={{0,2},{2,0},{4,6},{6,4},{8,10},{10,8},{12,14},{14,12},{1,3},{3,1},... | collective-permute-start | bytes 393224 | tf_op jit(solution)/shard_map/ppermute | solution.py:63
  8.3 6.6 %collective-permute-start.1 = (bf16[32,1024]{1,0:T(8,128)(2,1)S(1)}, bf16[32,1024]{1,0:T(8,128)(2,1)S(1)}, u32[]{:S(2)}, u32[]{:S(2)}) collective-permute-start(bf16[32,1024]{1,0:T(8,128)(2,1)S(1)} %get-tuple-element.63), channel_id=1, source_target_pairs={{0,12},{2,14},{4,8},{6,10},{8,4},{10,6},{12,0},{14,2},{1,13},{3,15... | collective-permute-start | bytes 196616 | tf_op jit(solution)/shard_map/ppermute | solution.py:63
  12.2 5.4 %collective-permute-start.2 = (bf16[32,1024]{1,0:T(8,128)(2,1)S(1)}, bf16[32,1024]{1,0:T(8,128)(2,1)S(1)}, u32[]{:S(2)}, u32[]{:S(2)}) collective-permute-start(bf16[32,1024]{1,0:T(8,128)(2,1)S(1)} %get-tuple-element.64), channel_id=1, source_target_pairs={{0,8},{2,10},{4,12},{6,14},{8,0},{10,2},{12,4},{14,6},{1,9},{3,11}... | collective-permute-start | bytes 196616 | tf_op jit(solution)/shard_map/ppermute | solution.py:63
  12.2 5.4 %collective-permute-start.3 = (bf16[32,1024]{1,0:T(8,128)(2,1)S(1)}, bf16[32,1024]{1,0:T(8,128)(2,1)S(1)}, u32[]{:S(2)}, u32[]{:S(2)}) collective-permute-start(bf16[32,1024]{1,0:T(8,128)(2,1)S(1)} %get-tuple-element.65), channel_id=1, source_target_pairs={{0,4},{2,6},{4,0},{6,2},{8,12},{10,14},{12,8},{14,10},{1,5},{3,7},... | collective-permute-start | bytes 196616 | tf_op jit(solution)/shard_map/ppermute | solution.py:63
  21.1 1.6 %copy-start.1 = (f32[100,256]{1,0:T(8,128)S(1)}, f32[100,256]{1,0:T(8,128)}, u32[]{:S(2)}) copy-start(f32[100,256]{1,0:T(8,128)} %truth_ref.1) | copy-start | bytes 307204
  21.1 1.6 %copy-start.2 = (f32[256]{0:T(256)S(1)}, f32[256]{0:T(256)}, u32[]{:S(2)}) copy-start(f32[256]{0:T(256)} %cell_ref.1) | copy-start | bytes 3076
  21.1 1.6 %collective-permute-start.4 = (bf16[2,100,256]{2,1,0:T(8,128)(2,1)S(1)}, bf16[2,100,256]{2,1,0:T(8,128)(2,1)S(1)}, u32[]{:S(2)}, u32[]{:S(2)}) collective-permute-start(bf16[2,100,256]{2,1,0:T(8,128)(2,1)S(1)} %get-tuple-element.67), channel_id=1, source_target_pairs={{0,1},{1,0},{2,3},{3,2},{4,5},{5,4},{6,7},{7,6},{8,9},{9,8},{10,11... | collective-permute-start | bytes 307208 | tf_op jit(solution)/shard_map/ppermute | solution.py:63
  22.1 7.5 %collective-permute-start.6 = (bf16[2,4,64,128]{3,2,1,0:T(8,128)(2,1)S(1)}, bf16[2,4,64,128]{3,2,1,0:T(8,128)(2,1)S(1)}, u32[]{:S(2)}, u32[]{:S(2)}) collective-permute-start(bf16[2,4,64,128]{3,2,1,0:T(8,128)(2,1)S(1)} %get-tuple-element.79), channel_id=1, source_target_pairs={{0,1},{1,0},{2,3},{3,2},{4,5},{5,4},{6,7},{7,6},{8,9},{9,8},{10,11... | collective-permute-start | bytes 393224 | tf_op jit(solution)/shard_map/ppermute | solution.py:63
  24.2 3.1 %collective-permute-start.5 = (bf16[256,1152]{1,0:T(8,128)(2,1)S(1)}, bf16[256,1152]{1,0:T(8,128)(2,1)S(1)}, u32[]{:S(2)}, u32[]{:S(2)}) collective-permute-start(bf16[256,1152]{1,0:T(8,128)(2,1)S(1)} %get-tuple-element.77), channel_id=1, source_target_pairs={{0,1},{1,0},{2,3},{3,2},{4,5},{5,4},{6,7},{7,6},{8,9},{9,8},{10,11... | collective-permute-start | bytes 1769480 | tf_op jit(solution)/shard_map/ppermute | solution.py:63
  24.3 2.8 %collective-permute-start.7 = (bf16[256,1152]{1,0:T(8,128)(2,1)S(1)}, bf16[256,1152]{1,0:T(8,128)(2,1)S(1)}, u32[]{:S(2)}, u32[]{:S(2)}) collective-permute-start(bf16[256,1152]{1,0:T(8,128)(2,1)S(1)} %get-tuple-element.81), channel_id=1, source_target_pairs={{0,1},{1,0},{2,3},{3,2},{4,5},{5,4},{6,7},{7,6},{8,9},{9,8},{10,11... | collective-permute-start | bytes 1769480 | tf_op jit(solution)/shard_map/ppermute | solution.py:63
  27.5 9.8 %collective-permute-start.9 = (bf16[160,1024]{1,0:T(8,128)(2,1)S(1)}, bf16[160,1024]{1,0:T(8,128)(2,1)S(1)}, u32[]{:S(2)}, u32[]{:S(2)}) collective-permute-start(bf16[160,1024]{1,0:T(8,128)(2,1)S(1)} %shard_map.172.refs_0_), channel_id=1, source_target_pairs={{0,4},{2,6},{4,0},{6,2},{8,12},{10,14},{12,8},{14,10},{1,5},{3,7},... | collective-permute-start | bytes 983048 | tf_op jit(solution)/shard_map/ppermute | solution.py:63
  30.1 4.5 %collective-permute-start.8 = (bf16[8,16,1024]{2,1,0:T(8,128)(2,1)S(1)}, bf16[8,16,1024]{2,1,0:T(8,128)(2,1)S(1)}, u32[]{:S(2)}, u32[]{:S(2)}) collective-permute-start(bf16[8,16,1024]{2,1,0:T(8,128)(2,1)S(1)} %get-tuple-element.84.slots_ref.refs_3_), channel_id=1, source_target_pairs={{0,1},{1,0},{2,3},{3,2},{4,5},{5,4},{6,7},{7,6},{8,9},{9,8},{10,11... | collective-permute-start | bytes 786440 | tf_op jit(solution)/shard_map/ppermute | solution.py:63
  30.2 10.7 %collective-permute-start.11 = (bf16[128,1152]{1,0:T(8,128)(2,1)S(1)}, bf16[128,1152]{1,0:T(8,128)(2,1)S(1)}, u32[]{:S(2)}, u32[]{:S(2)}) collective-permute-start(bf16[128,1152]{1,0:T(8,128)(2,1)S(1)} %shard_map.171.refs_0_), channel_id=1, source_target_pairs={{0,2},{2,0},{4,6},{6,4},{8,10},{10,8},{12,14},{14,12},{1,3},{3,1},... | collective-permute-start | bytes 884744 | tf_op jit(solution)/shard_map/ppermute | solution.py:63
  31.7 9.1 %collective-permute-start.10 = (bf16[32,1024]{1,0:T(8,128)(2,1)S(1)}, bf16[32,1024]{1,0:T(8,128)(2,1)S(1)}, u32[]{:S(2)}, u32[]{:S(2)}) collective-permute-start(bf16[32,1024]{1,0:T(8,128)(2,1)S(1)} %get-tuple-element.86), channel_id=1, source_target_pairs={{0,12},{2,14},{4,8},{6,10},{8,4},{10,6},{12,0},{14,2},{1,13},{3,15... | collective-permute-start | bytes 196616 | tf_op jit(solution)/shard_map/ppermute | solution.py:63
  35.3 14.7 %collective-permute-start.15 = (bf16[160,1024]{1,0:T(8,128)(2,1)S(1)}, bf16[160,1024]{1,0:T(8,128)(2,1)S(1)}, u32[]{:S(2)}, u32[]{:S(2)}) collective-permute-start(bf16[160,1024]{1,0:T(8,128)(2,1)S(1)} %get-tuple-element.91), channel_id=1, source_target_pairs={{0,4},{2,6},{4,0},{6,2},{8,12},{10,14},{12,8},{14,10},{1,5},{3,7},... | collective-permute-start | bytes 983048 | tf_op jit(solution)/shard_map/ppermute | solution.py:63
  35.4 10.1 %collective-permute-start.14 = (bf16[32,1024]{1,0:T(8,128)(2,1)S(1)}, bf16[32,1024]{1,0:T(8,128)(2,1)S(1)}, u32[]{:S(2)}, u32[]{:S(2)}) collective-permute-start(bf16[32,1024]{1,0:T(8,128)(2,1)S(1)} %get-tuple-element.90), channel_id=1, source_target_pairs={{0,8},{2,10},{4,12},{6,14},{8,0},{10,2},{12,4},{14,6},{1,9},{3,11}... | collective-permute-start | bytes 196616 | tf_op jit(solution)/shard_map/ppermute | solution.py:63
  37.3 13.9 %collective-permute-start.17 = (bf16[128,1024]{1,0:T(8,128)(2,1)S(1)}, bf16[128,1024]{1,0:T(8,128)(2,1)S(1)}, u32[]{:S(2)}, u32[]{:S(2)}) collective-permute-start(bf16[128,1024]{1,0:T(8,128)(2,1)S(1)} %get-tuple-element.85.refs_0_), channel_id=1, source_target_pairs={{0,2},{2,0},{4,6},{6,4},{8,10},{10,8},{12,14},{14,12},{1,3},{3,1},... | collective-permute-start | bytes 786440 | tf_op jit(solution)/shard_map/ppermute | solution.py:63
  41.0 20.8 %collective-permute-start.13 = (bf16[64,1152]{1,0:T(8,128)(2,1)S(1)}, bf16[64,1152]{1,0:T(8,128)(2,1)S(1)}, u32[]{:S(2)}, u32[]{:S(2)}) collective-permute-start(bf16[64,1152]{1,0:T(8,128)(2,1)S(1)} %get-tuple-element.88), channel_id=1, source_target_pairs={{0,8},{2,10},{4,12},{6,14},{8,0},{10,2},{12,4},{14,6},{1,9},{3,11}... | collective-permute-start | bytes 442376 | tf_op jit(solution)/shard_map/ppermute | solution.py:63
  43.2 18.7 %collective-permute-start.12 = (bf16[64,1152]{1,0:T(8,128)(2,1)S(1)}, bf16[64,1152]{1,0:T(8,128)(2,1)S(1)}, u32[]{:S(2)}, u32[]{:S(2)}) collective-permute-start(bf16[64,1152]{1,0:T(8,128)(2,1)S(1)} %get-tuple-element.87.refs_0_), channel_id=1, source_target_pairs={{0,12},{2,14},{4,8},{6,10},{8,4},{10,6},{12,0},{14,2},{1,13},{3,15... | collective-permute-start | bytes 442376 | tf_op jit(solution)/shard_map/ppermute | solution.py:63
  50.1 11.9 %collective-permute-start.16 = (bf16[208,1024]{1,0:T(8,128)(2,1)S(1)}, bf16[208,1024]{1,0:T(8,128)(2,1)S(1)}, u32[]{:S(2)}, u32[]{:S(2)}) collective-permute-start(bf16[208,1024]{1,0:T(8,128)(2,1)S(1)} %shard_map.179), channel_id=1, source_target_pairs={{0,2},{2,0},{4,6},{6,4},{8,10},{10,8},{12,14},{14,12},{1,3},{3,1},... | collective-permute-start | bytes 1277960 | tf_op jit(solution)/shard_map/ppermute | solution.py:63
  51.2 13.1 %collective-permute-start.18 = (bf16[64,1024]{1,0:T(8,128)(2,1)S(1)}, bf16[64,1024]{1,0:T(8,128)(2,1)S(1)}, u32[]{:S(2)}, u32[]{:S(2)}) collective-permute-start(bf16[64,1024]{1,0:T(8,128)(2,1)S(1)} %get-tuple-element.97), channel_id=1, source_target_pairs={{0,12},{2,14},{4,8},{6,10},{8,4},{10,6},{12,0},{14,2},{1,13},{3,15... | collective-permute-start | bytes 393224 | tf_op jit(solution)/shard_map/ppermute | solution.py:63
  52.8 9.2 %copy-start = (bf16[1024,1024]{1,0:T(8,128)(2,1)S(1)}, bf16[1024,1024]{1,0:T(8,128)(2,1)}, u32[]{:S(2)}) copy-start(bf16[1024,1024]{1,0:T(8,128)(2,1)} %refs_2_.3) | copy-start | bytes 6291460
  52.8 15.6 %collective-permute-start.19 = (bf16[64,1024]{1,0:T(8,128)(2,1)S(1)}, bf16[64,1024]{1,0:T(8,128)(2,1)S(1)}, u32[]{:S(2)}, u32[]{:S(2)}) collective-permute-start(bf16[64,1024]{1,0:T(8,128)(2,1)S(1)} %get-tuple-element.98), channel_id=1, source_target_pairs={{0,8},{2,10},{4,12},{6,14},{8,0},{10,2},{12,4},{14,6},{1,9},{3,11}... | collective-permute-start | bytes 393224 | tf_op jit(solution)/shard_map/ppermute | solution.py:63

commit v5 on v4

--- a/solution.py
+++ b/solution.py
@@ -12,14 +12,7 @@
 tile = 256
 lanes = 128
 packed = 16
-cost_hints = {
-    "partial_kernel": 4,
-    "hidden_early_kernel": 3,
-    "local_kernel": 8,
-    "message_sum_kernel": 5,
-    "slot_kernel": 5,
-    "message_early_kernel": 5,
-}
+cost_hints = {"partial_kernel": 8, "hidden_early_kernel": 6}
 f32 = jnp.float32
 bf16 = jnp.bfloat16
 
@@ -183,6 +176,11 @@
         sent_ref[member] = field.astype(bf16)
 
 
+def halving_place(step, levels):
+    bits = levels.bit_length() - 1
+    return sum((1 - ((step >> bit) & 1)) << (bits - 1 - bit) for bit in range(bits))
+
+
 def turn_kernel(normed_ref, active_ref, own_ref, near_ref, *rest):
     far_refs, (normed_t_ref, active_t_ref, keep_ref, give_ref) = rest[:-4], rest[-4:]
     _, _, levels, block, _ = normed_t_ref.shape
@@ -201,10 +199,11 @@
                 if target is not None:
                     target[side, 1 - far, levels - 1 - step] = value
                     continue
+                spot = halving_place(step, levels)
                 for which, part_ref in enumerate((keep_ref, give_ref)):
                     @pl.when(side == which)
                     def _(part_ref=part_ref):
-                        part_ref[1 - far, levels - 1 - step] = value
+                        part_ref[1 - far, spot] = value
 
 
 def split_loss(part, variables):
@@ -323,10 +322,9 @@
             pack(out_ref, at + block, part.astype(bf16))
 
 
-def message_kernel(keep_ref, give_ref, slots_ref, other_ref, first_ref, own_ref, near_ref, *out_refs):
+def message_kernel(keep_ref, give_ref, slots_ref, other_ref, first_ref, second_ref, near_ref):
     depth, width = keep_ref.shape[-1], near_ref.shape[1]
-    rows = slots_ref.shape[1]
-    count, block = first_ref.shape[0], own_ref.shape[0]
+    count = first_ref.shape[0]
     for half in range(2):
         own = keep_ref[half].reshape(-1, depth)
         other = give_ref[half].reshape(-1, depth)
@@ -337,16 +335,31 @@
             total = mm(own, here, 1, 0) + mm(other, there, 1, 0)
             if half == 0:
                 first_ref[:, columns] = total[:count].astype(bf16)
-                own_ref[:, columns] = total[total.shape[0] - block :]
+                second_ref[:, columns] = total[count:].astype(bf16)
             else:
                 near_ref[:, columns] = total
-            for i, out_ref in enumerate(out_refs):
-                at = (1 - half) * block
-                out_ref[at : at + block, columns] = total[count + i * block : count + (i + 1) * block].astype(bf16)
-    for i, out_ref in enumerate(out_refs):
-        step = len(out_refs) - i
-        out_ref[2 * block : 2 * block + rows, :] = slots_ref[2 * step]
-        out_ref[2 * block + rows :, :] = slots_ref[2 * step + 1]
+
+
+def second_kernel(source_ref, out_ref):
+    out_ref[...] = source_ref[...]
+
+
+def step_kernel(near_ref, arrived_ref, slots_ref, out_ref):
+    rows = slots_ref.shape[1]
+    count = arrived_ref.shape[0]
+    out_ref[0:count, :] = (near_ref[0:count, :] + arrived_ref[...].astype(f32)).astype(bf16)
+    out_ref[count : count + rows, :] = slots_ref[2]
+    out_ref[count + rows :, :] = slots_ref[3]
+
+
+def halve_kernel(begin, near_ref, *rest):
+    arrived_refs, (send_ref, keep_ref) = rest[:-2], rest[-2:]
+    count = send_ref.shape[0]
+    for at, out_ref in ((0, send_ref), (count, keep_ref)):
+        total = near_ref[begin + at : begin + at + count, :]
+        for r in arrived_refs:
+            total = total + r[at : at + count, :].astype(f32)
+        out_ref[...] = total.astype(out_ref.dtype)
 
 
 def own_kernel(variables, width, held_ref, other_ref, *rest):
@@ -361,21 +374,16 @@
     out_ref[:, width:] = split_loss(part, variables)
 
 
-def last_kernel(early, hidden_ref, own_ref, slots_ref, *rest):
+def last_kernel(hidden_ref, slots_ref, *rest):
     arrived_refs, out_ref = rest[:-1], rest[-1]
     rows, width = slots_ref.shape[1:]
-    block = own_ref.shape[0]
+    block = hidden_ref.shape[0]
     out_ref[0:block, :] = hidden_ref[:, :width].astype(bf16)
     out_ref[block : block + packed, :] = jnp.zeros((packed, width), bf16)
     pack(out_ref, block, hidden_ref[:, width:].astype(bf16))
-    total = own_ref[...]
-    for r in arrived_refs[early:]:
-        total = total + r[block : 2 * block, :].astype(f32)
-    at = 2 * block + packed
-    out_ref[block + packed : at, :] = total.astype(bf16)
-    for i, r in enumerate(arrived_refs):
-        begin = rows if i < early else 2 * block + rows
-        out_ref[at : at + rows, :] = r[begin : begin + rows, :]
+    at = block + packed
+    for r in arrived_refs:
+        out_ref[at : at + rows, :] = r[r.shape[0] - rows :, :]
         at += rows
     out_ref[at:, :] = slots_ref[1]
 
@@ -388,13 +396,6 @@
         out_ref[:, :width] = (total + arrived_ref[here, :width].astype(f32)).astype(bf16)
         part = split_loss(part + arrived_ref[here, width:].astype(f32), variables)
         out_ref[:, width:] = part.astype(bf16)
-
-
-def message_early_kernel(near_ref, arrived_ref, *out_refs):
-    block = out_refs[0].shape[0]
-    for i, out_ref in enumerate(out_refs):
-        here = slice(i * block, (i + 1) * block)
-        out_ref[...] = (near_ref[here, :] + arrived_ref[here, :].astype(f32)).astype(bf16)
 
 
 def back_kernel(inner_ref, w_hidden_ref, gain_ref, unit_ref, inverse_ref, grad_ref, scaled_ref):
@@ -430,7 +431,7 @@
         send_ref[each:, :] = slots_ref[2 * step + 1]
 
 
-def owner_kernel(early, block, pick_ref, w_msg_ref, slots_ref, last_ref, *rest):
+def owner_kernel(pick_ref, w_msg_ref, slots_ref, last_ref, *rest):
     arrived_refs, (grad_ref, token_ref, held_ref) = rest[:-3], rest[-3:]
     token_ref[...] = jnp.zeros_like(token_ref)
     peers, rows, width = slots_ref.shape
@@ -441,7 +442,7 @@
         if i == levels - 1:
             held_ref[spot] = slots_ref[0]
         else:
-            at = 0 if i < early else 2 * block
+            at = arrived_refs[i].shape[0] - 2 * rows
             held_ref[spot] = arrived_refs[i][at : at + rows, :]
         held_ref[spot + 1] = last_ref[begin + i * rows : begin + (i + 1) * rows, :]
     nodes = mm(pick_ref[...], held_ref[...].reshape(peers * rows, width), 0, 0).astype(bf16)
@@ -475,14 +476,8 @@
     loss_ref[0] = jnp.sum(jnp.where(spots & first, part[:8], 0.0)) * scale
 
 
-def message_sum_kernel(near_ref, last_ref, *rest):
-    out_ref = rest[-1]
-    block = out_ref.shape[0]
-    total = near_ref[near_ref.shape[0] - block :, :]
-    total = total + last_ref[block + packed : 2 * block + packed, :].astype(f32)
-    for r in rest[:-1]:
-        total = total + r[0:block, :].astype(f32)
-    out_ref[...] = total
+def message_sum_kernel(keep_ref, arrived_ref, out_ref):
+    out_ref[...] = keep_ref[...] + arrived_ref[...].astype(f32)
 
 
 def on_device(
@@ -615,23 +610,20 @@
     )
     slots, *slots_sent = call(
         slot_kernel,
-        [((peers, rows_peer, width), bf16)] + [((2 * rows_peer, width), bf16)] * early,
+        [((peers, rows_peer, width), bf16)] + [((2 * rows_peer, width), bf16)] * (levels - 2),
         [share, grad_hidden],
         limit=6,
         after=[received_other],
     )
     slots_other = swap(slots, "member", cores, 1)
-    slots_arrived = spread(slots_sent, steps[:early])
-    message_first, message_own, message_near, *message_across = call(
+    slots_arrived = spread(slots_sent, steps[:-1])
+    message_first, message_second, message_near = call(
         message_kernel,
-        [((count, width), bf16), ((block, width), f32), ((half, width), f32)]
-        + [((2 * block + 2 * rows_peer, width), bf16)] * (levels - 1 - early),
+        [((half // 2, width), bf16)] * 2 + [((half, width), f32)],
         [received_keep, received_other, slots, slots_other],
         limit=10,
     )
     message_first_other = swap(message_first, "space", peers, 1)
-    message_across_parts = spread(message_across, steps[early:])
-    slots_arrived += message_across_parts
     (hidden_own,) = call(
         functools.partial(own_kernel, variables, width),
         [((block, wide), f32)],
@@ -643,38 +635,62 @@
         [((block, wide), bf16)] * early,
         [held_near, near_other, first_other],
         limit=6,
-        after=[message_first, hidden_own, slots_arrived[0]],
+        after=[message_first, hidden_own] + slots_arrived,
     )
     hidden_parts = spread(hidden_early, steps[:early])
-    message_early = call(
-        message_early_kernel,
-        [((block, width), bf16)] * early,
-        [message_near, message_first_other],
-        limit=6,
+    (message_step,) = call(
+        step_kernel,
+        [((half // 2 + 2 * rows_peer, width), bf16)],
+        [message_near, message_first_other, slots],
+        limit=4,
         after=hidden_early[:1],
     )
-    message_parts = spread(message_early, steps[:early])
-    (last,) = call(
-        functools.partial(last_kernel, early),
-        [((2 * block + packed + levels * rows_peer, width), bf16)],
-        [hidden_own, message_own, slots] + slots_arrived,
-        limit=4,
-    )
-    last_other = swap(last, "space", peers, 1)
+    message_other = swap(message_step, "space", peers, 2)
+    (message_second,) = call(
+        second_kernel, [((half // 2, width), bf16)], [message_second], limit=4, after=[message_step]
+    )
+    message_second_other = swap(message_second, "space", peers, 1)
+    slots_arrived.append(message_other)
     (partial,) = call(
         functools.partial(partial_kernel, variables, width, early),
         [((block, wide), f32)],
         [held_near, near_other] + hidden_parts + across_parts,
         limit=4,
     )
+    (last,) = call(
+        last_kernel,
+        [((block + packed + levels * rows_peer, width), bf16)],
+        [hidden_own, slots] + slots_arrived,
+        limit=4,
+        after=[partial],
+    )
+    last_other = swap(last, "space", peers, 1)
+    message_send, message_keep = call(
+        functools.partial(halve_kernel, half // 2),
+        [((half // 4, width), bf16), ((half // 4, width), f32)],
+        [message_near, message_second_other, message_other],
+        limit=4,
+        after=[partial],
+    )
+    bit = 4
+    while bit < peers // 2:
+        message_other = swap(message_send, "space", peers, bit)
+        rows_left = message_send.shape[0] // 2
+        message_send, message_keep = call(
+            functools.partial(halve_kernel, 0),
+            [((rows_left, width), bf16), ((rows_left, width), f32)],
+            [message_keep, message_other],
+            limit=4,
+        )
+        bit *= 2
+    message_other = swap(message_send, "space", peers, bit)
     token = ((8, lanes), f32)
     latent_grad, latent_done = call(
-        functools.partial(owner_kernel, early, block),
+        owner_kernel,
         [(latents.shape, bf16), token],
         [pick, w_msg, slots, last_other] + slots_arrived,
         scratch=[pltpu.VMEM((peers, rows_peer, width), bf16)],
         limit=8,
-        after=[partial],
     )
     hidden_weight_grad, out_weight_grad, loss, hidden_done = call(
         functools.partial(hidden_sum_kernel, variables, 1.0 / (points * peers * variables)),
@@ -687,7 +703,7 @@
     (msg_weight_grad,) = call(
         message_sum_kernel,
         [((block, width), f32)],
-        [message_near, last_other] + message_parts + message_across_parts,
+        [message_keep, message_other],
         limit=6,
         after=[hidden_done],
     )

time: 69.4 us -> 70.1 us (1.010)
  waiting for transfers between devices: 25.9 us -> 31.9 us
  starting transfers between devices: 24.5 us -> 19.1 us
    ppermute x20, waiting for transfers between devices: 25.9 us -> 31.9 us  [swap(): return lax.ppermute(value, axis, [(i, i ^ step) for i in range(size)])]
    ppermute x20, starting transfers between devices: 24.5 us -> 19.1 us  [swap(): return lax.ppermute(value, axis, [(i, i ^ step) for i in range(size)])]
    pallas_call x20 -> x22, Pallas kernels: 17.9 us -> 18 us  [call(): pl.pallas_call(inner if count else body, out_shape=[jax.ShapeDtypeStruct(...]
  transfers between devices with their start and end apart: 20 -> 20, of which waited for: 10 -> 11; matrix products, arithmetic and copies ran while one was open for 0% -> 0% of each run, Pallas kernels for 18% -> 16%
where the time goes in v5:
time: 70.1 us; the launch traced here: 69.9 us
  waiting for transfers between devices  31.9 us (46%)
  starting transfers between devices  19.1 us (27%)
  Pallas kernels  18 us (26%)
  between operations  0.86 us (1%)
    ppermute x20, waiting for transfers between devices, swap(): return lax.ppermute(value, axis, [(i, i ^ step) for i in range(size)])  31.9 us
    ppermute x20, starting transfers between devices, swap(): return lax.ppermute(value, axis, [(i, i ^ step) for i in range(size)])  19.1 us
    pallas_call x22, Pallas kernels, call(): pl.pallas_call(inner if count else body, out_shape=[jax.ShapeDtypeStruct(...  18 us
  transfers between devices with their start and end apart: 20, of which 11 were waited for; matrix products, arithmetic and copies ran while one was open for 0% of the time, Pallas kernels for 16%

profile of v5, /device:TPU:0, one launch (start us, length us, event | category | flops | bytes accessed | tf_op | source)
XLA Modules:
  0.0 69.9 jit_solution(4677934006228249702)
XLA Ops:
  0.6 1.1 %shard_map.164 = (bf16[128,64]{1,0:T(8,128)(2,1)S(1)}, bf16[4,16,1024]{2,1,0:T(8,128)(2,1)S(1)}, bf16[4,16,1024]{2,1,0:T(8,128)(2,1)S(1)}) custom-call(s32[1,8,8]{2,1,0:T(8,128)} %lists_ref.1, bf16[2,32,1024]{2,1,0:T(8,128)(2,1)} %latents_ref.1), custom_call_target="tpu_custom_call" | custom-call | tf_op jit(solution)/shard_map/pallas_call | solution.py:39
  1.8 3.0 %collective-permute-start = (bf16[4,16,1024]{2,1,0:T(8,128)(2,1)S(1)}, bf16[4,16,1024]{2,1,0:T(8,128)(2,1)S(1)}, u32[]{:S(2)}, u32[]{:S(2)}) collective-permute-start(bf16[4,16,1024]{2,1,0:T(8,128)(2,1)S(1)} %get-tuple-element.61), channel_id=1, source_target_pairs={{0,2},{2,0},{4,6},{6,4},{8,10},{10,8},{12,14},{14,12},{1,3},{3,1},... | collective-permute-start | bytes 393224 | tf_op jit(solution)/shard_map/ppermute | solution.py:56
  4.8 2.6 %shard_map.165 = (bf16[256,512]{1,0:T(8,128)(2,1)S(1)}, bf16[1024,1024]{1,0:T(8,128)(2,1)S(1)}, f32[1024]{0:T(1024)S(1)}, bf16[256,1024]{1,0:T(8,128)(2,1)S(1)},...) custom-call(bf16[128,64]{1,0:T(8,128)(2,1)S(1)} %get-tuple-element.52.refs_0_.pick_ref, ...), custom_call_target="tpu_custom_call" | custom-call | tf_op jit(solution)/shard_map/pallas_call | solution.py:39
  7.4 0.9 %collective-permute-done.refs_2_.near_ref = bf16[4,16,1024]{2,1,0:T(8,128)(2,1)S(1)} collective-permute-done((bf16[4,16,1024]{2,1,0:T(8,128)(2,1)S(1)}, bf16[4,16,1024]{2,1,0:T(8,128)(2,1)S(1)}, u32[]{:S(2)}, u32[]{:S(2)}) %collective-permute-start) | collective-permute-done | bytes 131104 | tf_op jit(solution)/shard_map/ppermute | solution.py:56
  8.3 3.9 %collective-permute-start.1 = (bf16[32,1024]{1,0:T(8,128)(2,1)S(1)}, bf16[32,1024]{1,0:T(8,128)(2,1)S(1)}, u32[]{:S(2)}, u32[]{:S(2)}) collective-permute-start(bf16[32,1024]{1,0:T(8,128)(2,1)S(1)} %get-tuple-element.62), channel_id=1, source_target_pairs={{0,12},{2,14},{4,8},{6,10},{8,4},{10,6},{12,0},{14,2},{1,13},{3,15... | collective-permute-start | bytes 196616 | tf_op jit(solution)/shard_map/ppermute | solution.py:56
  12.2 0.6 collective-permute-start.3
  12.8 2.0 %collective-permute-done.1.rest_0_ = bf16[32,1024]{1,0:T(8,128)(2,1)S(1)} collective-permute-done((bf16[32,1024]{1,0:T(8,128)(2,1)S(1)}, bf16[32,1024]{1,0:T(8,128)(2,1)S(1)}, u32[]{:S(2)}, u32[]{:S(2)}) %collective-permute-start.1) | collective-permute-done | bytes 65568 | tf_op jit(solution)/shard_map/ppermute | solution.py:56
  14.9 2.7 %collective-permute-done.2.rest_1_ = bf16[32,1024]{1,0:T(8,128)(2,1)S(1)} collective-permute-done((bf16[32,1024]{1,0:T(8,128)(2,1)S(1)}, bf16[32,1024]{1,0:T(8,128)(2,1)S(1)}, u32[]{:S(2)}, u32[]{:S(2)}) %collective-permute-start.2) | collective-permute-done | bytes 65568 | tf_op jit(solution)/shard_map/ppermute | solution.py:56
  17.6 3.5 %shard_map.167 = (f32[2,100,256]{2,1,0:T(8,128)S(1)}, bf16[2,100,256]{2,1,0:T(8,128)(2,1)S(1)}, bf16[512,1024]{1,0:T(8,128)(2,1)S(1)}, bf16[512,1024]{1,0:T(8,12...) custom-call(bf16[1024,1024]{1,0:T(8,128)(2,1)S(1)} %get-tuple-element.53.w_msg_ref, ...), custom_call_target="tpu_custom_call" | custom-call | tf_op jit(solution)/shard_map/pallas_call | solution.py:39
  21.2 0.9 %shard_map.168 = (bf16[2,2,4,64,512]{4,3,2,1,0:T(8,128)(2,1)S(1)}, bf16[2,2,4,64,512]{4,3,2,1,0:T(8,128)(2,1)S(1)}, bf16[2,4,64,128]{3,2,1,0:T(8,128)(2,1)S(1)}, bf16[2,4,64,128]{3,2,1,0:T(8,128)(2,1)S(1)}) custom-call(bf16[512,1024]{1,0:T(8,128)(2,1)S(1)} %get-tuple-element.65.normed_ref, bf16[512,1024]{1,0:T(8,128)(2,1)S(1)} %get-tuple-element.66.active_ref, ...), custom_call_target="tpu_custom_call" | custom-call | tf_op jit(solution)/shard_map/pallas_call | solution.py:39
  22.5 1.5 %shard_map.169 = (bf16[512,1024]{1,0:T(8,128)(2,1)S(1)}, bf16[128,512]{1,0:T(8,128)(2,1)S(1)}, f32[1]{0:T(128)}, bf16[256,1152]{1,0:T(8,128)(2,1)S(1)}, bf16[256,1152]{1,0:T(8,128)(2,1)S(1)}) custom-call(f32[2,100,256]{2,1,0:T(8,128)S(1)} %get-tuple-element.68.own_ref, bf16[2,100,256]{2,1,0:T(8,128)(2,1)S(1)} %collective-permute-done.5.other_ref, ...), custom_call_target="tpu_custom_call" | custom-call | tf_op jit(solution)/shard_map/pallas_call | solution.py:39
  24.7 1.6 %shard_map.170 = (f32[256,1152]{1,0:T(8,128)S(1)}, f32[256,1152]{1,0:T(8,128)S(1)}) custom-call(f32[1]{0:T(128)} %get-tuple-element.73.loss_ref, bf16[2,2,4,64,512]{4,3,2,1,0:T(8,128)(2,1)S(1)} %get-tuple-element.71.normed_t_ref, bf16[2,2,4,64,512]{4,3,2,1,0:T(8,128)(2,1)S(1)} %get-tuple-element.72.active_t_ref, ...), custom_call_target="tpu_custom_call" | custom-call | tf_op jit(solution)/shard_map/pallas_call | solution.py:39
  27.1 0.5 collective-permute-start.9
  27.6 1.5 %collective-permute-start.12 = (bf16[128,1152]{1,0:T(8,128)(2,1)S(1)}, bf16[128,1152]{1,0:T(8,128)(2,1)S(1)}, u32[]{:S(2)}, u32[]{:S(2)}) collective-permute-start(bf16[128,1152]{1,0:T(8,128)(2,1)S(1)} %shard_map.171.refs_0_), channel_id=1, source_target_pairs={{0,2},{2,0},{4,6},{6,4},{8,10},{10,8},{12,14},{14,12},{1,3},{3,1},... | collective-permute-start | bytes 884744 | tf_op jit(solution)/shard_map/ppermute | solution.py:56
  29.1 1.6 %shard_map.173.refs_2_ = bf16[512,1024]{1,0:T(8,128)(2,1)S(1)} custom-call(bf16[160,1024]{1,0:T(8,128)(2,1)S(1)} %shard_map.172.refs_0_, bf16[512,1024]{1,0:T(8,128)(2,1)S(1)} %get-tuple-element.74.inner_ref.refs_1_, bf16[1024,1024]{1,0:T(8,128)(2,1)S(1)} %get-tuple-element.57.weights_ref.refs_2_, f32[1024]{0:T(1024)S(1)} %get-tuple-element.55.gain_ref.refs_3_, ...), custom_call_target="tpu_custom_call" | custom-call | tf_op jit(solution)/shard_map/pallas_call | solution.py:39
  30.7 0.4 shard_map.174
  31.3 2.9 %collective-permute-start.10 = (bf16[32,1024]{1,0:T(8,128)(2,1)S(1)}, bf16[32,1024]{1,0:T(8,128)(2,1)S(1)}, u32[]{:S(2)}, u32[]{:S(2)}) collective-permute-start(bf16[32,1024]{1,0:T(8,128)(2,1)S(1)} %get-tuple-element.85), channel_id=1, source_target_pairs={{0,12},{2,14},{4,8},{6,10},{8,4},{10,6},{12,0},{14,2},{1,13},{3,15... | collective-permute-start | bytes 196616 | tf_op jit(solution)/shard_map/ppermute | solution.py:56
  34.4 0.7 shard_map.175
  35.1 0.5 collective-permute-start.15
  35.6 1.3 %collective-permute-done.9.rest_0_.rest_2_ = bf16[160,1024]{1,0:T(8,128)(2,1)S(1)} collective-permute-done((bf16[160,1024]{1,0:T(8,128)(2,1)S(1)}, bf16[160,1024]{1,0:T(8,128)(2,1)S(1)}, u32[]{:S(2)}, u32[]{:S(2)}) %collective-permute-start.9) | collective-permute-done | bytes 327712 | tf_op jit(solution)/shard_map/ppermute | solution.py:56
  37.1 3.3 %collective-permute-done.10.refs_2_.refs_3_.rest_0_ = bf16[32,1024]{1,0:T(8,128)(2,1)S(1)} collective-permute-done((bf16[32,1024]{1,0:T(8,128)(2,1)S(1)}, bf16[32,1024]{1,0:T(8,128)(2,1)S(1)}, u32[]{:S(2)}, u32[]{:S(2)}) %collective-permute-start.10) | collective-permute-done | bytes 65568 | tf_op jit(solution)/shard_map/ppermute | solution.py:56
  40.4 1.4 %collective-permute-done.11.refs_3_.refs_4_.rest_1_ = bf16[32,1024]{1,0:T(8,128)(2,1)S(1)} collective-permute-done((bf16[32,1024]{1,0:T(8,128)(2,1)S(1)}, bf16[32,1024]{1,0:T(8,128)(2,1)S(1)}, u32[]{:S(2)}, u32[]{:S(2)}) %collective-permute-start.11) | collective-permute-done | bytes 65568 | tf_op jit(solution)/shard_map/ppermute | solution.py:56
  42.1 2.2 %collective-permute-start.13 = (bf16[64,1152]{1,0:T(8,128)(2,1)S(1)}, bf16[64,1152]{1,0:T(8,128)(2,1)S(1)}, u32[]{:S(2)}, u32[]{:S(2)}) collective-permute-start(bf16[64,1152]{1,0:T(8,128)(2,1)S(1)} %get-tuple-element.87.refs_0_), channel_id=1, source_target_pairs={{0,12},{2,14},{4,8},{6,10},{8,4},{10,6},{12,0},{14,2},{1,13},{3,15... | collective-permute-start | bytes 442376 | tf_op jit(solution)/shard_map/ppermute | solution.py:56
  44.4 1.4 %collective-permute-start.16 = (bf16[160,1024]{1,0:T(8,128)(2,1)S(1)}, bf16[160,1024]{1,0:T(8,128)(2,1)S(1)}, u32[]{:S(2)}, u32[]{:S(2)}) collective-permute-start(bf16[160,1024]{1,0:T(8,128)(2,1)S(1)} %shard_map.179.refs_0_), channel_id=1, source_target_pairs={{0,4},{2,6},{4,0},{6,2},{8,12},{10,14},{12,8},{14,10},{1,5},{3,7},... | collective-permute-start | bytes 983048 | tf_op jit(solution)/shard_map/ppermute | solution.py:56
  45.8 0.8 %collective-permute-start.18 = (bf16[128,1024]{1,0:T(8,128)(2,1)S(1)}, bf16[128,1024]{1,0:T(8,128)(2,1)S(1)}, u32[]{:S(2)}, u32[]{:S(2)}) collective-permute-start(bf16[128,1024]{1,0:T(8,128)(2,1)S(1)} %shard_map.183), channel_id=1, source_target_pairs={{0,2},{2,0},{4,6},{6,4},{8,10},{10,8},{12,14},{14,12},{1,3},{3,1},... | collective-permute-start | bytes 786440 | tf_op jit(solution)/shard_map/ppermute | solution.py:56
  46.6 7.2 %collective-permute-done.14.rest_1_ = bf16[64,1152]{1,0:T(8,128)(2,1)S(1)} collective-permute-done((bf16[64,1152]{1,0:T(8,128)(2,1)S(1)}, bf16[64,1152]{1,0:T(8,128)(2,1)S(1)}, u32[]{:S(2)}, u32[]{:S(2)}) %collective-permute-start.14) | collective-permute-done | bytes 147488 | tf_op jit(solution)/shard_map/ppermute | solution.py:56
  53.9 5.2 %collective-permute-done.16.refs_5_.rest_2_.refs_3_ = bf16[160,1024]{1,0:T(8,128)(2,1)S(1)} collective-permute-done((bf16[160,1024]{1,0:T(8,128)(2,1)S(1)}, bf16[160,1024]{1,0:T(8,128)(2,1)S(1)}, u32[]{:S(2)}, u32[]{:S(2)}) %collective-permute-start.16) | collective-permute-done | bytes 327712 | tf_op jit(solution)/shard_map/ppermute | solution.py:56
  59.3 0.5 collective-permute-start.19
  59.8 7.1 %collective-permute-done.17.last_ref.refs_2_ = bf16[144,1024]{1,0:T(8,128)(2,1)S(1)} collective-permute-done((bf16[144,1024]{1,0:T(8,128)(2,1)S(1)}, bf16[144,1024]{1,0:T(8,128)(2,1)S(1)}, u32[]{:S(2)}, u32[]{:S(2)}) %collective-permute-start.17) | collective-permute-done | bytes 294944 | tf_op jit(solution)/shard_map/ppermute | solution.py:56
  66.9 1.5 %shard_map.181 = (bf16[2,32,1024]{2,1,0:T(8,128)(2,1)}, f32[8,128]{1,0:T(8,128)S(1)}) custom-call(bf16[128,64]{1,0:T(8,128)(2,1)S(1)} %get-tuple-element.52.refs_0_.pick_ref, bf16[1024,1024]{1,0:T(8,128)(2,1)S(1)} %copy-done, bf16[8,16,1024]{2,1,0:T(8,128)(2,1)S(1)} %get-tuple-element.82.slots_ref.refs_3_.refs_2_, ...), custom_call_target="tpu_custom_call" | custom-call | tf_op jit(solution)/shard_map/pallas_call | solution.py:39
  68.4 0.7 %shard_map.182 = (f32[64,1024]{1,0:T(8,128)}, f32[64,100]{1,0:T(8,128)}, f32[1]{0:T(128)}, f32[8,128]{1,0:T(8,128)S(1)}) custom-call(f32[8,128]{1,0:T(8,128)S(1)} %get-tuple-element.91.refs_0_, f32[64,1152]{1,0:T(8,128)S(1)} %shard_map.178.refs_0_.refs_1_, bf16[144,1024]{1,0:T(8,128)(2,1)S(1)} %collective-permute-done.17.last_ref.refs_2_), custom_call_target="tpu_custom_call" | custom-call | tf_op jit(solution)/shard_map/pallas_call | solution.py:39
  69.2 0.7 %shard_map.185 = f32[64,1024]{1,0:T(8,128)} custom-call(f32[8,128]{1,0:T(8,128)S(1)} %get-tuple-element.93.refs_0_, f32[64,1024]{1,0:T(8,128)S(1)} %get-tuple-element.95.refs_1_, bf16[64,1024]{1,0:T(8,128)(2,1)S(1)} %collective-permute-done.19.refs_2_), custom_call_target="tpu_custom_call" | custom-call | tf_op jit(solution)/shard_map/pallas_call | solution.py:39
  (36 shorter events, 3.1 us)
Async XLA Ops:
  1.8 6.5 %collective-permute-start = (bf16[4,16,1024]{2,1,0:T(8,128)(2,1)S(1)}, bf16[4,16,1024]{2,1,0:T(8,128)(2,1)S(1)}, u32[]{:S(2)}, u32[]{:S(2)}) collective-permute-start(bf16[4,16,1024]{2,1,0:T(8,128)(2,1)S(1)} %get-tuple-element.61), channel_id=1, source_target_pairs={{0,2},{2,0},{4,6},{6,4},{8,10},{10,8},{12,14},{14,12},{1,3},{3,1},... | collective-permute-start | bytes 393224 | tf_op jit(solution)/shard_map/ppermute | solution.py:56
  8.3 6.6 %collective-permute-start.1 = (bf16[32,1024]{1,0:T(8,128)(2,1)S(1)}, bf16[32,1024]{1,0:T(8,128)(2,1)S(1)}, u32[]{:S(2)}, u32[]{:S(2)}) collective-permute-start(bf16[32,1024]{1,0:T(8,128)(2,1)S(1)} %get-tuple-element.62), channel_id=1, source_target_pairs={{0,12},{2,14},{4,8},{6,10},{8,4},{10,6},{12,0},{14,2},{1,13},{3,15... | collective-permute-start | bytes 196616 | tf_op jit(solution)/shard_map/ppermute | solution.py:56
  12.2 5.4 %collective-permute-start.2 = (bf16[32,1024]{1,0:T(8,128)(2,1)S(1)}, bf16[32,1024]{1,0:T(8,128)(2,1)S(1)}, u32[]{:S(2)}, u32[]{:S(2)}) collective-permute-start(bf16[32,1024]{1,0:T(8,128)(2,1)S(1)} %get-tuple-element.63), channel_id=1, source_target_pairs={{0,8},{2,10},{4,12},{6,14},{8,0},{10,2},{12,4},{14,6},{1,9},{3,11}... | collective-permute-start | bytes 196616 | tf_op jit(solution)/shard_map/ppermute | solution.py:56
  12.2 5.4 %collective-permute-start.3 = (bf16[32,1024]{1,0:T(8,128)(2,1)S(1)}, bf16[32,1024]{1,0:T(8,128)(2,1)S(1)}, u32[]{:S(2)}, u32[]{:S(2)}) collective-permute-start(bf16[32,1024]{1,0:T(8,128)(2,1)S(1)} %get-tuple-element.64), channel_id=1, source_target_pairs={{0,4},{2,6},{4,0},{6,2},{8,12},{10,14},{12,8},{14,10},{1,5},{3,7},... | collective-permute-start | bytes 196616 | tf_op jit(solution)/shard_map/ppermute | solution.py:56
  21.1 1.4 %copy-start.1 = (f32[100,256]{1,0:T(8,128)S(1)}, f32[100,256]{1,0:T(8,128)}, u32[]{:S(2)}) copy-start(f32[100,256]{1,0:T(8,128)} %truth_ref.1) | copy-start | bytes 307204
  21.1 1.4 %copy-start.2 = (f32[256]{0:T(256)S(1)}, f32[256]{0:T(256)}, u32[]{:S(2)}) copy-start(f32[256]{0:T(256)} %cell_ref.1) | copy-start | bytes 3076
  21.1 1.4 %collective-permute-start.5 = (bf16[2,100,256]{2,1,0:T(8,128)(2,1)S(1)}, bf16[2,100,256]{2,1,0:T(8,128)(2,1)S(1)}, u32[]{:S(2)}, u32[]{:S(2)}) collective-permute-start(bf16[2,100,256]{2,1,0:T(8,128)(2,1)S(1)} %get-tuple-element.69), channel_id=1, source_target_pairs={{0,1},{1,0},{2,3},{3,2},{4,5},{5,4},{6,7},{7,6},{8,9},{9,8},{10,11... | collective-permute-start | bytes 307208 | tf_op jit(solution)/shard_map/ppermute | solution.py:56
  24.0 2.3 %collective-permute-start.6 = (bf16[256,1152]{1,0:T(8,128)(2,1)S(1)}, bf16[256,1152]{1,0:T(8,128)(2,1)S(1)}, u32[]{:S(2)}, u32[]{:S(2)}) collective-permute-start(bf16[256,1152]{1,0:T(8,128)(2,1)S(1)} %get-tuple-element.77), channel_id=1, source_target_pairs={{0,1},{1,0},{2,3},{3,2},{4,5},{5,4},{6,7},{7,6},{8,9},{9,8},{10,11... | collective-permute-start | bytes 1769480 | tf_op jit(solution)/shard_map/ppermute | solution.py:56
  24.2 2.7 %collective-permute-start.7 = (bf16[256,1152]{1,0:T(8,128)(2,1)S(1)}, bf16[256,1152]{1,0:T(8,128)(2,1)S(1)}, u32[]{:S(2)}, u32[]{:S(2)}) collective-permute-start(bf16[256,1152]{1,0:T(8,128)(2,1)S(1)} %get-tuple-element.79), channel_id=1, source_target_pairs={{0,1},{1,0},{2,3},{3,2},{4,5},{5,4},{6,7},{7,6},{8,9},{9,8},{10,11... | collective-permute-start | bytes 1769480 | tf_op jit(solution)/shard_map/ppermute | solution.py:56
  24.6 6.1 %collective-permute-start.4 = (bf16[2,4,64,128]{3,2,1,0:T(8,128)(2,1)S(1)}, bf16[2,4,64,128]{3,2,1,0:T(8,128)(2,1)S(1)}, u32[]{:S(2)}, u32[]{:S(2)}) collective-permute-start(bf16[2,4,64,128]{3,2,1,0:T(8,128)(2,1)S(1)} %get-tuple-element.67), channel_id=1, source_target_pairs={{0,1},{1,0},{2,3},{3,2},{4,5},{5,4},{6,7},{7,6},{8,9},{9,8},{10,11... | collective-permute-start | bytes 393224 | tf_op jit(solution)/shard_map/ppermute | solution.py:56
  27.1 9.8 %collective-permute-start.9 = (bf16[160,1024]{1,0:T(8,128)(2,1)S(1)}, bf16[160,1024]{1,0:T(8,128)(2,1)S(1)}, u32[]{:S(2)}, u32[]{:S(2)}) collective-permute-start(bf16[160,1024]{1,0:T(8,128)(2,1)S(1)} %shard_map.172.refs_0_), channel_id=1, source_target_pairs={{0,4},{2,6},{4,0},{6,2},{8,12},{10,14},{12,8},{14,10},{1,5},{3,7},... | collective-permute-start | bytes 983048 | tf_op jit(solution)/shard_map/ppermute | solution.py:56
  27.6 14.3 %collective-permute-start.12 = (bf16[128,1152]{1,0:T(8,128)(2,1)S(1)}, bf16[128,1152]{1,0:T(8,128)(2,1)S(1)}, u32[]{:S(2)}, u32[]{:S(2)}) collective-permute-start(bf16[128,1152]{1,0:T(8,128)(2,1)S(1)} %shard_map.171.refs_0_), channel_id=1, source_target_pairs={{0,2},{2,0},{4,6},{6,4},{8,10},{10,8},{12,14},{14,12},{1,3},{3,1},... | collective-permute-start | bytes 884744 | tf_op jit(solution)/shard_map/ppermute | solution.py:56
  31.2 3.2 %collective-permute-start.8 = (bf16[8,16,1024]{2,1,0:T(8,128)(2,1)S(1)}, bf16[8,16,1024]{2,1,0:T(8,128)(2,1)S(1)}, u32[]{:S(2)}, u32[]{:S(2)}) collective-permute-start(bf16[8,16,1024]{2,1,0:T(8,128)(2,1)S(1)} %get-tuple-element.82.slots_ref.refs_3_.refs_2_), channel_id=1, source_target_pairs={{0,1},{1,0},{2,3},{3,2},{4,5},{5,4},{6,7},{7,6},{8,9},{9,8},{10,11... | collective-permute-start | bytes 786440 | tf_op jit(solution)/shard_map/ppermute | solution.py:56
  31.3 9.1 %collective-permute-start.10 = (bf16[32,1024]{1,0:T(8,128)(2,1)S(1)}, bf16[32,1024]{1,0:T(8,128)(2,1)S(1)}, u32[]{:S(2)}, u32[]{:S(2)}) collective-permute-start(bf16[32,1024]{1,0:T(8,128)(2,1)S(1)} %get-tuple-element.85), channel_id=1, source_target_pairs={{0,12},{2,14},{4,8},{6,10},{8,4},{10,6},{12,0},{14,2},{1,13},{3,15... | collective-permute-start | bytes 196616 | tf_op jit(solution)/shard_map/ppermute | solution.py:56
  34.2 7.7 %collective-permute-start.11 = (bf16[32,1024]{1,0:T(8,128)(2,1)S(1)}, bf16[32,1024]{1,0:T(8,128)(2,1)S(1)}, u32[]{:S(2)}, u32[]{:S(2)}) collective-permute-start(bf16[32,1024]{1,0:T(8,128)(2,1)S(1)} %get-tuple-element.86), channel_id=1, source_target_pairs={{0,8},{2,10},{4,12},{6,14},{8,0},{10,2},{12,4},{14,6},{1,9},{3,11}... | collective-permute-start | bytes 196616 | tf_op jit(solution)/shard_map/ppermute | solution.py:56
  35.1 9.2 %collective-permute-start.15 = (bf16[128,1024]{1,0:T(8,128)(2,1)S(1)}, bf16[128,1024]{1,0:T(8,128)(2,1)S(1)}, u32[]{:S(2)}, u32[]{:S(2)}) collective-permute-start(bf16[128,1024]{1,0:T(8,128)(2,1)S(1)} %get-tuple-element.84.refs_0_), channel_id=1, source_target_pairs={{0,2},{2,0},{4,6},{6,4},{8,10},{10,8},{12,14},{14,12},{1,3},{3,1},... | collective-permute-start | bytes 786440 | tf_op jit(solution)/shard_map/ppermute | solution.py:56
  42.1 11.7 %collective-permute-start.14 = (bf16[64,1152]{1,0:T(8,128)(2,1)S(1)}, bf16[64,1152]{1,0:T(8,128)(2,1)S(1)}, u32[]{:S(2)}, u32[]{:S(2)}) collective-permute-start(bf16[64,1152]{1,0:T(8,128)(2,1)S(1)} %get-tuple-element.88), channel_id=1, source_target_pairs={{0,8},{2,10},{4,12},{6,14},{8,0},{10,2},{12,4},{14,6},{1,9},{3,11}... | collective-permute-start | bytes 442376 | tf_op jit(solution)/shard_map/ppermute | solution.py:56
  42.1 11.6 %collective-permute-start.13 = (bf16[64,1152]{1,0:T(8,128)(2,1)S(1)}, bf16[64,1152]{1,0:T(8,128)(2,1)S(1)}, u32[]{:S(2)}, u32[]{:S(2)}) collective-permute-start(bf16[64,1152]{1,0:T(8,128)(2,1)S(1)} %get-tuple-element.87.refs_0_), channel_id=1, source_target_pairs={{0,12},{2,14},{4,8},{6,10},{8,4},{10,6},{12,0},{14,2},{1,13},{3,15... | collective-permute-start | bytes 442376 | tf_op jit(solution)/shard_map/ppermute | solution.py:56
  44.4 14.7 %collective-permute-start.16 = (bf16[160,1024]{1,0:T(8,128)(2,1)S(1)}, bf16[160,1024]{1,0:T(8,128)(2,1)S(1)}, u32[]{:S(2)}, u32[]{:S(2)}) collective-permute-start(bf16[160,1024]{1,0:T(8,128)(2,1)S(1)} %shard_map.179.refs_0_), channel_id=1, source_target_pairs={{0,4},{2,6},{4,0},{6,2},{8,12},{10,14},{12,8},{14,10},{1,5},{3,7},... | collective-permute-start | bytes 983048 | tf_op jit(solution)/shard_map/ppermute | solution.py:56
  45.8 13.5 %collective-permute-start.18 = (bf16[128,1024]{1,0:T(8,128)(2,1)S(1)}, bf16[128,1024]{1,0:T(8,128)(2,1)S(1)}, u32[]{:S(2)}, u32[]{:S(2)}) collective-permute-start(bf16[128,1024]{1,0:T(8,128)(2,1)S(1)} %shard_map.183), channel_id=1, source_target_pairs={{0,2},{2,0},{4,6},{6,4},{8,10},{10,8},{12,14},{14,12},{1,3},{3,1},... | collective-permute-start | bytes 786440 | tf_op jit(solution)/shard_map/ppermute | solution.py:56
  53.9 13.0 %copy-start = (bf16[1024,1024]{1,0:T(8,128)(2,1)S(1)}, bf16[1024,1024]{1,0:T(8,128)(2,1)}, u32[]{:S(2)}) copy-start(bf16[1024,1024]{1,0:T(8,128)(2,1)} %w_msg_ref.1) | copy-start | bytes 6291460
  59.1 7.8 %collective-permute-start.17 = (bf16[144,1024]{1,0:T(8,128)(2,1)S(1)}, bf16[144,1024]{1,0:T(8,128)(2,1)S(1)}, u32[]{:S(2)}, u32[]{:S(2)}) collective-permute-start(bf16[144,1024]{1,0:T(8,128)(2,1)S(1)} %shard_map.180), channel_id=1, source_target_pairs={{0,2},{2,0},{4,6},{6,4},{8,10},{10,8},{12,14},{14,12},{1,3},{3,1},... | collective-permute-start | bytes 884744 | tf_op jit(solution)/shard_map/ppermute | solution.py:56
  59.3 9.9 %collective-permute-start.19 = (bf16[64,1024]{1,0:T(8,128)(2,1)S(1)}, bf16[64,1024]{1,0:T(8,128)(2,1)S(1)}, u32[]{:S(2)}, u32[]{:S(2)}) collective-permute-start(bf16[64,1024]{1,0:T(8,128)(2,1)S(1)} %get-tuple-element.96), channel_id=1, source_target_pairs={{0,8},{2,10},{4,12},{6,14},{8,0},{10,2},{12,4},{14,6},{1,9},{3,11}... | collective-permute-start | bytes 393224 | tf_op jit(solution)/shard_map/ppermute | solution.py:56

commit v6 on v5

--- a/solution.py
+++ b/solution.py
@@ -322,8 +322,9 @@
             pack(out_ref, at + block, part.astype(bf16))
 
 
-def message_kernel(keep_ref, give_ref, slots_ref, other_ref, first_ref, second_ref, near_ref):
+def message_kernel(keep_ref, give_ref, slots_ref, other_ref, first_ref, second_ref, near_ref, slot_far_ref):
     depth, width = keep_ref.shape[-1], near_ref.shape[1]
+    slot_far_ref[...] = slots_ref[slots_ref.shape[0] // 2 :]
     count = first_ref.shape[0]
     for half in range(2):
         own = keep_ref[half].reshape(-1, depth)
@@ -344,12 +345,9 @@
     out_ref[...] = source_ref[...]
 
 
-def step_kernel(near_ref, arrived_ref, slots_ref, out_ref):
-    rows = slots_ref.shape[1]
-    count = arrived_ref.shape[0]
-    out_ref[0:count, :] = (near_ref[0:count, :] + arrived_ref[...].astype(f32)).astype(bf16)
-    out_ref[count : count + rows, :] = slots_ref[2]
-    out_ref[count + rows :, :] = slots_ref[3]
+def step_kernel(near_ref, arrived_ref, out_ref):
+    count = out_ref.shape[0]
+    out_ref[...] = (near_ref[0:count, :] + arrived_ref[...].astype(f32)).astype(bf16)
 
 
 def halve_kernel(begin, near_ref, *rest):
@@ -374,18 +372,27 @@
     out_ref[:, width:] = split_loss(part, variables)
 
 
-def last_kernel(hidden_ref, slots_ref, *rest):
-    arrived_refs, out_ref = rest[:-1], rest[-1]
-    rows, width = slots_ref.shape[1:]
+def fold_kernel(kept_ref, arrived_ref, send_ref, keep_ref):
+    half, _, rows, _ = keep_ref.shape
+    count = arrived_ref.shape[1]
+    for at, out_ref in ((0, keep_ref), (half, send_ref)):
+        for i in range(half):
+            for j in range(count):
+                out_ref[i, j] = kept_ref[at + i, j]
+                out_ref[i, count + j] = arrived_ref[at + i, j]
+
+
+def last_kernel(hidden_ref, kept_ref, arrived_ref, out_ref):
+    count, rows, width = kept_ref.shape[1:]
     block = hidden_ref.shape[0]
     out_ref[0:block, :] = hidden_ref[:, :width].astype(bf16)
     out_ref[block : block + packed, :] = jnp.zeros((packed, width), bf16)
     pack(out_ref, block, hidden_ref[:, width:].astype(bf16))
     at = block + packed
-    for r in arrived_refs:
-        out_ref[at : at + rows, :] = r[r.shape[0] - rows :, :]
-        at += rows
-    out_ref[at:, :] = slots_ref[1]
+    for source_ref in (kept_ref, arrived_ref):
+        for j in range(count):
+            out_ref[at : at + rows, :] = source_ref[1, j]
+            at += rows
 
 
 def hidden_early_kernel(variables, width, held_ref, other_ref, arrived_ref, *out_refs):
@@ -418,33 +425,28 @@
             ).astype(bf16)
 
 
-def slot_kernel(share_ref, grad_ref, slots_ref, *send_refs):
+def slot_kernel(share_ref, grad_ref, slots_ref):
     peers, each, width = slots_ref.shape
     rows = peers * each
     for begin in range(0, width, tile):
         columns = slice(begin, begin + tile)
         both = mm(share_ref[...], grad_ref[:, columns], 1, 0)
         slots_ref[:, :, columns] = (both[:rows] + both[rows:]).astype(bf16).reshape(peers, each, tile)
-    for i, send_ref in enumerate(send_refs):
-        step = peers // 2 - 1 - i
-        send_ref[0:each, :] = slots_ref[2 * step]
-        send_ref[each:, :] = slots_ref[2 * step + 1]
-
-
-def owner_kernel(pick_ref, w_msg_ref, slots_ref, last_ref, *rest):
-    arrived_refs, (grad_ref, token_ref, held_ref) = rest[:-3], rest[-3:]
+
+
+def owner_kernel(pick_ref, w_msg_ref, kept_ref, arrived_ref, last_ref, grad_ref, token_ref, held_ref):
     token_ref[...] = jnp.zeros_like(token_ref)
-    peers, rows, width = slots_ref.shape
-    levels = peers // 2
-    begin = last_ref.shape[0] - levels * rows
-    for i in range(levels):
-        spot = 2 * (levels - 1 - i)
-        if i == levels - 1:
-            held_ref[spot] = slots_ref[0]
-        else:
-            at = arrived_refs[i].shape[0] - 2 * rows
-            held_ref[spot] = arrived_refs[i][at : at + rows, :]
-        held_ref[spot + 1] = last_ref[begin + i * rows : begin + (i + 1) * rows, :]
+    peers, rows, width = held_ref.shape
+    count = kept_ref.shape[1]
+    begin = last_ref.shape[0] - 2 * count * rows
+    order = [0]
+    for bit in reversed(range(peers.bit_length() - 1)):
+        order += [x ^ (1 << bit) for x in order]
+    for j in range(count):
+        held_ref[order[j]] = kept_ref[0, j]
+        held_ref[order[count + j]] = arrived_ref[0, j]
+    for j in range(2 * count):
+        held_ref[order[2 * count + j]] = last_ref[begin + j * rows : begin + (j + 1) * rows, :]
     nodes = mm(pick_ref[...], held_ref[...].reshape(peers * rows, width), 0, 0).astype(bf16)
     grad_ref[...] = mm(nodes, w_msg_ref[...], 1, 1).astype(bf16).reshape(grad_ref.shape)
 
@@ -608,18 +610,19 @@
         limit=14,
         after=[across[0]],
     )
-    slots, *slots_sent = call(
+    (slots,) = call(
         slot_kernel,
-        [((peers, rows_peer, width), bf16)] + [((2 * rows_peer, width), bf16)] * (levels - 2),
+        [((peers, rows_peer, width), bf16)],
         [share, grad_hidden],
         limit=6,
         after=[received_other],
     )
     slots_other = swap(slots, "member", cores, 1)
-    slots_arrived = spread(slots_sent, steps[:-1])
-    message_first, message_second, message_near = call(
+    message_first, message_second, message_near, slots_sent = call(
         message_kernel,
-        [((half // 2, width), bf16)] * 2 + [((half, width), f32)],
+        [((half // 2, width), bf16)] * 2
+        + [((half, width), f32)]
+        + [((levels, rows_peer, width), bf16)],
         [received_keep, received_other, slots, slots_other],
         limit=10,
     )
@@ -635,13 +638,13 @@
         [((block, wide), bf16)] * early,
         [held_near, near_other, first_other],
         limit=6,
-        after=[message_first, hidden_own] + slots_arrived,
+        after=[message_first, hidden_own],
     )
     hidden_parts = spread(hidden_early, steps[:early])
     (message_step,) = call(
         step_kernel,
-        [((half // 2 + 2 * rows_peer, width), bf16)],
-        [message_near, message_first_other, slots],
+        [((half // 2, width), bf16)],
+        [message_near, message_first_other],
         limit=4,
         after=hidden_early[:1],
     )
@@ -650,7 +653,18 @@
         second_kernel, [((half // 2, width), bf16)], [message_second], limit=4, after=[message_step]
     )
     message_second_other = swap(message_second, "space", peers, 1)
-    slots_arrived.append(message_other)
+    slots_kept = slots.reshape(peers, 1, rows_peer, width)
+    slots_sent = slots_sent.reshape(levels, 1, rows_peer, width)
+    bit = levels
+    while True:
+        slots_other = swap(slots_sent, "space", peers, bit)
+        if bit == 2:
+            break
+        folded = (bit // 2, 2 * levels // bit, rows_peer, width)
+        slots_sent, slots_kept = call(
+            fold_kernel, [(folded, bf16)] * 2, [slots_kept, slots_other], limit=4, after=[message_second]
+        )
+        bit //= 2
     (partial,) = call(
         functools.partial(partial_kernel, variables, width, early),
         [((block, wide), f32)],
@@ -660,9 +674,9 @@
     (last,) = call(
         last_kernel,
         [((block + packed + levels * rows_peer, width), bf16)],
-        [hidden_own, slots] + slots_arrived,
+        [hidden_own, slots_kept, slots_other],
         limit=4,
-        after=[partial],
+        after=[message_second],
     )
     last_other = swap(last, "space", peers, 1)
     message_send, message_keep = call(
@@ -688,7 +702,7 @@
     latent_grad, latent_done = call(
         owner_kernel,
         [(latents.shape, bf16), token],
-        [pick, w_msg, slots, last_other] + slots_arrived,
+        [pick, w_msg, slots_kept, slots_other, last_other],
         scratch=[pltpu.VMEM((peers, rows_peer, width), bf16)],
         limit=8,
     )

time: 70.1 us -> 69.7 us (level)
  waiting for transfers between devices: 31.9 us -> 29.2 us
  starting transfers between devices: 19.1 us -> 21.3 us
    ppermute x20, waiting for transfers between devices: 31.9 us -> 29.2 us  [swap(): return lax.ppermute(value, axis, [(i, i ^ step) for i in range(size)])]
    ppermute x20, starting transfers between devices: 19.1 us -> 21.3 us  [swap(): return lax.ppermute(value, axis, [(i, i ^ step) for i in range(size)])]
    pallas_call x22 -> x23, Pallas kernels: 18 us -> 18 us  [call(): pl.pallas_call(inner if count else body, out_shape=[jax.ShapeDtypeStruct(...]
  transfers between devices with their start and end apart: 20 -> 20, of which waited for: 11 -> 13; matrix products, arithmetic and copies ran while one was open for 0% -> 0% of each run, Pallas kernels for 16% -> 16%
where the time goes in v6:
time: 69.7 us; the launch traced here: 69.4 us
  waiting for transfers between devices  29.2 us (42%)
  starting transfers between devices  21.3 us (31%)
  Pallas kernels  18 us (26%)
  between operations  0.84 us (1%)
    ppermute x20, waiting for transfers between devices, swap(): return lax.ppermute(value, axis, [(i, i ^ step) for i in range(size)])  29.2 us
    ppermute x20, starting transfers between devices, swap(): return lax.ppermute(value, axis, [(i, i ^ step) for i in range(size)])  21.3 us
    pallas_call x23, Pallas kernels, call(): pl.pallas_call(inner if count else body, out_shape=[jax.ShapeDtypeStruct(...  18 us
  transfers between devices with their start and end apart: 20, of which 13 were waited for; matrix products, arithmetic and copies ran while one was open for 0% of the time, Pallas kernels for 16%

profile of v6, /device:TPU:0, one launch (start us, length us, event | category | flops | bytes accessed | tf_op | source)
XLA Modules:
  0.0 69.4 jit_solution(3062287615777440615)
XLA Ops:
  0.6 1.1 %shard_map.164 = (bf16[128,64]{1,0:T(8,128)(2,1)S(1)}, bf16[4,16,1024]{2,1,0:T(8,128)(2,1)S(1)}, bf16[4,16,1024]{2,1,0:T(8,128)(2,1)S(1)}) custom-call(s32[1,8,8]{2,1,0:T(8,128)} %lists_ref.1, bf16[2,32,1024]{2,1,0:T(8,128)(2,1)} %latents_ref.1), custom_call_target="tpu_custom_call" | custom-call | tf_op jit(solution)/shard_map/pallas_call | solution.py:39
  1.8 3.0 %collective-permute-start = (bf16[4,16,1024]{2,1,0:T(8,128)(2,1)S(1)}, bf16[4,16,1024]{2,1,0:T(8,128)(2,1)S(1)}, u32[]{:S(2)}, u32[]{:S(2)}) collective-permute-start(bf16[4,16,1024]{2,1,0:T(8,128)(2,1)S(1)} %get-tuple-element.61), channel_id=1, source_target_pairs={{0,2},{2,0},{4,6},{6,4},{8,10},{10,8},{12,14},{14,12},{1,3},{3,1},... | collective-permute-start | bytes 393224 | tf_op jit(solution)/shard_map/ppermute | solution.py:56
  4.8 2.6 %shard_map.165 = (bf16[256,512]{1,0:T(8,128)(2,1)S(1)}, bf16[1024,1024]{1,0:T(8,128)(2,1)S(1)}, f32[1024]{0:T(1024)S(1)}, bf16[256,1024]{1,0:T(8,128)(2,1)S(1)},...) custom-call(bf16[128,64]{1,0:T(8,128)(2,1)S(1)} %get-tuple-element.52.refs_0_.pick_ref, ...), custom_call_target="tpu_custom_call" | custom-call | tf_op jit(solution)/shard_map/pallas_call | solution.py:39
  7.4 0.9 %collective-permute-done.refs_2_.near_ref = bf16[4,16,1024]{2,1,0:T(8,128)(2,1)S(1)} collective-permute-done((bf16[4,16,1024]{2,1,0:T(8,128)(2,1)S(1)}, bf16[4,16,1024]{2,1,0:T(8,128)(2,1)S(1)}, u32[]{:S(2)}, u32[]{:S(2)}) %collective-permute-start) | collective-permute-done | bytes 131104 | tf_op jit(solution)/shard_map/ppermute | solution.py:56
  8.3 3.9 %collective-permute-start.1 = (bf16[32,1024]{1,0:T(8,128)(2,1)S(1)}, bf16[32,1024]{1,0:T(8,128)(2,1)S(1)}, u32[]{:S(2)}, u32[]{:S(2)}) collective-permute-start(bf16[32,1024]{1,0:T(8,128)(2,1)S(1)} %get-tuple-element.62), channel_id=1, source_target_pairs={{0,12},{2,14},{4,8},{6,10},{8,4},{10,6},{12,0},{14,2},{1,13},{3,15... | collective-permute-start | bytes 196616 | tf_op jit(solution)/shard_map/ppermute | solution.py:56
  12.2 0.6 collective-permute-start.3
  12.8 2.0 %collective-permute-done.1.rest_0_ = bf16[32,1024]{1,0:T(8,128)(2,1)S(1)} collective-permute-done((bf16[32,1024]{1,0:T(8,128)(2,1)S(1)}, bf16[32,1024]{1,0:T(8,128)(2,1)S(1)}, u32[]{:S(2)}, u32[]{:S(2)}) %collective-permute-start.1) | collective-permute-done | bytes 65568 | tf_op jit(solution)/shard_map/ppermute | solution.py:56
  14.9 2.7 %collective-permute-done.2.rest_1_ = bf16[32,1024]{1,0:T(8,128)(2,1)S(1)} collective-permute-done((bf16[32,1024]{1,0:T(8,128)(2,1)S(1)}, bf16[32,1024]{1,0:T(8,128)(2,1)S(1)}, u32[]{:S(2)}, u32[]{:S(2)}) %collective-permute-start.2) | collective-permute-done | bytes 65568 | tf_op jit(solution)/shard_map/ppermute | solution.py:56
  17.6 3.5 %shard_map.167 = (f32[2,100,256]{2,1,0:T(8,128)S(1)}, bf16[2,100,256]{2,1,0:T(8,128)(2,1)S(1)}, bf16[512,1024]{1,0:T(8,128)(2,1)S(1)}, bf16[512,1024]{1,0:T(8,12...) custom-call(bf16[1024,1024]{1,0:T(8,128)(2,1)S(1)} %get-tuple-element.53.w_msg_ref, ...), custom_call_target="tpu_custom_call" | custom-call | tf_op jit(solution)/shard_map/pallas_call | solution.py:39
  21.2 0.9 %shard_map.168 = (bf16[2,2,4,64,512]{4,3,2,1,0:T(8,128)(2,1)S(1)}, bf16[2,2,4,64,512]{4,3,2,1,0:T(8,128)(2,1)S(1)}, bf16[2,4,64,128]{3,2,1,0:T(8,128)(2,1)S(1)}, bf16[2,4,64,128]{3,2,1,0:T(8,128)(2,1)S(1)}) custom-call(bf16[512,1024]{1,0:T(8,128)(2,1)S(1)} %get-tuple-element.65.normed_ref, bf16[512,1024]{1,0:T(8,128)(2,1)S(1)} %get-tuple-element.66.active_ref, ...), custom_call_target="tpu_custom_call" | custom-call | tf_op jit(solution)/shard_map/pallas_call | solution.py:39
  22.5 1.5 %shard_map.169 = (bf16[512,1024]{1,0:T(8,128)(2,1)S(1)}, bf16[128,512]{1,0:T(8,128)(2,1)S(1)}, f32[1]{0:T(128)}, bf16[256,1152]{1,0:T(8,128)(2,1)S(1)}, bf16[256,1152]{1,0:T(8,128)(2,1)S(1)}) custom-call(f32[2,100,256]{2,1,0:T(8,128)S(1)} %get-tuple-element.69.own_ref, bf16[2,100,256]{2,1,0:T(8,128)(2,1)S(1)} %collective-permute-done.5.other_ref, ...), custom_call_target="tpu_custom_call" | custom-call | tf_op jit(solution)/shard_map/pallas_call | solution.py:39
  24.7 1.6 %shard_map.170 = (f32[256,1152]{1,0:T(8,128)S(1)}, f32[256,1152]{1,0:T(8,128)S(1)}) custom-call(f32[1]{0:T(128)} %get-tuple-element.74.loss_ref, bf16[2,2,4,64,512]{4,3,2,1,0:T(8,128)(2,1)S(1)} %get-tuple-element.72.normed_t_ref, bf16[2,2,4,64,512]{4,3,2,1,0:T(8,128)(2,1)S(1)} %get-tuple-element.73.active_t_ref, ...), custom_call_target="tpu_custom_call" | custom-call | tf_op jit(solution)/shard_map/pallas_call | solution.py:39
  27.1 0.5 collective-permute-start.9
  27.6 1.5 %collective-permute-start.10 = (bf16[128,1152]{1,0:T(8,128)(2,1)S(1)}, bf16[128,1152]{1,0:T(8,128)(2,1)S(1)}, u32[]{:S(2)}, u32[]{:S(2)}) collective-permute-start(bf16[128,1152]{1,0:T(8,128)(2,1)S(1)} %shard_map.171.refs_0_), channel_id=1, source_target_pairs={{0,2},{2,0},{4,6},{6,4},{8,10},{10,8},{12,14},{14,12},{1,3},{3,1},... | collective-permute-start | bytes 884744 | tf_op jit(solution)/shard_map/ppermute | solution.py:56
  29.1 1.6 %shard_map.173.refs_2_ = bf16[512,1024]{1,0:T(8,128)(2,1)S(1)} custom-call(bf16[160,1024]{1,0:T(8,128)(2,1)S(1)} %shard_map.172.refs_0_, bf16[512,1024]{1,0:T(8,128)(2,1)S(1)} %get-tuple-element.75.inner_ref.refs_1_, bf16[1024,1024]{1,0:T(8,128)(2,1)S(1)} %get-tuple-element.57.weights_ref.refs_2_, f32[1024]{0:T(1024)S(1)} %get-tuple-element.55.gain_ref.refs_3_, ...), custom_call_target="tpu_custom_call" | custom-call | tf_op jit(solution)/shard_map/pallas_call | solution.py:39
  31.2 1.5 %collective-permute-done.8.other_ref = bf16[8,16,1024]{2,1,0:T(8,128)(2,1)S(1)} collective-permute-done((bf16[8,16,1024]{2,1,0:T(8,128)(2,1)S(1)}, bf16[8,16,1024]{2,1,0:T(8,128)(2,1)S(1)}, u32[]{:S(2)}, u32[]{:S(2)}) %collective-permute-start.8) | collective-permute-done | bytes 262176 | tf_op jit(solution)/shard_map/ppermute | solution.py:56
  32.8 0.7 shard_map.175
  33.5 2.4 %collective-permute-start.12 = (bf16[4,1,16,1024]{3,2,1,0:T(8,128)(2,1)S(1)}, bf16[4,1,16,1024]{3,2,1,0:T(8,128)(2,1)S(1)}, u32[]{:S(2)}, u32[]{:S(2)}) collective-permute-start(bf16[4,1,16,1024]{3,2,1,0:T(8,128)(2,1)S(1)} %bitcast.5), channel_id=1, source_target_pairs={{0,8},{2,10},{4,12},{6,14},{8,0},{10,2},{12,4},{14,6},{1,9},{3,11}... | collective-permute-start | bytes 393224 | tf_op jit(solution)/shard_map/ppermute | solution.py:56
  36.4 0.5 collective-permute-done.9.rest_0_.rest_2_
  37.3 1.9 %collective-permute-start.16 = (bf16[64,1152]{1,0:T(8,128)(2,1)S(1)}, bf16[64,1152]{1,0:T(8,128)(2,1)S(1)}, u32[]{:S(2)}, u32[]{:S(2)}) collective-permute-start(bf16[64,1152]{1,0:T(8,128)(2,1)S(1)} %get-tuple-element.92), channel_id=1, source_target_pairs={{0,8},{2,10},{4,12},{6,14},{8,0},{10,2},{12,4},{14,6},{1,9},{3,11}... | collective-permute-start | bytes 442376 | tf_op jit(solution)/shard_map/ppermute | solution.py:56
  39.2 1.4 %collective-permute-start.15 = (bf16[64,1152]{1,0:T(8,128)(2,1)S(1)}, bf16[64,1152]{1,0:T(8,128)(2,1)S(1)}, u32[]{:S(2)}, u32[]{:S(2)}) collective-permute-start(bf16[64,1152]{1,0:T(8,128)(2,1)S(1)} %get-tuple-element.84.refs_0_), channel_id=1, source_target_pairs={{0,12},{2,14},{4,8},{6,10},{8,4},{10,6},{12,0},{14,2},{1,13},{3,15... | collective-permute-start | bytes 442376 | tf_op jit(solution)/shard_map/ppermute | solution.py:56
  40.6 3.3 %collective-permute-done.11.refs_2_ = bf16[128,1024]{1,0:T(8,128)(2,1)S(1)} collective-permute-done((bf16[128,1024]{1,0:T(8,128)(2,1)S(1)}, bf16[128,1024]{1,0:T(8,128)(2,1)S(1)}, u32[]{:S(2)}, u32[]{:S(2)}) %collective-permute-start.11) | collective-permute-done | bytes 262176 | tf_op jit(solution)/shard_map/ppermute | solution.py:56
  44.0 5.9 %collective-permute-done.12.refs_2_ = bf16[4,1,16,1024]{3,2,1,0:T(8,128)(2,1)S(1)} collective-permute-done((bf16[4,1,16,1024]{3,2,1,0:T(8,128)(2,1)S(1)}, bf16[4,1,16,1024]{3,2,1,0:T(8,128)(2,1)S(1)}, u32[]{:S(2)}, u32[]{:S(2)}) %collective-permute-start.12) | collective-permute-done | bytes 131104 | tf_op jit(solution)/shard_map/ppermute | solution.py:56
  50.5 1.9 %collective-permute-start.18 = (bf16[128,1024]{1,0:T(8,128)(2,1)S(1)}, bf16[128,1024]{1,0:T(8,128)(2,1)S(1)}, u32[]{:S(2)}, u32[]{:S(2)}) collective-permute-start(bf16[128,1024]{1,0:T(8,128)(2,1)S(1)} %shard_map.178.refs_0_), channel_id=1, source_target_pairs={{0,4},{2,6},{4,0},{6,2},{8,12},{10,14},{12,8},{14,10},{1,5},{3,7},... | collective-permute-start | bytes 786440 | tf_op jit(solution)/shard_map/ppermute | solution.py:56
  52.5 4.0 %collective-permute-done.13.refs_3_.arrived_ref = bf16[2,2,16,1024]{3,2,1,0:T(8,128)(2,1)S(1)} collective-permute-done((bf16[2,2,16,1024]{3,2,1,0:T(8,128)(2,1)S(1)}, bf16[2,2,16,1024]{3,2,1,0:T(8,128)(2,1)S(1)}, u32[]{:S(2)}, u32[]{:S(2)}) %collective-permute-start.13) | collective-permute-done | bytes 131104 | tf_op jit(solution)/shard_map/ppermute | solution.py:56
  57.1 3.6 %collective-permute-done.18.refs_3_ = bf16[128,1024]{1,0:T(8,128)(2,1)S(1)} collective-permute-done((bf16[128,1024]{1,0:T(8,128)(2,1)S(1)}, bf16[128,1024]{1,0:T(8,128)(2,1)S(1)}, u32[]{:S(2)}, u32[]{:S(2)}) %collective-permute-start.18) | collective-permute-done | bytes 262176 | tf_op jit(solution)/shard_map/ppermute | solution.py:56
  60.8 1.7 %collective-permute-start.19 = (bf16[64,1024]{1,0:T(8,128)(2,1)S(1)}, bf16[64,1024]{1,0:T(8,128)(2,1)S(1)}, u32[]{:S(2)}, u32[]{:S(2)}) collective-permute-start(bf16[64,1024]{1,0:T(8,128)(2,1)S(1)} %get-tuple-element.96), channel_id=1, source_target_pairs={{0,8},{2,10},{4,12},{6,14},{8,0},{10,2},{12,4},{14,6},{1,9},{3,11}... | collective-permute-start | bytes 393224 | tf_op jit(solution)/shard_map/ppermute | solution.py:56
  62.4 0.8 %collective-permute-done.14.last_ref.refs_2_ = bf16[144,1024]{1,0:T(8,128)(2,1)S(1)} collective-permute-done((bf16[144,1024]{1,0:T(8,128)(2,1)S(1)}, bf16[144,1024]{1,0:T(8,128)(2,1)S(1)}, u32[]{:S(2)}, u32[]{:S(2)}) %collective-permute-start.14) | collective-permute-done | bytes 294944 | tf_op jit(solution)/shard_map/ppermute | solution.py:56
  63.2 1.5 %shard_map.182 = (bf16[2,32,1024]{2,1,0:T(8,128)(2,1)}, f32[8,128]{1,0:T(8,128)S(1)}) custom-call(bf16[128,64]{1,0:T(8,128)(2,1)S(1)} %get-tuple-element.52.refs_0_.pick_ref, bf16[1024,1024]{1,0:T(8,128)(2,1)S(1)} %copy-done, bf16[2,2,16,1024]{3,2,1,0:T(8,128)(2,1)S(1)} %get-tuple-element.88.refs_2_.kept_ref, ...), custom_call_target="tpu_custom_call" | custom-call | tf_op jit(solution)/shard_map/pallas_call | solution.py:39
  64.8 0.7 %shard_map.184 = (f32[64,1024]{1,0:T(8,128)}, f32[64,100]{1,0:T(8,128)}, f32[1]{0:T(128)}, f32[8,128]{1,0:T(8,128)S(1)}) custom-call(f32[8,128]{1,0:T(8,128)S(1)} %get-tuple-element.91.refs_0_, f32[64,1152]{1,0:T(8,128)S(1)} %shard_map.183.refs_1_.refs_0_, bf16[144,1024]{1,0:T(8,128)(2,1)S(1)} %collective-permute-done.14.last_ref.refs_2_), custom_call_target="tpu_custom_call" | custom-call | tf_op jit(solution)/shard_map/pallas_call | solution.py:39
  65.5 3.2 %collective-permute-done.19.refs_2_ = bf16[64,1024]{1,0:T(8,128)(2,1)S(1)} collective-permute-done((bf16[64,1024]{1,0:T(8,128)(2,1)S(1)}, bf16[64,1024]{1,0:T(8,128)(2,1)S(1)}, u32[]{:S(2)}, u32[]{:S(2)}) %collective-permute-start.19) | collective-permute-done | bytes 131104 | tf_op jit(solution)/shard_map/ppermute | solution.py:56
  68.7 0.7 %shard_map.186 = f32[64,1024]{1,0:T(8,128)} custom-call(f32[8,128]{1,0:T(8,128)S(1)} %get-tuple-element.94.refs_0_, f32[64,1024]{1,0:T(8,128)S(1)} %get-tuple-element.95.refs_1_, bf16[64,1024]{1,0:T(8,128)(2,1)S(1)} %collective-permute-done.19.refs_2_), custom_call_target="tpu_custom_call" | custom-call | tf_op jit(solution)/shard_map/pallas_call | solution.py:39
  (37 shorter events, 4.8 us)
Async XLA Ops:
  1.8 6.5 %collective-permute-start = (bf16[4,16,1024]{2,1,0:T(8,128)(2,1)S(1)}, bf16[4,16,1024]{2,1,0:T(8,128)(2,1)S(1)}, u32[]{:S(2)}, u32[]{:S(2)}) collective-permute-start(bf16[4,16,1024]{2,1,0:T(8,128)(2,1)S(1)} %get-tuple-element.61), channel_id=1, source_target_pairs={{0,2},{2,0},{4,6},{6,4},{8,10},{10,8},{12,14},{14,12},{1,3},{3,1},... | collective-permute-start | bytes 393224 | tf_op jit(solution)/shard_map/ppermute | solution.py:56
  8.3 6.6 %collective-permute-start.1 = (bf16[32,1024]{1,0:T(8,128)(2,1)S(1)}, bf16[32,1024]{1,0:T(8,128)(2,1)S(1)}, u32[]{:S(2)}, u32[]{:S(2)}) collective-permute-start(bf16[32,1024]{1,0:T(8,128)(2,1)S(1)} %get-tuple-element.62), channel_id=1, source_target_pairs={{0,12},{2,14},{4,8},{6,10},{8,4},{10,6},{12,0},{14,2},{1,13},{3,15... | collective-permute-start | bytes 196616 | tf_op jit(solution)/shard_map/ppermute | solution.py:56
  12.2 5.4 %collective-permute-start.2 = (bf16[32,1024]{1,0:T(8,128)(2,1)S(1)}, bf16[32,1024]{1,0:T(8,128)(2,1)S(1)}, u32[]{:S(2)}, u32[]{:S(2)}) collective-permute-start(bf16[32,1024]{1,0:T(8,128)(2,1)S(1)} %get-tuple-element.63), channel_id=1, source_target_pairs={{0,8},{2,10},{4,12},{6,14},{8,0},{10,2},{12,4},{14,6},{1,9},{3,11}... | collective-permute-start | bytes 196616 | tf_op jit(solution)/shard_map/ppermute | solution.py:56
  12.2 5.4 %collective-permute-start.3 = (bf16[32,1024]{1,0:T(8,128)(2,1)S(1)}, bf16[32,1024]{1,0:T(8,128)(2,1)S(1)}, u32[]{:S(2)}, u32[]{:S(2)}) collective-permute-start(bf16[32,1024]{1,0:T(8,128)(2,1)S(1)} %get-tuple-element.64), channel_id=1, source_target_pairs={{0,4},{2,6},{4,0},{6,2},{8,12},{10,14},{12,8},{14,10},{1,5},{3,7},... | collective-permute-start | bytes 196616 | tf_op jit(solution)/shard_map/ppermute | solution.py:56
  21.1 1.4 %copy-start.1 = (f32[100,256]{1,0:T(8,128)S(1)}, f32[100,256]{1,0:T(8,128)}, u32[]{:S(2)}) copy-start(f32[100,256]{1,0:T(8,128)} %truth_ref.1) | copy-start | bytes 307204
  21.1 1.4 %copy-start.2 = (f32[256]{0:T(256)S(1)}, f32[256]{0:T(256)}, u32[]{:S(2)}) copy-start(f32[256]{0:T(256)} %cell_ref.1) | copy-start | bytes 3076
  21.1 1.4 %collective-permute-start.5 = (bf16[2,100,256]{2,1,0:T(8,128)(2,1)S(1)}, bf16[2,100,256]{2,1,0:T(8,128)(2,1)S(1)}, u32[]{:S(2)}, u32[]{:S(2)}) collective-permute-start(bf16[2,100,256]{2,1,0:T(8,128)(2,1)S(1)} %get-tuple-element.70), channel_id=1, source_target_pairs={{0,1},{1,0},{2,3},{3,2},{4,5},{5,4},{6,7},{7,6},{8,9},{9,8},{10,11... | collective-permute-start | bytes 307208 | tf_op jit(solution)/shard_map/ppermute | solution.py:56
  24.0 2.3 %collective-permute-start.6 = (bf16[256,1152]{1,0:T(8,128)(2,1)S(1)}, bf16[256,1152]{1,0:T(8,128)(2,1)S(1)}, u32[]{:S(2)}, u32[]{:S(2)}) collective-permute-start(bf16[256,1152]{1,0:T(8,128)(2,1)S(1)} %get-tuple-element.78), channel_id=1, source_target_pairs={{0,1},{1,0},{2,3},{3,2},{4,5},{5,4},{6,7},{7,6},{8,9},{9,8},{10,11... | collective-permute-start | bytes 1769480 | tf_op jit(solution)/shard_map/ppermute | solution.py:56
  24.2 2.7 %collective-permute-start.7 = (bf16[256,1152]{1,0:T(8,128)(2,1)S(1)}, bf16[256,1152]{1,0:T(8,128)(2,1)S(1)}, u32[]{:S(2)}, u32[]{:S(2)}) collective-permute-start(bf16[256,1152]{1,0:T(8,128)(2,1)S(1)} %get-tuple-element.80), channel_id=1, source_target_pairs={{0,1},{1,0},{2,3},{3,2},{4,5},{5,4},{6,7},{7,6},{8,9},{9,8},{10,11... | collective-permute-start | bytes 1769480 | tf_op jit(solution)/shard_map/ppermute | solution.py:56
  24.6 6.1 %collective-permute-start.4 = (bf16[2,4,64,128]{3,2,1,0:T(8,128)(2,1)S(1)}, bf16[2,4,64,128]{3,2,1,0:T(8,128)(2,1)S(1)}, u32[]{:S(2)}, u32[]{:S(2)}) collective-permute-start(bf16[2,4,64,128]{3,2,1,0:T(8,128)(2,1)S(1)} %get-tuple-element.68), channel_id=1, source_target_pairs={{0,1},{1,0},{2,3},{3,2},{4,5},{5,4},{6,7},{7,6},{8,9},{9,8},{10,11... | collective-permute-start | bytes 393224 | tf_op jit(solution)/shard_map/ppermute | solution.py:56
  27.1 9.8 %collective-permute-start.9 = (bf16[160,1024]{1,0:T(8,128)(2,1)S(1)}, bf16[160,1024]{1,0:T(8,128)(2,1)S(1)}, u32[]{:S(2)}, u32[]{:S(2)}) collective-permute-start(bf16[160,1024]{1,0:T(8,128)(2,1)S(1)} %shard_map.172.refs_0_), channel_id=1, source_target_pairs={{0,4},{2,6},{4,0},{6,2},{8,12},{10,14},{12,8},{14,10},{1,5},{3,7},... | collective-permute-start | bytes 983048 | tf_op jit(solution)/shard_map/ppermute | solution.py:56
  27.6 9.5 %collective-permute-start.10 = (bf16[128,1152]{1,0:T(8,128)(2,1)S(1)}, bf16[128,1152]{1,0:T(8,128)(2,1)S(1)}, u32[]{:S(2)}, u32[]{:S(2)}) collective-permute-start(bf16[128,1152]{1,0:T(8,128)(2,1)S(1)} %shard_map.171.refs_0_), channel_id=1, source_target_pairs={{0,2},{2,0},{4,6},{6,4},{8,10},{10,8},{12,14},{14,12},{1,3},{3,1},... | collective-permute-start | bytes 884744 | tf_op jit(solution)/shard_map/ppermute | solution.py:56
  31.2 1.6 %collective-permute-start.8 = (bf16[8,16,1024]{2,1,0:T(8,128)(2,1)S(1)}, bf16[8,16,1024]{2,1,0:T(8,128)(2,1)S(1)}, u32[]{:S(2)}, u32[]{:S(2)}) collective-permute-start(bf16[8,16,1024]{2,1,0:T(8,128)(2,1)S(1)} %shard_map.174.slots_ref), channel_id=1, source_target_pairs={{0,1},{1,0},{2,3},{3,2},{4,5},{5,4},{6,7},{7,6},{8,9},{9,8},{10,11... | collective-permute-start | bytes 786440 | tf_op jit(solution)/shard_map/ppermute | solution.py:56
  33.5 16.4 %collective-permute-start.12 = (bf16[4,1,16,1024]{3,2,1,0:T(8,128)(2,1)S(1)}, bf16[4,1,16,1024]{3,2,1,0:T(8,128)(2,1)S(1)}, u32[]{:S(2)}, u32[]{:S(2)}) collective-permute-start(bf16[4,1,16,1024]{3,2,1,0:T(8,128)(2,1)S(1)} %bitcast.5), channel_id=1, source_target_pairs={{0,8},{2,10},{4,12},{6,14},{8,0},{10,2},{12,4},{14,6},{1,9},{3,11}... | collective-permute-start | bytes 393224 | tf_op jit(solution)/shard_map/ppermute | solution.py:56
  35.9 8.1 %collective-permute-start.11 = (bf16[128,1024]{1,0:T(8,128)(2,1)S(1)}, bf16[128,1024]{1,0:T(8,128)(2,1)S(1)}, u32[]{:S(2)}, u32[]{:S(2)}) collective-permute-start(bf16[128,1024]{1,0:T(8,128)(2,1)S(1)} %get-tuple-element.83.refs_0_), channel_id=1, source_target_pairs={{0,2},{2,0},{4,6},{6,4},{8,10},{10,8},{12,14},{14,12},{1,3},{3,1},... | collective-permute-start | bytes 786440 | tf_op jit(solution)/shard_map/ppermute | solution.py:56
  37.3 19.6 %collective-permute-start.16 = (bf16[64,1152]{1,0:T(8,128)(2,1)S(1)}, bf16[64,1152]{1,0:T(8,128)(2,1)S(1)}, u32[]{:S(2)}, u32[]{:S(2)}) collective-permute-start(bf16[64,1152]{1,0:T(8,128)(2,1)S(1)} %get-tuple-element.92), channel_id=1, source_target_pairs={{0,8},{2,10},{4,12},{6,14},{8,0},{10,2},{12,4},{14,6},{1,9},{3,11}... | collective-permute-start | bytes 442376 | tf_op jit(solution)/shard_map/ppermute | solution.py:56
  39.2 17.7 %collective-permute-start.15 = (bf16[64,1152]{1,0:T(8,128)(2,1)S(1)}, bf16[64,1152]{1,0:T(8,128)(2,1)S(1)}, u32[]{:S(2)}, u32[]{:S(2)}) collective-permute-start(bf16[64,1152]{1,0:T(8,128)(2,1)S(1)} %get-tuple-element.84.refs_0_), channel_id=1, source_target_pairs={{0,12},{2,14},{4,8},{6,10},{8,4},{10,6},{12,0},{14,2},{1,13},{3,15... | collective-permute-start | bytes 442376 | tf_op jit(solution)/shard_map/ppermute | solution.py:56
  49.9 6.5 %collective-permute-start.13 = (bf16[2,2,16,1024]{3,2,1,0:T(8,128)(2,1)S(1)}, bf16[2,2,16,1024]{3,2,1,0:T(8,128)(2,1)S(1)}, u32[]{:S(2)}, u32[]{:S(2)}) collective-permute-start(bf16[2,2,16,1024]{3,2,1,0:T(8,128)(2,1)S(1)} %get-tuple-element.89), channel_id=1, source_target_pairs={{0,4},{2,6},{4,0},{6,2},{8,12},{10,14},{12,8},{14,10},{1,5},{3,7},... | collective-permute-start | bytes 393224 | tf_op jit(solution)/shard_map/ppermute | solution.py:56
  50.0 7.1 %collective-permute-start.17 = (bf16[128,1024]{1,0:T(8,128)(2,1)S(1)}, bf16[128,1024]{1,0:T(8,128)(2,1)S(1)}, u32[]{:S(2)}, u32[]{:S(2)}) collective-permute-start(bf16[128,1024]{1,0:T(8,128)(2,1)S(1)} %shard_map.179.refs_0_), channel_id=1, source_target_pairs={{0,2},{2,0},{4,6},{6,4},{8,10},{10,8},{12,14},{14,12},{1,3},{3,1},... | collective-permute-start | bytes 786440 | tf_op jit(solution)/shard_map/ppermute | solution.py:56
  50.5 10.2 %collective-permute-start.18 = (bf16[128,1024]{1,0:T(8,128)(2,1)S(1)}, bf16[128,1024]{1,0:T(8,128)(2,1)S(1)}, u32[]{:S(2)}, u32[]{:S(2)}) collective-permute-start(bf16[128,1024]{1,0:T(8,128)(2,1)S(1)} %shard_map.178.refs_0_), channel_id=1, source_target_pairs={{0,4},{2,6},{4,0},{6,2},{8,12},{10,14},{12,8},{14,10},{1,5},{3,7},... | collective-permute-start | bytes 786440 | tf_op jit(solution)/shard_map/ppermute | solution.py:56
  56.5 6.8 %collective-permute-start.14 = (bf16[144,1024]{1,0:T(8,128)(2,1)S(1)}, bf16[144,1024]{1,0:T(8,128)(2,1)S(1)}, u32[]{:S(2)}, u32[]{:S(2)}) collective-permute-start(bf16[144,1024]{1,0:T(8,128)(2,1)S(1)} %shard_map.181), channel_id=1, source_target_pairs={{0,2},{2,0},{4,6},{6,4},{8,10},{10,8},{12,14},{14,12},{1,3},{3,1},... | collective-permute-start | bytes 884744 | tf_op jit(solution)/shard_map/ppermute | solution.py:56
  57.0 6.3 %copy-start = (bf16[1024,1024]{1,0:T(8,128)(2,1)S(1)}, bf16[1024,1024]{1,0:T(8,128)(2,1)}, u32[]{:S(2)}) copy-start(bf16[1024,1024]{1,0:T(8,128)(2,1)} %w_msg_ref.1) | copy-start | bytes 6291460
  60.8 7.9 %collective-permute-start.19 = (bf16[64,1024]{1,0:T(8,128)(2,1)S(1)}, bf16[64,1024]{1,0:T(8,128)(2,1)S(1)}, u32[]{:S(2)}, u32[]{:S(2)}) collective-permute-start(bf16[64,1024]{1,0:T(8,128)(2,1)S(1)} %get-tuple-element.96), channel_id=1, source_target_pairs={{0,8},{2,10},{4,12},{6,14},{8,0},{10,2},{12,4},{14,6},{1,9},{3,11}... | collective-permute-start | bytes 393224 | tf_op jit(solution)/shard_map/ppermute | solution.py:56

commit v7 on v3

--- a/solution.py
+++ b/solution.py
@@ -12,14 +12,7 @@
 tile = 256
 lanes = 128
 packed = 16
-cost_hints = {
-    "back_kernel": 8,
-    "slot_kernel": 4,
-    "hidden_early_kernel": 4,
-    "message_early_kernel": 4,
-    "late_kernel": 4,
-    "message_sum_kernel": 8,
-}
+cost_hints = {"back_kernel": 8, "slot_kernel": 4, "hidden_early_kernel": 4}
 f32 = jnp.float32
 bf16 = jnp.bfloat16
 
@@ -360,11 +353,9 @@
         out_ref[:, width:] = part.astype(bf16)
 
 
-def message_early_kernel(near_ref, arrived_ref, *out_refs):
-    block = out_refs[0].shape[0]
-    for i, out_ref in enumerate(out_refs):
-        here = slice(i * block, (i + 1) * block)
-        out_ref[...] = (near_ref[here, :] + arrived_ref[here, :].astype(f32)).astype(bf16)
+def message_early_kernel(begin, near_ref, arrived_ref, out_ref):
+    here = slice(begin, begin + out_ref.shape[0])
+    out_ref[...] = (near_ref[here, :] + arrived_ref[here, :].astype(f32)).astype(bf16)
 
 
 def late_kernel(variables, early, held_ref, other_ref, near_ref, arrived_ref, *out_refs):
@@ -606,32 +597,38 @@
     )
     message_first_other = swap(message_first, "space", peers, 1)
     middle_other = swap(middle, "space", peers, 1)
+    hidden_early = call(
+        functools.partial(hidden_early_kernel, variables, width),
+        [((block, wide), bf16)] * early,
+        [held_near, near_other, first_other],
+        limit=6,
+        after=[message_first] + slots_arrived,
+    )
+    hidden_parts = spread(hidden_early, steps[:early])
+    message_parts, pieces = [], []
+    for i in range(early):
+        (piece,) = call(
+            functools.partial(message_early_kernel, i * block),
+            [((block, width), bf16)],
+            [message_near, message_first_other],
+            limit=6,
+        )
+        pieces.append(piece)
+        message_parts.append(swap(piece, "space", peers, steps[i]))
     (last,) = call(
         ride_kernel,
         [((2 * block + packed + levels * rows_peer, width), bf16)],
         [last, slots] + slots_arrived,
         limit=4,
+        after=[middle_other],
     )
     last_other = swap(last, "space", peers, 1)
-    hidden_early = call(
-        functools.partial(hidden_early_kernel, variables, width),
-        [((block, wide), bf16)] * early,
-        [held_near, near_other, first_other],
-        limit=6,
-    )
-    hidden_parts = spread(hidden_early, steps[:early])
-    message_early = call(
-        message_early_kernel,
-        [((block, width), bf16)] * early,
-        [message_near, message_first_other],
-        limit=6,
-    )
-    message_parts = spread(message_early, steps[:early])
     late = call(
         functools.partial(late_kernel, variables, early),
         [((2 * block + packed, width), bf16)] * (levels - 1 - early),
         [held_near, near_other, message_near, middle_other],
         limit=6,
+        after=hidden_parts + pieces,
     )
     late_parts = spread(late, steps[early:])
     token = ((8, lanes), f32)

time: 67.8 us -> 70.6 us (1.041)
  waiting for transfers between devices: 26.6 us -> 29.4 us
    ppermute x21, waiting for transfers between devices: 26.6 us -> 29.4 us  [swap(): return lax.ppermute(value, axis, [(i, i ^ step) for i in range(size)])]
    pallas_call x18 -> x19, Pallas kernels: 18.1 us -> 18.1 us  [call(): pl.pallas_call(inner if count else body, out_shape=[jax.ShapeDtypeStruct(...]
where the time goes in v7:
time: 70.6 us; the launch traced here: 70.4 us
  waiting for transfers between devices  29.4 us (42%)
  starting transfers between devices  22 us (31%)
  Pallas kernels  18.1 us (26%)
  between operations  0.84 us (1%)
    ppermute x21, waiting for transfers between devices, swap(): return lax.ppermute(value, axis, [(i, i ^ step) for i in range(size)])  29.4 us
    ppermute x21, starting transfers between devices, swap(): return lax.ppermute(value, axis, [(i, i ^ step) for i in range(size)])  22 us
    pallas_call x19, Pallas kernels, call(): pl.pallas_call(inner if count else body, out_shape=[jax.ShapeDtypeStruct(...  18.1 us
  transfers between devices with their start and end apart: 21, of which 10 were waited for; matrix products, arithmetic and copies ran while one was open for 0% of the time, Pallas kernels for 16%

profile of v7, /device:TPU:0, one launch (start us, length us, event | category | flops | bytes accessed | tf_op | source)
XLA Modules:
  0.0 70.4 jit_solution(5421336873374361768)
XLA Ops:
  0.6 1.1 %shard_map.164 = (bf16[128,64]{1,0:T(8,128)(2,1)S(1)}, bf16[4,16,1024]{2,1,0:T(8,128)(2,1)S(1)}, bf16[4,16,1024]{2,1,0:T(8,128)(2,1)S(1)}) custom-call(s32[1,8,8]{2,1,0:T(8,128)} %lists_ref.1, bf16[2,32,1024]{2,1,0:T(8,128)(2,1)} %latents_ref.1), custom_call_target="tpu_custom_call" | custom-call | tf_op jit(solution)/shard_map/pallas_call | solution.py:39
  1.8 3.0 %collective-permute-start = (bf16[4,16,1024]{2,1,0:T(8,128)(2,1)S(1)}, bf16[4,16,1024]{2,1,0:T(8,128)(2,1)S(1)}, u32[]{:S(2)}, u32[]{:S(2)}) collective-permute-start(bf16[4,16,1024]{2,1,0:T(8,128)(2,1)S(1)} %get-tuple-element.61), channel_id=1, source_target_pairs={{0,2},{2,0},{4,6},{6,4},{8,10},{10,8},{12,14},{14,12},{1,3},{3,1},... | collective-permute-start | bytes 393224 | tf_op jit(solution)/shard_map/ppermute | solution.py:56
  4.8 2.6 %shard_map.165 = (bf16[256,512]{1,0:T(8,128)(2,1)S(1)}, bf16[1024,1024]{1,0:T(8,128)(2,1)S(1)}, f32[1024]{0:T(1024)S(1)}, bf16[256,1024]{1,0:T(8,128)(2,1)S(1)},...) custom-call(bf16[128,64]{1,0:T(8,128)(2,1)S(1)} %get-tuple-element.52.refs_0_.pick_ref, ...), custom_call_target="tpu_custom_call" | custom-call | tf_op jit(solution)/shard_map/pallas_call | solution.py:39
  7.4 0.9 %collective-permute-done.refs_2_.near_ref = bf16[4,16,1024]{2,1,0:T(8,128)(2,1)S(1)} collective-permute-done((bf16[4,16,1024]{2,1,0:T(8,128)(2,1)S(1)}, bf16[4,16,1024]{2,1,0:T(8,128)(2,1)S(1)}, u32[]{:S(2)}, u32[]{:S(2)}) %collective-permute-start) | collective-permute-done | bytes 131104 | tf_op jit(solution)/shard_map/ppermute | solution.py:56
  8.3 3.9 %collective-permute-start.1 = (bf16[32,1024]{1,0:T(8,128)(2,1)S(1)}, bf16[32,1024]{1,0:T(8,128)(2,1)S(1)}, u32[]{:S(2)}, u32[]{:S(2)}) collective-permute-start(bf16[32,1024]{1,0:T(8,128)(2,1)S(1)} %get-tuple-element.62), channel_id=1, source_target_pairs={{0,12},{2,14},{4,8},{6,10},{8,4},{10,6},{12,0},{14,2},{1,13},{3,15... | collective-permute-start | bytes 196616 | tf_op jit(solution)/shard_map/ppermute | solution.py:56
  12.2 0.6 collective-permute-start.3
  12.8 2.0 %collective-permute-done.1.rest_0_ = bf16[32,1024]{1,0:T(8,128)(2,1)S(1)} collective-permute-done((bf16[32,1024]{1,0:T(8,128)(2,1)S(1)}, bf16[32,1024]{1,0:T(8,128)(2,1)S(1)}, u32[]{:S(2)}, u32[]{:S(2)}) %collective-permute-start.1) | collective-permute-done | bytes 65568 | tf_op jit(solution)/shard_map/ppermute | solution.py:56
  14.9 2.7 %collective-permute-done.2.rest_1_ = bf16[32,1024]{1,0:T(8,128)(2,1)S(1)} collective-permute-done((bf16[32,1024]{1,0:T(8,128)(2,1)S(1)}, bf16[32,1024]{1,0:T(8,128)(2,1)S(1)}, u32[]{:S(2)}, u32[]{:S(2)}) %collective-permute-start.2) | collective-permute-done | bytes 65568 | tf_op jit(solution)/shard_map/ppermute | solution.py:56
  17.6 3.5 %shard_map.167 = (f32[2,100,256]{2,1,0:T(8,128)S(1)}, bf16[2,100,256]{2,1,0:T(8,128)(2,1)S(1)}, bf16[512,1024]{1,0:T(8,128)(2,1)S(1)}, bf16[512,1024]{1,0:T(8,12...) custom-call(bf16[1024,1024]{1,0:T(8,128)(2,1)S(1)} %get-tuple-element.53.w_msg_ref, ...), custom_call_target="tpu_custom_call" | custom-call | tf_op jit(solution)/shard_map/pallas_call | solution.py:39
  21.1 0.9 %shard_map.168 = (bf16[2,2,4,64,512]{4,3,2,1,0:T(8,128)(2,1)S(1)}, bf16[2,2,4,64,512]{4,3,2,1,0:T(8,128)(2,1)S(1)}, bf16[2,4,64,128]{3,2,1,0:T(8,128)(2,1)S(1)}, bf16[2,4,64,128]{3,2,1,0:T(8,128)(2,1)S(1)}) custom-call(bf16[512,1024]{1,0:T(8,128)(2,1)S(1)} %get-tuple-element.68.normed_ref, bf16[512,1024]{1,0:T(8,128)(2,1)S(1)} %get-tuple-element.69.active_ref, ...), custom_call_target="tpu_custom_call" | custom-call | tf_op jit(solution)/shard_map/pallas_call | solution.py:39
  22.4 1.5 %shard_map.169 = (bf16[512,1024]{1,0:T(8,128)(2,1)S(1)}, bf16[128,512]{1,0:T(8,128)(2,1)S(1)}, f32[1]{0:T(128)}, bf16[256,1152]{1,0:T(8,128)(2,1)S(1)}, bf16[256,1152]{1,0:T(8,128)(2,1)S(1)}) custom-call(f32[2,100,256]{2,1,0:T(8,128)S(1)} %get-tuple-element.65.own_ref, bf16[2,100,256]{2,1,0:T(8,128)(2,1)S(1)} %collective-permute-done.4.other_ref, ...), custom_call_target="tpu_custom_call" | custom-call | tf_op jit(solution)/shard_map/pallas_call | solution.py:39
  24.7 1.6 %shard_map.170 = (f32[256,1152]{1,0:T(8,128)S(1)}, f32[256,1152]{1,0:T(8,128)S(1)}) custom-call(f32[1]{0:T(128)} %get-tuple-element.74.loss_ref, bf16[2,2,4,64,512]{4,3,2,1,0:T(8,128)(2,1)S(1)} %get-tuple-element.70.normed_t_ref, bf16[2,2,4,64,512]{4,3,2,1,0:T(8,128)(2,1)S(1)} %get-tuple-element.71.active_t_ref, ...), custom_call_target="tpu_custom_call" | custom-call | tf_op jit(solution)/shard_map/pallas_call | solution.py:39
  26.6 1.6 %collective-permute-start.14 = (bf16[128,1152]{1,0:T(8,128)(2,1)S(1)}, bf16[128,1152]{1,0:T(8,128)(2,1)S(1)}, u32[]{:S(2)}, u32[]{:S(2)}) collective-permute-start(bf16[128,1152]{1,0:T(8,128)(2,1)S(1)} %shard_map.171.refs_0_), channel_id=1, source_target_pairs={{0,2},{2,0},{4,6},{6,4},{8,10},{10,8},{12,14},{14,12},{1,3},{3,1},... | collective-permute-start | bytes 884744 | tf_op jit(solution)/shard_map/ppermute | solution.py:56
  28.2 1.7 %shard_map.172.refs_3_ = bf16[512,1024]{1,0:T(8,128)(2,1)S(1)} custom-call(bf16[128,1152]{1,0:T(8,128)(2,1)S(1)} %shard_map.171.refs_0_, bf16[512,1024]{1,0:T(8,128)(2,1)S(1)} %get-tuple-element.75.inner_ref.refs_1_, bf16[1024,1024]{1,0:T(8,128)(2,1)S(1)} %get-tuple-element.57.weights_ref.refs_2_, f32[1024]{0:T(1024)S(1)} %get-tuple-element.55.gain_ref.refs_3_, ...), custom_call_target="tpu_custom_call" | custom-call | flops 8000000000 | tf_op jit(solution)/shard_map/pallas_call | solution.py:39
  30.4 2.2 %collective-permute-start.10 = (bf16[32,1024]{1,0:T(8,128)(2,1)S(1)}, bf16[32,1024]{1,0:T(8,128)(2,1)S(1)}, u32[]{:S(2)}, u32[]{:S(2)}) collective-permute-start(bf16[32,1024]{1,0:T(8,128)(2,1)S(1)} %get-tuple-element.85), channel_id=1, source_target_pairs={{0,12},{2,14},{4,8},{6,10},{8,4},{10,6},{12,0},{14,2},{1,13},{3,15... | collective-permute-start | bytes 196616 | tf_op jit(solution)/shard_map/ppermute | solution.py:56
  32.6 2.2 %collective-permute-start.12 = (bf16[32,1024]{1,0:T(8,128)(2,1)S(1)}, bf16[32,1024]{1,0:T(8,128)(2,1)S(1)}, u32[]{:S(2)}, u32[]{:S(2)}) collective-permute-start(bf16[32,1024]{1,0:T(8,128)(2,1)S(1)} %get-tuple-element.87), channel_id=1, source_target_pairs={{0,4},{2,6},{4,0},{6,2},{8,12},{10,14},{12,8},{14,10},{1,5},{3,7},... | collective-permute-start | bytes 196616 | tf_op jit(solution)/shard_map/ppermute | solution.py:56
  34.8 0.7 %shard_map.174 = (bf16[128,1024]{1,0:T(8,128)(2,1)S(1)}, bf16[144,1024]{1,0:T(8,128)(2,1)S(1)}, bf16[144,1024]{1,0:T(8,128)(2,1)S(1)}, f32[256,1024]{1,0:T(8,128)S(1)}) custom-call(bf16[2,4,64,128]{3,2,1,0:T(8,128)(2,1)S(1)} %get-tuple-element.82.keep_ref, bf16[2,4,64,128]{3,2,1,0:T(8,128)(2,1)S(1)} %collective-permute-done.6.refs_1_.give_ref, ...), custom_call_target="tpu_custom_call" | custom-call | tf_op jit(solution)/shard_map/pallas_call | solution.py:39
  35.6 0.5 collective-permute-start.17
  36.1 1.1 %collective-permute-done.10.refs_3_.rest_0_.refs_1_ = bf16[32,1024]{1,0:T(8,128)(2,1)S(1)} collective-permute-done((bf16[32,1024]{1,0:T(8,128)(2,1)S(1)}, bf16[32,1024]{1,0:T(8,128)(2,1)S(1)}, u32[]{:S(2)}, u32[]{:S(2)}) %collective-permute-start.10) | collective-permute-done | bytes 65568 | tf_op jit(solution)/shard_map/ppermute | solution.py:56
  37.2 0.5 collective-permute-start.9
  37.7 1.8 %collective-permute-done.11.refs_4_.rest_1_.refs_2_ = bf16[32,1024]{1,0:T(8,128)(2,1)S(1)} collective-permute-done((bf16[32,1024]{1,0:T(8,128)(2,1)S(1)}, bf16[32,1024]{1,0:T(8,128)(2,1)S(1)}, u32[]{:S(2)}, u32[]{:S(2)}) %collective-permute-start.11) | collective-permute-done | bytes 65568 | tf_op jit(solution)/shard_map/ppermute | solution.py:56
  39.7 2.4 %collective-permute-start.15 = (bf16[64,1152]{1,0:T(8,128)(2,1)S(1)}, bf16[64,1152]{1,0:T(8,128)(2,1)S(1)}, u32[]{:S(2)}, u32[]{:S(2)}) collective-permute-start(bf16[64,1152]{1,0:T(8,128)(2,1)S(1)} %get-tuple-element.92), channel_id=1, source_target_pairs={{0,12},{2,14},{4,8},{6,10},{8,4},{10,6},{12,0},{14,2},{1,13},{3,15... | collective-permute-start | bytes 442376 | tf_op jit(solution)/shard_map/ppermute | solution.py:56
  42.1 7.7 %collective-permute-done.9.refs_0_.refs_7_ = bf16[144,1024]{1,0:T(8,128)(2,1)S(1)} collective-permute-done((bf16[144,1024]{1,0:T(8,128)(2,1)S(1)}, bf16[144,1024]{1,0:T(8,128)(2,1)S(1)}, u32[]{:S(2)}, u32[]{:S(2)}) %collective-permute-start.9) | collective-permute-done | bytes 294944 | tf_op jit(solution)/shard_map/ppermute | solution.py:56
  49.8 0.5 collective-permute-start.13
  50.5 4.1 %collective-permute-done.16.refs_1_.refs_5_ = bf16[64,1152]{1,0:T(8,128)(2,1)S(1)} collective-permute-done((bf16[64,1152]{1,0:T(8,128)(2,1)S(1)}, bf16[64,1152]{1,0:T(8,128)(2,1)S(1)}, u32[]{:S(2)}, u32[]{:S(2)}) %collective-permute-start.16) | collective-permute-done | bytes 147488 | tf_op jit(solution)/shard_map/ppermute | solution.py:56
  54.9 1.6 %collective-permute-start.19 = (bf16[64,1024]{1,0:T(8,128)(2,1)S(1)}, bf16[64,1024]{1,0:T(8,128)(2,1)S(1)}, u32[]{:S(2)}, u32[]{:S(2)}) collective-permute-start(bf16[64,1024]{1,0:T(8,128)(2,1)S(1)} %shard_map.178.refs_2_), channel_id=1, source_target_pairs={{0,12},{2,14},{4,8},{6,10},{8,4},{10,6},{12,0},{14,2},{1,13},{3,15... | collective-permute-start | bytes 393224 | tf_op jit(solution)/shard_map/ppermute | solution.py:56
  56.5 1.9 %collective-permute-start.20 = (bf16[64,1024]{1,0:T(8,128)(2,1)S(1)}, bf16[64,1024]{1,0:T(8,128)(2,1)S(1)}, u32[]{:S(2)}, u32[]{:S(2)}) collective-permute-start(bf16[64,1024]{1,0:T(8,128)(2,1)S(1)} %shard_map.179.refs_3_), channel_id=1, source_target_pairs={{0,8},{2,10},{4,12},{6,14},{8,0},{10,2},{12,4},{14,6},{1,9},{3,11}... | collective-permute-start | bytes 393224 | tf_op jit(solution)/shard_map/ppermute | solution.py:56
  58.3 2.0 %collective-permute-done.13.last_ref.refs_3_.refs_2_ = bf16[208,1024]{1,0:T(8,128)(2,1)S(1)} collective-permute-done((bf16[208,1024]{1,0:T(8,128)(2,1)S(1)}, bf16[208,1024]{1,0:T(8,128)(2,1)S(1)}, u32[]{:S(2)}, u32[]{:S(2)}) %collective-permute-start.13) | collective-permute-done | bytes 426016 | tf_op jit(solution)/shard_map/ppermute | solution.py:56
  60.3 1.5 %shard_map.176 = (bf16[2,32,1024]{2,1,0:T(8,128)(2,1)}, f32[8,128]{1,0:T(8,128)S(1)}) custom-call(bf16[128,64]{1,0:T(8,128)(2,1)S(1)} %get-tuple-element.52.refs_0_.pick_ref, bf16[1024,1024]{1,0:T(8,128)(2,1)S(1)} %copy-done, bf16[8,16,1024]{2,1,0:T(8,128)(2,1)S(1)} %get-tuple-element.81.slots_ref.refs_2_, ...), custom_call_target="tpu_custom_call" | custom-call | tf_op jit(solution)/shard_map/pallas_call | solution.py:39
  61.8 6.8 %collective-permute-done.18.refs_6_.refs_5_ = bf16[144,1024]{1,0:T(8,128)(2,1)S(1)} collective-permute-done((bf16[144,1024]{1,0:T(8,128)(2,1)S(1)}, bf16[144,1024]{1,0:T(8,128)(2,1)S(1)}, u32[]{:S(2)}, u32[]{:S(2)}) %collective-permute-start.18) | collective-permute-done | bytes 294944 | tf_op jit(solution)/shard_map/ppermute | solution.py:56
  68.6 1.0 %shard_map.181 = (f32[64,1024]{1,0:T(8,128)}, f32[64,100]{1,0:T(8,128)}, f32[1]{0:T(128)}, f32[8,128]{1,0:T(8,128)S(1)}) custom-call(f32[8,128]{1,0:T(8,128)S(1)} %get-tuple-element.89.refs_0_, f32[256,1152]{1,0:T(8,128)S(1)} %get-tuple-element.90.refs_4_.refs_1_, bf16[256,1152]{1,0:T(8,128)(2,1)S(1)} %collective-permute-done.5.refs_0_.refs_5_.refs_2_, ...), custom_call_target="tpu_custom_call" | custom-call | tf_op jit(solution)/shard_map/pallas_call | solution.py:39
  69.6 0.8 %shard_map.182 = f32[64,1024]{1,0:T(8,128)} custom-call(f32[8,128]{1,0:T(8,128)S(1)} %get-tuple-element.96.refs_0_, f32[256,1024]{1,0:T(8,128)S(1)} %get-tuple-element.94.near_ref.refs_6_.refs_1_, bf16[208,1024]{1,0:T(8,128)(2,1)S(1)} %collective-permute-done.13.last_ref.refs_3_.refs_2_, bf16[64,1024]{1,0:T(8,128)(2,1)S(1)} %collective-permute-done.19.refs_3_, ...), custom_call_target="tpu_custom_call" | custom-call | tf_op jit(solution)/shard_map/pallas_call | solution.py:39
  (35 shorter events, 2.6 us)
Async XLA Ops:
  1.8 6.5 %collective-permute-start = (bf16[4,16,1024]{2,1,0:T(8,128)(2,1)S(1)}, bf16[4,16,1024]{2,1,0:T(8,128)(2,1)S(1)}, u32[]{:S(2)}, u32[]{:S(2)}) collective-permute-start(bf16[4,16,1024]{2,1,0:T(8,128)(2,1)S(1)} %get-tuple-element.61), channel_id=1, source_target_pairs={{0,2},{2,0},{4,6},{6,4},{8,10},{10,8},{12,14},{14,12},{1,3},{3,1},... | collective-permute-start | bytes 393224 | tf_op jit(solution)/shard_map/ppermute | solution.py:56
  8.3 6.6 %collective-permute-start.1 = (bf16[32,1024]{1,0:T(8,128)(2,1)S(1)}, bf16[32,1024]{1,0:T(8,128)(2,1)S(1)}, u32[]{:S(2)}, u32[]{:S(2)}) collective-permute-start(bf16[32,1024]{1,0:T(8,128)(2,1)S(1)} %get-tuple-element.62), channel_id=1, source_target_pairs={{0,12},{2,14},{4,8},{6,10},{8,4},{10,6},{12,0},{14,2},{1,13},{3,15... | collective-permute-start | bytes 196616 | tf_op jit(solution)/shard_map/ppermute | solution.py:56
  12.2 5.4 %collective-permute-start.2 = (bf16[32,1024]{1,0:T(8,128)(2,1)S(1)}, bf16[32,1024]{1,0:T(8,128)(2,1)S(1)}, u32[]{:S(2)}, u32[]{:S(2)}) collective-permute-start(bf16[32,1024]{1,0:T(8,128)(2,1)S(1)} %get-tuple-element.63), channel_id=1, source_target_pairs={{0,8},{2,10},{4,12},{6,14},{8,0},{10,2},{12,4},{14,6},{1,9},{3,11}... | collective-permute-start | bytes 196616 | tf_op jit(solution)/shard_map/ppermute | solution.py:56
  12.2 5.4 %collective-permute-start.3 = (bf16[32,1024]{1,0:T(8,128)(2,1)S(1)}, bf16[32,1024]{1,0:T(8,128)(2,1)S(1)}, u32[]{:S(2)}, u32[]{:S(2)}) collective-permute-start(bf16[32,1024]{1,0:T(8,128)(2,1)S(1)} %get-tuple-element.64), channel_id=1, source_target_pairs={{0,4},{2,6},{4,0},{6,2},{8,12},{10,14},{12,8},{14,10},{1,5},{3,7},... | collective-permute-start | bytes 196616 | tf_op jit(solution)/shard_map/ppermute | solution.py:56
  21.0 1.4 %copy-start.1 = (f32[100,256]{1,0:T(8,128)S(1)}, f32[100,256]{1,0:T(8,128)}, u32[]{:S(2)}) copy-start(f32[100,256]{1,0:T(8,128)} %truth_ref.1) | copy-start | bytes 307204
  21.1 1.4 %copy-start.2 = (f32[256]{0:T(256)S(1)}, f32[256]{0:T(256)}, u32[]{:S(2)}) copy-start(f32[256]{0:T(256)} %cell_ref.1) | copy-start | bytes 3076
  21.1 1.4 %collective-permute-start.4 = (bf16[2,100,256]{2,1,0:T(8,128)(2,1)S(1)}, bf16[2,100,256]{2,1,0:T(8,128)(2,1)S(1)}, u32[]{:S(2)}, u32[]{:S(2)}) collective-permute-start(bf16[2,100,256]{2,1,0:T(8,128)(2,1)S(1)} %get-tuple-element.66), channel_id=1, source_target_pairs={{0,1},{1,0},{2,3},{3,2},{4,5},{5,4},{6,7},{7,6},{8,9},{9,8},{10,11... | collective-permute-start | bytes 307208 | tf_op jit(solution)/shard_map/ppermute | solution.py:56
  24.0 2.4 %collective-permute-start.7 = (bf16[256,1152]{1,0:T(8,128)(2,1)S(1)}, bf16[256,1152]{1,0:T(8,128)(2,1)S(1)}, u32[]{:S(2)}, u32[]{:S(2)}) collective-permute-start(bf16[256,1152]{1,0:T(8,128)(2,1)S(1)} %get-tuple-element.78), channel_id=1, source_target_pairs={{0,1},{1,0},{2,3},{3,2},{4,5},{5,4},{6,7},{7,6},{8,9},{9,8},{10,11... | collective-permute-start | bytes 1769480 | tf_op jit(solution)/shard_map/ppermute | solution.py:56
  24.2 5.6 %collective-permute-start.6 = (bf16[2,4,64,128]{3,2,1,0:T(8,128)(2,1)S(1)}, bf16[2,4,64,128]{3,2,1,0:T(8,128)(2,1)S(1)}, u32[]{:S(2)}, u32[]{:S(2)}) collective-permute-start(bf16[2,4,64,128]{3,2,1,0:T(8,128)(2,1)S(1)} %get-tuple-element.73), channel_id=1, source_target_pairs={{0,1},{1,0},{2,3},{3,2},{4,5},{5,4},{6,7},{7,6},{8,9},{9,8},{10,11... | collective-permute-start | bytes 393224 | tf_op jit(solution)/shard_map/ppermute | solution.py:56
  24.6 5.3 %collective-permute-start.5 = (bf16[256,1152]{1,0:T(8,128)(2,1)S(1)}, bf16[256,1152]{1,0:T(8,128)(2,1)S(1)}, u32[]{:S(2)}, u32[]{:S(2)}) collective-permute-start(bf16[256,1152]{1,0:T(8,128)(2,1)S(1)} %get-tuple-element.72), channel_id=1, source_target_pairs={{0,1},{1,0},{2,3},{3,2},{4,5},{5,4},{6,7},{7,6},{8,9},{9,8},{10,11... | collective-permute-start | bytes 1769480 | tf_op jit(solution)/shard_map/ppermute | solution.py:56
  26.6 13.0 %collective-permute-start.14 = (bf16[128,1152]{1,0:T(8,128)(2,1)S(1)}, bf16[128,1152]{1,0:T(8,128)(2,1)S(1)}, u32[]{:S(2)}, u32[]{:S(2)}) collective-permute-start(bf16[128,1152]{1,0:T(8,128)(2,1)S(1)} %shard_map.171.refs_0_), channel_id=1, source_target_pairs={{0,2},{2,0},{4,6},{6,4},{8,10},{10,8},{12,14},{14,12},{1,3},{3,1},... | collective-permute-start | bytes 884744 | tf_op jit(solution)/shard_map/ppermute | solution.py:56
  30.3 4.5 %collective-permute-start.8 = (bf16[8,16,1024]{2,1,0:T(8,128)(2,1)S(1)}, bf16[8,16,1024]{2,1,0:T(8,128)(2,1)S(1)}, u32[]{:S(2)}, u32[]{:S(2)}) collective-permute-start(bf16[8,16,1024]{2,1,0:T(8,128)(2,1)S(1)} %get-tuple-element.81.slots_ref.refs_2_), channel_id=1, source_target_pairs={{0,1},{1,0},{2,3},{3,2},{4,5},{5,4},{6,7},{7,6},{8,9},{9,8},{10,11... | collective-permute-start | bytes 786440 | tf_op jit(solution)/shard_map/ppermute | solution.py:56
  30.4 6.8 %collective-permute-start.10 = (bf16[32,1024]{1,0:T(8,128)(2,1)S(1)}, bf16[32,1024]{1,0:T(8,128)(2,1)S(1)}, u32[]{:S(2)}, u32[]{:S(2)}) collective-permute-start(bf16[32,1024]{1,0:T(8,128)(2,1)S(1)} %get-tuple-element.85), channel_id=1, source_target_pairs={{0,12},{2,14},{4,8},{6,10},{8,4},{10,6},{12,0},{14,2},{1,13},{3,15... | collective-permute-start | bytes 196616 | tf_op jit(solution)/shard_map/ppermute | solution.py:56
  32.6 6.9 %collective-permute-start.11 = (bf16[32,1024]{1,0:T(8,128)(2,1)S(1)}, bf16[32,1024]{1,0:T(8,128)(2,1)S(1)}, u32[]{:S(2)}, u32[]{:S(2)}) collective-permute-start(bf16[32,1024]{1,0:T(8,128)(2,1)S(1)} %get-tuple-element.86), channel_id=1, source_target_pairs={{0,8},{2,10},{4,12},{6,14},{8,0},{10,2},{12,4},{14,6},{1,9},{3,11}... | collective-permute-start | bytes 196616 | tf_op jit(solution)/shard_map/ppermute | solution.py:56
  32.6 6.9 %collective-permute-start.12 = (bf16[32,1024]{1,0:T(8,128)(2,1)S(1)}, bf16[32,1024]{1,0:T(8,128)(2,1)S(1)}, u32[]{:S(2)}, u32[]{:S(2)}) collective-permute-start(bf16[32,1024]{1,0:T(8,128)(2,1)S(1)} %get-tuple-element.87), channel_id=1, source_target_pairs={{0,4},{2,6},{4,0},{6,2},{8,12},{10,14},{12,8},{14,10},{1,5},{3,7},... | collective-permute-start | bytes 196616 | tf_op jit(solution)/shard_map/ppermute | solution.py:56
  35.6 14.8 %collective-permute-start.17 = (bf16[128,1024]{1,0:T(8,128)(2,1)S(1)}, bf16[128,1024]{1,0:T(8,128)(2,1)S(1)}, u32[]{:S(2)}, u32[]{:S(2)}) collective-permute-start(bf16[128,1024]{1,0:T(8,128)(2,1)S(1)} %get-tuple-element.91.refs_0_), channel_id=1, source_target_pairs={{0,2},{2,0},{4,6},{6,4},{8,10},{10,8},{12,14},{14,12},{1,3},{3,1},... | collective-permute-start | bytes 786440 | tf_op jit(solution)/shard_map/ppermute | solution.py:56
  37.2 12.5 %collective-permute-start.9 = (bf16[144,1024]{1,0:T(8,128)(2,1)S(1)}, bf16[144,1024]{1,0:T(8,128)(2,1)S(1)}, u32[]{:S(2)}, u32[]{:S(2)}) collective-permute-start(bf16[144,1024]{1,0:T(8,128)(2,1)S(1)} %get-tuple-element.83), channel_id=1, source_target_pairs={{0,2},{2,0},{4,6},{6,4},{8,10},{10,8},{12,14},{14,12},{1,3},{3,1},... | collective-permute-start | bytes 884744 | tf_op jit(solution)/shard_map/ppermute | solution.py:56
  39.7 10.7 %collective-permute-start.15 = (bf16[64,1152]{1,0:T(8,128)(2,1)S(1)}, bf16[64,1152]{1,0:T(8,128)(2,1)S(1)}, u32[]{:S(2)}, u32[]{:S(2)}) collective-permute-start(bf16[64,1152]{1,0:T(8,128)(2,1)S(1)} %get-tuple-element.92), channel_id=1, source_target_pairs={{0,12},{2,14},{4,8},{6,10},{8,4},{10,6},{12,0},{14,2},{1,13},{3,15... | collective-permute-start | bytes 442376 | tf_op jit(solution)/shard_map/ppermute | solution.py:56
  42.1 12.4 %collective-permute-start.16 = (bf16[64,1152]{1,0:T(8,128)(2,1)S(1)}, bf16[64,1152]{1,0:T(8,128)(2,1)S(1)}, u32[]{:S(2)}, u32[]{:S(2)}) collective-permute-start(bf16[64,1152]{1,0:T(8,128)(2,1)S(1)} %get-tuple-element.93), channel_id=1, source_target_pairs={{0,8},{2,10},{4,12},{6,14},{8,0},{10,2},{12,4},{14,6},{1,9},{3,11}... | collective-permute-start | bytes 442376 | tf_op jit(solution)/shard_map/ppermute | solution.py:56
  49.8 10.5 %collective-permute-start.13 = (bf16[208,1024]{1,0:T(8,128)(2,1)S(1)}, bf16[208,1024]{1,0:T(8,128)(2,1)S(1)}, u32[]{:S(2)}, u32[]{:S(2)}) collective-permute-start(bf16[208,1024]{1,0:T(8,128)(2,1)S(1)} %shard_map.175), channel_id=1, source_target_pairs={{0,2},{2,0},{4,6},{6,4},{8,10},{10,8},{12,14},{14,12},{1,3},{3,1},... | collective-permute-start | bytes 1277960 | tf_op jit(solution)/shard_map/ppermute | solution.py:56
  50.4 9.9 %copy-start = (bf16[1024,1024]{1,0:T(8,128)(2,1)S(1)}, bf16[1024,1024]{1,0:T(8,128)(2,1)}, u32[]{:S(2)}) copy-start(bf16[1024,1024]{1,0:T(8,128)(2,1)} %w_msg_ref.1) | copy-start | bytes 6291460
  54.8 13.8 %collective-permute-start.18 = (bf16[144,1024]{1,0:T(8,128)(2,1)S(1)}, bf16[144,1024]{1,0:T(8,128)(2,1)S(1)}, u32[]{:S(2)}, u32[]{:S(2)}) collective-permute-start(bf16[144,1024]{1,0:T(8,128)(2,1)S(1)} %shard_map.180), channel_id=1, source_target_pairs={{0,4},{2,6},{4,0},{6,2},{8,12},{10,14},{12,8},{14,10},{1,5},{3,7},... | collective-permute-start | bytes 884744 | tf_op jit(solution)/shard_map/ppermute | solution.py:56
  54.9 14.7 %collective-permute-start.19 = (bf16[64,1024]{1,0:T(8,128)(2,1)S(1)}, bf16[64,1024]{1,0:T(8,128)(2,1)S(1)}, u32[]{:S(2)}, u32[]{:S(2)}) collective-permute-start(bf16[64,1024]{1,0:T(8,128)(2,1)S(1)} %shard_map.178.refs_2_), channel_id=1, source_target_pairs={{0,12},{2,14},{4,8},{6,10},{8,4},{10,6},{12,0},{14,2},{1,13},{3,15... | collective-permute-start | bytes 393224 | tf_op jit(solution)/shard_map/ppermute | solution.py:56
  56.5 13.1 %collective-permute-start.20 = (bf16[64,1024]{1,0:T(8,128)(2,1)S(1)}, bf16[64,1024]{1,0:T(8,128)(2,1)S(1)}, u32[]{:S(2)}, u32[]{:S(2)}) collective-permute-start(bf16[64,1024]{1,0:T(8,128)(2,1)S(1)} %shard_map.179.refs_3_), channel_id=1, source_target_pairs={{0,8},{2,10},{4,12},{6,14},{8,0},{10,2},{12,4},{14,6},{1,9},{3,11}... | collective-permute-start | bytes 393224 | tf_op jit(solution)/shard_map/ppermute | solution.py:56

commit v8 on v3

--- a/solution.py
+++ b/solution.py
@@ -360,11 +360,9 @@
         out_ref[:, width:] = part.astype(bf16)
 
 
-def message_early_kernel(near_ref, arrived_ref, *out_refs):
-    block = out_refs[0].shape[0]
-    for i, out_ref in enumerate(out_refs):
-        here = slice(i * block, (i + 1) * block)
-        out_ref[...] = (near_ref[here, :] + arrived_ref[here, :].astype(f32)).astype(bf16)
+def message_early_kernel(begin, near_ref, arrived_ref, out_ref):
+    here = slice(begin, begin + out_ref.shape[0])
+    out_ref[...] = (near_ref[here, :] + arrived_ref[here, :].astype(f32)).astype(bf16)
 
 
 def late_kernel(variables, early, held_ref, other_ref, near_ref, arrived_ref, *out_refs):
@@ -620,13 +618,16 @@
         limit=6,
     )
     hidden_parts = spread(hidden_early, steps[:early])
-    message_early = call(
-        message_early_kernel,
-        [((block, width), bf16)] * early,
-        [message_near, message_first_other],
-        limit=6,
-    )
-    message_parts = spread(message_early, steps[:early])
+    message_parts = []
+    for i in range(early):
+        (piece,) = call(
+            functools.partial(message_early_kernel, i * block),
+            [((block, width), bf16)],
+            [message_near, message_first_other],
+            limit=6,
+            after=hidden_parts[:i],
+        )
+        message_parts.append(swap(piece, "space", peers, steps[i]))
     late = call(
         functools.partial(late_kernel, variables, early),
         [((2 * block + packed, width), bf16)] * (levels - 1 - early),

time: 67.8 us -> 67.2 us (level)
  waiting for transfers between devices: 26.6 us -> 22.1 us
  starting transfers between devices: 22 us -> 25.9 us
    ppermute x21, waiting for transfers between devices: 26.6 us -> 22.1 us  [swap(): return lax.ppermute(value, axis, [(i, i ^ step) for i in range(size)])]
    ppermute x21, starting transfers between devices: 22 us -> 25.9 us  [swap(): return lax.ppermute(value, axis, [(i, i ^ step) for i in range(size)])]
    pallas_call x18 -> x19, Pallas kernels: 18.1 us -> 18.1 us  [call(): pl.pallas_call(inner if count else body, out_shape=[jax.ShapeDtypeStruct(...]
  transfers between devices with their start and end apart: 21 -> 21, of which waited for: 10 -> 11; matrix products, arithmetic and copies ran while one was open for 0% -> 0% of each run, Pallas kernels for 16% -> 17%
where the time goes in v8:
time: 67.2 us; the launch traced here: 66.9 us
  starting transfers between devices  25.9 us (39%)
  waiting for transfers between devices  22.1 us (33%)
  Pallas kernels  18.1 us (27%)
  between operations  0.83 us (1%)
    ppermute x21, starting transfers between devices, swap(): return lax.ppermute(value, axis, [(i, i ^ step) for i in range(size)])  25.9 us
    ppermute x21, waiting for transfers between devices, swap(): return lax.ppermute(value, axis, [(i, i ^ step) for i in range(size)])  22.1 us
    pallas_call x19, Pallas kernels, call(): pl.pallas_call(inner if count else body, out_shape=[jax.ShapeDtypeStruct(...  18.1 us
  transfers between devices with their start and end apart: 21, of which 11 were waited for; matrix products, arithmetic and copies ran while one was open for 0% of the time, Pallas kernels for 17%

profile of v8, /device:TPU:0, one launch (start us, length us, event | category | flops | bytes accessed | tf_op | source)
XLA Modules:
  0.0 66.9 jit_solution(15423449744879238262)
XLA Ops:
  0.6 1.1 %shard_map.164 = (bf16[128,64]{1,0:T(8,128)(2,1)S(1)}, bf16[4,16,1024]{2,1,0:T(8,128)(2,1)S(1)}, bf16[4,16,1024]{2,1,0:T(8,128)(2,1)S(1)}) custom-call(s32[1,8,8]{2,1,0:T(8,128)} %lists_ref.1, bf16[2,32,1024]{2,1,0:T(8,128)(2,1)} %latents_ref.1), custom_call_target="tpu_custom_call" | custom-call | tf_op jit(solution)/shard_map/pallas_call | solution.py:46
  1.8 3.0 %collective-permute-start = (bf16[4,16,1024]{2,1,0:T(8,128)(2,1)S(1)}, bf16[4,16,1024]{2,1,0:T(8,128)(2,1)S(1)}, u32[]{:S(2)}, u32[]{:S(2)}) collective-permute-start(bf16[4,16,1024]{2,1,0:T(8,128)(2,1)S(1)} %get-tuple-element.61), channel_id=1, source_target_pairs={{0,2},{2,0},{4,6},{6,4},{8,10},{10,8},{12,14},{14,12},{1,3},{3,1},... | collective-permute-start | bytes 393224 | tf_op jit(solution)/shard_map/ppermute | solution.py:63
  4.8 2.6 %shard_map.165 = (bf16[256,512]{1,0:T(8,128)(2,1)S(1)}, bf16[1024,1024]{1,0:T(8,128)(2,1)S(1)}, f32[1024]{0:T(1024)S(1)}, bf16[256,1024]{1,0:T(8,128)(2,1)S(1)},...) custom-call(bf16[128,64]{1,0:T(8,128)(2,1)S(1)} %get-tuple-element.52.refs_0_.pick_ref, ...), custom_call_target="tpu_custom_call" | custom-call | tf_op jit(solution)/shard_map/pallas_call | solution.py:46
  7.4 0.9 %collective-permute-done.refs_2_.near_ref = bf16[4,16,1024]{2,1,0:T(8,128)(2,1)S(1)} collective-permute-done((bf16[4,16,1024]{2,1,0:T(8,128)(2,1)S(1)}, bf16[4,16,1024]{2,1,0:T(8,128)(2,1)S(1)}, u32[]{:S(2)}, u32[]{:S(2)}) %collective-permute-start) | collective-permute-done | bytes 131104 | tf_op jit(solution)/shard_map/ppermute | solution.py:63
  8.3 3.9 %collective-permute-start.1 = (bf16[32,1024]{1,0:T(8,128)(2,1)S(1)}, bf16[32,1024]{1,0:T(8,128)(2,1)S(1)}, u32[]{:S(2)}, u32[]{:S(2)}) collective-permute-start(bf16[32,1024]{1,0:T(8,128)(2,1)S(1)} %get-tuple-element.62), channel_id=1, source_target_pairs={{0,12},{2,14},{4,8},{6,10},{8,4},{10,6},{12,0},{14,2},{1,13},{3,15... | collective-permute-start | bytes 196616 | tf_op jit(solution)/shard_map/ppermute | solution.py:63
  12.2 0.6 collective-permute-start.3
  12.8 2.0 %collective-permute-done.1.rest_0_ = bf16[32,1024]{1,0:T(8,128)(2,1)S(1)} collective-permute-done((bf16[32,1024]{1,0:T(8,128)(2,1)S(1)}, bf16[32,1024]{1,0:T(8,128)(2,1)S(1)}, u32[]{:S(2)}, u32[]{:S(2)}) %collective-permute-start.1) | collective-permute-done | bytes 65568 | tf_op jit(solution)/shard_map/ppermute | solution.py:63
  14.9 2.7 %collective-permute-done.2.rest_1_ = bf16[32,1024]{1,0:T(8,128)(2,1)S(1)} collective-permute-done((bf16[32,1024]{1,0:T(8,128)(2,1)S(1)}, bf16[32,1024]{1,0:T(8,128)(2,1)S(1)}, u32[]{:S(2)}, u32[]{:S(2)}) %collective-permute-start.2) | collective-permute-done | bytes 65568 | tf_op jit(solution)/shard_map/ppermute | solution.py:63
  17.6 3.5 %shard_map.167 = (f32[2,100,256]{2,1,0:T(8,128)S(1)}, bf16[2,100,256]{2,1,0:T(8,128)(2,1)S(1)}, bf16[512,1024]{1,0:T(8,128)(2,1)S(1)}, bf16[512,1024]{1,0:T(8,12...) custom-call(bf16[1024,1024]{1,0:T(8,128)(2,1)S(1)} %get-tuple-element.53.w_msg_ref, ...), custom_call_target="tpu_custom_call" | custom-call | tf_op jit(solution)/shard_map/pallas_call | solution.py:46
  21.1 0.9 %shard_map.168 = (bf16[2,2,4,64,512]{4,3,2,1,0:T(8,128)(2,1)S(1)}, bf16[2,2,4,64,512]{4,3,2,1,0:T(8,128)(2,1)S(1)}, bf16[2,4,64,128]{3,2,1,0:T(8,128)(2,1)S(1)}, bf16[2,4,64,128]{3,2,1,0:T(8,128)(2,1)S(1)}) custom-call(bf16[512,1024]{1,0:T(8,128)(2,1)S(1)} %get-tuple-element.68.normed_ref, bf16[512,1024]{1,0:T(8,128)(2,1)S(1)} %get-tuple-element.69.active_ref, ...), custom_call_target="tpu_custom_call" | custom-call | tf_op jit(solution)/shard_map/pallas_call | solution.py:46
  22.4 1.6 %shard_map.169 = (bf16[512,1024]{1,0:T(8,128)(2,1)S(1)}, bf16[128,512]{1,0:T(8,128)(2,1)S(1)}, f32[1]{0:T(128)}, bf16[256,1152]{1,0:T(8,128)(2,1)S(1)}, bf16[256,1152]{1,0:T(8,128)(2,1)S(1)}) custom-call(f32[2,100,256]{2,1,0:T(8,128)S(1)} %get-tuple-element.65.own_ref, bf16[2,100,256]{2,1,0:T(8,128)(2,1)S(1)} %collective-permute-done.4.other_ref, ...), custom_call_target="tpu_custom_call" | custom-call | tf_op jit(solution)/shard_map/pallas_call | solution.py:46
  24.7 1.6 %shard_map.170 = (f32[256,1152]{1,0:T(8,128)S(1)}, f32[256,1152]{1,0:T(8,128)S(1)}) custom-call(f32[1]{0:T(128)} %get-tuple-element.74.loss_ref, bf16[2,2,4,64,512]{4,3,2,1,0:T(8,128)(2,1)S(1)} %get-tuple-element.70.normed_t_ref, bf16[2,2,4,64,512]{4,3,2,1,0:T(8,128)(2,1)S(1)} %get-tuple-element.71.active_t_ref, ...), custom_call_target="tpu_custom_call" | custom-call | tf_op jit(solution)/shard_map/pallas_call | solution.py:46
  26.6 1.6 %collective-permute-start.13 = (bf16[128,1152]{1,0:T(8,128)(2,1)S(1)}, bf16[128,1152]{1,0:T(8,128)(2,1)S(1)}, u32[]{:S(2)}, u32[]{:S(2)}) collective-permute-start(bf16[128,1152]{1,0:T(8,128)(2,1)S(1)} %shard_map.171.refs_0_), channel_id=1, source_target_pairs={{0,2},{2,0},{4,6},{6,4},{8,10},{10,8},{12,14},{14,12},{1,3},{3,1},... | collective-permute-start | bytes 884744 | tf_op jit(solution)/shard_map/ppermute | solution.py:63
  28.2 1.7 %shard_map.172.refs_3_ = bf16[512,1024]{1,0:T(8,128)(2,1)S(1)} custom-call(bf16[128,1152]{1,0:T(8,128)(2,1)S(1)} %shard_map.171.refs_0_, bf16[512,1024]{1,0:T(8,128)(2,1)S(1)} %get-tuple-element.75.inner_ref.refs_1_, bf16[1024,1024]{1,0:T(8,128)(2,1)S(1)} %get-tuple-element.57.weights_ref.refs_2_, f32[1024]{0:T(1024)S(1)} %get-tuple-element.55.gain_ref.refs_3_, ...), custom_call_target="tpu_custom_call" | custom-call | flops 8000000000 | tf_op jit(solution)/shard_map/pallas_call | solution.py:46
  30.4 2.2 %collective-permute-start.9 = (bf16[32,1024]{1,0:T(8,128)(2,1)S(1)}, bf16[32,1024]{1,0:T(8,128)(2,1)S(1)}, u32[]{:S(2)}, u32[]{:S(2)}) collective-permute-start(bf16[32,1024]{1,0:T(8,128)(2,1)S(1)} %get-tuple-element.84), channel_id=1, source_target_pairs={{0,12},{2,14},{4,8},{6,10},{8,4},{10,6},{12,0},{14,2},{1,13},{3,15... | collective-permute-start | bytes 196616 | tf_op jit(solution)/shard_map/ppermute | solution.py:63
  32.7 2.2 %collective-permute-start.11 = (bf16[32,1024]{1,0:T(8,128)(2,1)S(1)}, bf16[32,1024]{1,0:T(8,128)(2,1)S(1)}, u32[]{:S(2)}, u32[]{:S(2)}) collective-permute-start(bf16[32,1024]{1,0:T(8,128)(2,1)S(1)} %get-tuple-element.86), channel_id=1, source_target_pairs={{0,4},{2,6},{4,0},{6,2},{8,12},{10,14},{12,8},{14,10},{1,5},{3,7},... | collective-permute-start | bytes 196616 | tf_op jit(solution)/shard_map/ppermute | solution.py:63
  34.9 0.7 %shard_map.174 = (bf16[128,1024]{1,0:T(8,128)(2,1)S(1)}, bf16[144,1024]{1,0:T(8,128)(2,1)S(1)}, bf16[144,1024]{1,0:T(8,128)(2,1)S(1)}, f32[256,1024]{1,0:T(8,128)S(1)}) custom-call(bf16[2,4,64,128]{3,2,1,0:T(8,128)(2,1)S(1)} %get-tuple-element.82.keep_ref, bf16[2,4,64,128]{3,2,1,0:T(8,128)(2,1)S(1)} %collective-permute-done.6.refs_1_.give_ref, ...), custom_call_target="tpu_custom_call" | custom-call | tf_op jit(solution)/shard_map/pallas_call | solution.py:46
  35.6 0.5 collective-permute-start.18
  36.1 1.1 %collective-permute-done.9.rest_0_ = bf16[32,1024]{1,0:T(8,128)(2,1)S(1)} collective-permute-done((bf16[32,1024]{1,0:T(8,128)(2,1)S(1)}, bf16[32,1024]{1,0:T(8,128)(2,1)S(1)}, u32[]{:S(2)}, u32[]{:S(2)}) %collective-permute-start.9) | collective-permute-done | bytes 65568 | tf_op jit(solution)/shard_map/ppermute | solution.py:63
  37.7 1.8 %collective-permute-done.10.rest_1_ = bf16[32,1024]{1,0:T(8,128)(2,1)S(1)} collective-permute-done((bf16[32,1024]{1,0:T(8,128)(2,1)S(1)}, bf16[32,1024]{1,0:T(8,128)(2,1)S(1)}, u32[]{:S(2)}, u32[]{:S(2)}) %collective-permute-start.10) | collective-permute-done | bytes 65568 | tf_op jit(solution)/shard_map/ppermute | solution.py:63
  39.6 0.5 collective-permute-start.12
  40.3 2.4 %collective-permute-start.14 = (bf16[64,1152]{1,0:T(8,128)(2,1)S(1)}, bf16[64,1152]{1,0:T(8,128)(2,1)S(1)}, u32[]{:S(2)}, u32[]{:S(2)}) collective-permute-start(bf16[64,1152]{1,0:T(8,128)(2,1)S(1)} %get-tuple-element.90), channel_id=1, source_target_pairs={{0,12},{2,14},{4,8},{6,10},{8,4},{10,6},{12,0},{14,2},{1,13},{3,15... | collective-permute-start | bytes 442376 | tf_op jit(solution)/shard_map/ppermute | solution.py:63
  42.7 2.1 %collective-permute-done.18.arrived_ref.refs_2_ = bf16[128,1024]{1,0:T(8,128)(2,1)S(1)} collective-permute-done((bf16[128,1024]{1,0:T(8,128)(2,1)S(1)}, bf16[128,1024]{1,0:T(8,128)(2,1)S(1)}, u32[]{:S(2)}, u32[]{:S(2)}) %collective-permute-start.18) | collective-permute-done | bytes 262176 | tf_op jit(solution)/shard_map/ppermute | solution.py:63
  44.9 2.2 %collective-permute-start.19 = (bf16[64,1024]{1,0:T(8,128)(2,1)S(1)}, bf16[64,1024]{1,0:T(8,128)(2,1)S(1)}, u32[]{:S(2)}, u32[]{:S(2)}) collective-permute-start(bf16[64,1024]{1,0:T(8,128)(2,1)S(1)} %shard_map.180), channel_id=1, source_target_pairs={{0,12},{2,14},{4,8},{6,10},{8,4},{10,6},{12,0},{14,2},{1,13},{3,15... | collective-permute-start | bytes 393224 | tf_op jit(solution)/shard_map/ppermute | solution.py:63
  47.2 4.0 %collective-permute-done.16.arrived_ref = bf16[144,1024]{1,0:T(8,128)(2,1)S(1)} collective-permute-done((bf16[144,1024]{1,0:T(8,128)(2,1)S(1)}, bf16[144,1024]{1,0:T(8,128)(2,1)S(1)}, u32[]{:S(2)}, u32[]{:S(2)}) %collective-permute-start.16) | collective-permute-done | bytes 294944 | tf_op jit(solution)/shard_map/ppermute | solution.py:63
  51.6 5.1 %collective-permute-start.20 = (bf16[64,1024]{1,0:T(8,128)(2,1)S(1)}, bf16[64,1024]{1,0:T(8,128)(2,1)S(1)}, u32[]{:S(2)}, u32[]{:S(2)}) collective-permute-start(bf16[64,1024]{1,0:T(8,128)(2,1)S(1)} %shard_map.181), channel_id=1, source_target_pairs={{0,8},{2,10},{4,12},{6,14},{8,0},{10,2},{12,4},{14,6},{1,9},{3,11}... | collective-permute-start | bytes 393224 | tf_op jit(solution)/shard_map/ppermute | solution.py:63
  56.7 2.2 %collective-permute-done.12.last_ref.refs_3_.refs_2_ = bf16[208,1024]{1,0:T(8,128)(2,1)S(1)} collective-permute-done((bf16[208,1024]{1,0:T(8,128)(2,1)S(1)}, bf16[208,1024]{1,0:T(8,128)(2,1)S(1)}, u32[]{:S(2)}, u32[]{:S(2)}) %collective-permute-start.12) | collective-permute-done | bytes 426016 | tf_op jit(solution)/shard_map/ppermute | solution.py:63
  58.9 1.5 %shard_map.176 = (bf16[2,32,1024]{2,1,0:T(8,128)(2,1)}, f32[8,128]{1,0:T(8,128)S(1)}) custom-call(bf16[128,64]{1,0:T(8,128)(2,1)S(1)} %get-tuple-element.52.refs_0_.pick_ref, bf16[1024,1024]{1,0:T(8,128)(2,1)S(1)} %copy-done, bf16[8,16,1024]{2,1,0:T(8,128)(2,1)S(1)} %get-tuple-element.81.slots_ref, ...), custom_call_target="tpu_custom_call" | custom-call | tf_op jit(solution)/shard_map/pallas_call | solution.py:46
  60.5 2.7 %collective-permute-done.17.refs_6_.refs_5_ = bf16[144,1024]{1,0:T(8,128)(2,1)S(1)} collective-permute-done((bf16[144,1024]{1,0:T(8,128)(2,1)S(1)}, bf16[144,1024]{1,0:T(8,128)(2,1)S(1)}, u32[]{:S(2)}, u32[]{:S(2)}) %collective-permute-start.17) | collective-permute-done | bytes 294944 | tf_op jit(solution)/shard_map/ppermute | solution.py:63
  63.1 1.0 %shard_map.179 = (f32[64,1024]{1,0:T(8,128)}, f32[64,100]{1,0:T(8,128)}, f32[1]{0:T(128)}, f32[8,128]{1,0:T(8,128)S(1)}) custom-call(f32[8,128]{1,0:T(8,128)S(1)} %get-tuple-element.88.refs_0_, f32[256,1152]{1,0:T(8,128)S(1)} %get-tuple-element.89.held_ref.refs_1_, bf16[256,1152]{1,0:T(8,128)(2,1)S(1)} %collective-permute-done.5.refs_0_.other_ref.refs_2_, ...), custom_call_target="tpu_custom_call" | custom-call | tf_op jit(solution)/shard_map/pallas_call | solution.py:46
  64.1 2.0 %collective-permute-done.20.refs_4_ = bf16[64,1024]{1,0:T(8,128)(2,1)S(1)} collective-permute-done((bf16[64,1024]{1,0:T(8,128)(2,1)S(1)}, bf16[64,1024]{1,0:T(8,128)(2,1)S(1)}, u32[]{:S(2)}, u32[]{:S(2)}) %collective-permute-start.20) | collective-permute-done | bytes 131104 | tf_op jit(solution)/shard_map/ppermute | solution.py:63
  66.1 0.8 %shard_map.182 = f32[64,1024]{1,0:T(8,128)} custom-call(f32[8,128]{1,0:T(8,128)S(1)} %get-tuple-element.95.refs_0_, f32[256,1024]{1,0:T(8,128)S(1)} %get-tuple-element.92.near_ref.refs_1_, bf16[208,1024]{1,0:T(8,128)(2,1)S(1)} %collective-permute-done.12.last_ref.refs_3_.refs_2_, bf16[64,1024]{1,0:T(8,128)(2,1)S(1)} %collective-permute-done.19.refs_3_, ...), custom_call_target="tpu_custom_call" | custom-call | flops 8000000000 | tf_op jit(solution)/shard_map/pallas_call | solution.py:46
  (35 shorter events, 3.0 us)
Async XLA Ops:
  1.8 6.5 %collective-permute-start = (bf16[4,16,1024]{2,1,0:T(8,128)(2,1)S(1)}, bf16[4,16,1024]{2,1,0:T(8,128)(2,1)S(1)}, u32[]{:S(2)}, u32[]{:S(2)}) collective-permute-start(bf16[4,16,1024]{2,1,0:T(8,128)(2,1)S(1)} %get-tuple-element.61), channel_id=1, source_target_pairs={{0,2},{2,0},{4,6},{6,4},{8,10},{10,8},{12,14},{14,12},{1,3},{3,1},... | collective-permute-start | bytes 393224 | tf_op jit(solution)/shard_map/ppermute | solution.py:63
  8.3 6.6 %collective-permute-start.1 = (bf16[32,1024]{1,0:T(8,128)(2,1)S(1)}, bf16[32,1024]{1,0:T(8,128)(2,1)S(1)}, u32[]{:S(2)}, u32[]{:S(2)}) collective-permute-start(bf16[32,1024]{1,0:T(8,128)(2,1)S(1)} %get-tuple-element.62), channel_id=1, source_target_pairs={{0,12},{2,14},{4,8},{6,10},{8,4},{10,6},{12,0},{14,2},{1,13},{3,15... | collective-permute-start | bytes 196616 | tf_op jit(solution)/shard_map/ppermute | solution.py:63
  12.2 5.4 %collective-permute-start.2 = (bf16[32,1024]{1,0:T(8,128)(2,1)S(1)}, bf16[32,1024]{1,0:T(8,128)(2,1)S(1)}, u32[]{:S(2)}, u32[]{:S(2)}) collective-permute-start(bf16[32,1024]{1,0:T(8,128)(2,1)S(1)} %get-tuple-element.63), channel_id=1, source_target_pairs={{0,8},{2,10},{4,12},{6,14},{8,0},{10,2},{12,4},{14,6},{1,9},{3,11}... | collective-permute-start | bytes 196616 | tf_op jit(solution)/shard_map/ppermute | solution.py:63
  12.2 5.4 %collective-permute-start.3 = (bf16[32,1024]{1,0:T(8,128)(2,1)S(1)}, bf16[32,1024]{1,0:T(8,128)(2,1)S(1)}, u32[]{:S(2)}, u32[]{:S(2)}) collective-permute-start(bf16[32,1024]{1,0:T(8,128)(2,1)S(1)} %get-tuple-element.64), channel_id=1, source_target_pairs={{0,4},{2,6},{4,0},{6,2},{8,12},{10,14},{12,8},{14,10},{1,5},{3,7},... | collective-permute-start | bytes 196616 | tf_op jit(solution)/shard_map/ppermute | solution.py:63
  21.0 1.4 %copy-start.1 = (f32[100,256]{1,0:T(8,128)S(1)}, f32[100,256]{1,0:T(8,128)}, u32[]{:S(2)}) copy-start(f32[100,256]{1,0:T(8,128)} %truth_ref.1) | copy-start | bytes 307204
  21.1 1.4 %copy-start.2 = (f32[256]{0:T(256)S(1)}, f32[256]{0:T(256)}, u32[]{:S(2)}) copy-start(f32[256]{0:T(256)} %cell_ref.1) | copy-start | bytes 3076
  21.1 1.4 %collective-permute-start.4 = (bf16[2,100,256]{2,1,0:T(8,128)(2,1)S(1)}, bf16[2,100,256]{2,1,0:T(8,128)(2,1)S(1)}, u32[]{:S(2)}, u32[]{:S(2)}) collective-permute-start(bf16[2,100,256]{2,1,0:T(8,128)(2,1)S(1)} %get-tuple-element.66), channel_id=1, source_target_pairs={{0,1},{1,0},{2,3},{3,2},{4,5},{5,4},{6,7},{7,6},{8,9},{9,8},{10,11... | collective-permute-start | bytes 307208 | tf_op jit(solution)/shard_map/ppermute | solution.py:63
  24.0 2.3 %collective-permute-start.7 = (bf16[256,1152]{1,0:T(8,128)(2,1)S(1)}, bf16[256,1152]{1,0:T(8,128)(2,1)S(1)}, u32[]{:S(2)}, u32[]{:S(2)}) collective-permute-start(bf16[256,1152]{1,0:T(8,128)(2,1)S(1)} %get-tuple-element.78), channel_id=1, source_target_pairs={{0,1},{1,0},{2,3},{3,2},{4,5},{5,4},{6,7},{7,6},{8,9},{9,8},{10,11... | collective-permute-start | bytes 1769480 | tf_op jit(solution)/shard_map/ppermute | solution.py:63
  24.2 5.6 %collective-permute-start.6 = (bf16[2,4,64,128]{3,2,1,0:T(8,128)(2,1)S(1)}, bf16[2,4,64,128]{3,2,1,0:T(8,128)(2,1)S(1)}, u32[]{:S(2)}, u32[]{:S(2)}) collective-permute-start(bf16[2,4,64,128]{3,2,1,0:T(8,128)(2,1)S(1)} %get-tuple-element.73), channel_id=1, source_target_pairs={{0,1},{1,0},{2,3},{3,2},{4,5},{5,4},{6,7},{7,6},{8,9},{9,8},{10,11... | collective-permute-start | bytes 393224 | tf_op jit(solution)/shard_map/ppermute | solution.py:63
  24.6 5.3 %collective-permute-start.5 = (bf16[256,1152]{1,0:T(8,128)(2,1)S(1)}, bf16[256,1152]{1,0:T(8,128)(2,1)S(1)}, u32[]{:S(2)}, u32[]{:S(2)}) collective-permute-start(bf16[256,1152]{1,0:T(8,128)(2,1)S(1)} %get-tuple-element.72), channel_id=1, source_target_pairs={{0,1},{1,0},{2,3},{3,2},{4,5},{5,4},{6,7},{7,6},{8,9},{9,8},{10,11... | collective-permute-start | bytes 1769480 | tf_op jit(solution)/shard_map/ppermute | solution.py:63
  26.6 13.6 %collective-permute-start.13 = (bf16[128,1152]{1,0:T(8,128)(2,1)S(1)}, bf16[128,1152]{1,0:T(8,128)(2,1)S(1)}, u32[]{:S(2)}, u32[]{:S(2)}) collective-permute-start(bf16[128,1152]{1,0:T(8,128)(2,1)S(1)} %shard_map.171.refs_0_), channel_id=1, source_target_pairs={{0,2},{2,0},{4,6},{6,4},{8,10},{10,8},{12,14},{14,12},{1,3},{3,1},... | collective-permute-start | bytes 884744 | tf_op jit(solution)/shard_map/ppermute | solution.py:63
  30.3 4.5 %collective-permute-start.8 = (bf16[8,16,1024]{2,1,0:T(8,128)(2,1)S(1)}, bf16[8,16,1024]{2,1,0:T(8,128)(2,1)S(1)}, u32[]{:S(2)}, u32[]{:S(2)}) collective-permute-start(bf16[8,16,1024]{2,1,0:T(8,128)(2,1)S(1)} %get-tuple-element.81.slots_ref), channel_id=1, source_target_pairs={{0,1},{1,0},{2,3},{3,2},{4,5},{5,4},{6,7},{7,6},{8,9},{9,8},{10,11... | collective-permute-start | bytes 786440 | tf_op jit(solution)/shard_map/ppermute | solution.py:63
  30.4 6.8 %collective-permute-start.9 = (bf16[32,1024]{1,0:T(8,128)(2,1)S(1)}, bf16[32,1024]{1,0:T(8,128)(2,1)S(1)}, u32[]{:S(2)}, u32[]{:S(2)}) collective-permute-start(bf16[32,1024]{1,0:T(8,128)(2,1)S(1)} %get-tuple-element.84), channel_id=1, source_target_pairs={{0,12},{2,14},{4,8},{6,10},{8,4},{10,6},{12,0},{14,2},{1,13},{3,15... | collective-permute-start | bytes 196616 | tf_op jit(solution)/shard_map/ppermute | solution.py:63
  32.7 6.9 %collective-permute-start.10 = (bf16[32,1024]{1,0:T(8,128)(2,1)S(1)}, bf16[32,1024]{1,0:T(8,128)(2,1)S(1)}, u32[]{:S(2)}, u32[]{:S(2)}) collective-permute-start(bf16[32,1024]{1,0:T(8,128)(2,1)S(1)} %get-tuple-element.85), channel_id=1, source_target_pairs={{0,8},{2,10},{4,12},{6,14},{8,0},{10,2},{12,4},{14,6},{1,9},{3,11}... | collective-permute-start | bytes 196616 | tf_op jit(solution)/shard_map/ppermute | solution.py:63
  32.7 6.9 %collective-permute-start.11 = (bf16[32,1024]{1,0:T(8,128)(2,1)S(1)}, bf16[32,1024]{1,0:T(8,128)(2,1)S(1)}, u32[]{:S(2)}, u32[]{:S(2)}) collective-permute-start(bf16[32,1024]{1,0:T(8,128)(2,1)S(1)} %get-tuple-element.86), channel_id=1, source_target_pairs={{0,4},{2,6},{4,0},{6,2},{8,12},{10,14},{12,8},{14,10},{1,5},{3,7},... | collective-permute-start | bytes 196616 | tf_op jit(solution)/shard_map/ppermute | solution.py:63
  35.6 9.3 %collective-permute-start.18 = (bf16[128,1024]{1,0:T(8,128)(2,1)S(1)}, bf16[128,1024]{1,0:T(8,128)(2,1)S(1)}, u32[]{:S(2)}, u32[]{:S(2)}) collective-permute-start(bf16[128,1024]{1,0:T(8,128)(2,1)S(1)} %get-tuple-element.96), channel_id=1, source_target_pairs={{0,2},{2,0},{4,6},{6,4},{8,10},{10,8},{12,14},{14,12},{1,3},{3,1},... | collective-permute-start | bytes 786440 | tf_op jit(solution)/shard_map/ppermute | solution.py:63
  37.3 14.0 %collective-permute-start.16 = (bf16[144,1024]{1,0:T(8,128)(2,1)S(1)}, bf16[144,1024]{1,0:T(8,128)(2,1)S(1)}, u32[]{:S(2)}, u32[]{:S(2)}) collective-permute-start(bf16[144,1024]{1,0:T(8,128)(2,1)S(1)} %get-tuple-element.93), channel_id=1, source_target_pairs={{0,2},{2,0},{4,6},{6,4},{8,10},{10,8},{12,14},{14,12},{1,3},{3,1},... | collective-permute-start | bytes 884744 | tf_op jit(solution)/shard_map/ppermute | solution.py:63
  39.6 19.4 %collective-permute-start.12 = (bf16[208,1024]{1,0:T(8,128)(2,1)S(1)}, bf16[208,1024]{1,0:T(8,128)(2,1)S(1)}, u32[]{:S(2)}, u32[]{:S(2)}) collective-permute-start(bf16[208,1024]{1,0:T(8,128)(2,1)S(1)} %shard_map.175), channel_id=1, source_target_pairs={{0,2},{2,0},{4,6},{6,4},{8,10},{10,8},{12,14},{14,12},{1,3},{3,1},... | collective-permute-start | bytes 1277960 | tf_op jit(solution)/shard_map/ppermute | solution.py:63
  40.3 11.2 %collective-permute-start.14 = (bf16[64,1152]{1,0:T(8,128)(2,1)S(1)}, bf16[64,1152]{1,0:T(8,128)(2,1)S(1)}, u32[]{:S(2)}, u32[]{:S(2)}) collective-permute-start(bf16[64,1152]{1,0:T(8,128)(2,1)S(1)} %get-tuple-element.90), channel_id=1, source_target_pairs={{0,12},{2,14},{4,8},{6,10},{8,4},{10,6},{12,0},{14,2},{1,13},{3,15... | collective-permute-start | bytes 442376 | tf_op jit(solution)/shard_map/ppermute | solution.py:63
  42.7 17.7 %collective-permute-start.15 = (bf16[64,1152]{1,0:T(8,128)(2,1)S(1)}, bf16[64,1152]{1,0:T(8,128)(2,1)S(1)}, u32[]{:S(2)}, u32[]{:S(2)}) collective-permute-start(bf16[64,1152]{1,0:T(8,128)(2,1)S(1)} %get-tuple-element.91), channel_id=1, source_target_pairs={{0,8},{2,10},{4,12},{6,14},{8,0},{10,2},{12,4},{14,6},{1,9},{3,11}... | collective-permute-start | bytes 442376 | tf_op jit(solution)/shard_map/ppermute | solution.py:63
  44.9 19.2 %collective-permute-start.19 = (bf16[64,1024]{1,0:T(8,128)(2,1)S(1)}, bf16[64,1024]{1,0:T(8,128)(2,1)S(1)}, u32[]{:S(2)}, u32[]{:S(2)}) collective-permute-start(bf16[64,1024]{1,0:T(8,128)(2,1)S(1)} %shard_map.180), channel_id=1, source_target_pairs={{0,12},{2,14},{4,8},{6,10},{8,4},{10,6},{12,0},{14,2},{1,13},{3,15... | collective-permute-start | bytes 393224 | tf_op jit(solution)/shard_map/ppermute | solution.py:63
  51.4 7.5 %copy-start = (bf16[1024,1024]{1,0:T(8,128)(2,1)S(1)}, bf16[1024,1024]{1,0:T(8,128)(2,1)}, u32[]{:S(2)}) copy-start(bf16[1024,1024]{1,0:T(8,128)(2,1)} %w_msg_ref.1) | copy-start | bytes 6291460
  51.5 11.7 %collective-permute-start.17 = (bf16[144,1024]{1,0:T(8,128)(2,1)S(1)}, bf16[144,1024]{1,0:T(8,128)(2,1)S(1)}, u32[]{:S(2)}, u32[]{:S(2)}) collective-permute-start(bf16[144,1024]{1,0:T(8,128)(2,1)S(1)} %shard_map.178), channel_id=1, source_target_pairs={{0,4},{2,6},{4,0},{6,2},{8,12},{10,14},{12,8},{14,10},{1,5},{3,7},... | collective-permute-start | bytes 884744 | tf_op jit(solution)/shard_map/ppermute | solution.py:63
  51.6 14.6 %collective-permute-start.20 = (bf16[64,1024]{1,0:T(8,128)(2,1)S(1)}, bf16[64,1024]{1,0:T(8,128)(2,1)S(1)}, u32[]{:S(2)}, u32[]{:S(2)}) collective-permute-start(bf16[64,1024]{1,0:T(8,128)(2,1)S(1)} %shard_map.181), channel_id=1, source_target_pairs={{0,8},{2,10},{4,12},{6,14},{8,0},{10,2},{12,4},{14,6},{1,9},{3,11}... | collective-permute-start | bytes 393224 | tf_op jit(solution)/shard_map/ppermute | solution.py:63

commit v9 on v8

--- a/solution.py
+++ b/solution.py
@@ -604,20 +604,21 @@
     )
     message_first_other = swap(message_first, "space", peers, 1)
     middle_other = swap(middle, "space", peers, 1)
+    hidden_early = call(
+        functools.partial(hidden_early_kernel, variables, width),
+        [((block, wide), bf16)] * early,
+        [held_near, near_other, first_other],
+        limit=6,
+    )
+    hidden_parts = spread(hidden_early, steps[:early])
     (last,) = call(
         ride_kernel,
         [((2 * block + packed + levels * rows_peer, width), bf16)],
         [last, slots] + slots_arrived,
         limit=4,
+        after=hidden_early[:1],
     )
     last_other = swap(last, "space", peers, 1)
-    hidden_early = call(
-        functools.partial(hidden_early_kernel, variables, width),
-        [((block, wide), bf16)] * early,
-        [held_near, near_other, first_other],
-        limit=6,
-    )
-    hidden_parts = spread(hidden_early, steps[:early])
     message_parts = []
     for i in range(early):
         (piece,) = call(

time: 67.2 us -> 65.2 us (0.970)
  waiting for transfers between devices: 22.1 us -> 16.2 us
  starting transfers between devices: 25.9 us -> 29.8 us
    ppermute x21, waiting for transfers between devices: 22.1 us -> 16.2 us  [swap(): return lax.ppermute(value, axis, [(i, i ^ step) for i in range(size)])]
    ppermute x21, starting transfers between devices: 25.9 us -> 29.8 us  [swap(): return lax.ppermute(value, axis, [(i, i ^ step) for i in range(size)])]
  transfers between devices with their start and end apart: 21 -> 21, of which waited for: 11 -> 8; matrix products, arithmetic and copies ran while one was open for 0% -> 0% of each run, Pallas kernels for 17% -> 17%
where the time goes in v9:
time: 65.2 us; the launch traced here: 64.9 us
  starting transfers between devices  29.8 us (46%)
  Pallas kernels  18.1 us (28%)
  waiting for transfers between devices  16.2 us (25%)
  between operations  0.84 us (1%)
    ppermute x21, starting transfers between devices, swap(): return lax.ppermute(value, axis, [(i, i ^ step) for i in range(size)])  29.8 us
    pallas_call x19, Pallas kernels, call(): pl.pallas_call(inner if count else body, out_shape=[jax.ShapeDtypeStruct(...  18.1 us
    ppermute x21, waiting for transfers between devices, swap(): return lax.ppermute(value, axis, [(i, i ^ step) for i in range(size)])  16.2 us
  transfers between devices with their start and end apart: 21, of which 8 were waited for; matrix products, arithmetic and copies ran while one was open for 0% of the time, Pallas kernels for 17%

profile of v9, /device:TPU:0, one launch (start us, length us, event | category | flops | bytes accessed | tf_op | source)
XLA Modules:
  0.0 64.9 jit_solution(10201313933735770986)
XLA Ops:
  0.6 1.1 %shard_map.164 = (bf16[128,64]{1,0:T(8,128)(2,1)S(1)}, bf16[4,16,1024]{2,1,0:T(8,128)(2,1)S(1)}, bf16[4,16,1024]{2,1,0:T(8,128)(2,1)S(1)}) custom-call(s32[1,8,8]{2,1,0:T(8,128)} %lists_ref.1, bf16[2,32,1024]{2,1,0:T(8,128)(2,1)} %latents_ref.1), custom_call_target="tpu_custom_call" | custom-call | tf_op jit(solution)/shard_map/pallas_call | solution.py:46
  1.8 3.0 %collective-permute-start = (bf16[4,16,1024]{2,1,0:T(8,128)(2,1)S(1)}, bf16[4,16,1024]{2,1,0:T(8,128)(2,1)S(1)}, u32[]{:S(2)}, u32[]{:S(2)}) collective-permute-start(bf16[4,16,1024]{2,1,0:T(8,128)(2,1)S(1)} %get-tuple-element.61), channel_id=1, source_target_pairs={{0,2},{2,0},{4,6},{6,4},{8,10},{10,8},{12,14},{14,12},{1,3},{3,1},... | collective-permute-start | bytes 393224 | tf_op jit(solution)/shard_map/ppermute | solution.py:63
  4.8 2.6 %shard_map.165 = (bf16[256,512]{1,0:T(8,128)(2,1)S(1)}, bf16[1024,1024]{1,0:T(8,128)(2,1)S(1)}, f32[1024]{0:T(1024)S(1)}, bf16[256,1024]{1,0:T(8,128)(2,1)S(1)},...) custom-call(bf16[128,64]{1,0:T(8,128)(2,1)S(1)} %get-tuple-element.52.refs_0_.pick_ref, ...), custom_call_target="tpu_custom_call" | custom-call | tf_op jit(solution)/shard_map/pallas_call | solution.py:46
  7.4 0.9 %collective-permute-done.refs_2_.near_ref = bf16[4,16,1024]{2,1,0:T(8,128)(2,1)S(1)} collective-permute-done((bf16[4,16,1024]{2,1,0:T(8,128)(2,1)S(1)}, bf16[4,16,1024]{2,1,0:T(8,128)(2,1)S(1)}, u32[]{:S(2)}, u32[]{:S(2)}) %collective-permute-start) | collective-permute-done | bytes 131104 | tf_op jit(solution)/shard_map/ppermute | solution.py:63
  8.3 3.9 %collective-permute-start.1 = (bf16[32,1024]{1,0:T(8,128)(2,1)S(1)}, bf16[32,1024]{1,0:T(8,128)(2,1)S(1)}, u32[]{:S(2)}, u32[]{:S(2)}) collective-permute-start(bf16[32,1024]{1,0:T(8,128)(2,1)S(1)} %get-tuple-element.62), channel_id=1, source_target_pairs={{0,12},{2,14},{4,8},{6,10},{8,4},{10,6},{12,0},{14,2},{1,13},{3,15... | collective-permute-start | bytes 196616 | tf_op jit(solution)/shard_map/ppermute | solution.py:63
  12.2 0.6 collective-permute-start.3
  12.8 2.0 %collective-permute-done.1.rest_0_ = bf16[32,1024]{1,0:T(8,128)(2,1)S(1)} collective-permute-done((bf16[32,1024]{1,0:T(8,128)(2,1)S(1)}, bf16[32,1024]{1,0:T(8,128)(2,1)S(1)}, u32[]{:S(2)}, u32[]{:S(2)}) %collective-permute-start.1) | collective-permute-done | bytes 65568 | tf_op jit(solution)/shard_map/ppermute | solution.py:63
  14.9 2.7 %collective-permute-done.2.rest_1_ = bf16[32,1024]{1,0:T(8,128)(2,1)S(1)} collective-permute-done((bf16[32,1024]{1,0:T(8,128)(2,1)S(1)}, bf16[32,1024]{1,0:T(8,128)(2,1)S(1)}, u32[]{:S(2)}, u32[]{:S(2)}) %collective-permute-start.2) | collective-permute-done | bytes 65568 | tf_op jit(solution)/shard_map/ppermute | solution.py:63
  17.6 3.5 %shard_map.167 = (f32[2,100,256]{2,1,0:T(8,128)S(1)}, bf16[2,100,256]{2,1,0:T(8,128)(2,1)S(1)}, bf16[512,1024]{1,0:T(8,128)(2,1)S(1)}, bf16[512,1024]{1,0:T(8,12...) custom-call(bf16[1024,1024]{1,0:T(8,128)(2,1)S(1)} %get-tuple-element.53.w_msg_ref, ...), custom_call_target="tpu_custom_call" | custom-call | tf_op jit(solution)/shard_map/pallas_call | solution.py:46
  21.1 0.9 %shard_map.168 = (bf16[2,2,4,64,512]{4,3,2,1,0:T(8,128)(2,1)S(1)}, bf16[2,2,4,64,512]{4,3,2,1,0:T(8,128)(2,1)S(1)}, bf16[2,4,64,128]{3,2,1,0:T(8,128)(2,1)S(1)}, bf16[2,4,64,128]{3,2,1,0:T(8,128)(2,1)S(1)}) custom-call(bf16[512,1024]{1,0:T(8,128)(2,1)S(1)} %get-tuple-element.68.normed_ref, bf16[512,1024]{1,0:T(8,128)(2,1)S(1)} %get-tuple-element.69.active_ref, ...), custom_call_target="tpu_custom_call" | custom-call | tf_op jit(solution)/shard_map/pallas_call | solution.py:46
  22.4 1.6 %shard_map.169 = (bf16[512,1024]{1,0:T(8,128)(2,1)S(1)}, bf16[128,512]{1,0:T(8,128)(2,1)S(1)}, f32[1]{0:T(128)}, bf16[256,1152]{1,0:T(8,128)(2,1)S(1)}, bf16[256,1152]{1,0:T(8,128)(2,1)S(1)}) custom-call(f32[2,100,256]{2,1,0:T(8,128)S(1)} %get-tuple-element.65.own_ref, bf16[2,100,256]{2,1,0:T(8,128)(2,1)S(1)} %collective-permute-done.4.other_ref, ...), custom_call_target="tpu_custom_call" | custom-call | tf_op jit(solution)/shard_map/pallas_call | solution.py:46
  24.7 1.6 %shard_map.170 = (f32[256,1152]{1,0:T(8,128)S(1)}, f32[256,1152]{1,0:T(8,128)S(1)}) custom-call(f32[1]{0:T(128)} %get-tuple-element.74.loss_ref, bf16[2,2,4,64,512]{4,3,2,1,0:T(8,128)(2,1)S(1)} %get-tuple-element.70.normed_t_ref, bf16[2,2,4,64,512]{4,3,2,1,0:T(8,128)(2,1)S(1)} %get-tuple-element.71.active_t_ref, ...), custom_call_target="tpu_custom_call" | custom-call | tf_op jit(solution)/shard_map/pallas_call | solution.py:46
  26.6 1.6 %collective-permute-start.8 = (bf16[128,1152]{1,0:T(8,128)(2,1)S(1)}, bf16[128,1152]{1,0:T(8,128)(2,1)S(1)}, u32[]{:S(2)}, u32[]{:S(2)}) collective-permute-start(bf16[128,1152]{1,0:T(8,128)(2,1)S(1)} %shard_map.171.refs_0_), channel_id=1, source_target_pairs={{0,2},{2,0},{4,6},{6,4},{8,10},{10,8},{12,14},{14,12},{1,3},{3,1},... | collective-permute-start | bytes 884744 | tf_op jit(solution)/shard_map/ppermute | solution.py:63
  28.2 1.7 %shard_map.172.refs_3_ = bf16[512,1024]{1,0:T(8,128)(2,1)S(1)} custom-call(bf16[128,1152]{1,0:T(8,128)(2,1)S(1)} %shard_map.171.refs_0_, bf16[512,1024]{1,0:T(8,128)(2,1)S(1)} %get-tuple-element.75.inner_ref.refs_1_, bf16[1024,1024]{1,0:T(8,128)(2,1)S(1)} %get-tuple-element.57.weights_ref.refs_2_, f32[1024]{0:T(1024)S(1)} %get-tuple-element.55.gain_ref.refs_3_, ...), custom_call_target="tpu_custom_call" | custom-call | flops 8000000000 | tf_op jit(solution)/shard_map/pallas_call | solution.py:46
  29.9 0.4 shard_map.173
  30.4 2.2 %collective-permute-start.10 = (bf16[32,1024]{1,0:T(8,128)(2,1)S(1)}, bf16[32,1024]{1,0:T(8,128)(2,1)S(1)}, u32[]{:S(2)}, u32[]{:S(2)}) collective-permute-start(bf16[32,1024]{1,0:T(8,128)(2,1)S(1)} %get-tuple-element.86), channel_id=1, source_target_pairs={{0,12},{2,14},{4,8},{6,10},{8,4},{10,6},{12,0},{14,2},{1,13},{3,15... | collective-permute-start | bytes 196616 | tf_op jit(solution)/shard_map/ppermute | solution.py:63
  32.7 2.2 %collective-permute-start.12 = (bf16[32,1024]{1,0:T(8,128)(2,1)S(1)}, bf16[32,1024]{1,0:T(8,128)(2,1)S(1)}, u32[]{:S(2)}, u32[]{:S(2)}) collective-permute-start(bf16[32,1024]{1,0:T(8,128)(2,1)S(1)} %get-tuple-element.88), channel_id=1, source_target_pairs={{0,4},{2,6},{4,0},{6,2},{8,12},{10,14},{12,8},{14,10},{1,5},{3,7},... | collective-permute-start | bytes 196616 | tf_op jit(solution)/shard_map/ppermute | solution.py:63
  34.9 0.7 %shard_map.175 = (bf16[128,1024]{1,0:T(8,128)(2,1)S(1)}, bf16[144,1024]{1,0:T(8,128)(2,1)S(1)}, bf16[144,1024]{1,0:T(8,128)(2,1)S(1)}, f32[256,1024]{1,0:T(8,128)S(1)}) custom-call(bf16[2,4,64,128]{3,2,1,0:T(8,128)(2,1)S(1)} %get-tuple-element.84.keep_ref, bf16[2,4,64,128]{3,2,1,0:T(8,128)(2,1)S(1)} %collective-permute-done.6.refs_1_.give_ref, ...), custom_call_target="tpu_custom_call" | custom-call | tf_op jit(solution)/shard_map/pallas_call | solution.py:46
  35.6 0.5 collective-permute-start.18
  36.1 1.5 %collective-permute-start.16 = (bf16[144,1024]{1,0:T(8,128)(2,1)S(1)}, bf16[144,1024]{1,0:T(8,128)(2,1)S(1)}, u32[]{:S(2)}, u32[]{:S(2)}) collective-permute-start(bf16[144,1024]{1,0:T(8,128)(2,1)S(1)} %get-tuple-element.93), channel_id=1, source_target_pairs={{0,2},{2,0},{4,6},{6,4},{8,10},{10,8},{12,14},{14,12},{1,3},{3,1},... | collective-permute-start | bytes 884744 | tf_op jit(solution)/shard_map/ppermute | solution.py:63
  37.9 1.6 %collective-permute-start.15 = (bf16[64,1152]{1,0:T(8,128)(2,1)S(1)}, bf16[64,1152]{1,0:T(8,128)(2,1)S(1)}, u32[]{:S(2)}, u32[]{:S(2)}) collective-permute-start(bf16[64,1152]{1,0:T(8,128)(2,1)S(1)} %get-tuple-element.91), channel_id=1, source_target_pairs={{0,8},{2,10},{4,12},{6,14},{8,0},{10,2},{12,4},{14,6},{1,9},{3,11}... | collective-permute-start | bytes 442376 | tf_op jit(solution)/shard_map/ppermute | solution.py:63
  39.5 2.3 %collective-permute-start.14 = (bf16[64,1152]{1,0:T(8,128)(2,1)S(1)}, bf16[64,1152]{1,0:T(8,128)(2,1)S(1)}, u32[]{:S(2)}, u32[]{:S(2)}) collective-permute-start(bf16[64,1152]{1,0:T(8,128)(2,1)S(1)} %get-tuple-element.83.refs_0_), channel_id=1, source_target_pairs={{0,12},{2,14},{4,8},{6,10},{8,4},{10,6},{12,0},{14,2},{1,13},{3,15... | collective-permute-start | bytes 442376 | tf_op jit(solution)/shard_map/ppermute | solution.py:63
  41.9 0.6 collective-permute-start.13
  42.5 2.4 %collective-permute-done.18.arrived_ref.refs_2_ = bf16[128,1024]{1,0:T(8,128)(2,1)S(1)} collective-permute-done((bf16[128,1024]{1,0:T(8,128)(2,1)S(1)}, bf16[128,1024]{1,0:T(8,128)(2,1)S(1)}, u32[]{:S(2)}, u32[]{:S(2)}) %collective-permute-start.18) | collective-permute-done | bytes 262176 | tf_op jit(solution)/shard_map/ppermute | solution.py:63
  44.9 2.2 %collective-permute-start.19 = (bf16[64,1024]{1,0:T(8,128)(2,1)S(1)}, bf16[64,1024]{1,0:T(8,128)(2,1)S(1)}, u32[]{:S(2)}, u32[]{:S(2)}) collective-permute-start(bf16[64,1024]{1,0:T(8,128)(2,1)S(1)} %shard_map.180), channel_id=1, source_target_pairs={{0,12},{2,14},{4,8},{6,10},{8,4},{10,6},{12,0},{14,2},{1,13},{3,15... | collective-permute-start | bytes 393224 | tf_op jit(solution)/shard_map/ppermute | solution.py:63
  47.2 4.0 %collective-permute-done.16.arrived_ref = bf16[144,1024]{1,0:T(8,128)(2,1)S(1)} collective-permute-done((bf16[144,1024]{1,0:T(8,128)(2,1)S(1)}, bf16[144,1024]{1,0:T(8,128)(2,1)S(1)}, u32[]{:S(2)}, u32[]{:S(2)}) %collective-permute-start.16) | collective-permute-done | bytes 294944 | tf_op jit(solution)/shard_map/ppermute | solution.py:63
  51.6 6.4 %collective-permute-start.20 = (bf16[64,1024]{1,0:T(8,128)(2,1)S(1)}, bf16[64,1024]{1,0:T(8,128)(2,1)S(1)}, u32[]{:S(2)}, u32[]{:S(2)}) collective-permute-start(bf16[64,1024]{1,0:T(8,128)(2,1)S(1)} %shard_map.181), channel_id=1, source_target_pairs={{0,8},{2,10},{4,12},{6,14},{8,0},{10,2},{12,4},{14,6},{1,9},{3,11}... | collective-permute-start | bytes 393224 | tf_op jit(solution)/shard_map/ppermute | solution.py:63
  58.0 1.0 %collective-permute-done.13.last_ref.refs_3_.refs_2_ = bf16[208,1024]{1,0:T(8,128)(2,1)S(1)} collective-permute-done((bf16[208,1024]{1,0:T(8,128)(2,1)S(1)}, bf16[208,1024]{1,0:T(8,128)(2,1)S(1)}, u32[]{:S(2)}, u32[]{:S(2)}) %collective-permute-start.13) | collective-permute-done | bytes 426016 | tf_op jit(solution)/shard_map/ppermute | solution.py:63
  58.9 1.5 %shard_map.177 = (bf16[2,32,1024]{2,1,0:T(8,128)(2,1)}, f32[8,128]{1,0:T(8,128)S(1)}) custom-call(bf16[128,64]{1,0:T(8,128)(2,1)S(1)} %get-tuple-element.52.refs_0_.pick_ref, bf16[1024,1024]{1,0:T(8,128)(2,1)S(1)} %copy-done, bf16[8,16,1024]{2,1,0:T(8,128)(2,1)S(1)} %get-tuple-element.81.slots_ref.refs_2_, ...), custom_call_target="tpu_custom_call" | custom-call | tf_op jit(solution)/shard_map/pallas_call | solution.py:46
  60.5 1.0 %shard_map.179 = (f32[64,1024]{1,0:T(8,128)}, f32[64,100]{1,0:T(8,128)}, f32[1]{0:T(128)}, f32[8,128]{1,0:T(8,128)S(1)}) custom-call(f32[8,128]{1,0:T(8,128)S(1)} %get-tuple-element.90.refs_0_, f32[256,1152]{1,0:T(8,128)S(1)} %get-tuple-element.82.held_ref.refs_1_, bf16[256,1152]{1,0:T(8,128)(2,1)S(1)} %collective-permute-done.5.refs_0_.other_ref.refs_2_, ...), custom_call_target="tpu_custom_call" | custom-call | tf_op jit(solution)/shard_map/pallas_call | solution.py:46
  61.5 2.7 %collective-permute-done.20.refs_4_ = bf16[64,1024]{1,0:T(8,128)(2,1)S(1)} collective-permute-done((bf16[64,1024]{1,0:T(8,128)(2,1)S(1)}, bf16[64,1024]{1,0:T(8,128)(2,1)S(1)}, u32[]{:S(2)}, u32[]{:S(2)}) %collective-permute-start.20) | collective-permute-done | bytes 131104 | tf_op jit(solution)/shard_map/ppermute | solution.py:63
  64.2 0.8 %shard_map.182 = f32[64,1024]{1,0:T(8,128)} custom-call(f32[8,128]{1,0:T(8,128)S(1)} %get-tuple-element.95.refs_0_, f32[256,1024]{1,0:T(8,128)S(1)} %get-tuple-element.92.near_ref.refs_1_, bf16[208,1024]{1,0:T(8,128)(2,1)S(1)} %collective-permute-done.13.last_ref.refs_3_.refs_2_, bf16[64,1024]{1,0:T(8,128)(2,1)S(1)} %collective-permute-done.19.refs_3_, ...), custom_call_target="tpu_custom_call" | custom-call | flops 8000000000 | tf_op jit(solution)/shard_map/pallas_call | solution.py:46
  (35 shorter events, 2.1 us)
Async XLA Ops:
  1.8 6.5 %collective-permute-start = (bf16[4,16,1024]{2,1,0:T(8,128)(2,1)S(1)}, bf16[4,16,1024]{2,1,0:T(8,128)(2,1)S(1)}, u32[]{:S(2)}, u32[]{:S(2)}) collective-permute-start(bf16[4,16,1024]{2,1,0:T(8,128)(2,1)S(1)} %get-tuple-element.61), channel_id=1, source_target_pairs={{0,2},{2,0},{4,6},{6,4},{8,10},{10,8},{12,14},{14,12},{1,3},{3,1},... | collective-permute-start | bytes 393224 | tf_op jit(solution)/shard_map/ppermute | solution.py:63
  8.3 6.6 %collective-permute-start.1 = (bf16[32,1024]{1,0:T(8,128)(2,1)S(1)}, bf16[32,1024]{1,0:T(8,128)(2,1)S(1)}, u32[]{:S(2)}, u32[]{:S(2)}) collective-permute-start(bf16[32,1024]{1,0:T(8,128)(2,1)S(1)} %get-tuple-element.62), channel_id=1, source_target_pairs={{0,12},{2,14},{4,8},{6,10},{8,4},{10,6},{12,0},{14,2},{1,13},{3,15... | collective-permute-start | bytes 196616 | tf_op jit(solution)/shard_map/ppermute | solution.py:63
  12.2 5.4 %collective-permute-start.2 = (bf16[32,1024]{1,0:T(8,128)(2,1)S(1)}, bf16[32,1024]{1,0:T(8,128)(2,1)S(1)}, u32[]{:S(2)}, u32[]{:S(2)}) collective-permute-start(bf16[32,1024]{1,0:T(8,128)(2,1)S(1)} %get-tuple-element.63), channel_id=1, source_target_pairs={{0,8},{2,10},{4,12},{6,14},{8,0},{10,2},{12,4},{14,6},{1,9},{3,11}... | collective-permute-start | bytes 196616 | tf_op jit(solution)/shard_map/ppermute | solution.py:63
  12.2 5.4 %collective-permute-start.3 = (bf16[32,1024]{1,0:T(8,128)(2,1)S(1)}, bf16[32,1024]{1,0:T(8,128)(2,1)S(1)}, u32[]{:S(2)}, u32[]{:S(2)}) collective-permute-start(bf16[32,1024]{1,0:T(8,128)(2,1)S(1)} %get-tuple-element.64), channel_id=1, source_target_pairs={{0,4},{2,6},{4,0},{6,2},{8,12},{10,14},{12,8},{14,10},{1,5},{3,7},... | collective-permute-start | bytes 196616 | tf_op jit(solution)/shard_map/ppermute | solution.py:63
  21.0 1.4 %copy-start.1 = (f32[100,256]{1,0:T(8,128)S(1)}, f32[100,256]{1,0:T(8,128)}, u32[]{:S(2)}) copy-start(f32[100,256]{1,0:T(8,128)} %truth_ref.1) | copy-start | bytes 307204
  21.1 1.4 %copy-start.2 = (f32[256]{0:T(256)S(1)}, f32[256]{0:T(256)}, u32[]{:S(2)}) copy-start(f32[256]{0:T(256)} %cell_ref.1) | copy-start | bytes 3076
  21.1 1.4 %collective-permute-start.4 = (bf16[2,100,256]{2,1,0:T(8,128)(2,1)S(1)}, bf16[2,100,256]{2,1,0:T(8,128)(2,1)S(1)}, u32[]{:S(2)}, u32[]{:S(2)}) collective-permute-start(bf16[2,100,256]{2,1,0:T(8,128)(2,1)S(1)} %get-tuple-element.66), channel_id=1, source_target_pairs={{0,1},{1,0},{2,3},{3,2},{4,5},{5,4},{6,7},{7,6},{8,9},{9,8},{10,11... | collective-permute-start | bytes 307208 | tf_op jit(solution)/shard_map/ppermute | solution.py:63
  24.0 2.3 %collective-permute-start.7 = (bf16[256,1152]{1,0:T(8,128)(2,1)S(1)}, bf16[256,1152]{1,0:T(8,128)(2,1)S(1)}, u32[]{:S(2)}, u32[]{:S(2)}) collective-permute-start(bf16[256,1152]{1,0:T(8,128)(2,1)S(1)} %get-tuple-element.78), channel_id=1, source_target_pairs={{0,1},{1,0},{2,3},{3,2},{4,5},{5,4},{6,7},{7,6},{8,9},{9,8},{10,11... | collective-permute-start | bytes 1769480 | tf_op jit(solution)/shard_map/ppermute | solution.py:63
  24.2 5.6 %collective-permute-start.6 = (bf16[2,4,64,128]{3,2,1,0:T(8,128)(2,1)S(1)}, bf16[2,4,64,128]{3,2,1,0:T(8,128)(2,1)S(1)}, u32[]{:S(2)}, u32[]{:S(2)}) collective-permute-start(bf16[2,4,64,128]{3,2,1,0:T(8,128)(2,1)S(1)} %get-tuple-element.73), channel_id=1, source_target_pairs={{0,1},{1,0},{2,3},{3,2},{4,5},{5,4},{6,7},{7,6},{8,9},{9,8},{10,11... | collective-permute-start | bytes 393224 | tf_op jit(solution)/shard_map/ppermute | solution.py:63
  24.6 5.3 %collective-permute-start.5 = (bf16[256,1152]{1,0:T(8,128)(2,1)S(1)}, bf16[256,1152]{1,0:T(8,128)(2,1)S(1)}, u32[]{:S(2)}, u32[]{:S(2)}) collective-permute-start(bf16[256,1152]{1,0:T(8,128)(2,1)S(1)} %get-tuple-element.72), channel_id=1, source_target_pairs={{0,1},{1,0},{2,3},{3,2},{4,5},{5,4},{6,7},{7,6},{8,9},{9,8},{10,11... | collective-permute-start | bytes 1769480 | tf_op jit(solution)/shard_map/ppermute | solution.py:63
  26.6 9.6 %collective-permute-start.8 = (bf16[128,1152]{1,0:T(8,128)(2,1)S(1)}, bf16[128,1152]{1,0:T(8,128)(2,1)S(1)}, u32[]{:S(2)}, u32[]{:S(2)}) collective-permute-start(bf16[128,1152]{1,0:T(8,128)(2,1)S(1)} %shard_map.171.refs_0_), channel_id=1, source_target_pairs={{0,2},{2,0},{4,6},{6,4},{8,10},{10,8},{12,14},{14,12},{1,3},{3,1},... | collective-permute-start | bytes 884744 | tf_op jit(solution)/shard_map/ppermute | solution.py:63
  30.3 4.5 %collective-permute-start.9 = (bf16[8,16,1024]{2,1,0:T(8,128)(2,1)S(1)}, bf16[8,16,1024]{2,1,0:T(8,128)(2,1)S(1)}, u32[]{:S(2)}, u32[]{:S(2)}) collective-permute-start(bf16[8,16,1024]{2,1,0:T(8,128)(2,1)S(1)} %get-tuple-element.81.slots_ref.refs_2_), channel_id=1, source_target_pairs={{0,1},{1,0},{2,3},{3,2},{4,5},{5,4},{6,7},{7,6},{8,9},{9,8},{10,11... | collective-permute-start | bytes 786440 | tf_op jit(solution)/shard_map/ppermute | solution.py:63
  30.4 7.5 %collective-permute-start.10 = (bf16[32,1024]{1,0:T(8,128)(2,1)S(1)}, bf16[32,1024]{1,0:T(8,128)(2,1)S(1)}, u32[]{:S(2)}, u32[]{:S(2)}) collective-permute-start(bf16[32,1024]{1,0:T(8,128)(2,1)S(1)} %get-tuple-element.86), channel_id=1, source_target_pairs={{0,12},{2,14},{4,8},{6,10},{8,4},{10,6},{12,0},{14,2},{1,13},{3,15... | collective-permute-start | bytes 196616 | tf_op jit(solution)/shard_map/ppermute | solution.py:63
  32.7 6.9 %collective-permute-start.11 = (bf16[32,1024]{1,0:T(8,128)(2,1)S(1)}, bf16[32,1024]{1,0:T(8,128)(2,1)S(1)}, u32[]{:S(2)}, u32[]{:S(2)}) collective-permute-start(bf16[32,1024]{1,0:T(8,128)(2,1)S(1)} %get-tuple-element.87), channel_id=1, source_target_pairs={{0,8},{2,10},{4,12},{6,14},{8,0},{10,2},{12,4},{14,6},{1,9},{3,11}... | collective-permute-start | bytes 196616 | tf_op jit(solution)/shard_map/ppermute | solution.py:63
  32.7 9.2 %collective-permute-start.12 = (bf16[32,1024]{1,0:T(8,128)(2,1)S(1)}, bf16[32,1024]{1,0:T(8,128)(2,1)S(1)}, u32[]{:S(2)}, u32[]{:S(2)}) collective-permute-start(bf16[32,1024]{1,0:T(8,128)(2,1)S(1)} %get-tuple-element.88), channel_id=1, source_target_pairs={{0,4},{2,6},{4,0},{6,2},{8,12},{10,14},{12,8},{14,10},{1,5},{3,7},... | collective-permute-start | bytes 196616 | tf_op jit(solution)/shard_map/ppermute | solution.py:63
  35.6 9.3 %collective-permute-start.18 = (bf16[128,1024]{1,0:T(8,128)(2,1)S(1)}, bf16[128,1024]{1,0:T(8,128)(2,1)S(1)}, u32[]{:S(2)}, u32[]{:S(2)}) collective-permute-start(bf16[128,1024]{1,0:T(8,128)(2,1)S(1)} %get-tuple-element.96), channel_id=1, source_target_pairs={{0,2},{2,0},{4,6},{6,4},{8,10},{10,8},{12,14},{14,12},{1,3},{3,1},... | collective-permute-start | bytes 786440 | tf_op jit(solution)/shard_map/ppermute | solution.py:63
  36.1 15.1 %collective-permute-start.16 = (bf16[144,1024]{1,0:T(8,128)(2,1)S(1)}, bf16[144,1024]{1,0:T(8,128)(2,1)S(1)}, u32[]{:S(2)}, u32[]{:S(2)}) collective-permute-start(bf16[144,1024]{1,0:T(8,128)(2,1)S(1)} %get-tuple-element.93), channel_id=1, source_target_pairs={{0,2},{2,0},{4,6},{6,4},{8,10},{10,8},{12,14},{14,12},{1,3},{3,1},... | collective-permute-start | bytes 884744 | tf_op jit(solution)/shard_map/ppermute | solution.py:63
  37.9 22.5 %collective-permute-start.15 = (bf16[64,1152]{1,0:T(8,128)(2,1)S(1)}, bf16[64,1152]{1,0:T(8,128)(2,1)S(1)}, u32[]{:S(2)}, u32[]{:S(2)}) collective-permute-start(bf16[64,1152]{1,0:T(8,128)(2,1)S(1)} %get-tuple-element.91), channel_id=1, source_target_pairs={{0,8},{2,10},{4,12},{6,14},{8,0},{10,2},{12,4},{14,6},{1,9},{3,11}... | collective-permute-start | bytes 442376 | tf_op jit(solution)/shard_map/ppermute | solution.py:63
  39.5 12.0 %collective-permute-start.14 = (bf16[64,1152]{1,0:T(8,128)(2,1)S(1)}, bf16[64,1152]{1,0:T(8,128)(2,1)S(1)}, u32[]{:S(2)}, u32[]{:S(2)}) collective-permute-start(bf16[64,1152]{1,0:T(8,128)(2,1)S(1)} %get-tuple-element.83.refs_0_), channel_id=1, source_target_pairs={{0,12},{2,14},{4,8},{6,10},{8,4},{10,6},{12,0},{14,2},{1,13},{3,15... | collective-permute-start | bytes 442376 | tf_op jit(solution)/shard_map/ppermute | solution.py:63
  41.9 17.0 %collective-permute-start.13 = (bf16[208,1024]{1,0:T(8,128)(2,1)S(1)}, bf16[208,1024]{1,0:T(8,128)(2,1)S(1)}, u32[]{:S(2)}, u32[]{:S(2)}) collective-permute-start(bf16[208,1024]{1,0:T(8,128)(2,1)S(1)} %shard_map.176), channel_id=1, source_target_pairs={{0,2},{2,0},{4,6},{6,4},{8,10},{10,8},{12,14},{14,12},{1,3},{3,1},... | collective-permute-start | bytes 1277960 | tf_op jit(solution)/shard_map/ppermute | solution.py:63
  44.9 16.5 %collective-permute-start.19 = (bf16[64,1024]{1,0:T(8,128)(2,1)S(1)}, bf16[64,1024]{1,0:T(8,128)(2,1)S(1)}, u32[]{:S(2)}, u32[]{:S(2)}) collective-permute-start(bf16[64,1024]{1,0:T(8,128)(2,1)S(1)} %shard_map.180), channel_id=1, source_target_pairs={{0,12},{2,14},{4,8},{6,10},{8,4},{10,6},{12,0},{14,2},{1,13},{3,15... | collective-permute-start | bytes 393224 | tf_op jit(solution)/shard_map/ppermute | solution.py:63
  51.4 7.5 %copy-start = (bf16[1024,1024]{1,0:T(8,128)(2,1)S(1)}, bf16[1024,1024]{1,0:T(8,128)(2,1)}, u32[]{:S(2)}) copy-start(bf16[1024,1024]{1,0:T(8,128)(2,1)} %w_msg_ref.1) | copy-start | bytes 6291460
  51.5 9.0 %collective-permute-start.17 = (bf16[144,1024]{1,0:T(8,128)(2,1)S(1)}, bf16[144,1024]{1,0:T(8,128)(2,1)S(1)}, u32[]{:S(2)}, u32[]{:S(2)}) collective-permute-start(bf16[144,1024]{1,0:T(8,128)(2,1)S(1)} %shard_map.178), channel_id=1, source_target_pairs={{0,4},{2,6},{4,0},{6,2},{8,12},{10,14},{12,8},{14,10},{1,5},{3,7},... | collective-permute-start | bytes 884744 | tf_op jit(solution)/shard_map/ppermute | solution.py:63
  51.6 12.6 %collective-permute-start.20 = (bf16[64,1024]{1,0:T(8,128)(2,1)S(1)}, bf16[64,1024]{1,0:T(8,128)(2,1)S(1)}, u32[]{:S(2)}, u32[]{:S(2)}) collective-permute-start(bf16[64,1024]{1,0:T(8,128)(2,1)S(1)} %shard_map.181), channel_id=1, source_target_pairs={{0,8},{2,10},{4,12},{6,14},{8,0},{10,2},{12,4},{14,6},{1,9},{3,11}... | collective-permute-start | bytes 393224 | tf_op jit(solution)/shard_map/ppermute | solution.py:63

commit v10 on v9

--- a/solution.py
+++ b/solution.py
@@ -626,7 +626,7 @@
             [((block, width), bf16)],
             [message_near, message_first_other],
             limit=6,
-            after=hidden_parts[:i],
+            after=hidden_parts[1 : 1 + i],
         )
         message_parts.append(swap(piece, "space", peers, steps[i]))
     late = call(

time: 65.2 us -> 65.2 us (level)
  starting transfers between devices: 29.8 us -> 25 us
  waiting for transfers between devices: 16.2 us -> 21 us
    ppermute x21, waiting for transfers between devices: 16.2 us -> 21 us  [swap(): return lax.ppermute(value, axis, [(i, i ^ step) for i in range(size)])]
    ppermute x21, starting transfers between devices: 29.8 us -> 25 us  [swap(): return lax.ppermute(value, axis, [(i, i ^ step) for i in range(size)])]
  transfers between devices with their start and end apart: 21 -> 21, of which waited for: 8 -> 9; matrix products, arithmetic and copies ran while one was open for 0% -> 0% of each run, Pallas kernels for 17% -> 17%
where the time goes in v10:
time: 65.2 us; the launch traced here: 65 us
  starting transfers between devices  25 us (38%)
  waiting for transfers between devices  21 us (32%)
  Pallas kernels  18.1 us (28%)
  between operations  0.83 us (1%)
    ppermute x21, starting transfers between devices, swap(): return lax.ppermute(value, axis, [(i, i ^ step) for i in range(size)])  25 us
    ppermute x21, waiting for transfers between devices, swap(): return lax.ppermute(value, axis, [(i, i ^ step) for i in range(size)])  21 us
    pallas_call x19, Pallas kernels, call(): pl.pallas_call(inner if count else body, out_shape=[jax.ShapeDtypeStruct(...  18.1 us
  transfers between devices with their start and end apart: 21, of which 9 were waited for; matrix products, arithmetic and copies ran while one was open for 0% of the time, Pallas kernels for 17%

profile of v10, /device:TPU:0, one launch (start us, length us, event | category | flops | bytes accessed | tf_op | source)
XLA Modules:
  0.0 65.0 jit_solution(8996266463691651176)
XLA Ops:
  0.6 1.1 %shard_map.164 = (bf16[128,64]{1,0:T(8,128)(2,1)S(1)}, bf16[4,16,1024]{2,1,0:T(8,128)(2,1)S(1)}, bf16[4,16,1024]{2,1,0:T(8,128)(2,1)S(1)}) custom-call(s32[1,8,8]{2,1,0:T(8,128)} %lists_ref.1, bf16[2,32,1024]{2,1,0:T(8,128)(2,1)} %latents_ref.1), custom_call_target="tpu_custom_call" | custom-call | tf_op jit(solution)/shard_map/pallas_call | solution.py:46
  1.8 3.0 %collective-permute-start = (bf16[4,16,1024]{2,1,0:T(8,128)(2,1)S(1)}, bf16[4,16,1024]{2,1,0:T(8,128)(2,1)S(1)}, u32[]{:S(2)}, u32[]{:S(2)}) collective-permute-start(bf16[4,16,1024]{2,1,0:T(8,128)(2,1)S(1)} %get-tuple-element.61), channel_id=1, source_target_pairs={{0,2},{2,0},{4,6},{6,4},{8,10},{10,8},{12,14},{14,12},{1,3},{3,1},... | collective-permute-start | bytes 393224 | tf_op jit(solution)/shard_map/ppermute | solution.py:63
  4.8 2.6 %shard_map.165 = (bf16[256,512]{1,0:T(8,128)(2,1)S(1)}, bf16[1024,1024]{1,0:T(8,128)(2,1)S(1)}, f32[1024]{0:T(1024)S(1)}, bf16[256,1024]{1,0:T(8,128)(2,1)S(1)},...) custom-call(bf16[128,64]{1,0:T(8,128)(2,1)S(1)} %get-tuple-element.52.refs_0_.pick_ref, ...), custom_call_target="tpu_custom_call" | custom-call | tf_op jit(solution)/shard_map/pallas_call | solution.py:46
  7.4 0.9 %collective-permute-done.refs_2_.near_ref = bf16[4,16,1024]{2,1,0:T(8,128)(2,1)S(1)} collective-permute-done((bf16[4,16,1024]{2,1,0:T(8,128)(2,1)S(1)}, bf16[4,16,1024]{2,1,0:T(8,128)(2,1)S(1)}, u32[]{:S(2)}, u32[]{:S(2)}) %collective-permute-start) | collective-permute-done | bytes 131104 | tf_op jit(solution)/shard_map/ppermute | solution.py:63
  8.3 3.9 %collective-permute-start.1 = (bf16[32,1024]{1,0:T(8,128)(2,1)S(1)}, bf16[32,1024]{1,0:T(8,128)(2,1)S(1)}, u32[]{:S(2)}, u32[]{:S(2)}) collective-permute-start(bf16[32,1024]{1,0:T(8,128)(2,1)S(1)} %get-tuple-element.62), channel_id=1, source_target_pairs={{0,12},{2,14},{4,8},{6,10},{8,4},{10,6},{12,0},{14,2},{1,13},{3,15... | collective-permute-start | bytes 196616 | tf_op jit(solution)/shard_map/ppermute | solution.py:63
  12.2 0.6 collective-permute-start.3
  12.8 2.0 %collective-permute-done.1.rest_0_ = bf16[32,1024]{1,0:T(8,128)(2,1)S(1)} collective-permute-done((bf16[32,1024]{1,0:T(8,128)(2,1)S(1)}, bf16[32,1024]{1,0:T(8,128)(2,1)S(1)}, u32[]{:S(2)}, u32[]{:S(2)}) %collective-permute-start.1) | collective-permute-done | bytes 65568 | tf_op jit(solution)/shard_map/ppermute | solution.py:63
  14.9 2.7 %collective-permute-done.2.rest_1_ = bf16[32,1024]{1,0:T(8,128)(2,1)S(1)} collective-permute-done((bf16[32,1024]{1,0:T(8,128)(2,1)S(1)}, bf16[32,1024]{1,0:T(8,128)(2,1)S(1)}, u32[]{:S(2)}, u32[]{:S(2)}) %collective-permute-start.2) | collective-permute-done | bytes 65568 | tf_op jit(solution)/shard_map/ppermute | solution.py:63
  17.6 3.5 %shard_map.167 = (f32[2,100,256]{2,1,0:T(8,128)S(1)}, bf16[2,100,256]{2,1,0:T(8,128)(2,1)S(1)}, bf16[512,1024]{1,0:T(8,128)(2,1)S(1)}, bf16[512,1024]{1,0:T(8,12...) custom-call(bf16[1024,1024]{1,0:T(8,128)(2,1)S(1)} %get-tuple-element.53.w_msg_ref, ...), custom_call_target="tpu_custom_call" | custom-call | tf_op jit(solution)/shard_map/pallas_call | solution.py:46
  21.1 0.9 %shard_map.168 = (bf16[2,2,4,64,512]{4,3,2,1,0:T(8,128)(2,1)S(1)}, bf16[2,2,4,64,512]{4,3,2,1,0:T(8,128)(2,1)S(1)}, bf16[2,4,64,128]{3,2,1,0:T(8,128)(2,1)S(1)}, bf16[2,4,64,128]{3,2,1,0:T(8,128)(2,1)S(1)}) custom-call(bf16[512,1024]{1,0:T(8,128)(2,1)S(1)} %get-tuple-element.68.normed_ref, bf16[512,1024]{1,0:T(8,128)(2,1)S(1)} %get-tuple-element.69.active_ref, ...), custom_call_target="tpu_custom_call" | custom-call | tf_op jit(solution)/shard_map/pallas_call | solution.py:46
  22.4 1.6 %shard_map.169 = (bf16[512,1024]{1,0:T(8,128)(2,1)S(1)}, bf16[128,512]{1,0:T(8,128)(2,1)S(1)}, f32[1]{0:T(128)}, bf16[256,1152]{1,0:T(8,128)(2,1)S(1)}, bf16[256,1152]{1,0:T(8,128)(2,1)S(1)}) custom-call(f32[2,100,256]{2,1,0:T(8,128)S(1)} %get-tuple-element.65.own_ref, bf16[2,100,256]{2,1,0:T(8,128)(2,1)S(1)} %collective-permute-done.4.other_ref, ...), custom_call_target="tpu_custom_call" | custom-call | tf_op jit(solution)/shard_map/pallas_call | solution.py:46
  24.7 1.6 %shard_map.170 = (f32[256,1152]{1,0:T(8,128)S(1)}, f32[256,1152]{1,0:T(8,128)S(1)}) custom-call(f32[1]{0:T(128)} %get-tuple-element.74.loss_ref, bf16[2,2,4,64,512]{4,3,2,1,0:T(8,128)(2,1)S(1)} %get-tuple-element.70.normed_t_ref, bf16[2,2,4,64,512]{4,3,2,1,0:T(8,128)(2,1)S(1)} %get-tuple-element.71.active_t_ref, ...), custom_call_target="tpu_custom_call" | custom-call | tf_op jit(solution)/shard_map/pallas_call | solution.py:46
  26.6 1.6 %collective-permute-start.8 = (bf16[128,1152]{1,0:T(8,128)(2,1)S(1)}, bf16[128,1152]{1,0:T(8,128)(2,1)S(1)}, u32[]{:S(2)}, u32[]{:S(2)}) collective-permute-start(bf16[128,1152]{1,0:T(8,128)(2,1)S(1)} %shard_map.171.refs_0_), channel_id=1, source_target_pairs={{0,2},{2,0},{4,6},{6,4},{8,10},{10,8},{12,14},{14,12},{1,3},{3,1},... | collective-permute-start | bytes 884744 | tf_op jit(solution)/shard_map/ppermute | solution.py:63
  28.2 1.7 %shard_map.172.refs_3_ = bf16[512,1024]{1,0:T(8,128)(2,1)S(1)} custom-call(bf16[128,1152]{1,0:T(8,128)(2,1)S(1)} %shard_map.171.refs_0_, bf16[512,1024]{1,0:T(8,128)(2,1)S(1)} %get-tuple-element.75.inner_ref.refs_1_, bf16[1024,1024]{1,0:T(8,128)(2,1)S(1)} %get-tuple-element.57.weights_ref.refs_2_, f32[1024]{0:T(1024)S(1)} %get-tuple-element.55.gain_ref.refs_3_, ...), custom_call_target="tpu_custom_call" | custom-call | flops 8000000000 | tf_op jit(solution)/shard_map/pallas_call | solution.py:46
  30.4 2.2 %collective-permute-start.10 = (bf16[32,1024]{1,0:T(8,128)(2,1)S(1)}, bf16[32,1024]{1,0:T(8,128)(2,1)S(1)}, u32[]{:S(2)}, u32[]{:S(2)}) collective-permute-start(bf16[32,1024]{1,0:T(8,128)(2,1)S(1)} %get-tuple-element.86), channel_id=1, source_target_pairs={{0,12},{2,14},{4,8},{6,10},{8,4},{10,6},{12,0},{14,2},{1,13},{3,15... | collective-permute-start | bytes 196616 | tf_op jit(solution)/shard_map/ppermute | solution.py:63
  32.7 2.2 %collective-permute-start.12 = (bf16[32,1024]{1,0:T(8,128)(2,1)S(1)}, bf16[32,1024]{1,0:T(8,128)(2,1)S(1)}, u32[]{:S(2)}, u32[]{:S(2)}) collective-permute-start(bf16[32,1024]{1,0:T(8,128)(2,1)S(1)} %get-tuple-element.88), channel_id=1, source_target_pairs={{0,4},{2,6},{4,0},{6,2},{8,12},{10,14},{12,8},{14,10},{1,5},{3,7},... | collective-permute-start | bytes 196616 | tf_op jit(solution)/shard_map/ppermute | solution.py:63
  34.9 0.7 %shard_map.175 = (bf16[128,1024]{1,0:T(8,128)(2,1)S(1)}, bf16[144,1024]{1,0:T(8,128)(2,1)S(1)}, bf16[144,1024]{1,0:T(8,128)(2,1)S(1)}, f32[256,1024]{1,0:T(8,128)S(1)}) custom-call(bf16[2,4,64,128]{3,2,1,0:T(8,128)(2,1)S(1)} %get-tuple-element.84.keep_ref, bf16[2,4,64,128]{3,2,1,0:T(8,128)(2,1)S(1)} %collective-permute-done.6.refs_1_.give_ref, ...), custom_call_target="tpu_custom_call" | custom-call | tf_op jit(solution)/shard_map/pallas_call | solution.py:46
  35.6 0.5 collective-permute-start.18
  36.1 1.5 %collective-permute-start.16 = (bf16[144,1024]{1,0:T(8,128)(2,1)S(1)}, bf16[144,1024]{1,0:T(8,128)(2,1)S(1)}, u32[]{:S(2)}, u32[]{:S(2)}) collective-permute-start(bf16[144,1024]{1,0:T(8,128)(2,1)S(1)} %get-tuple-element.93), channel_id=1, source_target_pairs={{0,2},{2,0},{4,6},{6,4},{8,10},{10,8},{12,14},{14,12},{1,3},{3,1},... | collective-permute-start | bytes 884744 | tf_op jit(solution)/shard_map/ppermute | solution.py:63
  37.9 1.6 %collective-permute-start.15 = (bf16[64,1152]{1,0:T(8,128)(2,1)S(1)}, bf16[64,1152]{1,0:T(8,128)(2,1)S(1)}, u32[]{:S(2)}, u32[]{:S(2)}) collective-permute-start(bf16[64,1152]{1,0:T(8,128)(2,1)S(1)} %get-tuple-element.91), channel_id=1, source_target_pairs={{0,8},{2,10},{4,12},{6,14},{8,0},{10,2},{12,4},{14,6},{1,9},{3,11}... | collective-permute-start | bytes 442376 | tf_op jit(solution)/shard_map/ppermute | solution.py:63
  39.5 2.3 %collective-permute-start.14 = (bf16[64,1152]{1,0:T(8,128)(2,1)S(1)}, bf16[64,1152]{1,0:T(8,128)(2,1)S(1)}, u32[]{:S(2)}, u32[]{:S(2)}) collective-permute-start(bf16[64,1152]{1,0:T(8,128)(2,1)S(1)} %get-tuple-element.83.refs_0_), channel_id=1, source_target_pairs={{0,12},{2,14},{4,8},{6,10},{8,4},{10,6},{12,0},{14,2},{1,13},{3,15... | collective-permute-start | bytes 442376 | tf_op jit(solution)/shard_map/ppermute | solution.py:63
  41.9 0.6 collective-permute-start.13
  42.5 2.4 %collective-permute-done.18.arrived_ref.refs_2_ = bf16[128,1024]{1,0:T(8,128)(2,1)S(1)} collective-permute-done((bf16[128,1024]{1,0:T(8,128)(2,1)S(1)}, bf16[128,1024]{1,0:T(8,128)(2,1)S(1)}, u32[]{:S(2)}, u32[]{:S(2)}) %collective-permute-start.18) | collective-permute-done | bytes 262176 | tf_op jit(solution)/shard_map/ppermute | solution.py:63
  44.9 2.2 %collective-permute-start.19 = (bf16[64,1024]{1,0:T(8,128)(2,1)S(1)}, bf16[64,1024]{1,0:T(8,128)(2,1)S(1)}, u32[]{:S(2)}, u32[]{:S(2)}) collective-permute-start(bf16[64,1024]{1,0:T(8,128)(2,1)S(1)} %shard_map.180), channel_id=1, source_target_pairs={{0,12},{2,14},{4,8},{6,10},{8,4},{10,6},{12,0},{14,2},{1,13},{3,15... | collective-permute-start | bytes 393224 | tf_op jit(solution)/shard_map/ppermute | solution.py:63
  47.2 4.0 %collective-permute-done.16.arrived_ref = bf16[144,1024]{1,0:T(8,128)(2,1)S(1)} collective-permute-done((bf16[144,1024]{1,0:T(8,128)(2,1)S(1)}, bf16[144,1024]{1,0:T(8,128)(2,1)S(1)}, u32[]{:S(2)}, u32[]{:S(2)}) %collective-permute-start.16) | collective-permute-done | bytes 294944 | tf_op jit(solution)/shard_map/ppermute | solution.py:63
  51.5 1.2 %collective-permute-done.15.refs_5_.refs_0_ = bf16[64,1152]{1,0:T(8,128)(2,1)S(1)} collective-permute-done((bf16[64,1152]{1,0:T(8,128)(2,1)S(1)}, bf16[64,1152]{1,0:T(8,128)(2,1)S(1)}, u32[]{:S(2)}, u32[]{:S(2)}) %collective-permute-start.15) | collective-permute-done | bytes 147488 | tf_op jit(solution)/shard_map/ppermute | solution.py:63
  52.8 1.6 %collective-permute-start.20 = (bf16[64,1024]{1,0:T(8,128)(2,1)S(1)}, bf16[64,1024]{1,0:T(8,128)(2,1)S(1)}, u32[]{:S(2)}, u32[]{:S(2)}) collective-permute-start(bf16[64,1024]{1,0:T(8,128)(2,1)S(1)} %shard_map.181), channel_id=1, source_target_pairs={{0,8},{2,10},{4,12},{6,14},{8,0},{10,2},{12,4},{14,6},{1,9},{3,11}... | collective-permute-start | bytes 393224 | tf_op jit(solution)/shard_map/ppermute | solution.py:63
  54.4 4.6 %collective-permute-done.13.last_ref.refs_3_.refs_2_ = bf16[208,1024]{1,0:T(8,128)(2,1)S(1)} collective-permute-done((bf16[208,1024]{1,0:T(8,128)(2,1)S(1)}, bf16[208,1024]{1,0:T(8,128)(2,1)S(1)}, u32[]{:S(2)}, u32[]{:S(2)}) %collective-permute-start.13) | collective-permute-done | bytes 426016 | tf_op jit(solution)/shard_map/ppermute | solution.py:63
  58.9 1.5 %shard_map.177 = (bf16[2,32,1024]{2,1,0:T(8,128)(2,1)}, f32[8,128]{1,0:T(8,128)S(1)}) custom-call(bf16[128,64]{1,0:T(8,128)(2,1)S(1)} %get-tuple-element.52.refs_0_.pick_ref, bf16[1024,1024]{1,0:T(8,128)(2,1)S(1)} %copy-done, bf16[8,16,1024]{2,1,0:T(8,128)(2,1)S(1)} %get-tuple-element.81.slots_ref.refs_2_, ...), custom_call_target="tpu_custom_call" | custom-call | tf_op jit(solution)/shard_map/pallas_call | solution.py:46
  60.5 1.0 %shard_map.179 = (f32[64,1024]{1,0:T(8,128)}, f32[64,100]{1,0:T(8,128)}, f32[1]{0:T(128)}, f32[8,128]{1,0:T(8,128)S(1)}) custom-call(f32[8,128]{1,0:T(8,128)S(1)} %get-tuple-element.90.refs_0_, f32[256,1152]{1,0:T(8,128)S(1)} %get-tuple-element.82.held_ref.refs_1_, bf16[256,1152]{1,0:T(8,128)(2,1)S(1)} %collective-permute-done.5.refs_0_.other_ref.refs_2_, ...), custom_call_target="tpu_custom_call" | custom-call | tf_op jit(solution)/shard_map/pallas_call | solution.py:46
  61.5 2.7 %collective-permute-done.20.refs_4_ = bf16[64,1024]{1,0:T(8,128)(2,1)S(1)} collective-permute-done((bf16[64,1024]{1,0:T(8,128)(2,1)S(1)}, bf16[64,1024]{1,0:T(8,128)(2,1)S(1)}, u32[]{:S(2)}, u32[]{:S(2)}) %collective-permute-start.20) | collective-permute-done | bytes 131104 | tf_op jit(solution)/shard_map/ppermute | solution.py:63
  64.2 0.8 %shard_map.182 = f32[64,1024]{1,0:T(8,128)} custom-call(f32[8,128]{1,0:T(8,128)S(1)} %get-tuple-element.95.refs_0_, f32[256,1024]{1,0:T(8,128)S(1)} %get-tuple-element.92.near_ref.refs_1_, bf16[208,1024]{1,0:T(8,128)(2,1)S(1)} %collective-permute-done.13.last_ref.refs_3_.refs_2_, bf16[64,1024]{1,0:T(8,128)(2,1)S(1)} %collective-permute-done.19.refs_3_, ...), custom_call_target="tpu_custom_call" | custom-call | flops 8000000000 | tf_op jit(solution)/shard_map/pallas_call | solution.py:46
  (35 shorter events, 2.6 us)
Async XLA Ops:
  1.8 6.5 %collective-permute-start = (bf16[4,16,1024]{2,1,0:T(8,128)(2,1)S(1)}, bf16[4,16,1024]{2,1,0:T(8,128)(2,1)S(1)}, u32[]{:S(2)}, u32[]{:S(2)}) collective-permute-start(bf16[4,16,1024]{2,1,0:T(8,128)(2,1)S(1)} %get-tuple-element.61), channel_id=1, source_target_pairs={{0,2},{2,0},{4,6},{6,4},{8,10},{10,8},{12,14},{14,12},{1,3},{3,1},... | collective-permute-start | bytes 393224 | tf_op jit(solution)/shard_map/ppermute | solution.py:63
  8.3 6.6 %collective-permute-start.1 = (bf16[32,1024]{1,0:T(8,128)(2,1)S(1)}, bf16[32,1024]{1,0:T(8,128)(2,1)S(1)}, u32[]{:S(2)}, u32[]{:S(2)}) collective-permute-start(bf16[32,1024]{1,0:T(8,128)(2,1)S(1)} %get-tuple-element.62), channel_id=1, source_target_pairs={{0,12},{2,14},{4,8},{6,10},{8,4},{10,6},{12,0},{14,2},{1,13},{3,15... | collective-permute-start | bytes 196616 | tf_op jit(solution)/shard_map/ppermute | solution.py:63
  12.2 5.4 %collective-permute-start.2 = (bf16[32,1024]{1,0:T(8,128)(2,1)S(1)}, bf16[32,1024]{1,0:T(8,128)(2,1)S(1)}, u32[]{:S(2)}, u32[]{:S(2)}) collective-permute-start(bf16[32,1024]{1,0:T(8,128)(2,1)S(1)} %get-tuple-element.63), channel_id=1, source_target_pairs={{0,8},{2,10},{4,12},{6,14},{8,0},{10,2},{12,4},{14,6},{1,9},{3,11}... | collective-permute-start | bytes 196616 | tf_op jit(solution)/shard_map/ppermute | solution.py:63
  12.2 5.4 %collective-permute-start.3 = (bf16[32,1024]{1,0:T(8,128)(2,1)S(1)}, bf16[32,1024]{1,0:T(8,128)(2,1)S(1)}, u32[]{:S(2)}, u32[]{:S(2)}) collective-permute-start(bf16[32,1024]{1,0:T(8,128)(2,1)S(1)} %get-tuple-element.64), channel_id=1, source_target_pairs={{0,4},{2,6},{4,0},{6,2},{8,12},{10,14},{12,8},{14,10},{1,5},{3,7},... | collective-permute-start | bytes 196616 | tf_op jit(solution)/shard_map/ppermute | solution.py:63
  21.0 1.4 %copy-start.1 = (f32[100,256]{1,0:T(8,128)S(1)}, f32[100,256]{1,0:T(8,128)}, u32[]{:S(2)}) copy-start(f32[100,256]{1,0:T(8,128)} %truth_ref.1) | copy-start | bytes 307204
  21.1 1.4 %copy-start.2 = (f32[256]{0:T(256)S(1)}, f32[256]{0:T(256)}, u32[]{:S(2)}) copy-start(f32[256]{0:T(256)} %cell_ref.1) | copy-start | bytes 3076
  21.1 1.4 %collective-permute-start.4 = (bf16[2,100,256]{2,1,0:T(8,128)(2,1)S(1)}, bf16[2,100,256]{2,1,0:T(8,128)(2,1)S(1)}, u32[]{:S(2)}, u32[]{:S(2)}) collective-permute-start(bf16[2,100,256]{2,1,0:T(8,128)(2,1)S(1)} %get-tuple-element.66), channel_id=1, source_target_pairs={{0,1},{1,0},{2,3},{3,2},{4,5},{5,4},{6,7},{7,6},{8,9},{9,8},{10,11... | collective-permute-start | bytes 307208 | tf_op jit(solution)/shard_map/ppermute | solution.py:63
  24.0 2.3 %collective-permute-start.7 = (bf16[256,1152]{1,0:T(8,128)(2,1)S(1)}, bf16[256,1152]{1,0:T(8,128)(2,1)S(1)}, u32[]{:S(2)}, u32[]{:S(2)}) collective-permute-start(bf16[256,1152]{1,0:T(8,128)(2,1)S(1)} %get-tuple-element.78), channel_id=1, source_target_pairs={{0,1},{1,0},{2,3},{3,2},{4,5},{5,4},{6,7},{7,6},{8,9},{9,8},{10,11... | collective-permute-start | bytes 1769480 | tf_op jit(solution)/shard_map/ppermute | solution.py:63
  24.2 5.6 %collective-permute-start.6 = (bf16[2,4,64,128]{3,2,1,0:T(8,128)(2,1)S(1)}, bf16[2,4,64,128]{3,2,1,0:T(8,128)(2,1)S(1)}, u32[]{:S(2)}, u32[]{:S(2)}) collective-permute-start(bf16[2,4,64,128]{3,2,1,0:T(8,128)(2,1)S(1)} %get-tuple-element.73), channel_id=1, source_target_pairs={{0,1},{1,0},{2,3},{3,2},{4,5},{5,4},{6,7},{7,6},{8,9},{9,8},{10,11... | collective-permute-start | bytes 393224 | tf_op jit(solution)/shard_map/ppermute | solution.py:63
  24.6 5.3 %collective-permute-start.5 = (bf16[256,1152]{1,0:T(8,128)(2,1)S(1)}, bf16[256,1152]{1,0:T(8,128)(2,1)S(1)}, u32[]{:S(2)}, u32[]{:S(2)}) collective-permute-start(bf16[256,1152]{1,0:T(8,128)(2,1)S(1)} %get-tuple-element.72), channel_id=1, source_target_pairs={{0,1},{1,0},{2,3},{3,2},{4,5},{5,4},{6,7},{7,6},{8,9},{9,8},{10,11... | collective-permute-start | bytes 1769480 | tf_op jit(solution)/shard_map/ppermute | solution.py:63
  26.6 9.6 %collective-permute-start.8 = (bf16[128,1152]{1,0:T(8,128)(2,1)S(1)}, bf16[128,1152]{1,0:T(8,128)(2,1)S(1)}, u32[]{:S(2)}, u32[]{:S(2)}) collective-permute-start(bf16[128,1152]{1,0:T(8,128)(2,1)S(1)} %shard_map.171.refs_0_), channel_id=1, source_target_pairs={{0,2},{2,0},{4,6},{6,4},{8,10},{10,8},{12,14},{14,12},{1,3},{3,1},... | collective-permute-start | bytes 884744 | tf_op jit(solution)/shard_map/ppermute | solution.py:63
  30.3 4.5 %collective-permute-start.9 = (bf16[8,16,1024]{2,1,0:T(8,128)(2,1)S(1)}, bf16[8,16,1024]{2,1,0:T(8,128)(2,1)S(1)}, u32[]{:S(2)}, u32[]{:S(2)}) collective-permute-start(bf16[8,16,1024]{2,1,0:T(8,128)(2,1)S(1)} %get-tuple-element.81.slots_ref.refs_2_), channel_id=1, source_target_pairs={{0,1},{1,0},{2,3},{3,2},{4,5},{5,4},{6,7},{7,6},{8,9},{9,8},{10,11... | collective-permute-start | bytes 786440 | tf_op jit(solution)/shard_map/ppermute | solution.py:63
  30.4 7.5 %collective-permute-start.10 = (bf16[32,1024]{1,0:T(8,128)(2,1)S(1)}, bf16[32,1024]{1,0:T(8,128)(2,1)S(1)}, u32[]{:S(2)}, u32[]{:S(2)}) collective-permute-start(bf16[32,1024]{1,0:T(8,128)(2,1)S(1)} %get-tuple-element.86), channel_id=1, source_target_pairs={{0,12},{2,14},{4,8},{6,10},{8,4},{10,6},{12,0},{14,2},{1,13},{3,15... | collective-permute-start | bytes 196616 | tf_op jit(solution)/shard_map/ppermute | solution.py:63
  32.7 6.9 %collective-permute-start.11 = (bf16[32,1024]{1,0:T(8,128)(2,1)S(1)}, bf16[32,1024]{1,0:T(8,128)(2,1)S(1)}, u32[]{:S(2)}, u32[]{:S(2)}) collective-permute-start(bf16[32,1024]{1,0:T(8,128)(2,1)S(1)} %get-tuple-element.87), channel_id=1, source_target_pairs={{0,8},{2,10},{4,12},{6,14},{8,0},{10,2},{12,4},{14,6},{1,9},{3,11}... | collective-permute-start | bytes 196616 | tf_op jit(solution)/shard_map/ppermute | solution.py:63
  32.7 9.2 %collective-permute-start.12 = (bf16[32,1024]{1,0:T(8,128)(2,1)S(1)}, bf16[32,1024]{1,0:T(8,128)(2,1)S(1)}, u32[]{:S(2)}, u32[]{:S(2)}) collective-permute-start(bf16[32,1024]{1,0:T(8,128)(2,1)S(1)} %get-tuple-element.88), channel_id=1, source_target_pairs={{0,4},{2,6},{4,0},{6,2},{8,12},{10,14},{12,8},{14,10},{1,5},{3,7},... | collective-permute-start | bytes 196616 | tf_op jit(solution)/shard_map/ppermute | solution.py:63
  35.6 9.3 %collective-permute-start.18 = (bf16[128,1024]{1,0:T(8,128)(2,1)S(1)}, bf16[128,1024]{1,0:T(8,128)(2,1)S(1)}, u32[]{:S(2)}, u32[]{:S(2)}) collective-permute-start(bf16[128,1024]{1,0:T(8,128)(2,1)S(1)} %get-tuple-element.96), channel_id=1, source_target_pairs={{0,2},{2,0},{4,6},{6,4},{8,10},{10,8},{12,14},{14,12},{1,3},{3,1},... | collective-permute-start | bytes 786440 | tf_op jit(solution)/shard_map/ppermute | solution.py:63
  36.1 15.1 %collective-permute-start.16 = (bf16[144,1024]{1,0:T(8,128)(2,1)S(1)}, bf16[144,1024]{1,0:T(8,128)(2,1)S(1)}, u32[]{:S(2)}, u32[]{:S(2)}) collective-permute-start(bf16[144,1024]{1,0:T(8,128)(2,1)S(1)} %get-tuple-element.93), channel_id=1, source_target_pairs={{0,2},{2,0},{4,6},{6,4},{8,10},{10,8},{12,14},{14,12},{1,3},{3,1},... | collective-permute-start | bytes 884744 | tf_op jit(solution)/shard_map/ppermute | solution.py:63
  37.9 14.8 %collective-permute-start.15 = (bf16[64,1152]{1,0:T(8,128)(2,1)S(1)}, bf16[64,1152]{1,0:T(8,128)(2,1)S(1)}, u32[]{:S(2)}, u32[]{:S(2)}) collective-permute-start(bf16[64,1152]{1,0:T(8,128)(2,1)S(1)} %get-tuple-element.91), channel_id=1, source_target_pairs={{0,8},{2,10},{4,12},{6,14},{8,0},{10,2},{12,4},{14,6},{1,9},{3,11}... | collective-permute-start | bytes 442376 | tf_op jit(solution)/shard_map/ppermute | solution.py:63
  39.5 20.9 %collective-permute-start.14 = (bf16[64,1152]{1,0:T(8,128)(2,1)S(1)}, bf16[64,1152]{1,0:T(8,128)(2,1)S(1)}, u32[]{:S(2)}, u32[]{:S(2)}) collective-permute-start(bf16[64,1152]{1,0:T(8,128)(2,1)S(1)} %get-tuple-element.83.refs_0_), channel_id=1, source_target_pairs={{0,12},{2,14},{4,8},{6,10},{8,4},{10,6},{12,0},{14,2},{1,13},{3,15... | collective-permute-start | bytes 442376 | tf_op jit(solution)/shard_map/ppermute | solution.py:63
  41.9 17.0 %collective-permute-start.13 = (bf16[208,1024]{1,0:T(8,128)(2,1)S(1)}, bf16[208,1024]{1,0:T(8,128)(2,1)S(1)}, u32[]{:S(2)}, u32[]{:S(2)}) collective-permute-start(bf16[208,1024]{1,0:T(8,128)(2,1)S(1)} %shard_map.176), channel_id=1, source_target_pairs={{0,2},{2,0},{4,6},{6,4},{8,10},{10,8},{12,14},{14,12},{1,3},{3,1},... | collective-permute-start | bytes 1277960 | tf_op jit(solution)/shard_map/ppermute | solution.py:63
  44.9 16.5 %collective-permute-start.19 = (bf16[64,1024]{1,0:T(8,128)(2,1)S(1)}, bf16[64,1024]{1,0:T(8,128)(2,1)S(1)}, u32[]{:S(2)}, u32[]{:S(2)}) collective-permute-start(bf16[64,1024]{1,0:T(8,128)(2,1)S(1)} %shard_map.180), channel_id=1, source_target_pairs={{0,12},{2,14},{4,8},{6,10},{8,4},{10,6},{12,0},{14,2},{1,13},{3,15... | collective-permute-start | bytes 393224 | tf_op jit(solution)/shard_map/ppermute | solution.py:63
  51.4 7.5 %copy-start = (bf16[1024,1024]{1,0:T(8,128)(2,1)S(1)}, bf16[1024,1024]{1,0:T(8,128)(2,1)}, u32[]{:S(2)}) copy-start(bf16[1024,1024]{1,0:T(8,128)(2,1)} %w_msg_ref.1) | copy-start | bytes 6291460
  51.5 9.0 %collective-permute-start.17 = (bf16[144,1024]{1,0:T(8,128)(2,1)S(1)}, bf16[144,1024]{1,0:T(8,128)(2,1)S(1)}, u32[]{:S(2)}, u32[]{:S(2)}) collective-permute-start(bf16[144,1024]{1,0:T(8,128)(2,1)S(1)} %shard_map.178), channel_id=1, source_target_pairs={{0,4},{2,6},{4,0},{6,2},{8,12},{10,14},{12,8},{14,10},{1,5},{3,7},... | collective-permute-start | bytes 884744 | tf_op jit(solution)/shard_map/ppermute | solution.py:63
  52.8 11.4 %collective-permute-start.20 = (bf16[64,1024]{1,0:T(8,128)(2,1)S(1)}, bf16[64,1024]{1,0:T(8,128)(2,1)S(1)}, u32[]{:S(2)}, u32[]{:S(2)}) collective-permute-start(bf16[64,1024]{1,0:T(8,128)(2,1)S(1)} %shard_map.181), channel_id=1, source_target_pairs={{0,8},{2,10},{4,12},{6,14},{8,0},{10,2},{12,4},{14,6},{1,9},{3,11}... | collective-permute-start | bytes 393224 | tf_op jit(solution)/shard_map/ppermute | solution.py:63

commit v11 on v10

--- a/solution.py
+++ b/solution.py
@@ -15,10 +15,10 @@
 cost_hints = {
     "back_kernel": 8,
     "slot_kernel": 4,
-    "hidden_early_kernel": 4,
+    "hidden_early_kernel": 8,
     "message_early_kernel": 4,
     "late_kernel": 4,
-    "message_sum_kernel": 8,
+    "owner_kernel": 8,
 }
 f32 = jnp.float32
 bf16 = jnp.bfloat16

time: 65.2 us -> 67 us (1.028)
  starting transfers between devices: 25 us -> 26.9 us
    ppermute x21, starting transfers between devices: 25 us -> 26.9 us  [swap(): return lax.ppermute(value, axis, [(i, i ^ step) for i in range(size)])]
  transfers between devices with their start and end apart: 21 -> 21, of which waited for: 9 -> 8; matrix products, arithmetic and copies ran while one was open for 0% -> 0% of each run, Pallas kernels for 17% -> 17%
where the time goes in v11:
time: 67 us; the launch traced here: 66.8 us
  starting transfers between devices  26.9 us (40%)
  waiting for transfers between devices  21 us (31%)
  Pallas kernels  18 us (27%)
  between operations  0.84 us (1%)
    ppermute x21, starting transfers between devices, swap(): return lax.ppermute(value, axis, [(i, i ^ step) for i in range(size)])  26.9 us
    ppermute x21, waiting for transfers between devices, swap(): return lax.ppermute(value, axis, [(i, i ^ step) for i in range(size)])  21 us
    pallas_call x19, Pallas kernels, call(): pl.pallas_call(inner if count else body, out_shape=[jax.ShapeDtypeStruct(...  18 us
  transfers between devices with their start and end apart: 21, of which 8 were waited for; matrix products, arithmetic and copies ran while one was open for 0% of the time, Pallas kernels for 17%

profile of v11, /device:TPU:0, one launch (start us, length us, event | category | flops | bytes accessed | tf_op | source)
XLA Modules:
  0.0 66.8 jit_solution(15803460427590342465)
XLA Ops:
  0.6 1.1 %shard_map.164 = (bf16[128,64]{1,0:T(8,128)(2,1)S(1)}, bf16[4,16,1024]{2,1,0:T(8,128)(2,1)S(1)}, bf16[4,16,1024]{2,1,0:T(8,128)(2,1)S(1)}) custom-call(s32[1,8,8]{2,1,0:T(8,128)} %lists_ref.1, bf16[2,32,1024]{2,1,0:T(8,128)(2,1)} %latents_ref.1), custom_call_target="tpu_custom_call" | custom-call | tf_op jit(solution)/shard_map/pallas_call | solution.py:46
  1.8 3.0 %collective-permute-start = (bf16[4,16,1024]{2,1,0:T(8,128)(2,1)S(1)}, bf16[4,16,1024]{2,1,0:T(8,128)(2,1)S(1)}, u32[]{:S(2)}, u32[]{:S(2)}) collective-permute-start(bf16[4,16,1024]{2,1,0:T(8,128)(2,1)S(1)} %get-tuple-element.61), channel_id=1, source_target_pairs={{0,2},{2,0},{4,6},{6,4},{8,10},{10,8},{12,14},{14,12},{1,3},{3,1},... | collective-permute-start | bytes 393224 | tf_op jit(solution)/shard_map/ppermute | solution.py:63
  4.8 2.6 %shard_map.165 = (bf16[256,512]{1,0:T(8,128)(2,1)S(1)}, bf16[1024,1024]{1,0:T(8,128)(2,1)S(1)}, f32[1024]{0:T(1024)S(1)}, bf16[256,1024]{1,0:T(8,128)(2,1)S(1)},...) custom-call(bf16[128,64]{1,0:T(8,128)(2,1)S(1)} %get-tuple-element.52.refs_0_.pick_ref, ...), custom_call_target="tpu_custom_call" | custom-call | tf_op jit(solution)/shard_map/pallas_call | solution.py:46
  7.4 0.9 %collective-permute-done.refs_2_.near_ref = bf16[4,16,1024]{2,1,0:T(8,128)(2,1)S(1)} collective-permute-done((bf16[4,16,1024]{2,1,0:T(8,128)(2,1)S(1)}, bf16[4,16,1024]{2,1,0:T(8,128)(2,1)S(1)}, u32[]{:S(2)}, u32[]{:S(2)}) %collective-permute-start) | collective-permute-done | bytes 131104 | tf_op jit(solution)/shard_map/ppermute | solution.py:63
  8.3 3.9 %collective-permute-start.1 = (bf16[32,1024]{1,0:T(8,128)(2,1)S(1)}, bf16[32,1024]{1,0:T(8,128)(2,1)S(1)}, u32[]{:S(2)}, u32[]{:S(2)}) collective-permute-start(bf16[32,1024]{1,0:T(8,128)(2,1)S(1)} %get-tuple-element.62), channel_id=1, source_target_pairs={{0,12},{2,14},{4,8},{6,10},{8,4},{10,6},{12,0},{14,2},{1,13},{3,15... | collective-permute-start | bytes 196616 | tf_op jit(solution)/shard_map/ppermute | solution.py:63
  12.2 0.6 collective-permute-start.3
  12.8 2.0 %collective-permute-done.1.rest_0_ = bf16[32,1024]{1,0:T(8,128)(2,1)S(1)} collective-permute-done((bf16[32,1024]{1,0:T(8,128)(2,1)S(1)}, bf16[32,1024]{1,0:T(8,128)(2,1)S(1)}, u32[]{:S(2)}, u32[]{:S(2)}) %collective-permute-start.1) | collective-permute-done | bytes 65568 | tf_op jit(solution)/shard_map/ppermute | solution.py:63
  14.9 2.7 %collective-permute-done.2.rest_1_ = bf16[32,1024]{1,0:T(8,128)(2,1)S(1)} collective-permute-done((bf16[32,1024]{1,0:T(8,128)(2,1)S(1)}, bf16[32,1024]{1,0:T(8,128)(2,1)S(1)}, u32[]{:S(2)}, u32[]{:S(2)}) %collective-permute-start.2) | collective-permute-done | bytes 65568 | tf_op jit(solution)/shard_map/ppermute | solution.py:63
  17.6 3.5 %shard_map.167 = (f32[2,100,256]{2,1,0:T(8,128)S(1)}, bf16[2,100,256]{2,1,0:T(8,128)(2,1)S(1)}, bf16[512,1024]{1,0:T(8,128)(2,1)S(1)}, bf16[512,1024]{1,0:T(8,12...) custom-call(bf16[1024,1024]{1,0:T(8,128)(2,1)S(1)} %get-tuple-element.53.w_msg_ref, ...), custom_call_target="tpu_custom_call" | custom-call | tf_op jit(solution)/shard_map/pallas_call | solution.py:46
  21.1 0.9 %shard_map.168 = (bf16[2,2,4,64,512]{4,3,2,1,0:T(8,128)(2,1)S(1)}, bf16[2,2,4,64,512]{4,3,2,1,0:T(8,128)(2,1)S(1)}, bf16[2,4,64,128]{3,2,1,0:T(8,128)(2,1)S(1)}, bf16[2,4,64,128]{3,2,1,0:T(8,128)(2,1)S(1)}) custom-call(bf16[512,1024]{1,0:T(8,128)(2,1)S(1)} %get-tuple-element.68.normed_ref, bf16[512,1024]{1,0:T(8,128)(2,1)S(1)} %get-tuple-element.69.active_ref, ...), custom_call_target="tpu_custom_call" | custom-call | tf_op jit(solution)/shard_map/pallas_call | solution.py:46
  22.4 1.6 %shard_map.169 = (bf16[512,1024]{1,0:T(8,128)(2,1)S(1)}, bf16[128,512]{1,0:T(8,128)(2,1)S(1)}, f32[1]{0:T(128)}, bf16[256,1152]{1,0:T(8,128)(2,1)S(1)}, bf16[256,1152]{1,0:T(8,128)(2,1)S(1)}) custom-call(f32[2,100,256]{2,1,0:T(8,128)S(1)} %get-tuple-element.65.own_ref, bf16[2,100,256]{2,1,0:T(8,128)(2,1)S(1)} %collective-permute-done.4.other_ref, ...), custom_call_target="tpu_custom_call" | custom-call | tf_op jit(solution)/shard_map/pallas_call | solution.py:46
  24.7 1.6 %shard_map.170 = (f32[256,1152]{1,0:T(8,128)S(1)}, f32[256,1152]{1,0:T(8,128)S(1)}) custom-call(f32[1]{0:T(128)} %get-tuple-element.74.loss_ref, bf16[2,2,4,64,512]{4,3,2,1,0:T(8,128)(2,1)S(1)} %get-tuple-element.70.normed_t_ref, bf16[2,2,4,64,512]{4,3,2,1,0:T(8,128)(2,1)S(1)} %get-tuple-element.71.active_t_ref, ...), custom_call_target="tpu_custom_call" | custom-call | tf_op jit(solution)/shard_map/pallas_call | solution.py:46
  26.6 1.6 %collective-permute-start.8 = (bf16[128,1152]{1,0:T(8,128)(2,1)S(1)}, bf16[128,1152]{1,0:T(8,128)(2,1)S(1)}, u32[]{:S(2)}, u32[]{:S(2)}) collective-permute-start(bf16[128,1152]{1,0:T(8,128)(2,1)S(1)} %shard_map.171.refs_0_), channel_id=1, source_target_pairs={{0,2},{2,0},{4,6},{6,4},{8,10},{10,8},{12,14},{14,12},{1,3},{3,1},... | collective-permute-start | bytes 884744 | tf_op jit(solution)/shard_map/ppermute | solution.py:63
  28.2 1.6 %shard_map.172.refs_3_ = bf16[512,1024]{1,0:T(8,128)(2,1)S(1)} custom-call(bf16[128,1152]{1,0:T(8,128)(2,1)S(1)} %shard_map.171.refs_0_, bf16[512,1024]{1,0:T(8,128)(2,1)S(1)} %get-tuple-element.75.inner_ref.refs_1_, bf16[1024,1024]{1,0:T(8,128)(2,1)S(1)} %get-tuple-element.57.weights_ref.refs_2_, f32[1024]{0:T(1024)S(1)} %get-tuple-element.55.gain_ref.refs_3_, ...), custom_call_target="tpu_custom_call" | custom-call | flops 8000000000 | tf_op jit(solution)/shard_map/pallas_call | solution.py:46
  29.8 0.4 shard_map.173
  30.4 2.2 %collective-permute-start.10 = (bf16[32,1024]{1,0:T(8,128)(2,1)S(1)}, bf16[32,1024]{1,0:T(8,128)(2,1)S(1)}, u32[]{:S(2)}, u32[]{:S(2)}) collective-permute-start(bf16[32,1024]{1,0:T(8,128)(2,1)S(1)} %get-tuple-element.86), channel_id=1, source_target_pairs={{0,12},{2,14},{4,8},{6,10},{8,4},{10,6},{12,0},{14,2},{1,13},{3,15... | collective-permute-start | bytes 196616 | tf_op jit(solution)/shard_map/ppermute | solution.py:63
  32.6 2.2 %collective-permute-start.12 = (bf16[32,1024]{1,0:T(8,128)(2,1)S(1)}, bf16[32,1024]{1,0:T(8,128)(2,1)S(1)}, u32[]{:S(2)}, u32[]{:S(2)}) collective-permute-start(bf16[32,1024]{1,0:T(8,128)(2,1)S(1)} %get-tuple-element.88), channel_id=1, source_target_pairs={{0,4},{2,6},{4,0},{6,2},{8,12},{10,14},{12,8},{14,10},{1,5},{3,7},... | collective-permute-start | bytes 196616 | tf_op jit(solution)/shard_map/ppermute | solution.py:63
  34.8 0.7 %shard_map.175 = (bf16[128,1024]{1,0:T(8,128)(2,1)S(1)}, bf16[144,1024]{1,0:T(8,128)(2,1)S(1)}, bf16[144,1024]{1,0:T(8,128)(2,1)S(1)}, f32[256,1024]{1,0:T(8,128)S(1)}) custom-call(bf16[2,4,64,128]{3,2,1,0:T(8,128)(2,1)S(1)} %get-tuple-element.84.keep_ref, bf16[2,4,64,128]{3,2,1,0:T(8,128)(2,1)S(1)} %collective-permute-done.6.refs_1_.give_ref, ...), custom_call_target="tpu_custom_call" | custom-call | tf_op jit(solution)/shard_map/pallas_call | solution.py:46
  35.5 0.6 collective-permute-start.18
  36.1 1.5 %collective-permute-start.16 = (bf16[144,1024]{1,0:T(8,128)(2,1)S(1)}, bf16[144,1024]{1,0:T(8,128)(2,1)S(1)}, u32[]{:S(2)}, u32[]{:S(2)}) collective-permute-start(bf16[144,1024]{1,0:T(8,128)(2,1)S(1)} %get-tuple-element.93), channel_id=1, source_target_pairs={{0,2},{2,0},{4,6},{6,4},{8,10},{10,8},{12,14},{14,12},{1,3},{3,1},... | collective-permute-start | bytes 884744 | tf_op jit(solution)/shard_map/ppermute | solution.py:63
  37.9 1.7 %collective-permute-start.15 = (bf16[64,1152]{1,0:T(8,128)(2,1)S(1)}, bf16[64,1152]{1,0:T(8,128)(2,1)S(1)}, u32[]{:S(2)}, u32[]{:S(2)}) collective-permute-start(bf16[64,1152]{1,0:T(8,128)(2,1)S(1)} %get-tuple-element.91), channel_id=1, source_target_pairs={{0,8},{2,10},{4,12},{6,14},{8,0},{10,2},{12,4},{14,6},{1,9},{3,11}... | collective-permute-start | bytes 442376 | tf_op jit(solution)/shard_map/ppermute | solution.py:63
  39.5 2.2 %collective-permute-start.14 = (bf16[64,1152]{1,0:T(8,128)(2,1)S(1)}, bf16[64,1152]{1,0:T(8,128)(2,1)S(1)}, u32[]{:S(2)}, u32[]{:S(2)}) collective-permute-start(bf16[64,1152]{1,0:T(8,128)(2,1)S(1)} %get-tuple-element.83.refs_0_), channel_id=1, source_target_pairs={{0,12},{2,14},{4,8},{6,10},{8,4},{10,6},{12,0},{14,2},{1,13},{3,15... | collective-permute-start | bytes 442376 | tf_op jit(solution)/shard_map/ppermute | solution.py:63
  41.8 0.6 collective-permute-start.13
  42.4 2.4 %collective-permute-done.18.arrived_ref.refs_2_ = bf16[128,1024]{1,0:T(8,128)(2,1)S(1)} collective-permute-done((bf16[128,1024]{1,0:T(8,128)(2,1)S(1)}, bf16[128,1024]{1,0:T(8,128)(2,1)S(1)}, u32[]{:S(2)}, u32[]{:S(2)}) %collective-permute-start.18) | collective-permute-done | bytes 262176 | tf_op jit(solution)/shard_map/ppermute | solution.py:63
  44.9 2.2 %collective-permute-start.19 = (bf16[64,1024]{1,0:T(8,128)(2,1)S(1)}, bf16[64,1024]{1,0:T(8,128)(2,1)S(1)}, u32[]{:S(2)}, u32[]{:S(2)}) collective-permute-start(bf16[64,1024]{1,0:T(8,128)(2,1)S(1)} %shard_map.180), channel_id=1, source_target_pairs={{0,12},{2,14},{4,8},{6,10},{8,4},{10,6},{12,0},{14,2},{1,13},{3,15... | collective-permute-start | bytes 393224 | tf_op jit(solution)/shard_map/ppermute | solution.py:63
  47.1 5.6 %collective-permute-done.15.refs_5_.refs_0_ = bf16[64,1152]{1,0:T(8,128)(2,1)S(1)} collective-permute-done((bf16[64,1152]{1,0:T(8,128)(2,1)S(1)}, bf16[64,1152]{1,0:T(8,128)(2,1)S(1)}, u32[]{:S(2)}, u32[]{:S(2)}) %collective-permute-start.15) | collective-permute-done | bytes 147488 | tf_op jit(solution)/shard_map/ppermute | solution.py:63
  53.1 3.5 %collective-permute-start.17 = (bf16[144,1024]{1,0:T(8,128)(2,1)S(1)}, bf16[144,1024]{1,0:T(8,128)(2,1)S(1)}, u32[]{:S(2)}, u32[]{:S(2)}) collective-permute-start(bf16[144,1024]{1,0:T(8,128)(2,1)S(1)} %shard_map.178), channel_id=1, source_target_pairs={{0,4},{2,6},{4,0},{6,2},{8,12},{10,14},{12,8},{14,10},{1,5},{3,7},... | collective-permute-start | bytes 884744 | tf_op jit(solution)/shard_map/ppermute | solution.py:63
  56.6 2.2 %collective-permute-done.13.last_ref.refs_3_.refs_2_ = bf16[208,1024]{1,0:T(8,128)(2,1)S(1)} collective-permute-done((bf16[208,1024]{1,0:T(8,128)(2,1)S(1)}, bf16[208,1024]{1,0:T(8,128)(2,1)S(1)}, u32[]{:S(2)}, u32[]{:S(2)}) %collective-permute-start.13) | collective-permute-done | bytes 426016 | tf_op jit(solution)/shard_map/ppermute | solution.py:63
  58.9 1.5 %shard_map.177 = (bf16[2,32,1024]{2,1,0:T(8,128)(2,1)}, f32[8,128]{1,0:T(8,128)S(1)}) custom-call(bf16[128,64]{1,0:T(8,128)(2,1)S(1)} %get-tuple-element.52.refs_0_.pick_ref, bf16[1024,1024]{1,0:T(8,128)(2,1)S(1)} %copy-done, bf16[8,16,1024]{2,1,0:T(8,128)(2,1)S(1)} %get-tuple-element.81.slots_ref.refs_2_, ...), custom_call_target="tpu_custom_call" | custom-call | flops 8000000000 | tf_op jit(solution)/shard_map/pallas_call | solution.py:46
  60.4 4.6 %collective-permute-done.17.refs_6_.refs_5_ = bf16[144,1024]{1,0:T(8,128)(2,1)S(1)} collective-permute-done((bf16[144,1024]{1,0:T(8,128)(2,1)S(1)}, bf16[144,1024]{1,0:T(8,128)(2,1)S(1)}, u32[]{:S(2)}, u32[]{:S(2)}) %collective-permute-start.17) | collective-permute-done | bytes 294944 | tf_op jit(solution)/shard_map/ppermute | solution.py:63
  65.0 1.0 %shard_map.179 = (f32[64,1024]{1,0:T(8,128)}, f32[64,100]{1,0:T(8,128)}, f32[1]{0:T(128)}, f32[8,128]{1,0:T(8,128)S(1)}) custom-call(f32[8,128]{1,0:T(8,128)S(1)} %get-tuple-element.90.refs_0_, f32[256,1152]{1,0:T(8,128)S(1)} %get-tuple-element.82.held_ref.refs_1_, bf16[256,1152]{1,0:T(8,128)(2,1)S(1)} %collective-permute-done.5.refs_0_.other_ref.refs_2_, ...), custom_call_target="tpu_custom_call" | custom-call | tf_op jit(solution)/shard_map/pallas_call | solution.py:46
  66.0 0.8 %shard_map.182 = f32[64,1024]{1,0:T(8,128)} custom-call(f32[8,128]{1,0:T(8,128)S(1)} %get-tuple-element.95.refs_0_, f32[256,1024]{1,0:T(8,128)S(1)} %get-tuple-element.92.near_ref.refs_1_, bf16[208,1024]{1,0:T(8,128)(2,1)S(1)} %collective-permute-done.13.last_ref.refs_3_.refs_2_, bf16[64,1024]{1,0:T(8,128)(2,1)S(1)} %collective-permute-done.19.refs_3_, ...), custom_call_target="tpu_custom_call" | custom-call | tf_op jit(solution)/shard_map/pallas_call | solution.py:46
  (35 shorter events, 2.1 us)
Async XLA Ops:
  1.8 6.5 %collective-permute-start = (bf16[4,16,1024]{2,1,0:T(8,128)(2,1)S(1)}, bf16[4,16,1024]{2,1,0:T(8,128)(2,1)S(1)}, u32[]{:S(2)}, u32[]{:S(2)}) collective-permute-start(bf16[4,16,1024]{2,1,0:T(8,128)(2,1)S(1)} %get-tuple-element.61), channel_id=1, source_target_pairs={{0,2},{2,0},{4,6},{6,4},{8,10},{10,8},{12,14},{14,12},{1,3},{3,1},... | collective-permute-start | bytes 393224 | tf_op jit(solution)/shard_map/ppermute | solution.py:63
  8.3 6.6 %collective-permute-start.1 = (bf16[32,1024]{1,0:T(8,128)(2,1)S(1)}, bf16[32,1024]{1,0:T(8,128)(2,1)S(1)}, u32[]{:S(2)}, u32[]{:S(2)}) collective-permute-start(bf16[32,1024]{1,0:T(8,128)(2,1)S(1)} %get-tuple-element.62), channel_id=1, source_target_pairs={{0,12},{2,14},{4,8},{6,10},{8,4},{10,6},{12,0},{14,2},{1,13},{3,15... | collective-permute-start | bytes 196616 | tf_op jit(solution)/shard_map/ppermute | solution.py:63
  12.2 5.4 %collective-permute-start.2 = (bf16[32,1024]{1,0:T(8,128)(2,1)S(1)}, bf16[32,1024]{1,0:T(8,128)(2,1)S(1)}, u32[]{:S(2)}, u32[]{:S(2)}) collective-permute-start(bf16[32,1024]{1,0:T(8,128)(2,1)S(1)} %get-tuple-element.63), channel_id=1, source_target_pairs={{0,8},{2,10},{4,12},{6,14},{8,0},{10,2},{12,4},{14,6},{1,9},{3,11}... | collective-permute-start | bytes 196616 | tf_op jit(solution)/shard_map/ppermute | solution.py:63
  12.2 5.4 %collective-permute-start.3 = (bf16[32,1024]{1,0:T(8,128)(2,1)S(1)}, bf16[32,1024]{1,0:T(8,128)(2,1)S(1)}, u32[]{:S(2)}, u32[]{:S(2)}) collective-permute-start(bf16[32,1024]{1,0:T(8,128)(2,1)S(1)} %get-tuple-element.64), channel_id=1, source_target_pairs={{0,4},{2,6},{4,0},{6,2},{8,12},{10,14},{12,8},{14,10},{1,5},{3,7},... | collective-permute-start | bytes 196616 | tf_op jit(solution)/shard_map/ppermute | solution.py:63
  21.0 1.4 %copy-start.1 = (f32[100,256]{1,0:T(8,128)S(1)}, f32[100,256]{1,0:T(8,128)}, u32[]{:S(2)}) copy-start(f32[100,256]{1,0:T(8,128)} %truth_ref.1) | copy-start | bytes 307204
  21.1 1.4 %copy-start.2 = (f32[256]{0:T(256)S(1)}, f32[256]{0:T(256)}, u32[]{:S(2)}) copy-start(f32[256]{0:T(256)} %cell_ref.1) | copy-start | bytes 3076
  21.1 1.4 %collective-permute-start.4 = (bf16[2,100,256]{2,1,0:T(8,128)(2,1)S(1)}, bf16[2,100,256]{2,1,0:T(8,128)(2,1)S(1)}, u32[]{:S(2)}, u32[]{:S(2)}) collective-permute-start(bf16[2,100,256]{2,1,0:T(8,128)(2,1)S(1)} %get-tuple-element.66), channel_id=1, source_target_pairs={{0,1},{1,0},{2,3},{3,2},{4,5},{5,4},{6,7},{7,6},{8,9},{9,8},{10,11... | collective-permute-start | bytes 307208 | tf_op jit(solution)/shard_map/ppermute | solution.py:63
  24.0 2.3 %collective-permute-start.7 = (bf16[256,1152]{1,0:T(8,128)(2,1)S(1)}, bf16[256,1152]{1,0:T(8,128)(2,1)S(1)}, u32[]{:S(2)}, u32[]{:S(2)}) collective-permute-start(bf16[256,1152]{1,0:T(8,128)(2,1)S(1)} %get-tuple-element.78), channel_id=1, source_target_pairs={{0,1},{1,0},{2,3},{3,2},{4,5},{5,4},{6,7},{7,6},{8,9},{9,8},{10,11... | collective-permute-start | bytes 1769480 | tf_op jit(solution)/shard_map/ppermute | solution.py:63
  24.2 5.6 %collective-permute-start.6 = (bf16[2,4,64,128]{3,2,1,0:T(8,128)(2,1)S(1)}, bf16[2,4,64,128]{3,2,1,0:T(8,128)(2,1)S(1)}, u32[]{:S(2)}, u32[]{:S(2)}) collective-permute-start(bf16[2,4,64,128]{3,2,1,0:T(8,128)(2,1)S(1)} %get-tuple-element.73), channel_id=1, source_target_pairs={{0,1},{1,0},{2,3},{3,2},{4,5},{5,4},{6,7},{7,6},{8,9},{9,8},{10,11... | collective-permute-start | bytes 393224 | tf_op jit(solution)/shard_map/ppermute | solution.py:63
  24.6 5.2 %collective-permute-start.5 = (bf16[256,1152]{1,0:T(8,128)(2,1)S(1)}, bf16[256,1152]{1,0:T(8,128)(2,1)S(1)}, u32[]{:S(2)}, u32[]{:S(2)}) collective-permute-start(bf16[256,1152]{1,0:T(8,128)(2,1)S(1)} %get-tuple-element.72), channel_id=1, source_target_pairs={{0,1},{1,0},{2,3},{3,2},{4,5},{5,4},{6,7},{7,6},{8,9},{9,8},{10,11... | collective-permute-start | bytes 1769480 | tf_op jit(solution)/shard_map/ppermute | solution.py:63
  26.6 9.5 %collective-permute-start.8 = (bf16[128,1152]{1,0:T(8,128)(2,1)S(1)}, bf16[128,1152]{1,0:T(8,128)(2,1)S(1)}, u32[]{:S(2)}, u32[]{:S(2)}) collective-permute-start(bf16[128,1152]{1,0:T(8,128)(2,1)S(1)} %shard_map.171.refs_0_), channel_id=1, source_target_pairs={{0,2},{2,0},{4,6},{6,4},{8,10},{10,8},{12,14},{14,12},{1,3},{3,1},... | collective-permute-start | bytes 884744 | tf_op jit(solution)/shard_map/ppermute | solution.py:63
  30.3 4.5 %collective-permute-start.9 = (bf16[8,16,1024]{2,1,0:T(8,128)(2,1)S(1)}, bf16[8,16,1024]{2,1,0:T(8,128)(2,1)S(1)}, u32[]{:S(2)}, u32[]{:S(2)}) collective-permute-start(bf16[8,16,1024]{2,1,0:T(8,128)(2,1)S(1)} %get-tuple-element.81.slots_ref.refs_2_), channel_id=1, source_target_pairs={{0,1},{1,0},{2,3},{3,2},{4,5},{5,4},{6,7},{7,6},{8,9},{9,8},{10,11... | collective-permute-start | bytes 786440 | tf_op jit(solution)/shard_map/ppermute | solution.py:63
  30.4 7.5 %collective-permute-start.10 = (bf16[32,1024]{1,0:T(8,128)(2,1)S(1)}, bf16[32,1024]{1,0:T(8,128)(2,1)S(1)}, u32[]{:S(2)}, u32[]{:S(2)}) collective-permute-start(bf16[32,1024]{1,0:T(8,128)(2,1)S(1)} %get-tuple-element.86), channel_id=1, source_target_pairs={{0,12},{2,14},{4,8},{6,10},{8,4},{10,6},{12,0},{14,2},{1,13},{3,15... | collective-permute-start | bytes 196616 | tf_op jit(solution)/shard_map/ppermute | solution.py:63
  32.6 7.0 %collective-permute-start.11 = (bf16[32,1024]{1,0:T(8,128)(2,1)S(1)}, bf16[32,1024]{1,0:T(8,128)(2,1)S(1)}, u32[]{:S(2)}, u32[]{:S(2)}) collective-permute-start(bf16[32,1024]{1,0:T(8,128)(2,1)S(1)} %get-tuple-element.87), channel_id=1, source_target_pairs={{0,8},{2,10},{4,12},{6,14},{8,0},{10,2},{12,4},{14,6},{1,9},{3,11}... | collective-permute-start | bytes 196616 | tf_op jit(solution)/shard_map/ppermute | solution.py:63
  32.6 9.2 %collective-permute-start.12 = (bf16[32,1024]{1,0:T(8,128)(2,1)S(1)}, bf16[32,1024]{1,0:T(8,128)(2,1)S(1)}, u32[]{:S(2)}, u32[]{:S(2)}) collective-permute-start(bf16[32,1024]{1,0:T(8,128)(2,1)S(1)} %get-tuple-element.88), channel_id=1, source_target_pairs={{0,4},{2,6},{4,0},{6,2},{8,12},{10,14},{12,8},{14,10},{1,5},{3,7},... | collective-permute-start | bytes 196616 | tf_op jit(solution)/shard_map/ppermute | solution.py:63
  35.5 9.3 %collective-permute-start.18 = (bf16[128,1024]{1,0:T(8,128)(2,1)S(1)}, bf16[128,1024]{1,0:T(8,128)(2,1)S(1)}, u32[]{:S(2)}, u32[]{:S(2)}) collective-permute-start(bf16[128,1024]{1,0:T(8,128)(2,1)S(1)} %get-tuple-element.96), channel_id=1, source_target_pairs={{0,2},{2,0},{4,6},{6,4},{8,10},{10,8},{12,14},{14,12},{1,3},{3,1},... | collective-permute-start | bytes 786440 | tf_op jit(solution)/shard_map/ppermute | solution.py:63
  36.1 16.8 %collective-permute-start.16 = (bf16[144,1024]{1,0:T(8,128)(2,1)S(1)}, bf16[144,1024]{1,0:T(8,128)(2,1)S(1)}, u32[]{:S(2)}, u32[]{:S(2)}) collective-permute-start(bf16[144,1024]{1,0:T(8,128)(2,1)S(1)} %get-tuple-element.93), channel_id=1, source_target_pairs={{0,2},{2,0},{4,6},{6,4},{8,10},{10,8},{12,14},{14,12},{1,3},{3,1},... | collective-permute-start | bytes 884744 | tf_op jit(solution)/shard_map/ppermute | solution.py:63
  37.9 14.9 %collective-permute-start.15 = (bf16[64,1152]{1,0:T(8,128)(2,1)S(1)}, bf16[64,1152]{1,0:T(8,128)(2,1)S(1)}, u32[]{:S(2)}, u32[]{:S(2)}) collective-permute-start(bf16[64,1152]{1,0:T(8,128)(2,1)S(1)} %get-tuple-element.91), channel_id=1, source_target_pairs={{0,8},{2,10},{4,12},{6,14},{8,0},{10,2},{12,4},{14,6},{1,9},{3,11}... | collective-permute-start | bytes 442376 | tf_op jit(solution)/shard_map/ppermute | solution.py:63
  39.5 20.9 %collective-permute-start.14 = (bf16[64,1152]{1,0:T(8,128)(2,1)S(1)}, bf16[64,1152]{1,0:T(8,128)(2,1)S(1)}, u32[]{:S(2)}, u32[]{:S(2)}) collective-permute-start(bf16[64,1152]{1,0:T(8,128)(2,1)S(1)} %get-tuple-element.83.refs_0_), channel_id=1, source_target_pairs={{0,12},{2,14},{4,8},{6,10},{8,4},{10,6},{12,0},{14,2},{1,13},{3,15... | collective-permute-start | bytes 442376 | tf_op jit(solution)/shard_map/ppermute | solution.py:63
  41.8 17.0 %collective-permute-start.13 = (bf16[208,1024]{1,0:T(8,128)(2,1)S(1)}, bf16[208,1024]{1,0:T(8,128)(2,1)S(1)}, u32[]{:S(2)}, u32[]{:S(2)}) collective-permute-start(bf16[208,1024]{1,0:T(8,128)(2,1)S(1)} %shard_map.176), channel_id=1, source_target_pairs={{0,2},{2,0},{4,6},{6,4},{8,10},{10,8},{12,14},{14,12},{1,3},{3,1},... | collective-permute-start | bytes 1277960 | tf_op jit(solution)/shard_map/ppermute | solution.py:63
  44.9 21.1 %collective-permute-start.19 = (bf16[64,1024]{1,0:T(8,128)(2,1)S(1)}, bf16[64,1024]{1,0:T(8,128)(2,1)S(1)}, u32[]{:S(2)}, u32[]{:S(2)}) collective-permute-start(bf16[64,1024]{1,0:T(8,128)(2,1)S(1)} %shard_map.180), channel_id=1, source_target_pairs={{0,12},{2,14},{4,8},{6,10},{8,4},{10,6},{12,0},{14,2},{1,13},{3,15... | collective-permute-start | bytes 393224 | tf_op jit(solution)/shard_map/ppermute | solution.py:63
  52.8 6.1 %copy-start = (bf16[1024,1024]{1,0:T(8,128)(2,1)S(1)}, bf16[1024,1024]{1,0:T(8,128)(2,1)}, u32[]{:S(2)}) copy-start(bf16[1024,1024]{1,0:T(8,128)(2,1)} %w_msg_ref.1) | copy-start | bytes 6291460
  52.8 13.2 %collective-permute-start.20 = (bf16[64,1024]{1,0:T(8,128)(2,1)S(1)}, bf16[64,1024]{1,0:T(8,128)(2,1)S(1)}, u32[]{:S(2)}, u32[]{:S(2)}) collective-permute-start(bf16[64,1024]{1,0:T(8,128)(2,1)S(1)} %shard_map.181), channel_id=1, source_target_pairs={{0,8},{2,10},{4,12},{6,14},{8,0},{10,2},{12,4},{14,6},{1,9},{3,11}... | collective-permute-start | bytes 393224 | tf_op jit(solution)/shard_map/ppermute | solution.py:63
  53.1 11.9 %collective-permute-start.17 = (bf16[144,1024]{1,0:T(8,128)(2,1)S(1)}, bf16[144,1024]{1,0:T(8,128)(2,1)S(1)}, u32[]{:S(2)}, u32[]{:S(2)}) collective-permute-start(bf16[144,1024]{1,0:T(8,128)(2,1)S(1)} %shard_map.178), channel_id=1, source_target_pairs={{0,4},{2,6},{4,0},{6,2},{8,12},{10,14},{12,8},{14,10},{1,5},{3,7},... | collective-permute-start | bytes 884744 | tf_op jit(solution)/shard_map/ppermute | solution.py:63

commit v12 on v10

--- a/solution.py
+++ b/solution.py
@@ -451,7 +451,7 @@
     loss_ref[0] = jnp.sum(jnp.where(spots & first, part[:8], 0.0)) * scale
 
 
-def message_sum_kernel(early, near_ref, last_ref, *rest):
+def message_partial_kernel(early, near_ref, last_ref, *rest):
     out_ref = rest[-1]
     block = out_ref.shape[0]
     total = near_ref[near_ref.shape[0] - block :, :]
@@ -460,6 +460,10 @@
         begin = 0 if i < early else block
         total = total + r[begin : begin + block, :].astype(f32)
     out_ref[...] = total
+
+
+def message_sum_kernel(partial_ref, arrived_ref, out_ref):
+    out_ref[...] = partial_ref[...] + arrived_ref[...].astype(f32)
 
 
 def on_device(
@@ -652,12 +656,15 @@
         scalar_outs=(2,),
         after=[latent_done],
     )
-    (msg_weight_grad,) = call(
-        functools.partial(message_sum_kernel, early),
+    (message_partial,) = call(
+        functools.partial(message_partial_kernel, early - 1),
         [((block, width), f32)],
-        [message_near, last_other] + message_parts + late_parts,
+        [message_near, last_other] + message_parts[:-1] + late_parts,
         limit=6,
         after=[hidden_done],
+    )
+    (msg_weight_grad,) = call(
+        message_sum_kernel, [((block, width), f32)], [message_partial, message_parts[-1]], limit=4
     )
     return (latent_grad, loss, msg_weight_grad, hidden_weight_grad, out_weight_grad)
 

time: 65.2 us -> 65.2 us (level)
    pallas_call x19 -> x20, Pallas kernels: 18.1 us -> 18.1 us  [call(): pl.pallas_call(inner if count else body, out_shape=[jax.ShapeDtypeStruct(...]
where the time goes in v12:
time: 65.2 us; the launch traced here: 64.9 us
  starting transfers between devices  24.9 us (38%)
  waiting for transfers between devices  21.1 us (32%)
  Pallas kernels  18.1 us (28%)
  between operations  0.83 us (1%)
    ppermute x21, starting transfers between devices, swap(): return lax.ppermute(value, axis, [(i, i ^ step) for i in range(size)])  24.9 us
    ppermute x21, waiting for transfers between devices, swap(): return lax.ppermute(value, axis, [(i, i ^ step) for i in range(size)])  21.1 us
    pallas_call x20, Pallas kernels, call(): pl.pallas_call(inner if count else body, out_shape=[jax.ShapeDtypeStruct(...  18.1 us
  transfers between devices with their start and end apart: 21, of which 9 were waited for; matrix products, arithmetic and copies ran while one was open for 0% of the time, Pallas kernels for 17%

profile of v12, /device:TPU:0, one launch (start us, length us, event | category | flops | bytes accessed | tf_op | source)
XLA Modules:
  0.0 64.9 jit_solution(4458550260975206844)
XLA Ops:
  0.6 1.1 %shard_map.164 = (bf16[128,64]{1,0:T(8,128)(2,1)S(1)}, bf16[4,16,1024]{2,1,0:T(8,128)(2,1)S(1)}, bf16[4,16,1024]{2,1,0:T(8,128)(2,1)S(1)}) custom-call(s32[1,8,8]{2,1,0:T(8,128)} %lists_ref.1, bf16[2,32,1024]{2,1,0:T(8,128)(2,1)} %latents_ref.1), custom_call_target="tpu_custom_call" | custom-call | tf_op jit(solution)/shard_map/pallas_call | solution.py:46
  1.8 3.0 %collective-permute-start = (bf16[4,16,1024]{2,1,0:T(8,128)(2,1)S(1)}, bf16[4,16,1024]{2,1,0:T(8,128)(2,1)S(1)}, u32[]{:S(2)}, u32[]{:S(2)}) collective-permute-start(bf16[4,16,1024]{2,1,0:T(8,128)(2,1)S(1)} %get-tuple-element.61), channel_id=1, source_target_pairs={{0,2},{2,0},{4,6},{6,4},{8,10},{10,8},{12,14},{14,12},{1,3},{3,1},... | collective-permute-start | bytes 393224 | tf_op jit(solution)/shard_map/ppermute | solution.py:63
  4.8 2.6 %shard_map.165 = (bf16[256,512]{1,0:T(8,128)(2,1)S(1)}, bf16[1024,1024]{1,0:T(8,128)(2,1)S(1)}, f32[1024]{0:T(1024)S(1)}, bf16[256,1024]{1,0:T(8,128)(2,1)S(1)},...) custom-call(bf16[128,64]{1,0:T(8,128)(2,1)S(1)} %get-tuple-element.52.refs_0_.pick_ref, ...), custom_call_target="tpu_custom_call" | custom-call | tf_op jit(solution)/shard_map/pallas_call | solution.py:46
  7.4 0.9 %collective-permute-done.refs_2_.near_ref = bf16[4,16,1024]{2,1,0:T(8,128)(2,1)S(1)} collective-permute-done((bf16[4,16,1024]{2,1,0:T(8,128)(2,1)S(1)}, bf16[4,16,1024]{2,1,0:T(8,128)(2,1)S(1)}, u32[]{:S(2)}, u32[]{:S(2)}) %collective-permute-start) | collective-permute-done | bytes 131104 | tf_op jit(solution)/shard_map/ppermute | solution.py:63
  8.3 3.9 %collective-permute-start.1 = (bf16[32,1024]{1,0:T(8,128)(2,1)S(1)}, bf16[32,1024]{1,0:T(8,128)(2,1)S(1)}, u32[]{:S(2)}, u32[]{:S(2)}) collective-permute-start(bf16[32,1024]{1,0:T(8,128)(2,1)S(1)} %get-tuple-element.62), channel_id=1, source_target_pairs={{0,12},{2,14},{4,8},{6,10},{8,4},{10,6},{12,0},{14,2},{1,13},{3,15... | collective-permute-start | bytes 196616 | tf_op jit(solution)/shard_map/ppermute | solution.py:63
  12.2 0.6 collective-permute-start.3
  12.8 2.0 %collective-permute-done.1.rest_0_ = bf16[32,1024]{1,0:T(8,128)(2,1)S(1)} collective-permute-done((bf16[32,1024]{1,0:T(8,128)(2,1)S(1)}, bf16[32,1024]{1,0:T(8,128)(2,1)S(1)}, u32[]{:S(2)}, u32[]{:S(2)}) %collective-permute-start.1) | collective-permute-done | bytes 65568 | tf_op jit(solution)/shard_map/ppermute | solution.py:63
  14.9 2.7 %collective-permute-done.2.rest_1_ = bf16[32,1024]{1,0:T(8,128)(2,1)S(1)} collective-permute-done((bf16[32,1024]{1,0:T(8,128)(2,1)S(1)}, bf16[32,1024]{1,0:T(8,128)(2,1)S(1)}, u32[]{:S(2)}, u32[]{:S(2)}) %collective-permute-start.2) | collective-permute-done | bytes 65568 | tf_op jit(solution)/shard_map/ppermute | solution.py:63
  17.6 3.5 %shard_map.167 = (f32[2,100,256]{2,1,0:T(8,128)S(1)}, bf16[2,100,256]{2,1,0:T(8,128)(2,1)S(1)}, bf16[512,1024]{1,0:T(8,128)(2,1)S(1)}, bf16[512,1024]{1,0:T(8,12...) custom-call(bf16[1024,1024]{1,0:T(8,128)(2,1)S(1)} %get-tuple-element.53.w_msg_ref, ...), custom_call_target="tpu_custom_call" | custom-call | tf_op jit(solution)/shard_map/pallas_call | solution.py:46
  21.1 0.9 %shard_map.168 = (bf16[2,2,4,64,512]{4,3,2,1,0:T(8,128)(2,1)S(1)}, bf16[2,2,4,64,512]{4,3,2,1,0:T(8,128)(2,1)S(1)}, bf16[2,4,64,128]{3,2,1,0:T(8,128)(2,1)S(1)}, bf16[2,4,64,128]{3,2,1,0:T(8,128)(2,1)S(1)}) custom-call(bf16[512,1024]{1,0:T(8,128)(2,1)S(1)} %get-tuple-element.68.normed_ref, bf16[512,1024]{1,0:T(8,128)(2,1)S(1)} %get-tuple-element.69.active_ref, ...), custom_call_target="tpu_custom_call" | custom-call | tf_op jit(solution)/shard_map/pallas_call | solution.py:46
  22.4 1.6 %shard_map.169 = (bf16[512,1024]{1,0:T(8,128)(2,1)S(1)}, bf16[128,512]{1,0:T(8,128)(2,1)S(1)}, f32[1]{0:T(128)}, bf16[256,1152]{1,0:T(8,128)(2,1)S(1)}, bf16[256,1152]{1,0:T(8,128)(2,1)S(1)}) custom-call(f32[2,100,256]{2,1,0:T(8,128)S(1)} %get-tuple-element.65.own_ref, bf16[2,100,256]{2,1,0:T(8,128)(2,1)S(1)} %collective-permute-done.4.other_ref, ...), custom_call_target="tpu_custom_call" | custom-call | tf_op jit(solution)/shard_map/pallas_call | solution.py:46
  24.7 1.6 %shard_map.170 = (f32[256,1152]{1,0:T(8,128)S(1)}, f32[256,1152]{1,0:T(8,128)S(1)}) custom-call(f32[1]{0:T(128)} %get-tuple-element.74.loss_ref, bf16[2,2,4,64,512]{4,3,2,1,0:T(8,128)(2,1)S(1)} %get-tuple-element.70.normed_t_ref, bf16[2,2,4,64,512]{4,3,2,1,0:T(8,128)(2,1)S(1)} %get-tuple-element.71.active_t_ref, ...), custom_call_target="tpu_custom_call" | custom-call | tf_op jit(solution)/shard_map/pallas_call | solution.py:46
  26.6 1.6 %collective-permute-start.8 = (bf16[128,1152]{1,0:T(8,128)(2,1)S(1)}, bf16[128,1152]{1,0:T(8,128)(2,1)S(1)}, u32[]{:S(2)}, u32[]{:S(2)}) collective-permute-start(bf16[128,1152]{1,0:T(8,128)(2,1)S(1)} %shard_map.171.refs_0_), channel_id=1, source_target_pairs={{0,2},{2,0},{4,6},{6,4},{8,10},{10,8},{12,14},{14,12},{1,3},{3,1},... | collective-permute-start | bytes 884744 | tf_op jit(solution)/shard_map/ppermute | solution.py:63
  28.2 1.6 %shard_map.172.refs_3_ = bf16[512,1024]{1,0:T(8,128)(2,1)S(1)} custom-call(bf16[128,1152]{1,0:T(8,128)(2,1)S(1)} %shard_map.171.refs_0_, bf16[512,1024]{1,0:T(8,128)(2,1)S(1)} %get-tuple-element.75.inner_ref.refs_1_, bf16[1024,1024]{1,0:T(8,128)(2,1)S(1)} %get-tuple-element.57.weights_ref.refs_2_, f32[1024]{0:T(1024)S(1)} %get-tuple-element.55.gain_ref.refs_3_, ...), custom_call_target="tpu_custom_call" | custom-call | flops 8000000000 | tf_op jit(solution)/shard_map/pallas_call | solution.py:46
  30.4 2.2 %collective-permute-start.10 = (bf16[32,1024]{1,0:T(8,128)(2,1)S(1)}, bf16[32,1024]{1,0:T(8,128)(2,1)S(1)}, u32[]{:S(2)}, u32[]{:S(2)}) collective-permute-start(bf16[32,1024]{1,0:T(8,128)(2,1)S(1)} %get-tuple-element.86), channel_id=1, source_target_pairs={{0,12},{2,14},{4,8},{6,10},{8,4},{10,6},{12,0},{14,2},{1,13},{3,15... | collective-permute-start | bytes 196616 | tf_op jit(solution)/shard_map/ppermute | solution.py:63
  32.6 2.2 %collective-permute-start.12 = (bf16[32,1024]{1,0:T(8,128)(2,1)S(1)}, bf16[32,1024]{1,0:T(8,128)(2,1)S(1)}, u32[]{:S(2)}, u32[]{:S(2)}) collective-permute-start(bf16[32,1024]{1,0:T(8,128)(2,1)S(1)} %get-tuple-element.88), channel_id=1, source_target_pairs={{0,4},{2,6},{4,0},{6,2},{8,12},{10,14},{12,8},{14,10},{1,5},{3,7},... | collective-permute-start | bytes 196616 | tf_op jit(solution)/shard_map/ppermute | solution.py:63
  34.8 0.7 %shard_map.175 = (bf16[128,1024]{1,0:T(8,128)(2,1)S(1)}, bf16[144,1024]{1,0:T(8,128)(2,1)S(1)}, bf16[144,1024]{1,0:T(8,128)(2,1)S(1)}, f32[256,1024]{1,0:T(8,128)S(1)}) custom-call(bf16[2,4,64,128]{3,2,1,0:T(8,128)(2,1)S(1)} %get-tuple-element.84.keep_ref, bf16[2,4,64,128]{3,2,1,0:T(8,128)(2,1)S(1)} %collective-permute-done.6.refs_1_.give_ref, ...), custom_call_target="tpu_custom_call" | custom-call | tf_op jit(solution)/shard_map/pallas_call | solution.py:46
  35.5 0.6 collective-permute-start.18
  36.1 1.5 %collective-permute-start.16 = (bf16[144,1024]{1,0:T(8,128)(2,1)S(1)}, bf16[144,1024]{1,0:T(8,128)(2,1)S(1)}, u32[]{:S(2)}, u32[]{:S(2)}) collective-permute-start(bf16[144,1024]{1,0:T(8,128)(2,1)S(1)} %get-tuple-element.93), channel_id=1, source_target_pairs={{0,2},{2,0},{4,6},{6,4},{8,10},{10,8},{12,14},{14,12},{1,3},{3,1},... | collective-permute-start | bytes 884744 | tf_op jit(solution)/shard_map/ppermute | solution.py:63
  37.9 1.7 %collective-permute-start.15 = (bf16[64,1152]{1,0:T(8,128)(2,1)S(1)}, bf16[64,1152]{1,0:T(8,128)(2,1)S(1)}, u32[]{:S(2)}, u32[]{:S(2)}) collective-permute-start(bf16[64,1152]{1,0:T(8,128)(2,1)S(1)} %get-tuple-element.91), channel_id=1, source_target_pairs={{0,8},{2,10},{4,12},{6,14},{8,0},{10,2},{12,4},{14,6},{1,9},{3,11}... | collective-permute-start | bytes 442376 | tf_op jit(solution)/shard_map/ppermute | solution.py:63
  39.5 2.2 %collective-permute-start.14 = (bf16[64,1152]{1,0:T(8,128)(2,1)S(1)}, bf16[64,1152]{1,0:T(8,128)(2,1)S(1)}, u32[]{:S(2)}, u32[]{:S(2)}) collective-permute-start(bf16[64,1152]{1,0:T(8,128)(2,1)S(1)} %get-tuple-element.83.refs_0_), channel_id=1, source_target_pairs={{0,12},{2,14},{4,8},{6,10},{8,4},{10,6},{12,0},{14,2},{1,13},{3,15... | collective-permute-start | bytes 442376 | tf_op jit(solution)/shard_map/ppermute | solution.py:63
  41.8 0.6 collective-permute-start.13
  42.4 2.4 %collective-permute-done.18.arrived_ref.refs_2_ = bf16[128,1024]{1,0:T(8,128)(2,1)S(1)} collective-permute-done((bf16[128,1024]{1,0:T(8,128)(2,1)S(1)}, bf16[128,1024]{1,0:T(8,128)(2,1)S(1)}, u32[]{:S(2)}, u32[]{:S(2)}) %collective-permute-start.18) | collective-permute-done | bytes 262176 | tf_op jit(solution)/shard_map/ppermute | solution.py:63
  44.9 2.2 %collective-permute-start.19 = (bf16[64,1024]{1,0:T(8,128)(2,1)S(1)}, bf16[64,1024]{1,0:T(8,128)(2,1)S(1)}, u32[]{:S(2)}, u32[]{:S(2)}) collective-permute-start(bf16[64,1024]{1,0:T(8,128)(2,1)S(1)} %shard_map.180), channel_id=1, source_target_pairs={{0,12},{2,14},{4,8},{6,10},{8,4},{10,6},{12,0},{14,2},{1,13},{3,15... | collective-permute-start | bytes 393224 | tf_op jit(solution)/shard_map/ppermute | solution.py:63
  47.1 4.0 %collective-permute-done.16.arrived_ref = bf16[144,1024]{1,0:T(8,128)(2,1)S(1)} collective-permute-done((bf16[144,1024]{1,0:T(8,128)(2,1)S(1)}, bf16[144,1024]{1,0:T(8,128)(2,1)S(1)}, u32[]{:S(2)}, u32[]{:S(2)}) %collective-permute-start.16) | collective-permute-done | bytes 294944 | tf_op jit(solution)/shard_map/ppermute | solution.py:63
  51.5 1.3 %collective-permute-done.15.refs_5_.refs_0_ = bf16[64,1152]{1,0:T(8,128)(2,1)S(1)} collective-permute-done((bf16[64,1152]{1,0:T(8,128)(2,1)S(1)}, bf16[64,1152]{1,0:T(8,128)(2,1)S(1)}, u32[]{:S(2)}, u32[]{:S(2)}) %collective-permute-start.15) | collective-permute-done | bytes 147488 | tf_op jit(solution)/shard_map/ppermute | solution.py:63
  52.8 1.5 %collective-permute-start.20 = (bf16[64,1024]{1,0:T(8,128)(2,1)S(1)}, bf16[64,1024]{1,0:T(8,128)(2,1)S(1)}, u32[]{:S(2)}, u32[]{:S(2)}) collective-permute-start(bf16[64,1024]{1,0:T(8,128)(2,1)S(1)} %shard_map.182), channel_id=1, source_target_pairs={{0,8},{2,10},{4,12},{6,14},{8,0},{10,2},{12,4},{14,6},{1,9},{3,11}... | collective-permute-start | bytes 393224 | tf_op jit(solution)/shard_map/ppermute | solution.py:63
  54.3 4.6 %collective-permute-done.13.last_ref.refs_3_.refs_2_ = bf16[208,1024]{1,0:T(8,128)(2,1)S(1)} collective-permute-done((bf16[208,1024]{1,0:T(8,128)(2,1)S(1)}, bf16[208,1024]{1,0:T(8,128)(2,1)S(1)}, u32[]{:S(2)}, u32[]{:S(2)}) %collective-permute-start.13) | collective-permute-done | bytes 426016 | tf_op jit(solution)/shard_map/ppermute | solution.py:63
  58.9 1.5 %shard_map.177 = (bf16[2,32,1024]{2,1,0:T(8,128)(2,1)}, f32[8,128]{1,0:T(8,128)S(1)}) custom-call(bf16[128,64]{1,0:T(8,128)(2,1)S(1)} %get-tuple-element.52.refs_0_.pick_ref, bf16[1024,1024]{1,0:T(8,128)(2,1)S(1)} %copy-done, bf16[8,16,1024]{2,1,0:T(8,128)(2,1)S(1)} %get-tuple-element.81.slots_ref.refs_2_, ...), custom_call_target="tpu_custom_call" | custom-call | tf_op jit(solution)/shard_map/pallas_call | solution.py:46
  60.4 1.0 %shard_map.179 = (f32[64,1024]{1,0:T(8,128)}, f32[64,100]{1,0:T(8,128)}, f32[1]{0:T(128)}, f32[8,128]{1,0:T(8,128)S(1)}) custom-call(f32[8,128]{1,0:T(8,128)S(1)} %get-tuple-element.90.refs_0_, f32[256,1152]{1,0:T(8,128)S(1)} %get-tuple-element.82.held_ref.refs_1_, bf16[256,1152]{1,0:T(8,128)(2,1)S(1)} %collective-permute-done.5.refs_0_.other_ref.refs_2_, ...), custom_call_target="tpu_custom_call" | custom-call | tf_op jit(solution)/shard_map/pallas_call | solution.py:46
  61.5 2.7 %collective-permute-done.20.arrived_ref = bf16[64,1024]{1,0:T(8,128)(2,1)S(1)} collective-permute-done((bf16[64,1024]{1,0:T(8,128)(2,1)S(1)}, bf16[64,1024]{1,0:T(8,128)(2,1)S(1)}, u32[]{:S(2)}, u32[]{:S(2)}) %collective-permute-start.20) | collective-permute-done | bytes 131104 | tf_op jit(solution)/shard_map/ppermute | solution.py:63
  64.2 0.7 %shard_map.183 = f32[64,1024]{1,0:T(8,128)} custom-call(f32[64,1024]{1,0:T(8,128)S(1)} %shard_map.181.partial_ref, bf16[64,1024]{1,0:T(8,128)(2,1)S(1)} %collective-permute-done.20.arrived_ref), custom_call_target="tpu_custom_call" | custom-call | flops 8000000000 | tf_op jit(solution)/shard_map/pallas_call | solution.py:46
  (36 shorter events, 2.7 us)
Async XLA Ops:
  1.8 6.5 %collective-permute-start = (bf16[4,16,1024]{2,1,0:T(8,128)(2,1)S(1)}, bf16[4,16,1024]{2,1,0:T(8,128)(2,1)S(1)}, u32[]{:S(2)}, u32[]{:S(2)}) collective-permute-start(bf16[4,16,1024]{2,1,0:T(8,128)(2,1)S(1)} %get-tuple-element.61), channel_id=1, source_target_pairs={{0,2},{2,0},{4,6},{6,4},{8,10},{10,8},{12,14},{14,12},{1,3},{3,1},... | collective-permute-start | bytes 393224 | tf_op jit(solution)/shard_map/ppermute | solution.py:63
  8.3 6.6 %collective-permute-start.1 = (bf16[32,1024]{1,0:T(8,128)(2,1)S(1)}, bf16[32,1024]{1,0:T(8,128)(2,1)S(1)}, u32[]{:S(2)}, u32[]{:S(2)}) collective-permute-start(bf16[32,1024]{1,0:T(8,128)(2,1)S(1)} %get-tuple-element.62), channel_id=1, source_target_pairs={{0,12},{2,14},{4,8},{6,10},{8,4},{10,6},{12,0},{14,2},{1,13},{3,15... | collective-permute-start | bytes 196616 | tf_op jit(solution)/shard_map/ppermute | solution.py:63
  12.2 5.4 %collective-permute-start.2 = (bf16[32,1024]{1,0:T(8,128)(2,1)S(1)}, bf16[32,1024]{1,0:T(8,128)(2,1)S(1)}, u32[]{:S(2)}, u32[]{:S(2)}) collective-permute-start(bf16[32,1024]{1,0:T(8,128)(2,1)S(1)} %get-tuple-element.63), channel_id=1, source_target_pairs={{0,8},{2,10},{4,12},{6,14},{8,0},{10,2},{12,4},{14,6},{1,9},{3,11}... | collective-permute-start | bytes 196616 | tf_op jit(solution)/shard_map/ppermute | solution.py:63
  12.2 5.4 %collective-permute-start.3 = (bf16[32,1024]{1,0:T(8,128)(2,1)S(1)}, bf16[32,1024]{1,0:T(8,128)(2,1)S(1)}, u32[]{:S(2)}, u32[]{:S(2)}) collective-permute-start(bf16[32,1024]{1,0:T(8,128)(2,1)S(1)} %get-tuple-element.64), channel_id=1, source_target_pairs={{0,4},{2,6},{4,0},{6,2},{8,12},{10,14},{12,8},{14,10},{1,5},{3,7},... | collective-permute-start | bytes 196616 | tf_op jit(solution)/shard_map/ppermute | solution.py:63
  21.0 1.4 %copy-start.1 = (f32[100,256]{1,0:T(8,128)S(1)}, f32[100,256]{1,0:T(8,128)}, u32[]{:S(2)}) copy-start(f32[100,256]{1,0:T(8,128)} %truth_ref.1) | copy-start | bytes 307204
  21.1 1.4 %copy-start.2 = (f32[256]{0:T(256)S(1)}, f32[256]{0:T(256)}, u32[]{:S(2)}) copy-start(f32[256]{0:T(256)} %cell_ref.1) | copy-start | bytes 3076
  21.1 1.4 %collective-permute-start.4 = (bf16[2,100,256]{2,1,0:T(8,128)(2,1)S(1)}, bf16[2,100,256]{2,1,0:T(8,128)(2,1)S(1)}, u32[]{:S(2)}, u32[]{:S(2)}) collective-permute-start(bf16[2,100,256]{2,1,0:T(8,128)(2,1)S(1)} %get-tuple-element.66), channel_id=1, source_target_pairs={{0,1},{1,0},{2,3},{3,2},{4,5},{5,4},{6,7},{7,6},{8,9},{9,8},{10,11... | collective-permute-start | bytes 307208 | tf_op jit(solution)/shard_map/ppermute | solution.py:63
  24.0 2.3 %collective-permute-start.7 = (bf16[256,1152]{1,0:T(8,128)(2,1)S(1)}, bf16[256,1152]{1,0:T(8,128)(2,1)S(1)}, u32[]{:S(2)}, u32[]{:S(2)}) collective-permute-start(bf16[256,1152]{1,0:T(8,128)(2,1)S(1)} %get-tuple-element.78), channel_id=1, source_target_pairs={{0,1},{1,0},{2,3},{3,2},{4,5},{5,4},{6,7},{7,6},{8,9},{9,8},{10,11... | collective-permute-start | bytes 1769480 | tf_op jit(solution)/shard_map/ppermute | solution.py:63
  24.2 5.6 %collective-permute-start.6 = (bf16[2,4,64,128]{3,2,1,0:T(8,128)(2,1)S(1)}, bf16[2,4,64,128]{3,2,1,0:T(8,128)(2,1)S(1)}, u32[]{:S(2)}, u32[]{:S(2)}) collective-permute-start(bf16[2,4,64,128]{3,2,1,0:T(8,128)(2,1)S(1)} %get-tuple-element.73), channel_id=1, source_target_pairs={{0,1},{1,0},{2,3},{3,2},{4,5},{5,4},{6,7},{7,6},{8,9},{9,8},{10,11... | collective-permute-start | bytes 393224 | tf_op jit(solution)/shard_map/ppermute | solution.py:63
  24.6 5.2 %collective-permute-start.5 = (bf16[256,1152]{1,0:T(8,128)(2,1)S(1)}, bf16[256,1152]{1,0:T(8,128)(2,1)S(1)}, u32[]{:S(2)}, u32[]{:S(2)}) collective-permute-start(bf16[256,1152]{1,0:T(8,128)(2,1)S(1)} %get-tuple-element.72), channel_id=1, source_target_pairs={{0,1},{1,0},{2,3},{3,2},{4,5},{5,4},{6,7},{7,6},{8,9},{9,8},{10,11... | collective-permute-start | bytes 1769480 | tf_op jit(solution)/shard_map/ppermute | solution.py:63
  26.6 9.5 %collective-permute-start.8 = (bf16[128,1152]{1,0:T(8,128)(2,1)S(1)}, bf16[128,1152]{1,0:T(8,128)(2,1)S(1)}, u32[]{:S(2)}, u32[]{:S(2)}) collective-permute-start(bf16[128,1152]{1,0:T(8,128)(2,1)S(1)} %shard_map.171.refs_0_), channel_id=1, source_target_pairs={{0,2},{2,0},{4,6},{6,4},{8,10},{10,8},{12,14},{14,12},{1,3},{3,1},... | collective-permute-start | bytes 884744 | tf_op jit(solution)/shard_map/ppermute | solution.py:63
  30.3 4.5 %collective-permute-start.9 = (bf16[8,16,1024]{2,1,0:T(8,128)(2,1)S(1)}, bf16[8,16,1024]{2,1,0:T(8,128)(2,1)S(1)}, u32[]{:S(2)}, u32[]{:S(2)}) collective-permute-start(bf16[8,16,1024]{2,1,0:T(8,128)(2,1)S(1)} %get-tuple-element.81.slots_ref.refs_2_), channel_id=1, source_target_pairs={{0,1},{1,0},{2,3},{3,2},{4,5},{5,4},{6,7},{7,6},{8,9},{9,8},{10,11... | collective-permute-start | bytes 786440 | tf_op jit(solution)/shard_map/ppermute | solution.py:63
  30.4 7.5 %collective-permute-start.10 = (bf16[32,1024]{1,0:T(8,128)(2,1)S(1)}, bf16[32,1024]{1,0:T(8,128)(2,1)S(1)}, u32[]{:S(2)}, u32[]{:S(2)}) collective-permute-start(bf16[32,1024]{1,0:T(8,128)(2,1)S(1)} %get-tuple-element.86), channel_id=1, source_target_pairs={{0,12},{2,14},{4,8},{6,10},{8,4},{10,6},{12,0},{14,2},{1,13},{3,15... | collective-permute-start | bytes 196616 | tf_op jit(solution)/shard_map/ppermute | solution.py:63
  32.6 7.0 %collective-permute-start.11 = (bf16[32,1024]{1,0:T(8,128)(2,1)S(1)}, bf16[32,1024]{1,0:T(8,128)(2,1)S(1)}, u32[]{:S(2)}, u32[]{:S(2)}) collective-permute-start(bf16[32,1024]{1,0:T(8,128)(2,1)S(1)} %get-tuple-element.87), channel_id=1, source_target_pairs={{0,8},{2,10},{4,12},{6,14},{8,0},{10,2},{12,4},{14,6},{1,9},{3,11}... | collective-permute-start | bytes 196616 | tf_op jit(solution)/shard_map/ppermute | solution.py:63
  32.6 9.2 %collective-permute-start.12 = (bf16[32,1024]{1,0:T(8,128)(2,1)S(1)}, bf16[32,1024]{1,0:T(8,128)(2,1)S(1)}, u32[]{:S(2)}, u32[]{:S(2)}) collective-permute-start(bf16[32,1024]{1,0:T(8,128)(2,1)S(1)} %get-tuple-element.88), channel_id=1, source_target_pairs={{0,4},{2,6},{4,0},{6,2},{8,12},{10,14},{12,8},{14,10},{1,5},{3,7},... | collective-permute-start | bytes 196616 | tf_op jit(solution)/shard_map/ppermute | solution.py:63
  35.5 9.3 %collective-permute-start.18 = (bf16[128,1024]{1,0:T(8,128)(2,1)S(1)}, bf16[128,1024]{1,0:T(8,128)(2,1)S(1)}, u32[]{:S(2)}, u32[]{:S(2)}) collective-permute-start(bf16[128,1024]{1,0:T(8,128)(2,1)S(1)} %get-tuple-element.96), channel_id=1, source_target_pairs={{0,2},{2,0},{4,6},{6,4},{8,10},{10,8},{12,14},{14,12},{1,3},{3,1},... | collective-permute-start | bytes 786440 | tf_op jit(solution)/shard_map/ppermute | solution.py:63
  36.1 15.1 %collective-permute-start.16 = (bf16[144,1024]{1,0:T(8,128)(2,1)S(1)}, bf16[144,1024]{1,0:T(8,128)(2,1)S(1)}, u32[]{:S(2)}, u32[]{:S(2)}) collective-permute-start(bf16[144,1024]{1,0:T(8,128)(2,1)S(1)} %get-tuple-element.93), channel_id=1, source_target_pairs={{0,2},{2,0},{4,6},{6,4},{8,10},{10,8},{12,14},{14,12},{1,3},{3,1},... | collective-permute-start | bytes 884744 | tf_op jit(solution)/shard_map/ppermute | solution.py:63
  37.9 14.9 %collective-permute-start.15 = (bf16[64,1152]{1,0:T(8,128)(2,1)S(1)}, bf16[64,1152]{1,0:T(8,128)(2,1)S(1)}, u32[]{:S(2)}, u32[]{:S(2)}) collective-permute-start(bf16[64,1152]{1,0:T(8,128)(2,1)S(1)} %get-tuple-element.91), channel_id=1, source_target_pairs={{0,8},{2,10},{4,12},{6,14},{8,0},{10,2},{12,4},{14,6},{1,9},{3,11}... | collective-permute-start | bytes 442376 | tf_op jit(solution)/shard_map/ppermute | solution.py:63
  39.5 20.9 %collective-permute-start.14 = (bf16[64,1152]{1,0:T(8,128)(2,1)S(1)}, bf16[64,1152]{1,0:T(8,128)(2,1)S(1)}, u32[]{:S(2)}, u32[]{:S(2)}) collective-permute-start(bf16[64,1152]{1,0:T(8,128)(2,1)S(1)} %get-tuple-element.83.refs_0_), channel_id=1, source_target_pairs={{0,12},{2,14},{4,8},{6,10},{8,4},{10,6},{12,0},{14,2},{1,13},{3,15... | collective-permute-start | bytes 442376 | tf_op jit(solution)/shard_map/ppermute | solution.py:63
  41.8 17.0 %collective-permute-start.13 = (bf16[208,1024]{1,0:T(8,128)(2,1)S(1)}, bf16[208,1024]{1,0:T(8,128)(2,1)S(1)}, u32[]{:S(2)}, u32[]{:S(2)}) collective-permute-start(bf16[208,1024]{1,0:T(8,128)(2,1)S(1)} %shard_map.176), channel_id=1, source_target_pairs={{0,2},{2,0},{4,6},{6,4},{8,10},{10,8},{12,14},{14,12},{1,3},{3,1},... | collective-permute-start | bytes 1277960 | tf_op jit(solution)/shard_map/ppermute | solution.py:63
  44.9 16.5 %collective-permute-start.19 = (bf16[64,1024]{1,0:T(8,128)(2,1)S(1)}, bf16[64,1024]{1,0:T(8,128)(2,1)S(1)}, u32[]{:S(2)}, u32[]{:S(2)}) collective-permute-start(bf16[64,1024]{1,0:T(8,128)(2,1)S(1)} %shard_map.180), channel_id=1, source_target_pairs={{0,12},{2,14},{4,8},{6,10},{8,4},{10,6},{12,0},{14,2},{1,13},{3,15... | collective-permute-start | bytes 393224 | tf_op jit(solution)/shard_map/ppermute | solution.py:63
  51.4 7.5 %copy-start = (bf16[1024,1024]{1,0:T(8,128)(2,1)S(1)}, bf16[1024,1024]{1,0:T(8,128)(2,1)}, u32[]{:S(2)}) copy-start(bf16[1024,1024]{1,0:T(8,128)(2,1)} %w_msg_ref.1) | copy-start | bytes 6291460
  51.4 9.0 %collective-permute-start.17 = (bf16[144,1024]{1,0:T(8,128)(2,1)S(1)}, bf16[144,1024]{1,0:T(8,128)(2,1)S(1)}, u32[]{:S(2)}, u32[]{:S(2)}) collective-permute-start(bf16[144,1024]{1,0:T(8,128)(2,1)S(1)} %shard_map.178), channel_id=1, source_target_pairs={{0,4},{2,6},{4,0},{6,2},{8,12},{10,14},{12,8},{14,10},{1,5},{3,7},... | collective-permute-start | bytes 884744 | tf_op jit(solution)/shard_map/ppermute | solution.py:63
  52.8 11.4 %collective-permute-start.20 = (bf16[64,1024]{1,0:T(8,128)(2,1)S(1)}, bf16[64,1024]{1,0:T(8,128)(2,1)S(1)}, u32[]{:S(2)}, u32[]{:S(2)}) collective-permute-start(bf16[64,1024]{1,0:T(8,128)(2,1)S(1)} %shard_map.182), channel_id=1, source_target_pairs={{0,8},{2,10},{4,12},{6,14},{8,0},{10,2},{12,4},{14,6},{1,9},{3,11}... | collective-permute-start | bytes 393224 | tf_op jit(solution)/shard_map/ppermute | solution.py:63

commit v13 on v12

--- a/solution.py
+++ b/solution.py
@@ -291,11 +291,10 @@
     return jnp.concatenate(parts, axis=0).astype(f32)
 
 
-def local_kernel(variables, loss_ref, normed_t_ref, active_t_ref, inner_ref, pred_ref, far_ref, near_ref):
-    for half, out_ref in ((0, far_ref), (1, near_ref)):
-        weight_parts(
-            normed_t_ref, active_t_ref, inner_ref, pred_ref[...], loss_ref[0], variables, 0, half, out_ref
-        )
+def local_kernel(variables, half, loss_ref, normed_t_ref, active_t_ref, inner_ref, pred_ref, out_ref):
+    weight_parts(
+        normed_t_ref, active_t_ref, inner_ref, pred_ref[...], loss_ref[0], variables, 0, half, out_ref
+    )
 
 
 def pair_sum(variables, width, held_ref, other_ref, begin, count):
@@ -564,13 +563,18 @@
     )
     far_other = swap(far, "member", cores, 1)
     near_other = swap(near, "member", cores, 1)
-    held_far, held_near = call(
-        functools.partial(local_kernel, variables),
-        [((half, wide), f32)] * 2,
-        [loss_part, normed_t, active_t, grad_inner, pred],
-        limit=12,
-        scalars=(0,),
-    )
+    def local(half, after):
+        (held,) = call(
+            functools.partial(local_kernel, variables, half),
+            [((levels * block, wide), f32)],
+            [loss_part, normed_t, active_t, grad_inner, pred],
+            limit=12,
+            scalars=(0,),
+            after=after,
+        )
+        return held
+
+    held_far = local(0, [])
     (first,) = call(
         functools.partial(first_kernel, variables, width),
         [((count, wide), bf16)],
@@ -578,6 +582,7 @@
         limit=6,
     )
     first_other = swap(first, "space", peers, 1)
+    held_near = local(1, [first])
     (grad_hidden,) = call(
         back_kernel,
         [((rows_all, width), bf16)],

time: 65.2 us -> 66.1 us (1.014)
  Pallas kernels: 18.1 us -> 19 us
    pallas_call x20 -> x21, Pallas kernels: 18.1 us -> 19 us  [call(): pl.pallas_call(inner if count else body, out_shape=[jax.ShapeDtypeStruct(...]
  transfers between devices with their start and end apart: 21 -> 21, of which waited for: 9 -> 11; matrix products, arithmetic and copies ran while one was open for 0% -> 0% of each run, Pallas kernels for 17% -> 18%
where the time goes in v13:
time: 66.1 us; the launch traced here: 65.9 us
  starting transfers between devices  24.8 us (38%)
  waiting for transfers between devices  21.2 us (32%)
  Pallas kernels  19 us (29%)
  between operations  0.84 us (1%)
    ppermute x21, starting transfers between devices, swap(): return lax.ppermute(value, axis, [(i, i ^ step) for i in range(size)])  24.8 us
    ppermute x21, waiting for transfers between devices, swap(): return lax.ppermute(value, axis, [(i, i ^ step) for i in range(size)])  21.2 us
    pallas_call x21, Pallas kernels, call(): pl.pallas_call(inner if count else body, out_shape=[jax.ShapeDtypeStruct(...  19 us
  transfers between devices with their start and end apart: 21, of which 11 were waited for; matrix products, arithmetic and copies ran while one was open for 0% of the time, Pallas kernels for 18%

profile of v13, /device:TPU:0, one launch (start us, length us, event | category | flops | bytes accessed | tf_op | source)
XLA Modules:
  0.0 65.9 jit_solution(11064659917807697649)
XLA Ops:
  0.6 1.1 %shard_map.164 = (bf16[128,64]{1,0:T(8,128)(2,1)S(1)}, bf16[4,16,1024]{2,1,0:T(8,128)(2,1)S(1)}, bf16[4,16,1024]{2,1,0:T(8,128)(2,1)S(1)}) custom-call(s32[1,8,8]{2,1,0:T(8,128)} %lists_ref.1, bf16[2,32,1024]{2,1,0:T(8,128)(2,1)} %latents_ref.1), custom_call_target="tpu_custom_call" | custom-call | tf_op jit(solution)/shard_map/pallas_call | solution.py:46
  1.8 3.0 %collective-permute-start = (bf16[4,16,1024]{2,1,0:T(8,128)(2,1)S(1)}, bf16[4,16,1024]{2,1,0:T(8,128)(2,1)S(1)}, u32[]{:S(2)}, u32[]{:S(2)}) collective-permute-start(bf16[4,16,1024]{2,1,0:T(8,128)(2,1)S(1)} %get-tuple-element.59), channel_id=1, source_target_pairs={{0,2},{2,0},{4,6},{6,4},{8,10},{10,8},{12,14},{14,12},{1,3},{3,1},... | collective-permute-start | bytes 393224 | tf_op jit(solution)/shard_map/ppermute | solution.py:63
  4.8 2.6 %shard_map.165 = (bf16[256,512]{1,0:T(8,128)(2,1)S(1)}, bf16[1024,1024]{1,0:T(8,128)(2,1)S(1)}, f32[1024]{0:T(1024)S(1)}, bf16[256,1024]{1,0:T(8,128)(2,1)S(1)},...) custom-call(bf16[128,64]{1,0:T(8,128)(2,1)S(1)} %get-tuple-element.50.refs_0_.pick_ref, ...), custom_call_target="tpu_custom_call" | custom-call | tf_op jit(solution)/shard_map/pallas_call | solution.py:46
  7.4 0.9 %collective-permute-done.refs_2_.near_ref = bf16[4,16,1024]{2,1,0:T(8,128)(2,1)S(1)} collective-permute-done((bf16[4,16,1024]{2,1,0:T(8,128)(2,1)S(1)}, bf16[4,16,1024]{2,1,0:T(8,128)(2,1)S(1)}, u32[]{:S(2)}, u32[]{:S(2)}) %collective-permute-start) | collective-permute-done | bytes 131104 | tf_op jit(solution)/shard_map/ppermute | solution.py:63
  8.3 3.9 %collective-permute-start.1 = (bf16[32,1024]{1,0:T(8,128)(2,1)S(1)}, bf16[32,1024]{1,0:T(8,128)(2,1)S(1)}, u32[]{:S(2)}, u32[]{:S(2)}) collective-permute-start(bf16[32,1024]{1,0:T(8,128)(2,1)S(1)} %get-tuple-element.60), channel_id=1, source_target_pairs={{0,12},{2,14},{4,8},{6,10},{8,4},{10,6},{12,0},{14,2},{1,13},{3,15... | collective-permute-start | bytes 196616 | tf_op jit(solution)/shard_map/ppermute | solution.py:63
  12.2 0.6 collective-permute-start.3
  12.8 2.0 %collective-permute-done.1.rest_0_ = bf16[32,1024]{1,0:T(8,128)(2,1)S(1)} collective-permute-done((bf16[32,1024]{1,0:T(8,128)(2,1)S(1)}, bf16[32,1024]{1,0:T(8,128)(2,1)S(1)}, u32[]{:S(2)}, u32[]{:S(2)}) %collective-permute-start.1) | collective-permute-done | bytes 65568 | tf_op jit(solution)/shard_map/ppermute | solution.py:63
  14.9 2.7 %collective-permute-done.2.rest_1_ = bf16[32,1024]{1,0:T(8,128)(2,1)S(1)} collective-permute-done((bf16[32,1024]{1,0:T(8,128)(2,1)S(1)}, bf16[32,1024]{1,0:T(8,128)(2,1)S(1)}, u32[]{:S(2)}, u32[]{:S(2)}) %collective-permute-start.2) | collective-permute-done | bytes 65568 | tf_op jit(solution)/shard_map/ppermute | solution.py:63
  17.6 3.5 %shard_map.167 = (f32[2,100,256]{2,1,0:T(8,128)S(1)}, bf16[2,100,256]{2,1,0:T(8,128)(2,1)S(1)}, bf16[512,1024]{1,0:T(8,128)(2,1)S(1)}, bf16[512,1024]{1,0:T(8,12...) custom-call(bf16[1024,1024]{1,0:T(8,128)(2,1)S(1)} %get-tuple-element.51.w_msg_ref, ...), custom_call_target="tpu_custom_call" | custom-call | tf_op jit(solution)/shard_map/pallas_call | solution.py:46
  21.2 0.9 %shard_map.168 = (bf16[2,2,4,64,512]{4,3,2,1,0:T(8,128)(2,1)S(1)}, bf16[2,2,4,64,512]{4,3,2,1,0:T(8,128)(2,1)S(1)}, bf16[2,4,64,128]{3,2,1,0:T(8,128)(2,1)S(1)}, bf16[2,4,64,128]{3,2,1,0:T(8,128)(2,1)S(1)}) custom-call(bf16[512,1024]{1,0:T(8,128)(2,1)S(1)} %get-tuple-element.66.normed_ref, bf16[512,1024]{1,0:T(8,128)(2,1)S(1)} %get-tuple-element.67.active_ref, ...), custom_call_target="tpu_custom_call" | custom-call | tf_op jit(solution)/shard_map/pallas_call | solution.py:46
  22.5 1.5 %shard_map.169 = (bf16[512,1024]{1,0:T(8,128)(2,1)S(1)}, bf16[128,512]{1,0:T(8,128)(2,1)S(1)}, f32[1]{0:T(128)}, bf16[256,1152]{1,0:T(8,128)(2,1)S(1)}, bf16[256,1152]{1,0:T(8,128)(2,1)S(1)}) custom-call(f32[2,100,256]{2,1,0:T(8,128)S(1)} %get-tuple-element.63.own_ref, bf16[2,100,256]{2,1,0:T(8,128)(2,1)S(1)} %collective-permute-done.4.other_ref, ...), custom_call_target="tpu_custom_call" | custom-call | tf_op jit(solution)/shard_map/pallas_call | solution.py:46
  24.7 1.2 %shard_map.170.held_ref = f32[256,1152]{1,0:T(8,128)S(1)} custom-call(f32[1]{0:T(128)} %get-tuple-element.72.loss_ref.refs_1_, bf16[2,2,4,64,512]{4,3,2,1,0:T(8,128)(2,1)S(1)} %get-tuple-element.68.normed_t_ref.refs_2_, bf16[2,2,4,64,512]{4,3,2,1,0:T(8,128)(2,1)S(1)} %get-tuple-element.69.active_t_ref.refs_3_, ...), custom_call_target="tpu_custom_call" | custom-call | tf_op jit(solution)/shard_map/pallas_call | solution.py:46
  26.3 1.6 %collective-permute-start.8 = (bf16[128,1152]{1,0:T(8,128)(2,1)S(1)}, bf16[128,1152]{1,0:T(8,128)(2,1)S(1)}, u32[]{:S(2)}, u32[]{:S(2)}) collective-permute-start(bf16[128,1152]{1,0:T(8,128)(2,1)S(1)} %shard_map.171.refs_0_), channel_id=1, source_target_pairs={{0,2},{2,0},{4,6},{6,4},{8,10},{10,8},{12,14},{14,12},{1,3},{3,1},... | collective-permute-start | bytes 884744 | tf_op jit(solution)/shard_map/ppermute | solution.py:63
  27.9 1.7 %shard_map.172.refs_3_ = bf16[512,1024]{1,0:T(8,128)(2,1)S(1)} custom-call(bf16[128,1152]{1,0:T(8,128)(2,1)S(1)} %shard_map.171.refs_0_, bf16[512,1024]{1,0:T(8,128)(2,1)S(1)} %get-tuple-element.73.inner_ref.refs_1_.refs_4_, bf16[1024,1024]{1,0:T(8,128)(2,1)S(1)} %get-tuple-element.55.weights_ref.refs_2_, f32[1024]{0:T(1024)S(1)} %get-tuple-element.53.gain_ref.refs_3_, ...), custom_call_target="tpu_custom_call" | custom-call | flops 8000000000 | tf_op jit(solution)/shard_map/pallas_call | solution.py:46
  30.1 1.2 %shard_map.174.held_ref.refs_1_ = f32[256,1152]{1,0:T(8,128)S(1)} custom-call(bf16[128,1152]{1,0:T(8,128)(2,1)S(1)} %shard_map.171.refs_0_, f32[1]{0:T(128)} %get-tuple-element.72.loss_ref.refs_1_, bf16[2,2,4,64,512]{4,3,2,1,0:T(8,128)(2,1)S(1)} %get-tuple-element.68.normed_t_ref.refs_2_, ...), custom_call_target="tpu_custom_call" | custom-call | tf_op jit(solution)/shard_map/pallas_call | solution.py:46
  31.4 2.2 %collective-permute-start.10 = (bf16[32,1024]{1,0:T(8,128)(2,1)S(1)}, bf16[32,1024]{1,0:T(8,128)(2,1)S(1)}, u32[]{:S(2)}, u32[]{:S(2)}) collective-permute-start(bf16[32,1024]{1,0:T(8,128)(2,1)S(1)} %get-tuple-element.82), channel_id=1, source_target_pairs={{0,12},{2,14},{4,8},{6,10},{8,4},{10,6},{12,0},{14,2},{1,13},{3,15... | collective-permute-start | bytes 196616 | tf_op jit(solution)/shard_map/ppermute | solution.py:63
  33.6 2.2 %collective-permute-start.12 = (bf16[32,1024]{1,0:T(8,128)(2,1)S(1)}, bf16[32,1024]{1,0:T(8,128)(2,1)S(1)}, u32[]{:S(2)}, u32[]{:S(2)}) collective-permute-start(bf16[32,1024]{1,0:T(8,128)(2,1)S(1)} %get-tuple-element.84), channel_id=1, source_target_pairs={{0,4},{2,6},{4,0},{6,2},{8,12},{10,14},{12,8},{14,10},{1,5},{3,7},... | collective-permute-start | bytes 196616 | tf_op jit(solution)/shard_map/ppermute | solution.py:63
  35.8 0.7 %shard_map.176 = (bf16[128,1024]{1,0:T(8,128)(2,1)S(1)}, bf16[144,1024]{1,0:T(8,128)(2,1)S(1)}, bf16[144,1024]{1,0:T(8,128)(2,1)S(1)}, f32[256,1024]{1,0:T(8,128)S(1)}) custom-call(bf16[2,4,64,128]{3,2,1,0:T(8,128)(2,1)S(1)} %get-tuple-element.80.keep_ref, bf16[2,4,64,128]{3,2,1,0:T(8,128)(2,1)S(1)} %collective-permute-done.6.refs_1_.give_ref, ...), custom_call_target="tpu_custom_call" | custom-call | tf_op jit(solution)/shard_map/pallas_call | solution.py:46
  37.1 1.5 %collective-permute-start.16 = (bf16[144,1024]{1,0:T(8,128)(2,1)S(1)}, bf16[144,1024]{1,0:T(8,128)(2,1)S(1)}, u32[]{:S(2)}, u32[]{:S(2)}) collective-permute-start(bf16[144,1024]{1,0:T(8,128)(2,1)S(1)} %get-tuple-element.89), channel_id=1, source_target_pairs={{0,2},{2,0},{4,6},{6,4},{8,10},{10,8},{12,14},{14,12},{1,3},{3,1},... | collective-permute-start | bytes 884744 | tf_op jit(solution)/shard_map/ppermute | solution.py:63
  38.9 1.4 %collective-permute-start.15 = (bf16[64,1152]{1,0:T(8,128)(2,1)S(1)}, bf16[64,1152]{1,0:T(8,128)(2,1)S(1)}, u32[]{:S(2)}, u32[]{:S(2)}) collective-permute-start(bf16[64,1152]{1,0:T(8,128)(2,1)S(1)} %get-tuple-element.87), channel_id=1, source_target_pairs={{0,8},{2,10},{4,12},{6,14},{8,0},{10,2},{12,4},{14,6},{1,9},{3,11}... | collective-permute-start | bytes 442376 | tf_op jit(solution)/shard_map/ppermute | solution.py:63
  40.5 2.3 %collective-permute-start.14 = (bf16[64,1152]{1,0:T(8,128)(2,1)S(1)}, bf16[64,1152]{1,0:T(8,128)(2,1)S(1)}, u32[]{:S(2)}, u32[]{:S(2)}) collective-permute-start(bf16[64,1152]{1,0:T(8,128)(2,1)S(1)} %get-tuple-element.79.refs_0_), channel_id=1, source_target_pairs={{0,12},{2,14},{4,8},{6,10},{8,4},{10,6},{12,0},{14,2},{1,13},{3,15... | collective-permute-start | bytes 442376 | tf_op jit(solution)/shard_map/ppermute | solution.py:63
  42.9 0.6 collective-permute-start.13
  43.5 2.4 %collective-permute-done.18.arrived_ref.refs_2_ = bf16[128,1024]{1,0:T(8,128)(2,1)S(1)} collective-permute-done((bf16[128,1024]{1,0:T(8,128)(2,1)S(1)}, bf16[128,1024]{1,0:T(8,128)(2,1)S(1)}, u32[]{:S(2)}, u32[]{:S(2)}) %collective-permute-start.18) | collective-permute-done | bytes 262176 | tf_op jit(solution)/shard_map/ppermute | solution.py:63
  45.9 2.2 %collective-permute-start.19 = (bf16[64,1024]{1,0:T(8,128)(2,1)S(1)}, bf16[64,1024]{1,0:T(8,128)(2,1)S(1)}, u32[]{:S(2)}, u32[]{:S(2)}) collective-permute-start(bf16[64,1024]{1,0:T(8,128)(2,1)S(1)} %shard_map.181), channel_id=1, source_target_pairs={{0,12},{2,14},{4,8},{6,10},{8,4},{10,6},{12,0},{14,2},{1,13},{3,15... | collective-permute-start | bytes 393224 | tf_op jit(solution)/shard_map/ppermute | solution.py:63
  48.1 4.1 %collective-permute-done.16.arrived_ref = bf16[144,1024]{1,0:T(8,128)(2,1)S(1)} collective-permute-done((bf16[144,1024]{1,0:T(8,128)(2,1)S(1)}, bf16[144,1024]{1,0:T(8,128)(2,1)S(1)}, u32[]{:S(2)}, u32[]{:S(2)}) %collective-permute-start.16) | collective-permute-done | bytes 294944 | tf_op jit(solution)/shard_map/ppermute | solution.py:63
  52.5 1.2 %collective-permute-done.15.refs_5_.refs_0_ = bf16[64,1152]{1,0:T(8,128)(2,1)S(1)} collective-permute-done((bf16[64,1152]{1,0:T(8,128)(2,1)S(1)}, bf16[64,1152]{1,0:T(8,128)(2,1)S(1)}, u32[]{:S(2)}, u32[]{:S(2)}) %collective-permute-start.15) | collective-permute-done | bytes 147488 | tf_op jit(solution)/shard_map/ppermute | solution.py:63
  53.7 1.6 %collective-permute-start.20 = (bf16[64,1024]{1,0:T(8,128)(2,1)S(1)}, bf16[64,1024]{1,0:T(8,128)(2,1)S(1)}, u32[]{:S(2)}, u32[]{:S(2)}) collective-permute-start(bf16[64,1024]{1,0:T(8,128)(2,1)S(1)} %shard_map.183), channel_id=1, source_target_pairs={{0,8},{2,10},{4,12},{6,14},{8,0},{10,2},{12,4},{14,6},{1,9},{3,11}... | collective-permute-start | bytes 393224 | tf_op jit(solution)/shard_map/ppermute | solution.py:63
  55.3 4.6 %collective-permute-done.13.last_ref.refs_3_.refs_2_ = bf16[208,1024]{1,0:T(8,128)(2,1)S(1)} collective-permute-done((bf16[208,1024]{1,0:T(8,128)(2,1)S(1)}, bf16[208,1024]{1,0:T(8,128)(2,1)S(1)}, u32[]{:S(2)}, u32[]{:S(2)}) %collective-permute-start.13) | collective-permute-done | bytes 426016 | tf_op jit(solution)/shard_map/ppermute | solution.py:63
  59.9 1.5 %shard_map.178 = (bf16[2,32,1024]{2,1,0:T(8,128)(2,1)}, f32[8,128]{1,0:T(8,128)S(1)}) custom-call(bf16[128,64]{1,0:T(8,128)(2,1)S(1)} %get-tuple-element.50.refs_0_.pick_ref, bf16[1024,1024]{1,0:T(8,128)(2,1)S(1)} %copy-done, bf16[8,16,1024]{2,1,0:T(8,128)(2,1)S(1)} %get-tuple-element.78.slots_ref.refs_2_, ...), custom_call_target="tpu_custom_call" | custom-call | tf_op jit(solution)/shard_map/pallas_call | solution.py:46
  61.5 1.0 %shard_map.180 = (f32[64,1024]{1,0:T(8,128)}, f32[64,100]{1,0:T(8,128)}, f32[1]{0:T(128)}, f32[8,128]{1,0:T(8,128)S(1)}) custom-call(f32[8,128]{1,0:T(8,128)S(1)} %get-tuple-element.86.refs_0_, f32[256,1152]{1,0:T(8,128)S(1)} %shard_map.174.held_ref.refs_1_, bf16[256,1152]{1,0:T(8,128)(2,1)S(1)} %collective-permute-done.5.refs_0_.other_ref.refs_2_, ...), custom_call_target="tpu_custom_call" | custom-call | tf_op jit(solution)/shard_map/pallas_call | solution.py:46
  62.5 2.6 %collective-permute-done.20.arrived_ref = bf16[64,1024]{1,0:T(8,128)(2,1)S(1)} collective-permute-done((bf16[64,1024]{1,0:T(8,128)(2,1)S(1)}, bf16[64,1024]{1,0:T(8,128)(2,1)S(1)}, u32[]{:S(2)}, u32[]{:S(2)}) %collective-permute-start.20) | collective-permute-done | bytes 131104 | tf_op jit(solution)/shard_map/ppermute | solution.py:63
  65.1 0.7 %shard_map.184 = f32[64,1024]{1,0:T(8,128)} custom-call(f32[64,1024]{1,0:T(8,128)S(1)} %shard_map.182.partial_ref, bf16[64,1024]{1,0:T(8,128)(2,1)S(1)} %collective-permute-done.20.arrived_ref), custom_call_target="tpu_custom_call" | custom-call | flops 8000000000 | tf_op jit(solution)/shard_map/pallas_call | solution.py:46
  (37 shorter events, 3.5 us)
Async XLA Ops:
  1.8 6.5 %collective-permute-start = (bf16[4,16,1024]{2,1,0:T(8,128)(2,1)S(1)}, bf16[4,16,1024]{2,1,0:T(8,128)(2,1)S(1)}, u32[]{:S(2)}, u32[]{:S(2)}) collective-permute-start(bf16[4,16,1024]{2,1,0:T(8,128)(2,1)S(1)} %get-tuple-element.59), channel_id=1, source_target_pairs={{0,2},{2,0},{4,6},{6,4},{8,10},{10,8},{12,14},{14,12},{1,3},{3,1},... | collective-permute-start | bytes 393224 | tf_op jit(solution)/shard_map/ppermute | solution.py:63
  8.3 6.6 %collective-permute-start.1 = (bf16[32,1024]{1,0:T(8,128)(2,1)S(1)}, bf16[32,1024]{1,0:T(8,128)(2,1)S(1)}, u32[]{:S(2)}, u32[]{:S(2)}) collective-permute-start(bf16[32,1024]{1,0:T(8,128)(2,1)S(1)} %get-tuple-element.60), channel_id=1, source_target_pairs={{0,12},{2,14},{4,8},{6,10},{8,4},{10,6},{12,0},{14,2},{1,13},{3,15... | collective-permute-start | bytes 196616 | tf_op jit(solution)/shard_map/ppermute | solution.py:63
  12.2 5.4 %collective-permute-start.2 = (bf16[32,1024]{1,0:T(8,128)(2,1)S(1)}, bf16[32,1024]{1,0:T(8,128)(2,1)S(1)}, u32[]{:S(2)}, u32[]{:S(2)}) collective-permute-start(bf16[32,1024]{1,0:T(8,128)(2,1)S(1)} %get-tuple-element.61), channel_id=1, source_target_pairs={{0,8},{2,10},{4,12},{6,14},{8,0},{10,2},{12,4},{14,6},{1,9},{3,11}... | collective-permute-start | bytes 196616 | tf_op jit(solution)/shard_map/ppermute | solution.py:63
  12.2 5.4 %collective-permute-start.3 = (bf16[32,1024]{1,0:T(8,128)(2,1)S(1)}, bf16[32,1024]{1,0:T(8,128)(2,1)S(1)}, u32[]{:S(2)}, u32[]{:S(2)}) collective-permute-start(bf16[32,1024]{1,0:T(8,128)(2,1)S(1)} %get-tuple-element.62), channel_id=1, source_target_pairs={{0,4},{2,6},{4,0},{6,2},{8,12},{10,14},{12,8},{14,10},{1,5},{3,7},... | collective-permute-start | bytes 196616 | tf_op jit(solution)/shard_map/ppermute | solution.py:63
  21.1 1.4 %copy-start.1 = (f32[100,256]{1,0:T(8,128)S(1)}, f32[100,256]{1,0:T(8,128)}, u32[]{:S(2)}) copy-start(f32[100,256]{1,0:T(8,128)} %truth_ref.1) | copy-start | bytes 307204
  21.1 1.4 %copy-start.2 = (f32[256]{0:T(256)S(1)}, f32[256]{0:T(256)}, u32[]{:S(2)}) copy-start(f32[256]{0:T(256)} %cell_ref.1) | copy-start | bytes 3076
  21.1 1.4 %collective-permute-start.4 = (bf16[2,100,256]{2,1,0:T(8,128)(2,1)S(1)}, bf16[2,100,256]{2,1,0:T(8,128)(2,1)S(1)}, u32[]{:S(2)}, u32[]{:S(2)}) collective-permute-start(bf16[2,100,256]{2,1,0:T(8,128)(2,1)S(1)} %get-tuple-element.64), channel_id=1, source_target_pairs={{0,1},{1,0},{2,3},{3,2},{4,5},{5,4},{6,7},{7,6},{8,9},{9,8},{10,11... | collective-permute-start | bytes 307208 | tf_op jit(solution)/shard_map/ppermute | solution.py:63
  24.0 2.1 %collective-permute-start.7 = (bf16[256,1152]{1,0:T(8,128)(2,1)S(1)}, bf16[256,1152]{1,0:T(8,128)(2,1)S(1)}, u32[]{:S(2)}, u32[]{:S(2)}) collective-permute-start(bf16[256,1152]{1,0:T(8,128)(2,1)S(1)} %get-tuple-element.75), channel_id=1, source_target_pairs={{0,1},{1,0},{2,3},{3,2},{4,5},{5,4},{6,7},{7,6},{8,9},{9,8},{10,11... | collective-permute-start | bytes 1769480 | tf_op jit(solution)/shard_map/ppermute | solution.py:63
  24.2 5.4 %collective-permute-start.6 = (bf16[2,4,64,128]{3,2,1,0:T(8,128)(2,1)S(1)}, bf16[2,4,64,128]{3,2,1,0:T(8,128)(2,1)S(1)}, u32[]{:S(2)}, u32[]{:S(2)}) collective-permute-start(bf16[2,4,64,128]{3,2,1,0:T(8,128)(2,1)S(1)} %get-tuple-element.71), channel_id=1, source_target_pairs={{0,1},{1,0},{2,3},{3,2},{4,5},{5,4},{6,7},{7,6},{8,9},{9,8},{10,11... | collective-permute-start | bytes 393224 | tf_op jit(solution)/shard_map/ppermute | solution.py:63
  24.6 5.0 %collective-permute-start.5 = (bf16[256,1152]{1,0:T(8,128)(2,1)S(1)}, bf16[256,1152]{1,0:T(8,128)(2,1)S(1)}, u32[]{:S(2)}, u32[]{:S(2)}) collective-permute-start(bf16[256,1152]{1,0:T(8,128)(2,1)S(1)} %get-tuple-element.70), channel_id=1, source_target_pairs={{0,1},{1,0},{2,3},{3,2},{4,5},{5,4},{6,7},{7,6},{8,9},{9,8},{10,11... | collective-permute-start | bytes 1769480 | tf_op jit(solution)/shard_map/ppermute | solution.py:63
  26.3 10.9 %collective-permute-start.8 = (bf16[128,1152]{1,0:T(8,128)(2,1)S(1)}, bf16[128,1152]{1,0:T(8,128)(2,1)S(1)}, u32[]{:S(2)}, u32[]{:S(2)}) collective-permute-start(bf16[128,1152]{1,0:T(8,128)(2,1)S(1)} %shard_map.171.refs_0_), channel_id=1, source_target_pairs={{0,2},{2,0},{4,6},{6,4},{8,10},{10,8},{12,14},{14,12},{1,3},{3,1},... | collective-permute-start | bytes 884744 | tf_op jit(solution)/shard_map/ppermute | solution.py:63
  30.1 5.8 %collective-permute-start.9 = (bf16[8,16,1024]{2,1,0:T(8,128)(2,1)S(1)}, bf16[8,16,1024]{2,1,0:T(8,128)(2,1)S(1)}, u32[]{:S(2)}, u32[]{:S(2)}) collective-permute-start(bf16[8,16,1024]{2,1,0:T(8,128)(2,1)S(1)} %get-tuple-element.78.slots_ref.refs_2_), channel_id=1, source_target_pairs={{0,1},{1,0},{2,3},{3,2},{4,5},{5,4},{6,7},{7,6},{8,9},{9,8},{10,11... | collective-permute-start | bytes 786440 | tf_op jit(solution)/shard_map/ppermute | solution.py:63
  31.4 7.5 %collective-permute-start.10 = (bf16[32,1024]{1,0:T(8,128)(2,1)S(1)}, bf16[32,1024]{1,0:T(8,128)(2,1)S(1)}, u32[]{:S(2)}, u32[]{:S(2)}) collective-permute-start(bf16[32,1024]{1,0:T(8,128)(2,1)S(1)} %get-tuple-element.82), channel_id=1, source_target_pairs={{0,12},{2,14},{4,8},{6,10},{8,4},{10,6},{12,0},{14,2},{1,13},{3,15... | collective-permute-start | bytes 196616 | tf_op jit(solution)/shard_map/ppermute | solution.py:63
  33.6 6.9 %collective-permute-start.11 = (bf16[32,1024]{1,0:T(8,128)(2,1)S(1)}, bf16[32,1024]{1,0:T(8,128)(2,1)S(1)}, u32[]{:S(2)}, u32[]{:S(2)}) collective-permute-start(bf16[32,1024]{1,0:T(8,128)(2,1)S(1)} %get-tuple-element.83), channel_id=1, source_target_pairs={{0,8},{2,10},{4,12},{6,14},{8,0},{10,2},{12,4},{14,6},{1,9},{3,11}... | collective-permute-start | bytes 196616 | tf_op jit(solution)/shard_map/ppermute | solution.py:63
  33.6 9.2 %collective-permute-start.12 = (bf16[32,1024]{1,0:T(8,128)(2,1)S(1)}, bf16[32,1024]{1,0:T(8,128)(2,1)S(1)}, u32[]{:S(2)}, u32[]{:S(2)}) collective-permute-start(bf16[32,1024]{1,0:T(8,128)(2,1)S(1)} %get-tuple-element.84), channel_id=1, source_target_pairs={{0,4},{2,6},{4,0},{6,2},{8,12},{10,14},{12,8},{14,10},{1,5},{3,7},... | collective-permute-start | bytes 196616 | tf_op jit(solution)/shard_map/ppermute | solution.py:63
  36.6 9.3 %collective-permute-start.18 = (bf16[128,1024]{1,0:T(8,128)(2,1)S(1)}, bf16[128,1024]{1,0:T(8,128)(2,1)S(1)}, u32[]{:S(2)}, u32[]{:S(2)}) collective-permute-start(bf16[128,1024]{1,0:T(8,128)(2,1)S(1)} %get-tuple-element.92), channel_id=1, source_target_pairs={{0,2},{2,0},{4,6},{6,4},{8,10},{10,8},{12,14},{14,12},{1,3},{3,1},... | collective-permute-start | bytes 786440 | tf_op jit(solution)/shard_map/ppermute | solution.py:63
  37.1 15.1 %collective-permute-start.16 = (bf16[144,1024]{1,0:T(8,128)(2,1)S(1)}, bf16[144,1024]{1,0:T(8,128)(2,1)S(1)}, u32[]{:S(2)}, u32[]{:S(2)}) collective-permute-start(bf16[144,1024]{1,0:T(8,128)(2,1)S(1)} %get-tuple-element.89), channel_id=1, source_target_pairs={{0,2},{2,0},{4,6},{6,4},{8,10},{10,8},{12,14},{14,12},{1,3},{3,1},... | collective-permute-start | bytes 884744 | tf_op jit(solution)/shard_map/ppermute | solution.py:63
  38.9 14.8 %collective-permute-start.15 = (bf16[64,1152]{1,0:T(8,128)(2,1)S(1)}, bf16[64,1152]{1,0:T(8,128)(2,1)S(1)}, u32[]{:S(2)}, u32[]{:S(2)}) collective-permute-start(bf16[64,1152]{1,0:T(8,128)(2,1)S(1)} %get-tuple-element.87), channel_id=1, source_target_pairs={{0,8},{2,10},{4,12},{6,14},{8,0},{10,2},{12,4},{14,6},{1,9},{3,11}... | collective-permute-start | bytes 442376 | tf_op jit(solution)/shard_map/ppermute | solution.py:63
  40.5 20.9 %collective-permute-start.14 = (bf16[64,1152]{1,0:T(8,128)(2,1)S(1)}, bf16[64,1152]{1,0:T(8,128)(2,1)S(1)}, u32[]{:S(2)}, u32[]{:S(2)}) collective-permute-start(bf16[64,1152]{1,0:T(8,128)(2,1)S(1)} %get-tuple-element.79.refs_0_), channel_id=1, source_target_pairs={{0,12},{2,14},{4,8},{6,10},{8,4},{10,6},{12,0},{14,2},{1,13},{3,15... | collective-permute-start | bytes 442376 | tf_op jit(solution)/shard_map/ppermute | solution.py:63
  42.9 17.0 %collective-permute-start.13 = (bf16[208,1024]{1,0:T(8,128)(2,1)S(1)}, bf16[208,1024]{1,0:T(8,128)(2,1)S(1)}, u32[]{:S(2)}, u32[]{:S(2)}) collective-permute-start(bf16[208,1024]{1,0:T(8,128)(2,1)S(1)} %shard_map.177), channel_id=1, source_target_pairs={{0,2},{2,0},{4,6},{6,4},{8,10},{10,8},{12,14},{14,12},{1,3},{3,1},... | collective-permute-start | bytes 1277960 | tf_op jit(solution)/shard_map/ppermute | solution.py:63
  45.9 16.6 %collective-permute-start.19 = (bf16[64,1024]{1,0:T(8,128)(2,1)S(1)}, bf16[64,1024]{1,0:T(8,128)(2,1)S(1)}, u32[]{:S(2)}, u32[]{:S(2)}) collective-permute-start(bf16[64,1024]{1,0:T(8,128)(2,1)S(1)} %shard_map.181), channel_id=1, source_target_pairs={{0,12},{2,14},{4,8},{6,10},{8,4},{10,6},{12,0},{14,2},{1,13},{3,15... | collective-permute-start | bytes 393224 | tf_op jit(solution)/shard_map/ppermute | solution.py:63
  52.4 7.5 %copy-start = (bf16[1024,1024]{1,0:T(8,128)(2,1)S(1)}, bf16[1024,1024]{1,0:T(8,128)(2,1)}, u32[]{:S(2)}) copy-start(bf16[1024,1024]{1,0:T(8,128)(2,1)} %w_msg_ref.1) | copy-start | bytes 6291460
  52.4 9.1 %collective-permute-start.17 = (bf16[144,1024]{1,0:T(8,128)(2,1)S(1)}, bf16[144,1024]{1,0:T(8,128)(2,1)S(1)}, u32[]{:S(2)}, u32[]{:S(2)}) collective-permute-start(bf16[144,1024]{1,0:T(8,128)(2,1)S(1)} %shard_map.179), channel_id=1, source_target_pairs={{0,4},{2,6},{4,0},{6,2},{8,12},{10,14},{12,8},{14,10},{1,5},{3,7},... | collective-permute-start | bytes 884744 | tf_op jit(solution)/shard_map/ppermute | solution.py:63
  53.7 11.4 %collective-permute-start.20 = (bf16[64,1024]{1,0:T(8,128)(2,1)S(1)}, bf16[64,1024]{1,0:T(8,128)(2,1)S(1)}, u32[]{:S(2)}, u32[]{:S(2)}) collective-permute-start(bf16[64,1024]{1,0:T(8,128)(2,1)S(1)} %shard_map.183), channel_id=1, source_target_pairs={{0,8},{2,10},{4,12},{6,14},{8,0},{10,2},{12,4},{14,6},{1,9},{3,11}... | collective-permute-start | bytes 393224 | tf_op jit(solution)/shard_map/ppermute | solution.py:63
